TPU v7x, 32 devices: a whole 2x2x4 slice. The times are simulated.
32 devices in a mesh: dp: 4 (over z), leaf: 8 (over y, x, core).
Axes of the slice: x: 2, y: 2, z: 4, core: 2. Of those that a mesh axis runs over, the one named last changes fastest.
Arguments:
- queries: bfloat16 [64, 128, 1024], P(('dp', 'leaf')), parts along dimension 0, may hold values from -99 to 99
- key_states: bfloat16 [64, 128, 128], P(('dp', 'leaf')), parts along dimension 0, may hold values from -4 to 4
- value_states: bfloat16 [64, 128, 128], P(('dp', 'leaf')), parts along dimension 0, may hold values from -6 to 6
- grad_output: bfloat16 [64, 128, 1024], P(('dp', 'leaf')), parts along dimension 0, may hold values from -120 to 120
- lengths: int32 [64], P(('dp', 'leaf')), parts along dimension 0, may hold values from 16 to 128, as said below
Outputs:
- grad_queries: bfloat16 [64, 128, 1024], P(('dp', 'leaf')), parts along dimension 0
- grad_keys: bfloat16 [64, 128, 128], P(('dp', 'leaf')), parts along dimension 0
- grad_values: bfloat16 [64, 128, 128], P(('dp', 'leaf')), parts along dimension 0
There are 4 independent parts, one for each index of `dp`. A program takes and returns all parts, laid end to end along the dimension named above; each array names one. Nothing has to cross between parts.
Inputs may be any that keep to these rules, and one draw needn't show every extreme that they name: `lengths`: every entry is at least 1; entry 0 (the prompt) is always 128.
All inputs are finite; a program needn't handle non-finite values.
Results may differ from a plain program's by a relative error of at most 0.0095.
Values may be sent and summed in bfloat16 or wider, within the bound.
No kernel may reach another device: no remote copies, remote signals or barrier semaphores. Data moves between devices by JAX's collectives and lax.ppermute only.
A program may use at most 64 MiB of HBM per device.

v0:
```python
import jax
import jax.numpy as jnp
from jax import lax
from jax.sharding import PartitionSpec as P


def partner(block, axis, bit):
    count = lax.axis_size(axis)
    route = []
    for low in range(count):
        high = low | 1 << bit
        if high != low and high < count:
            route += [(low, high), (high, low)]
    return lax.ppermute(block, axis, route)


def build_mask(query_level, query_length, path_length, seg_rows):
    path_slots = path_length.shape[0]
    levels = jnp.arange(path_slots, dtype=jnp.int32)[:, None]
    position = jnp.arange(seg_rows, dtype=jnp.int32)
    key_live = position[None, :] < path_length[:, None]
    before = (levels < query_level) & key_live
    same_level = (levels == query_level) & (position[None, :] < query_length)
    causal = position[None, None, :] <= position[:, None, None]
    allowed = before[None] | same_level[None] & causal
    return allowed.reshape(seg_rows, path_slots * seg_rows)


def attend_grad(query_block, grad_block, path_keys, path_values, allowed, head_count):
    query_rows = query_block.shape[0]
    head_width = path_keys.shape[-1]
    score_scale = head_width ** (-0.5)
    query_heads = query_block.reshape(query_rows, head_count, head_width)
    grad_heads = grad_block.reshape(query_rows, head_count, head_width)
    key_flat = path_keys.reshape(-1, head_width)
    value_flat = path_values.reshape(-1, head_width)
    scores = (
        jnp.einsum("qhd,kd->hqk", query_heads, key_flat, preferred_element_type=jnp.float32)
        * score_scale
    )
    scores = jnp.where(allowed[None], scores, -1e30)
    row_top = jnp.max(scores, axis=2, keepdims=True)
    row_total = jnp.sum(jnp.exp(scores - row_top), axis=2, keepdims=True)
    weights = jnp.exp(scores - (row_top + jnp.log(row_total)))
    weights_low = weights.astype(jnp.bfloat16)
    output = jnp.einsum("hqk,kd->qhd", weights_low, value_flat, preferred_element_type=jnp.float32)
    row_delta = jnp.sum(grad_heads.astype(jnp.float32) * output, axis=2)
    grad_value_terms = jnp.einsum(
        "hqk,qhd->kd", weights_low, grad_heads, preferred_element_type=jnp.float32
    )
    grad_weights = jnp.einsum(
        "qhd,kd->hqk", grad_heads, value_flat, preferred_element_type=jnp.float32
    )
    grad_scores = (weights * (grad_weights - row_delta.T[:, :, None]) * score_scale).astype(
        jnp.bfloat16
    )
    grad_query_block = jnp.einsum(
        "hqk,kd->qhd", grad_scores, key_flat, preferred_element_type=jnp.float32
    )
    grad_query_block = grad_query_block.reshape(query_rows, head_count * head_width).astype(
        jnp.bfloat16
    )
    grad_key_terms = jnp.einsum(
        "hqk,qhd->kd", grad_scores, query_heads, preferred_element_type=jnp.float32
    )
    return (
        grad_query_block,
        grad_key_terms.reshape(path_keys.shape),
        grad_value_terms.reshape(path_keys.shape),
    )


def body(queries, key_states, value_states, grad_output, lengths):
    leaf_count = lax.axis_size("leaf")
    tree_depth = leaf_count.bit_length() - 1
    leaf_index = lax.axis_index("leaf")
    seg_rows = key_states.shape[1]
    head_width = key_states.shape[2]
    head_count = queries.shape[2] // head_width
    owner_list = [jnp.zeros((), jnp.int32)]
    for depth_level in range(1, tree_depth + 1):
        shift_by = tree_depth - depth_level + 1
        owner_list.append((leaf_index >> shift_by << shift_by) + (1 << tree_depth - depth_level))
    owners = jnp.stack(owner_list)
    trailing = jnp.zeros((), jnp.int32)
    for bit_place in range(tree_depth):
        trailing = trailing + (leaf_index & (2 << bit_place) - 1 == 0).astype(jnp.int32)
    own_level = tree_depth - trailing
    all_keys, all_values, all_lengths = (
        lax.all_gather(key_states[0:1], "leaf", axis=0, tiled=True),
        lax.all_gather(value_states[0:1], "leaf", axis=0, tiled=True),
        lax.all_gather(lengths[0:1], "leaf", axis=0, tiled=True),
    )
    inner_keys = jnp.take(all_keys, owners, axis=0)
    inner_values = jnp.take(all_values, owners, axis=0)
    inner_lengths = jnp.take(all_lengths, owners, axis=0)
    path_keys = jnp.concatenate([inner_keys, key_states[1:2]], 0)
    path_values = jnp.concatenate([inner_values, value_states[1:2]], 0)
    path_length = jnp.concatenate([inner_lengths, lengths[1:2]], 0)
    position = jnp.arange(seg_rows, dtype=jnp.int32)
    query_levels = (own_level, jnp.asarray(tree_depth + 1, jnp.int32))
    grad_query_list = []
    key_terms = jnp.zeros(path_keys.shape, jnp.float32)
    value_terms = jnp.zeros(path_keys.shape, jnp.float32)
    for segment in range(2):
        allowed = build_mask(query_levels[segment], lengths[segment], path_length, seg_rows)
        live_rows = (position < lengths[segment])[:, None]
        cotangent = jnp.where(live_rows, grad_output[segment], jnp.zeros((), jnp.bfloat16))
        grad_query_block, grad_key_terms, grad_value_terms = attend_grad(
            queries[segment], cotangent, path_keys, path_values, allowed, head_count
        )
        grad_query_list.append(grad_query_block)
        key_terms = key_terms + grad_key_terms
        value_terms = value_terms + grad_value_terms
    inner_key_terms = key_terms[: tree_depth + 1]
    inner_value_terms = value_terms[: tree_depth + 1]
    for bit_place in range(tree_depth):
        shared_count = tree_depth - bit_place + 1
        other_keys, other_values = partner(
            (inner_key_terms[:shared_count], inner_value_terms[:shared_count]), "leaf", bit_place
        )
        inner_key_terms = jnp.concatenate(
            [inner_key_terms[:shared_count] + other_keys, inner_key_terms[shared_count:]], 0
        )
        inner_value_terms = jnp.concatenate(
            [inner_value_terms[:shared_count] + other_values, inner_value_terms[shared_count:]], 0
        )
    own_key_grad = lax.dynamic_index_in_dim(inner_key_terms, own_level, 0, keepdims=False)
    own_value_grad = lax.dynamic_index_in_dim(inner_value_terms, own_level, 0, keepdims=False)
    grad_queries = jnp.stack(grad_query_list, 0)
    grad_keys = jnp.stack([own_key_grad, key_terms[tree_depth + 1]], 0).astype(jnp.bfloat16)
    grad_values = jnp.stack([own_value_grad, value_terms[tree_depth + 1]], 0).astype(jnp.bfloat16)
    return (grad_queries, grad_keys, grad_values)


def solution(mesh):
    placed = (
        P(("dp", "leaf"), None, None),
        P(("dp", "leaf"), None, None),
        P(("dp", "leaf"), None, None),
        P(("dp", "leaf"), None, None),
        P(("dp", "leaf")),
    )
    return jax.shard_map(
        body,
        mesh=mesh,
        in_specs=placed,
        out_specs=(
            P(("dp", "leaf"), None, None),
            P(("dp", "leaf"), None, None),
            P(("dp", "leaf"), None, None),
        ),
        check_vma=False,
    )
```

profile of v0, /device:TPU:0, one launch (start us, length us, event | category | flops | bytes accessed | tf_op | source)
XLA Modules:
  0.0 83.7 jit_solution(17599752861054450327)
XLA Ops:
  0.6 1.2 %dynamic-slice = u32[1]{0:T(128)} dynamic-slice(u32[32]{0:T(128)} %constant.69, u32[]{:T(128)S(6)} %add.98), dynamic_slice_sizes={1} | dynamic-slice | bytes 12
  1.9 2.0 %fusion.91 = (s32[1]{0:T(128)}, s32[8]{0:T(128)S(1)}, s32[1]{0:T(128)}) fusion(s32[2]{0:T(128)} %param.11, s32[8]{0:T(128)S(1)} %broadcast.269, u32[]{:T(128)} %bitcast.7), kind=kLoop, calls=%fused_computation.141 | loop fusion | bytes 52 | tf_op jit(solution)/shard_map/slice | solution.py:92
  3.9 9.5 %all-reduce = s32[8]{0:T(128)S(1)} all-reduce(s32[8]{0:T(128)S(1)} %get-tuple-element.25), channel_id=1, replica_groups=mesh['dp'=4,'leaf'=8] {'leaf'}, use_global_device_ids=true, to_apply=%add | all-reduce | flops 8 | bytes 64
  14.3 0.8 fusion.90
  15.0 0.8 fusion.89
  15.8 8.6 %all_gather.11 = bf16[8,128,128]{2,1,0:T(8,128)(2,1)S(1)} all-gather(bf16[1,128,128]{2,1,0:T(8,128)(2,1)S(1)} %get-tuple-element.18), channel_id=1, replica_groups=mesh['dp'=4,'leaf'=8] {'leaf'}, dimensions={0}, use_global_device_ids=true | all-gather | bytes 294912 | tf_op jit(solution)/shard_map/all_gather | solution.py:91
  24.5 9.0 %all_gather.9 = bf16[8,128,128]{2,1,0:T(8,128)(2,1)S(1)} all-gather(bf16[1,128,128]{2,1,0:T(8,128)(2,1)S(1)} %get-tuple-element.20), channel_id=1, replica_groups=mesh['dp'=4,'leaf'=8] {'leaf'}, dimensions={0}, use_global_device_ids=true | all-gather | bytes 294912 | tf_op jit(solution)/shard_map/all_gather | solution.py:90
  35.4 1.8 %fusion.88 = (bf16[1,128,1024]{2,1,0:T(8,128)(2,1)}, bf16[1,128,1024]{2,1,0:T(8,128)(2,1)S(1)}) fusion(bf16[2,128,1024]{2,1,0:T(8,128)(2,1)} %param.7), kind=kLoop, calls=%fused_computation.138 | loop fusion | bytes 1048576 | tf_op jit(solution)/shard_map/slice | solution.py:110
  37.4 1.3 %iota_compare_fusion.1 = (pred[128]{0:T(512)(128)(4,1)S(1)}, pred[128]{0:T(512)(128)(4,1)S(1)}) fusion(s32[]{:T(128)} %bitcast.31, s32[]{:T(128)} %bitcast.13), kind=kLoop, calls=%fused_computation.113 | loop fusion | flops 256 | bytes 264 | tf_op jit(solution)/shard_map/lt | solution.py:23
  41.4 1.0 %fusion.87 = (bf16[1,128,1024]{2,1,0:T(8,128)(2,1)}, bf16[16,8,8,128]{3,1,2,0:T(8,128)(2,1)}, bf16[16,8,8,128]{3,1,2,0:T(8,128)(2,1)S(1)}, bf16[1,128,1024]{2,1,0:T(8,128)(2,1)}) fusion(bf16[2,128,1024]{2,1,0:T(8,128)(2,1)S(1)} %copy-done.9, pred[128]{0:T(512)(128)(4,1)S(1)} %get-tuple-element.40, pred[128]{0:T(512)(128)(4,1)S(1)} %get-tuple-element.39), kind=kLoop, calls=%fused_computation.137 | loop fusion | flops 262144 | bytes 1573120 | tf_op jit(solution)/shard_map/slice | solution.py:108
  42.3 1.8 %copy.65 = bf16[1,128,1024]{1,2,0:T(8,128)(2,1)} copy(bf16[1,128,1024]{2,1,0:T(8,128)(2,1)} %get-tuple-element.15) | data formatting | bytes 524288 | tf_op jit(solution)/shard_map/slice | solution.py:108
  44.1 0.8 copy.105
  44.9 1.1 %copy.102 = bf16[1,128,1024]{1,2,0:T(8,128)(2,1)S(1)} copy(bf16[1,128,1024]{2,1,0:T(8,128)(2,1)} %get-tuple-element.16) | data formatting | bytes 524288
  46.5 1.5 %copy-done = f32[640,128,8]{1,0,2:T(8,128)} copy-done((f32[640,128,8]{1,0,2:T(8,128)}, f32[640,128,8]{1,0,2:T(8,128)S(1)}, u32[]{:S(2)}) %copy-start) | copy-done | bytes 2621464
  48.6 1.8 %copy.57 = bf16[1,128,1024]{1,2,0:T(8,128)(2,1)} copy(bf16[1,128,1024]{2,1,0:T(8,128)(2,1)} %get-tuple-element.12) | data formatting | bytes 524288 | tf_op jit(solution)/shard_map/slice | solution.py:108
  50.4 1.1 %copy.104 = bf16[16,8,8,128]{3,2,1,0:T(8,128)(2,1)S(1)} copy(bf16[16,8,8,128]{3,1,2,0:T(8,128)(2,1)} %get-tuple-element.13) | data formatting | bytes 524288
  51.5 1.8 %fusion.50 = f32[128,8]{0,1:T(8,128)S(1)} fusion(bf16[640,128,1]{1,0,2:T(8,128)(2,1)} %bitcast.240, f32[640,128,8]{1,0,2:T(8,128)S(1)} %get-tuple-element.30, f32[8,128]{1,0:T(8,128)S(1)} %log_add_fusion, pred[128,640]{0,1:T(8,128)(4,1)} %copy-done.2, bf16[128,8,128]{0,2,1:T(8,128)(2,1)} %bitcast.250, pred[128]{0:T(512)(128)(4,1)S(1)} %get-tuple-element.39), kind=kOutput, calls=%fused_computation.53 | convolution fusion | flops 170916864 | bytes 3137664 | tf_op jit(solution)/shard_map/hqk,kd->qhd/dot_general | solution.py:46
  53.5 1.8 %fusion.53 = f32[128,8]{0,1:T(8,128)S(1)} fusion(bf16[640,128,1]{1,0,2:T(8,128)(2,1)} %bitcast.241, f32[640,128,8]{1,0,2:T(8,128)S(1)} %copy-done.1, f32[8,128]{1,0:T(8,128)S(1)} %log_add_fusion.1, pred[128,640]{0,1:T(8,128)(4,1)S(1)} %get-tuple-element.22, bf16[128,8,128]{0,2,1:T(8,128)(2,1)S(1)} %bitcast.244, pred[128]{0:T(512)(128)(4,1)S(1)} %get-tuple-element.40), kind=kOutput, calls=%fused_computation.54 | convolution fusion | flops 170916864 | bytes 3137664 | tf_op jit(solution)/shard_map/hqk,kd->qhd/dot_general | solution.py:46
  55.3 1.1 %fusion.17 = (bf16[640,8,128]{2,0,1:T(8,128)(2,1)S(1)}, bf16[640,8,128]{2,0,1:T(8,128)(2,1)S(1)}, f32[640,128,8]{1,0,2:T(8,128)S(1)}) fusion(f32[640,128,8]{1,0,2:T(8,128)S(1)} %get-tuple-element.30, f32[8,128]{1,0:T(8,128)S(1)} %log_add_fusion, pred[640,128]{1,0:T(8,128)(4,1)S(1)} %bitcast.239, f32[8,128]{1,0:T(8,128)S(1)} %bitcast.254, ...), kind=kOutput, calls=%fused_computation.32 | convolution fusion | flops 173015040 | bytes 8380416 | tf_op jit(solution)/shard_map/qhd,kd->hqk/dot_general | solution.py:51
  56.9 1.1 %fusion.16 = (bf16[640,8,128]{2,0,1:T(8,128)(2,1)S(1)}, bf16[640,8,128]{2,0,1:T(8,128)(2,1)S(1)}, f32[640,128,8]{1,0,2:T(8,128)S(1)}) fusion(f32[640,128,8]{1,0,2:T(8,128)S(1)} %copy-done.1, f32[8,128]{1,0:T(8,128)S(1)} %log_add_fusion.1, pred[640,128]{1,0:T(8,128)(4,1)S(1)} %bitcast.238, f32[8,128]{1,0:T(8,128)S(1)} %bitcast.252, ...), kind=kOutput, calls=%fused_computation.31 | convolution fusion | flops 173015040 | bytes 8380416 | tf_op jit(solution)/shard_map/qhd,kd->hqk/dot_general | solution.py:51
  61.5 1.7 %fusion.44 = bf16[128,8,128]{2,0,1:T(8,128)(2,1)} fusion(bf16[640,128,1]{1,0,2:T(8,128)(2,1)S(1)} %bitcast.232, f32[640,128,8]{1,0,2:T(8,128)S(1)} %get-tuple-element.33, f32[640,128,8]{1,0,2:T(8,128)S(1)} %get-tuple-element.30, f32[8,128]{1,0:T(8,128)S(1)} %bitcast.255, f32[8,128]{1,0:T(8,128)S(1)} %log_add_fusion, pred[128,640]{0,1:T(8,128)(4,1)S(1)} %copy-done.3), kind=kOutput, calls=%fused_computation.47 | convolution fusion | flops 172490752 | bytes 5758976 | tf_op jit(solution)/shard_map/hqk,kd->qhd/dot_general | solution.py:57
  63.2 1.0 %fusion.47 = bf16[128,8,128]{2,0,1:T(8,128)(2,1)S(1)} fusion(bf16[640,128,1]{1,0,2:T(8,128)(2,1)S(1)} %bitcast.233, f32[640,128,8]{1,0,2:T(8,128)S(1)} %get-tuple-element.34, f32[640,128,8]{1,0,2:T(8,128)S(1)} %copy-done.1, f32[8,128]{1,0:T(8,128)S(1)} %bitcast.253, f32[8,128]{1,0:T(8,128)S(1)} %log_add_fusion.1, pred[128,640]{0,1:T(8,128)(4,1)S(1)} %get-tuple-element.22), kind=kOutput, calls=%fused_computation.48 | convolution fusion | flops 172490752 | bytes 5758976 | tf_op jit(solution)/shard_map/hqk,kd->qhd/dot_general | solution.py:57
  64.6 0.8 %pad_maximum_fusion = bf16[2,128,1024]{2,1,0:T(8,128)(2,1)} fusion(bf16[1,128,1024]{2,1,0:T(8,128)(2,1)S(1)} %copy.71, bf16[1,128,1024]{2,1,0:T(8,128)(2,1)S(1)} %copy.70), kind=kLoop, calls=%fused_computation.57 | loop fusion | flops 262144 | bytes 1048576 | tf_op jit(solution)/shard_map/stack | solution.py:130
  65.4 1.0 %slice_add_fusion.5 = f32[4,128,128]{2,1,0:T(8,128)S(1)} fusion(f32[4,128,128]{2,1,0:T(8,128)} %collective-permute-done, f32[5,128,128]{2,1,0:T(8,128)S(1)} %fusion.56), kind=kLoop, calls=%fused_computation.136 | loop fusion | flops 65536 | bytes 786432 | tf_op jit(solution)/shard_map/add | solution.py:123
  66.4 0.9 %collective-permute-start.1 = (f32[3,128,128]{2,1,0:T(8,128)S(1)}, f32[3,128,128]{2,1,0:T(8,128)S(1)}, u32[]{:S(2)}, u32[]{:S(2)}) collective-permute-start(f32[3,128,128]{2,1,0:T(8,128)S(1)} %slice.105), channel_id=1, source_target_pairs={{0,2},{2,0},{1,3},{3,1},{4,6},{6,4},{5,7},{7,5},{8,10},{10,8},{9,1... | collective-permute-start | bytes 589832 | tf_op jit(solution)/shard_map/ppermute | solution.py:14
  67.4 1.0 %slice_add_fusion.4 = f32[4,128,128]{2,1,0:T(8,128)S(1)} fusion(f32[4,128,128]{2,1,0:T(8,128)} %collective-permute-done.3, f32[5,128,128]{2,1,0:T(8,128)S(1)} %fusion.57), kind=kLoop, calls=%fused_computation.135 | loop fusion | flops 65536 | bytes 786432 | tf_op jit(solution)/shard_map/add | solution.py:126
  68.4 1.2 %collective-permute-start.4 = (f32[3,128,128]{2,1,0:T(8,128)S(1)}, f32[3,128,128]{2,1,0:T(8,128)S(1)}, u32[]{:S(2)}, u32[]{:S(2)}) collective-permute-start(f32[3,128,128]{2,1,0:T(8,128)S(1)} %slice.110), channel_id=1, source_target_pairs={{0,2},{2,0},{1,3},{3,1},{4,6},{6,4},{5,7},{7,5},{8,10},{10,8},{9,1... | collective-permute-start | bytes 589832 | tf_op jit(solution)/shard_map/ppermute | solution.py:14
  69.6 4.6 %collective-permute-done.1 = f32[3,128,128]{2,1,0:T(8,128)S(1)} collective-permute-done((f32[3,128,128]{2,1,0:T(8,128)S(1)}, f32[3,128,128]{2,1,0:T(8,128)S(1)}, u32[]{:S(2)}, u32[]{:S(2)}) %collective-permute-start.1) | collective-permute-done | bytes 196640 | tf_op jit(solution)/shard_map/ppermute | solution.py:14
  74.3 0.9 %collective-permute-start.2 = (f32[2,128,128]{2,1,0:T(8,128)S(1)}, f32[2,128,128]{2,1,0:T(8,128)S(1)}, u32[]{:S(2)}, u32[]{:S(2)}) collective-permute-start(f32[2,128,128]{2,1,0:T(8,128)S(1)} %slice.106), channel_id=1, source_target_pairs={{0,4},{4,0},{1,5},{5,1},{2,6},{6,2},{3,7},{7,3},{8,12},{12,8},{9,1... | collective-permute-start | bytes 393224 | tf_op jit(solution)/shard_map/ppermute | solution.py:14
  75.2 2.7 %collective-permute-done.4 = f32[3,128,128]{2,1,0:T(8,128)S(1)} collective-permute-done((f32[3,128,128]{2,1,0:T(8,128)S(1)}, f32[3,128,128]{2,1,0:T(8,128)S(1)}, u32[]{:S(2)}, u32[]{:S(2)}) %collective-permute-start.4) | collective-permute-done | bytes 196640 | tf_op jit(solution)/shard_map/ppermute | solution.py:14
  77.9 0.9 %collective-permute-start.5 = (f32[2,128,128]{2,1,0:T(8,128)S(1)}, f32[2,128,128]{2,1,0:T(8,128)S(1)}, u32[]{:S(2)}, u32[]{:S(2)}) collective-permute-start(f32[2,128,128]{2,1,0:T(8,128)S(1)} %slice.111), channel_id=1, source_target_pairs={{0,4},{4,0},{1,5},{5,1},{2,6},{6,2},{3,7},{7,3},{8,12},{12,8},{9,1... | collective-permute-start | bytes 393224 | tf_op jit(solution)/shard_map/ppermute | solution.py:14
  80.0 2.9 %collective-permute-done.5 = f32[2,128,128]{2,1,0:T(8,128)S(1)} collective-permute-done((f32[2,128,128]{2,1,0:T(8,128)S(1)}, f32[2,128,128]{2,1,0:T(8,128)S(1)}, u32[]{:S(2)}, u32[]{:S(2)}) %collective-permute-start.5) | collective-permute-done | bytes 131104 | tf_op jit(solution)/shard_map/ppermute | solution.py:14
  (77 shorter events, 12.9 us)
Async XLA Ops:
  40.2 4.6 %copy-start.2 = (pred[128,640]{0,1:T(8,128)(4,1)}, pred[128,640]{0,1:T(8,128)(4,1)S(1)}, u32[]{:S(2)}) copy-start(pred[128,640]{0,1:T(8,128)(4,1)S(1)} %get-tuple-element.23) | copy-start | bytes 245764
  40.2 1.1 %copy-start.9 = (bf16[2,128,1024]{2,1,0:T(8,128)(2,1)S(1)}, bf16[2,128,1024]{2,1,0:T(8,128)(2,1)}, u32[]{:S(2)}) copy-start(bf16[2,128,1024]{2,1,0:T(8,128)(2,1)} %param.10) | copy-start | bytes 1572868
  46.5 1.5 %copy-start = (f32[640,128,8]{1,0,2:T(8,128)}, f32[640,128,8]{1,0,2:T(8,128)S(1)}, u32[]{:S(2)}) copy-start(f32[640,128,8]{1,0,2:T(8,128)S(1)} %get-tuple-element.32) | copy-start | bytes 7864324
  50.4 3.0 %copy-start.1 = (f32[640,128,8]{1,0,2:T(8,128)S(1)}, f32[640,128,8]{1,0,2:T(8,128)}, u32[]{:S(2)}) copy-start(f32[640,128,8]{1,0,2:T(8,128)} %copy-done) | copy-start | bytes 7864324
  50.4 3.0 %copy-start.5 = (bf16[1,128,1024]{1,2,0:T(8,128)(2,1)S(1)}, bf16[1,128,1024]{1,2,0:T(8,128)(2,1)}, u32[]{:S(2)}) copy-start(bf16[1,128,1024]{1,2,0:T(8,128)(2,1)} %copy.57) | copy-start | bytes 786436
  53.4 1.8 %copy-start.3 = (pred[128,640]{0,1:T(8,128)(4,1)S(1)}, pred[128,640]{0,1:T(8,128)(4,1)}, u32[]{:S(2)}) copy-start(pred[128,640]{0,1:T(8,128)(4,1)} %copy-done.2) | copy-start | bytes 245764
  53.4 1.8 %copy-start.4 = (bf16[5,128,128]{2,1,0:T(8,128)(2,1)S(1)}, bf16[5,128,128]{2,1,0:T(8,128)(2,1)}, u32[]{:S(2)}) copy-start(bf16[5,128,128]{2,1,0:T(8,128)(2,1)} %get-tuple-element.36) | copy-start | bytes 491524
  53.4 1.8 %copy-start.6 = (bf16[16,8,8,128]{3,2,1,0:T(8,128)(2,1)S(1)}, bf16[16,8,8,128]{3,2,1,0:T(8,128)(2,1)}, u32[]{:S(2)}) copy-start(bf16[16,8,8,128]{3,2,1,0:T(8,128)(2,1)} %copy.105) | copy-start | bytes 786436
  58.0 1.6 %copy-start.8 = (bf16[1,128,1024]{1,2,0:T(8,128)(2,1)S(1)}, bf16[1,128,1024]{1,2,0:T(8,128)(2,1)}, u32[]{:S(2)}) copy-start(bf16[1,128,1024]{1,2,0:T(8,128)(2,1)} %copy.65) | copy-start | bytes 786436
  59.2 6.2 %collective-permute-start = (f32[4,128,128]{2,1,0:T(8,128)}, f32[4,128,128]{2,1,0:T(8,128)}, u32[]{:S(2)}, u32[]{:S(2)}) collective-permute-start(f32[4,128,128]{2,1,0:T(8,128)} %slice.104), channel_id=1, source_target_pairs={{0,1},{1,0},{2,3},{3,2},{4,5},{5,4},{6,7},{7,6},{8,9},{9,8},{10,11... | collective-permute-start | bytes 786440 | tf_op jit(solution)/shard_map/ppermute | solution.py:14
  61.3 6.1 %collective-permute-start.3 = (f32[4,128,128]{2,1,0:T(8,128)}, f32[4,128,128]{2,1,0:T(8,128)}, u32[]{:S(2)}, u32[]{:S(2)}) collective-permute-start(f32[4,128,128]{2,1,0:T(8,128)} %slice.109), channel_id=1, source_target_pairs={{0,1},{1,0},{2,3},{3,2},{4,5},{5,4},{6,7},{7,6},{8,9},{9,8},{10,11... | collective-permute-start | bytes 786440 | tf_op jit(solution)/shard_map/ppermute | solution.py:14
  63.2 1.0 %copy-start.7 = (bf16[128,8,128]{2,0,1:T(8,128)(2,1)S(1)}, bf16[128,8,128]{2,0,1:T(8,128)(2,1)}, u32[]{:S(2)}) copy-start(bf16[128,8,128]{2,0,1:T(8,128)(2,1)} %fusion.44) | copy-start | bytes 786436
  66.4 7.8 %collective-permute-start.1 = (f32[3,128,128]{2,1,0:T(8,128)S(1)}, f32[3,128,128]{2,1,0:T(8,128)S(1)}, u32[]{:S(2)}, u32[]{:S(2)}) collective-permute-start(f32[3,128,128]{2,1,0:T(8,128)S(1)} %slice.105), channel_id=1, source_target_pairs={{0,2},{2,0},{1,3},{3,1},{4,6},{6,4},{5,7},{7,5},{8,10},{10,8},{9,1... | collective-permute-start | bytes 589832 | tf_op jit(solution)/shard_map/ppermute | solution.py:14
  68.4 9.5 %collective-permute-start.4 = (f32[3,128,128]{2,1,0:T(8,128)S(1)}, f32[3,128,128]{2,1,0:T(8,128)S(1)}, u32[]{:S(2)}, u32[]{:S(2)}) collective-permute-start(f32[3,128,128]{2,1,0:T(8,128)S(1)} %slice.110), channel_id=1, source_target_pairs={{0,2},{2,0},{1,3},{3,1},{4,6},{6,4},{5,7},{7,5},{8,10},{10,8},{9,1... | collective-permute-start | bytes 589832 | tf_op jit(solution)/shard_map/ppermute | solution.py:14
  74.3 5.0 %collective-permute-start.2 = (f32[2,128,128]{2,1,0:T(8,128)S(1)}, f32[2,128,128]{2,1,0:T(8,128)S(1)}, u32[]{:S(2)}, u32[]{:S(2)}) collective-permute-start(f32[2,128,128]{2,1,0:T(8,128)S(1)} %slice.106), channel_id=1, source_target_pairs={{0,4},{4,0},{1,5},{5,1},{2,6},{6,2},{3,7},{7,3},{8,12},{12,8},{9,1... | collective-permute-start | bytes 393224 | tf_op jit(solution)/shard_map/ppermute | solution.py:14
  77.9 5.0 %collective-permute-start.5 = (f32[2,128,128]{2,1,0:T(8,128)S(1)}, f32[2,128,128]{2,1,0:T(8,128)S(1)}, u32[]{:S(2)}, u32[]{:S(2)}) collective-permute-start(f32[2,128,128]{2,1,0:T(8,128)S(1)} %slice.111), channel_id=1, source_target_pairs={{0,4},{4,0},{1,5},{5,1},{2,6},{6,2},{3,7},{7,3},{8,12},{12,8},{9,1... | collective-permute-start | bytes 393224 | tf_op jit(solution)/shard_map/ppermute | solution.py:14
where the time goes:
time: 84.2 us; the launch traced here: 83.7 us
  blocking collectives  27.1 us (32%)
  local copies, waits for them, and re-layouts  18.6 us (22%)
  matrix products  11.6 us (14%)
  waiting for transfers between devices  10.7 us (13%)
  other arithmetic  10.1 us (12%)
  starting transfers between devices  4.53 us (5%)
  between operations  1.08 us (1%)
    ppermute x6, waiting for transfers between devices, partner(): return lax.ppermute(block, axis, route)  10.7 us
    unnamed x1, blocking collectives  9.46 us
    all_gather x1, blocking collectives, body(): lax.all_gather(key_states[0:1], 'leaf', axis=0, tiled=True)  8.95 us
    all_gather x1, blocking collectives, body(): lax.all_gather(value_states[0:1], 'leaf', axis=0, tiled=True)  8.64 us
    unnamed x26, local copies, waits for them, and re-layouts  5.98 us
    ppermute x6, starting transfers between devices, partner(): return lax.ppermute(block, axis, route)  4.53 us
    dot_general x2, matrix products, attend_grad(): jnp.einsum('hqk,kd->qhd', weights_low, value_flat, preferred_element_type...  3.61 us
    slice x2, local copies, waits for them, and re-layouts, body(): grad_output[segment]  3.58 us
  transfers between devices with their start and end apart: 6, of which 4 were waited for; matrix products, arithmetic and copies ran while one was open for 10% of the time, Pallas kernels for 0%

commit v1 on v0

v1 whole, which is shorter than its diff:
```python
import functools

import jax
import jax.numpy as jnp
from jax import lax
from jax.experimental import pallas as pl
from jax.experimental.pallas import tpu as pltpu
from jax.sharding import PartitionSpec as P

BF16 = jnp.bfloat16
F32 = jnp.float32
TAIL = 16
BIG = -1e30
LOG2E = 1.4426950408889634
NT = (((1,), (1,)), ((), ()))
NN = (((1,), (0,)), ((), ()))


def depth_of(count):
    return count.bit_length() - 1


def trailing_zeros(index, depth):
    total = jnp.zeros((), jnp.int32)
    for bit in range(depth):
        total = total + jnp.where((index & ((2 << bit) - 1)) == 0, 1, 0)
    return total


def owner_of(index, level, depth):
    if level == 0:
        return index * 0
    shift = depth - level + 1
    return ((index >> shift) << shift) + (1 << (depth - level))


def on_path(reader, owner, depth):
    return any(owner_of(reader, level, depth) == owner for level in range(depth + 1))


def down_pairs(mask, count):
    depth = depth_of(count)
    pairs = []
    for owner in range(0, count, 2):
        reader = owner ^ (mask << 1)
        if on_path(reader, owner, depth):
            pairs.append((owner, reader))
    return pairs


def pack_kernel(lengths_ref, key_ref, value_ref, pack_ref):
    rows = key_ref.shape[1]
    pack_ref[0:rows, :] = key_ref[0]
    pack_ref[rows : 2 * rows, :] = value_ref[0]
    length = lengths_ref[0].astype(F32)
    pack_ref[2 * rows :, :] = jnp.full((TAIL, pack_ref.shape[1]), length, F32).astype(BF16)


def make_pack(lengths, keys, values):
    rows, width = keys.shape[1:]
    first = pl.BlockSpec((1, rows, width), lambda step: (0, 0, 0))
    return pl.pallas_call(
        pack_kernel,
        grid=(1,),
        out_shape=jax.ShapeDtypeStruct((2 * rows + TAIL, width), BF16),
        in_specs=[pl.BlockSpec(memory_space=pltpu.SMEM), first, first],
        out_specs=pl.BlockSpec((2 * rows + TAIL, width), lambda step: (0, 0)),
        name="pack",
    )(lengths, keys, values)


def main_kernel(depth, heads, *refs):
    masks = (1 << (depth - 1)) - 1
    lengths_ref, query_ref, grad_ref, key_ref, value_ref, own_ref, mate_ref = refs[:7]
    near = refs[7 : 7 + masks]
    far = refs[7 + masks : 7 + 2 * masks]
    (
        grad_query_ref,
        leaf_ref,
        swap_ref,
        part_ref,
        keys_s,
        values_s,
        extra_s,
        keys_t,
        low_s,
        ds_s,
        query_s,
        cot_s,
    ) = refs[7 + 2 * masks :]
    rows, width = key_ref.shape[1:]
    index = lax.axis_index("leaf")
    parity = index & 1
    own_level = depth - trailing_zeros(index, depth)
    scale = width ** (-0.5)
    lane = lax.broadcasted_iota(jnp.int32, (rows, width), 1)
    row = lax.broadcasted_iota(jnp.int32, (rows, width), 0)
    row_f = row.astype(F32)

    levels = depth + 2
    for level in range(levels):
        span = slice(level * rows, (level + 1) * rows)
        if level == depth + 1:
            key_block, value_block = key_ref[1], value_ref[1]
            length = jnp.full((1, width), lengths_ref[1].astype(F32), F32)
        else:
            if level == depth:
                block = jnp.where(parity == 1, own_ref[...], mate_ref[...])
            else:
                even = index - parity
                pick = (even ^ owner_of(even, level, depth)) >> 1
                block = jnp.where(parity == 1, mate_ref[...], own_ref[...])
                for mask in range(1, masks + 1):
                    other = jnp.where(parity == 1, far[mask - 1][...], near[mask - 1][...])
                    block = jnp.where(pick == mask, other, block)
            key_block, value_block = block[:rows], block[rows : 2 * rows]
            length = block[2 * rows : 2 * rows + 1].astype(F32)
        keys_s[span, :] = key_block
        values_s[span, :] = value_block
        keys_t[:, span] = key_block.T
        dead = row_f >= length
        for segment in range(2):
            if segment == 0 and level == depth + 1:
                continue
            level_of = own_level if segment == 0 else depth + 1
            diagonal = jnp.where(row > 0, row, -1)
            column = jnp.where(level == level_of, diagonal, -1)
            column = jnp.where(dead | (level > level_of), 0, column)
            extra_s[segment, span, :] = jnp.where(lane == column, 1.0, 0.0).astype(BF16)

    ruled = jnp.where((lane > row) | (lane == 0), BIG, 0.0).astype(BF16)
    ruled = jnp.concatenate([ruled, ruled], 0)

    step_rows = 2 * rows
    for segment in range(2):
        count = (depth + 1 + segment) * rows
        live = row < lengths_ref[segment]
        keys_wide = jnp.concatenate([keys_s[:count, :], extra_s[segment, :count, :]], 1)
        for pair in range(heads // 2):
            at = (segment * (heads // 2) + pair) * step_rows
            here = slice(at, at + step_rows)
            columns = [slice(h * width, (h + 1) * width) for h in (2 * pair, 2 * pair + 1)]
            query = jnp.concatenate([query_ref[segment, :, c] for c in columns], 0)
            cot = jnp.concatenate(
                [jnp.where(live, grad_ref[segment, :, c], jnp.zeros((), BF16)) for c in columns], 0
            )
            query_s[here, :] = query
            cot_s[here, :] = cot
            scores = lax.dot_general(
                keys_wide,
                jnp.concatenate([query, ruled], 1),
                NT,
                preferred_element_type=F32,
            )
            top = jnp.max(scores, axis=0, keepdims=True)
            weights = jnp.exp2((scores - top) * (scale * LOG2E))
            total = jnp.sum(weights, axis=0, keepdims=True)
            weights = weights * (1.0 / total)
            low_s[:count, here] = weights.astype(BF16)
            grad_weights = lax.dot_general(
                values_s[:count, :], cot, NT, preferred_element_type=F32
            )
            delta = jnp.sum(weights * grad_weights, axis=0, keepdims=True)
            grad_scores = (weights * (grad_weights - delta)).astype(BF16)
            ds_s[:count, here] = grad_scores
            grad_query = lax.dot_general(
                keys_t[:, :count], grad_scores, NN, preferred_element_type=F32
            )
            grad_query = (grad_query * scale).astype(BF16).T
            for n, c in enumerate(columns):
                grad_query_ref[segment, :, c] = grad_query[n * rows : (n + 1) * rows]

    inner = (depth + 1) * rows
    half = heads * rows
    grad_keys = lax.dot_general(ds_s[:inner, :], query_s[...], NN, preferred_element_type=F32)
    grad_keys = grad_keys * scale
    grad_values = lax.dot_general(low_s[:inner, :], cot_s[...], NN, preferred_element_type=F32)
    leaf_keys = lax.dot_general(
        ds_s[inner:, half:], query_s[half:, :], NN, preferred_element_type=F32
    )
    leaf_values = lax.dot_general(
        low_s[inner:, half:], cot_s[half:, :], NN, preferred_element_type=F32
    )
    leaf_ref[0:rows, :] = (leaf_keys * scale).astype(BF16)
    leaf_ref[rows : 2 * rows, :] = leaf_values.astype(BF16)

    def put(ref, levels_at):
        for place, level in enumerate(levels_at):
            span = slice(level * rows, (level + 1) * rows)
            at = place * 2 * rows
            ref[at : at + rows, :] = grad_keys[span].astype(ref.dtype)
            ref[at + rows : at + 2 * rows, :] = grad_values[span].astype(ref.dtype)

    @pl.when(parity == 1)
    def _():
        put(swap_ref, range(depth))
        put(part_ref, [depth])

    @pl.when(parity == 0)
    def _():
        put(swap_ref, [depth])
        put(part_ref, range(depth))


def main_call(lengths, queries, grads, keys, values, own, mate, near, far, depth):
    rows, width = keys.shape[1:]
    heads = queries.shape[2] // width
    slots = (depth + 2) * rows
    total = 2 * heads * rows
    vmem = pl.BlockSpec(memory_space=pltpu.VMEM)
    return pl.pallas_call(
        functools.partial(main_kernel, depth, heads),
        out_shape=(
            jax.ShapeDtypeStruct(queries.shape, BF16),
            jax.ShapeDtypeStruct((2 * rows, width), BF16),
            jax.ShapeDtypeStruct((depth * 2 * rows, width), BF16),
            jax.ShapeDtypeStruct((depth * 2 * rows, width), F32),
        ),
        in_specs=[pl.BlockSpec(memory_space=pltpu.SMEM)] + [vmem] * (6 + len(near) + len(far)),
        out_specs=(vmem,) * 4,
        scratch_shapes=[
            pltpu.VMEM((slots, width), BF16),
            pltpu.VMEM((slots, width), BF16),
            pltpu.VMEM((2, slots, width), BF16),
            pltpu.VMEM((width, slots), BF16),
            pltpu.VMEM((slots, total), BF16),
            pltpu.VMEM((slots, total), BF16),
            pltpu.VMEM((total, width), BF16),
            pltpu.VMEM((total, width), BF16),
        ],
        compiler_params=pltpu.CompilerParams(vmem_limit_bytes=40 * 1024 * 1024),
        name="attend",
    )(lengths, queries, grads, keys, values, own, mate, *near, *far)


def combine_kernel(depth, part_ref, other_ref, own_ref, *rest):
    sends, both = rest[:-1], rest[-1]
    block = own_ref.shape[0]
    index = lax.axis_index("leaf")
    both[...] = part_ref[...] + other_ref[...].astype(F32)

    def take(level):
        return both[pl.ds(pl.multiple_of(level * block, block), block), :]

    own_level = depth - trailing_zeros(index, depth)
    own_ref[...] = take(jnp.where(index & 1 == 1, 0, own_level))
    for mask, ref in enumerate(sends, 1):
        target = (index - (index & 1)) ^ (mask << 1)
        ref[...] = take(depth - trailing_zeros(target, depth)).astype(BF16)


def combine_call(part, other, depth):
    masks = (1 << (depth - 1)) - 1
    block = part.shape[0] // depth
    width = part.shape[1]
    vmem = pl.BlockSpec(memory_space=pltpu.VMEM)
    return pl.pallas_call(
        functools.partial(combine_kernel, depth),
        out_shape=[jax.ShapeDtypeStruct((block, width), F32)]
        + [jax.ShapeDtypeStruct((block, width), BF16)] * masks,
        in_specs=[vmem] * 2,
        out_specs=[vmem] * (1 + masks),
        scratch_shapes=[pltpu.VMEM(part.shape, F32)],
        name="combine",
    )(part, other)


def final_kernel(leaf_ref, own_ref, *refs):
    arrived, (keys_ref, values_ref) = refs[:-2], refs[-2:]
    rows = keys_ref.shape[1]
    total = own_ref[...]
    for ref in arrived:
        total = total + ref[...].astype(F32)
    total = total.astype(BF16)
    keys_ref[0] = total[:rows]
    values_ref[0] = total[rows:]
    keys_ref[1] = leaf_ref[:rows, :]
    values_ref[1] = leaf_ref[rows:, :]


def final_call(leaf, own, arrived, shape):
    vmem = pl.BlockSpec(memory_space=pltpu.VMEM)
    return pl.pallas_call(
        final_kernel,
        out_shape=[jax.ShapeDtypeStruct(shape, BF16)] * 2,
        in_specs=[vmem] * (2 + len(arrived)),
        out_specs=[vmem] * 2,
        name="final",
    )(leaf, own, *arrived)


def body(queries, key_states, value_states, grad_output, lengths):
    count = lax.axis_size("leaf")
    depth = depth_of(count)
    masks = range(1, count // 2)
    swap_pairs = [(i, i ^ 1) for i in range(count)]
    forward_pairs = [(i, i + 1) for i in range(0, count, 2)]

    pack = make_pack(lengths, key_states, value_states)
    near = [lax.ppermute(pack, "leaf", down_pairs(m, count)) for m in masks]
    mate = lax.ppermute(pack, "leaf", swap_pairs)
    far = [lax.ppermute(block, "leaf", forward_pairs) for block in near]
    grad_queries, leaf, swap, part = main_call(
        lengths, queries, grad_output, key_states, value_states, pack, mate, near, far, depth
    )
    other = lax.ppermute(swap, "leaf", swap_pairs)
    own, *sends = combine_call(part, other, depth)
    arrived = [
        lax.ppermute(block, "leaf", [(b, a) for a, b in down_pairs(m, count)])
        for m, block in zip(masks, sends)
    ]
    grad_keys, grad_values = final_call(leaf, own, arrived, key_states.shape)
    return grad_queries, grad_keys, grad_values


def solution(mesh):
    segments = P(("dp", "leaf"), None, None)
    return jax.shard_map(
        body,
        mesh=mesh,
        in_specs=(segments, segments, segments, segments, P(("dp", "leaf"))),
        out_specs=(segments, segments, segments),
        check_vma=False,
    )
```

time: 84.2 us -> 50.7 us (0.60)
  blocking collectives: 27.1 us -> 0 us
  starting transfers between devices: 4.53 us -> 23.5 us
  local copies, waits for them, and re-layouts: 18.6 us -> 5.64 us
  matrix products: 11.6 us -> 0 us
  Pallas kernels: 0 us -> 11.6 us
  other arithmetic: 10.1 us -> 0 us
  waiting for transfers between devices: 10.7 us -> 8.61 us
    ppermute x6 -> x11, starting transfers between devices: 4.53 us -> 23.5 us  [the longest x3 10.1 us: body(): near = [lax.ppermute(pack, 'leaf', down_pairs(m, count)) for m in masks]]
    all_gather x2 -> x0, blocking collectives: 17.6 us -> none  [the longest x1 8.95 us: body(): lax.all_gather(key_states[0:1], 'leaf', axis=0, tiled=True)]
    pallas_call x0 -> x4, Pallas kernels: none -> 11.6 us  [the longest x1 6.7 us: main_call(): pl.pallas_call(functools.partial(main_kernel, depth, heads), out_shape=(j...]
    dot_general x12 -> x0, matrix products: 11.6 us -> none  [the longest x2 3.61 us: attend_grad(): jnp.einsum('hqk,kd->qhd', weights_low, value_flat, preferred_element_type...]
    slice x16 -> x0, local copies, waits for them, and re-layouts: 10.5 us -> none  [the longest x2 3.58 us: body(): grad_output[segment]]
    unnamed x1 -> x0, blocking collectives: 9.46 us -> none
    another operation x5 -> x0, other arithmetic: 2.2 us -> none  [the longest x1 0.84 us: body(): grad_queries = jnp.stack(grad_query_list, 0)]
    ppermute x6 -> x11, waiting for transfers between devices: 10.7 us -> 8.61 us  [the longest x3 5.95 us: body(): lax.ppermute(block, 'leaf', [(b, a) for a, b in down_pairs(m, count)])]
  transfers between devices with their start and end apart: 6 -> 11, of which waited for: 4 -> 5; matrix products, arithmetic and copies ran while one was open for 10% -> 0% of each run, Pallas kernels for 0% -> 0%
where the time goes in v1:
time: 50.7 us; the launch traced here: 50.1 us
  starting transfers between devices  23.5 us (46%)
  Pallas kernels  11.6 us (23%)
  waiting for transfers between devices  8.61 us (17%)
  local copies, waits for them, and re-layouts  5.64 us (11%)
  between operations  0.81 us (2%)
    ppermute x3, starting transfers between devices, body(): near = [lax.ppermute(pack, 'leaf', down_pairs(m, count)) for m in masks]  10.1 us
    ppermute x3, starting transfers between devices, body(): lax.ppermute(block, 'leaf', [(b, a) for a, b in down_pairs(m, count)])  7.96 us
    pallas_call x1, Pallas kernels, main_call(): pl.pallas_call(functools.partial(main_kernel, depth, heads), out_shape=(j...  6.7 us
    ppermute x3, waiting for transfers between devices, body(): lax.ppermute(block, 'leaf', [(b, a) for a, b in down_pairs(m, count)])  5.95 us
    unnamed x24, local copies, waits for them, and re-layouts  5.64 us
    ppermute x3, starting transfers between devices, body(): far = [lax.ppermute(block, 'leaf', forward_pairs) for block in near]  4.96 us
    pallas_call x1, Pallas kernels, combine_call(): pl.pallas_call(functools.partial(combine_kernel, depth), out_shape=[jax.S...  1.8 us
    pallas_call x1, Pallas kernels, final_call(): pl.pallas_call(final_kernel, out_shape=[jax.ShapeDtypeStruct(shape, BF16)...  1.67 us
  transfers between devices with their start and end apart: 11, of which 5 were waited for; matrix products, arithmetic and copies ran while one was open for 0% of the time, Pallas kernels for 0%

profile of v1, /device:TPU:0, one launch (start us, length us, event | category | flops | bytes accessed | tf_op | source)
XLA Modules:
  0.0 50.1 jit_solution(9993874910446712675)
XLA Ops:
  0.7 1.5 %pack.1.refs_5_ = bf16[272,128]{1,0:T(8,128)(2,1)} custom-call(s32[2]{0:T(128)} %refs_0_.1, bf16[2,128,128]{2,1,0:T(8,128)(2,1)} %refs_3_.1, bf16[2,128,128]{2,1,0:T(8,128)(2,1)} %refs_4_.1), custom_call_target="tpu_custom_call" | custom-call | tf_op jit(solution)/shard_map/pack/pallas_call | solution.py:62
  2.1 5.8 %collective-permute-start.3 = (bf16[272,128]{1,0:T(8,128)(2,1)}, bf16[272,128]{1,0:T(8,128)(2,1)S(1)}, u32[]{:S(2)}, u32[]{:S(2)}) collective-permute-start(bf16[272,128]{1,0:T(8,128)(2,1)} %pack.1.refs_5_), channel_id=1, source_target_pairs={{0,6},{4,2},{8,14},{12,10},{16,22},{20,18},{24,30},{28,26}} | collective-permute-start | bytes 208904 | tf_op jit(solution)/shard_map/ppermute | solution.py:300
  7.9 2.4 %collective-permute-start.2 = (bf16[272,128]{1,0:T(8,128)(2,1)}, bf16[272,128]{1,0:T(8,128)(2,1)S(1)}, u32[]{:S(2)}, u32[]{:S(2)}) collective-permute-start(bf16[272,128]{1,0:T(8,128)(2,1)} %pack.1.refs_5_), channel_id=1, source_target_pairs={{0,4},{4,0},{8,12},{12,8},{16,20},{20,16},{24,28},{28,24}} | collective-permute-start | bytes 208904 | tf_op jit(solution)/shard_map/ppermute | solution.py:300
  10.3 1.9 %collective-permute-start.1 = (bf16[272,128]{1,0:T(8,128)(2,1)}, bf16[272,128]{1,0:T(8,128)(2,1)S(1)}, u32[]{:S(2)}, u32[]{:S(2)}) collective-permute-start(bf16[272,128]{1,0:T(8,128)(2,1)} %pack.1.refs_5_), channel_id=1, source_target_pairs={{0,2},{2,0},{4,6},{6,4},{8,10},{10,8},{12,14},{14,12},{16,18},{18,... | collective-permute-start | bytes 208904 | tf_op jit(solution)/shard_map/ppermute | solution.py:300
  12.3 0.1 collective-permute-start
  12.4 0.0 collective-permute-done.3.refs_9_
  12.4 2.4 %collective-permute-start.6 = (bf16[272,128]{1,0:T(8,128)(2,1)S(1)}, bf16[272,128]{1,0:T(8,128)(2,1)S(1)}, u32[]{:S(2)}, u32[]{:S(2)}) collective-permute-start(bf16[272,128]{1,0:T(8,128)(2,1)S(1)} %collective-permute-done.3.refs_9_), channel_id=1, source_target_pairs={{0,1},{2,3},{4,5},{6,7},{8,9},{10,11},{12,13},{14,15},{16,17},{18,... | collective-permute-start | bytes 208904 | tf_op jit(solution)/shard_map/ppermute | solution.py:302
  14.8 0.0 collective-permute-done.2.refs_8_
  14.8 1.3 %collective-permute-start.5 = (bf16[272,128]{1,0:T(8,128)(2,1)S(1)}, bf16[272,128]{1,0:T(8,128)(2,1)S(1)}, u32[]{:S(2)}, u32[]{:S(2)}) collective-permute-start(bf16[272,128]{1,0:T(8,128)(2,1)S(1)} %collective-permute-done.2.refs_8_), channel_id=1, source_target_pairs={{0,1},{2,3},{4,5},{6,7},{8,9},{10,11},{12,13},{14,15},{16,17},{18,... | collective-permute-start | bytes 208904 | tf_op jit(solution)/shard_map/ppermute | solution.py:302
  16.1 0.7 %collective-permute-done.1.refs_7_ = bf16[272,128]{1,0:T(8,128)(2,1)S(1)} collective-permute-done((bf16[272,128]{1,0:T(8,128)(2,1)}, bf16[272,128]{1,0:T(8,128)(2,1)S(1)}, u32[]{:S(2)}, u32[]{:S(2)}) %collective-permute-start.1) | collective-permute-done | bytes 69664 | tf_op jit(solution)/shard_map/ppermute | solution.py:300
  16.8 1.3 %collective-permute-start.4 = (bf16[272,128]{1,0:T(8,128)(2,1)S(1)}, bf16[272,128]{1,0:T(8,128)(2,1)S(1)}, u32[]{:S(2)}, u32[]{:S(2)}) collective-permute-start(bf16[272,128]{1,0:T(8,128)(2,1)S(1)} %collective-permute-done.1.refs_7_), channel_id=1, source_target_pairs={{0,1},{2,3},{4,5},{6,7},{8,9},{10,11},{12,13},{14,15},{16,17},{18,... | collective-permute-start | bytes 208904 | tf_op jit(solution)/shard_map/ppermute | solution.py:302
  18.1 0.0 collective-permute-done.refs_6_
  18.1 0.0 collective-permute-done.6.refs_12_
  18.1 0.9 %collective-permute-done.4.refs_10_ = bf16[272,128]{1,0:T(8,128)(2,1)S(1)} collective-permute-done((bf16[272,128]{1,0:T(8,128)(2,1)S(1)}, bf16[272,128]{1,0:T(8,128)(2,1)S(1)}, u32[]{:S(2)}, u32[]{:S(2)}) %collective-permute-start.4) | collective-permute-done | bytes 69664 | tf_op jit(solution)/shard_map/ppermute | solution.py:302
  19.0 1.0 %copy-done = bf16[2,128,1024]{2,1,0:T(8,128)(2,1)S(1)} copy-done((bf16[2,128,1024]{2,1,0:T(8,128)(2,1)S(1)}, bf16[2,128,1024]{2,1,0:T(8,128)(2,1)}, u32[]{:S(2)}) %copy-start) | copy-done | bytes 524312
  20.0 1.0 %copy-done.1 = bf16[2,128,1024]{2,1,0:T(8,128)(2,1)S(1)} copy-done((bf16[2,128,1024]{2,1,0:T(8,128)(2,1)S(1)}, bf16[2,128,1024]{2,1,0:T(8,128)(2,1)}, u32[]{:S(2)}) %copy-start.1) | copy-done | bytes 524312
  21.0 0.9 %copy-done.3 = bf16[272,128]{1,0:T(8,128)(2,1)S(1)} copy-done((bf16[272,128]{1,0:T(8,128)(2,1)S(1)}, bf16[272,128]{1,0:T(8,128)(2,1)}, u32[]{:S(2)}) %copy-start.3) | copy-done | bytes 69656
  21.9 6.7 %attend.1 = (bf16[2,128,1024]{2,1,0:T(8,128)(2,1)}, bf16[256,128]{1,0:T(8,128)(2,1)S(1)}, bf16[768,128]{1,0:T(8,128)(2,1)S(1)}, f32[768,128]{1,0:T(8,128)S(1)}) custom-call(s32[2]{0:T(128)S(1)} %copy-done.7, bf16[2,128,1024]{2,1,0:T(8,128)(2,1)S(1)} %copy-done, bf16[2,128,1024]{2,1,0:T(8,128)(2,1)S(1)} %copy-done.1, bf16[2,128,128]{2,1,0:T(8,128)(2,1)S(1)} %copy-done.4, ...), custom_call_target="tpu_custom_call" | custom-call | tf_op jit(solution)/shard_map/attend/pallas_call | solution.py:211
  28.6 0.7 %copy-done.2 = f32[768,128]{1,0:T(8,128)} copy-done((f32[768,128]{1,0:T(8,128)}, f32[768,128]{1,0:T(8,128)S(1)}, u32[]{:S(2)}) %copy-start.2) | copy-done | bytes 393240
  29.4 0.6 %copy-done.6 = bf16[256,128]{1,0:T(8,128)(2,1)} copy-done((bf16[256,128]{1,0:T(8,128)(2,1)}, bf16[256,128]{1,0:T(8,128)(2,1)S(1)}, u32[]{:S(2)}) %copy-start.6) | copy-done | bytes 65560
  30.0 0.3 collective-permute-start.7
  30.3 1.1 %collective-permute-done.7.other_ref = bf16[768,128]{1,0:T(8,128)(2,1)S(1)} collective-permute-done((bf16[768,128]{1,0:T(8,128)(2,1)S(1)}, bf16[768,128]{1,0:T(8,128)(2,1)S(1)}, u32[]{:S(2)}, u32[]{:S(2)}) %collective-permute-start.7) | collective-permute-done | bytes 196640 | tf_op jit(solution)/shard_map/ppermute | solution.py:306
  31.4 0.7 %copy-done.8 = bf16[768,128]{1,0:T(8,128)(2,1)} copy-done((bf16[768,128]{1,0:T(8,128)(2,1)}, bf16[768,128]{1,0:T(8,128)(2,1)S(1)}, u32[]{:S(2)}) %copy-start.8) | copy-done | bytes 196632
  32.1 1.8 %combine.1 = (f32[256,128]{1,0:T(8,128)}, bf16[256,128]{1,0:T(8,128)(2,1)}, bf16[256,128]{1,0:T(8,128)(2,1)}, bf16[256,128]{1,0:T(8,128)(2,1)}) custom-call(f32[768,128]{1,0:T(8,128)} %copy-done.2, bf16[768,128]{1,0:T(8,128)(2,1)} %copy-done.8), custom_call_target="tpu_custom_call" | custom-call | tf_op jit(solution)/shard_map/combine/pallas_call | solution.py:257
  33.9 3.2 %collective-permute-start.8 = (bf16[256,128]{1,0:T(8,128)(2,1)}, bf16[256,128]{1,0:T(8,128)(2,1)S(1)}, u32[]{:S(2)}, u32[]{:S(2)}) collective-permute-start(bf16[256,128]{1,0:T(8,128)(2,1)} %get-tuple-element.18), channel_id=1, source_target_pairs={{2,0},{0,2},{6,4},{4,6},{10,8},{8,10},{14,12},{12,14},{18,16},{16,... | collective-permute-start | bytes 196616 | tf_op jit(solution)/shard_map/ppermute | solution.py:309
  37.2 3.4 %collective-permute-start.9 = (bf16[256,128]{1,0:T(8,128)(2,1)}, bf16[256,128]{1,0:T(8,128)(2,1)S(1)}, u32[]{:S(2)}, u32[]{:S(2)}) collective-permute-start(bf16[256,128]{1,0:T(8,128)(2,1)} %get-tuple-element.19), channel_id=1, source_target_pairs={{4,0},{0,4},{12,8},{8,12},{20,16},{16,20},{28,24},{24,28}} | collective-permute-start | bytes 196616 | tf_op jit(solution)/shard_map/ppermute | solution.py:309
  40.6 1.3 %collective-permute-start.10 = (bf16[256,128]{1,0:T(8,128)(2,1)}, bf16[256,128]{1,0:T(8,128)(2,1)S(1)}, u32[]{:S(2)}, u32[]{:S(2)}) collective-permute-start(bf16[256,128]{1,0:T(8,128)(2,1)} %get-tuple-element.20), channel_id=1, source_target_pairs={{6,0},{2,4},{14,8},{10,12},{22,16},{18,20},{30,24},{26,28}} | collective-permute-start | bytes 196616 | tf_op jit(solution)/shard_map/ppermute | solution.py:309
  41.9 0.0 collective-permute-done.8.refs_0_
  41.9 1.6 %collective-permute-done.9.refs_1_ = bf16[256,128]{1,0:T(8,128)(2,1)S(1)} collective-permute-done((bf16[256,128]{1,0:T(8,128)(2,1)}, bf16[256,128]{1,0:T(8,128)(2,1)S(1)}, u32[]{:S(2)}, u32[]{:S(2)}) %collective-permute-start.9) | collective-permute-done | bytes 65568 | tf_op jit(solution)/shard_map/ppermute | solution.py:309
  43.5 4.3 %collective-permute-done.10.refs_2_ = bf16[256,128]{1,0:T(8,128)(2,1)S(1)} collective-permute-done((bf16[256,128]{1,0:T(8,128)(2,1)}, bf16[256,128]{1,0:T(8,128)(2,1)S(1)}, u32[]{:S(2)}, u32[]{:S(2)}) %collective-permute-start.10) | collective-permute-done | bytes 65568 | tf_op jit(solution)/shard_map/ppermute | solution.py:309
  47.9 0.6 %copy-done.11 = bf16[256,128]{1,0:T(8,128)(2,1)} copy-done((bf16[256,128]{1,0:T(8,128)(2,1)}, bf16[256,128]{1,0:T(8,128)(2,1)S(1)}, u32[]{:S(2)}) %copy-start.11) | copy-done | bytes 65560
  48.5 1.7 %final.1 = (bf16[2,128,128]{2,1,0:T(8,128)(2,1)}, bf16[2,128,128]{2,1,0:T(8,128)(2,1)}) custom-call(bf16[256,128]{1,0:T(8,128)(2,1)} %copy-done.6, f32[256,128]{1,0:T(8,128)} %get-tuple-element.17.own_ref, bf16[256,128]{1,0:T(8,128)(2,1)} %copy-done.9, bf16[256,128]{1,0:T(8,128)(2,1)} %copy-done.10, bf16[256,128]{1,0:T(8,128)(2,1)} %copy-done.11), custom_call_target="tpu_custom_call" | custom-call | tf_op jit(solution)/shard_map/final/pallas_call | solution.py:283
  (18 shorter events, 0.0 us)
Async XLA Ops:
  0.6 18.3 %copy-start.7 = (s32[2]{0:T(128)S(1)}, s32[2]{0:T(128)}, u32[]{:S(2)}) copy-start(s32[2]{0:T(128)} %refs_0_.1) | copy-start | bytes 28
  0.6 18.3 %copy-start.5 = (bf16[2,128,128]{2,1,0:T(8,128)(2,1)S(1)}, bf16[2,128,128]{2,1,0:T(8,128)(2,1)}, u32[]{:S(2)}) copy-start(bf16[2,128,128]{2,1,0:T(8,128)(2,1)} %refs_4_.1) | copy-start | bytes 196612
  0.7 18.3 %copy-start.4 = (bf16[2,128,128]{2,1,0:T(8,128)(2,1)S(1)}, bf16[2,128,128]{2,1,0:T(8,128)(2,1)}, u32[]{:S(2)}) copy-start(bf16[2,128,128]{2,1,0:T(8,128)(2,1)} %refs_3_.1) | copy-start | bytes 196612
  2.1 10.2 %collective-permute-start.3 = (bf16[272,128]{1,0:T(8,128)(2,1)}, bf16[272,128]{1,0:T(8,128)(2,1)S(1)}, u32[]{:S(2)}, u32[]{:S(2)}) collective-permute-start(bf16[272,128]{1,0:T(8,128)(2,1)} %pack.1.refs_5_), channel_id=1, source_target_pairs={{0,6},{4,2},{8,14},{12,10},{16,22},{20,18},{24,30},{28,26}} | collective-permute-start | bytes 208904 | tf_op jit(solution)/shard_map/ppermute | solution.py:300
  7.9 6.8 %collective-permute-start.2 = (bf16[272,128]{1,0:T(8,128)(2,1)}, bf16[272,128]{1,0:T(8,128)(2,1)S(1)}, u32[]{:S(2)}, u32[]{:S(2)}) collective-permute-start(bf16[272,128]{1,0:T(8,128)(2,1)} %pack.1.refs_5_), channel_id=1, source_target_pairs={{0,4},{4,0},{8,12},{12,8},{16,20},{20,16},{24,28},{28,24}} | collective-permute-start | bytes 208904 | tf_op jit(solution)/shard_map/ppermute | solution.py:300
  10.3 6.4 %collective-permute-start.1 = (bf16[272,128]{1,0:T(8,128)(2,1)}, bf16[272,128]{1,0:T(8,128)(2,1)S(1)}, u32[]{:S(2)}, u32[]{:S(2)}) collective-permute-start(bf16[272,128]{1,0:T(8,128)(2,1)} %pack.1.refs_5_), channel_id=1, source_target_pairs={{0,2},{2,0},{4,6},{6,4},{8,10},{10,8},{12,14},{14,12},{16,18},{18,... | collective-permute-start | bytes 208904 | tf_op jit(solution)/shard_map/ppermute | solution.py:300
  12.3 5.8 %collective-permute-start = (bf16[272,128]{1,0:T(8,128)(2,1)}, bf16[272,128]{1,0:T(8,128)(2,1)S(1)}, u32[]{:S(2)}, u32[]{:S(2)}) collective-permute-start(bf16[272,128]{1,0:T(8,128)(2,1)} %pack.1.refs_5_), channel_id=1, source_target_pairs={{0,1},{1,0},{2,3},{3,2},{4,5},{5,4},{6,7},{7,6},{8,9},{9,8},{10,11... | collective-permute-start | bytes 208904 | tf_op jit(solution)/shard_map/ppermute | solution.py:301
  12.4 5.7 %collective-permute-start.6 = (bf16[272,128]{1,0:T(8,128)(2,1)S(1)}, bf16[272,128]{1,0:T(8,128)(2,1)S(1)}, u32[]{:S(2)}, u32[]{:S(2)}) collective-permute-start(bf16[272,128]{1,0:T(8,128)(2,1)S(1)} %collective-permute-done.3.refs_9_), channel_id=1, source_target_pairs={{0,1},{2,3},{4,5},{6,7},{8,9},{10,11},{12,13},{14,15},{16,17},{18,... | collective-permute-start | bytes 208904 | tf_op jit(solution)/shard_map/ppermute | solution.py:302
  14.8 3.3 %collective-permute-start.5 = (bf16[272,128]{1,0:T(8,128)(2,1)S(1)}, bf16[272,128]{1,0:T(8,128)(2,1)S(1)}, u32[]{:S(2)}, u32[]{:S(2)}) collective-permute-start(bf16[272,128]{1,0:T(8,128)(2,1)S(1)} %collective-permute-done.2.refs_8_), channel_id=1, source_target_pairs={{0,1},{2,3},{4,5},{6,7},{8,9},{10,11},{12,13},{14,15},{16,17},{18,... | collective-permute-start | bytes 208904 | tf_op jit(solution)/shard_map/ppermute | solution.py:302
  16.8 2.2 %collective-permute-start.4 = (bf16[272,128]{1,0:T(8,128)(2,1)S(1)}, bf16[272,128]{1,0:T(8,128)(2,1)S(1)}, u32[]{:S(2)}, u32[]{:S(2)}) collective-permute-start(bf16[272,128]{1,0:T(8,128)(2,1)S(1)} %collective-permute-done.1.refs_7_), channel_id=1, source_target_pairs={{0,1},{2,3},{4,5},{6,7},{8,9},{10,11},{12,13},{14,15},{16,17},{18,... | collective-permute-start | bytes 208904 | tf_op jit(solution)/shard_map/ppermute | solution.py:302
  18.9 1.0 %copy-start = (bf16[2,128,1024]{2,1,0:T(8,128)(2,1)S(1)}, bf16[2,128,1024]{2,1,0:T(8,128)(2,1)}, u32[]{:S(2)}) copy-start(bf16[2,128,1024]{2,1,0:T(8,128)(2,1)} %refs_1_.1) | copy-start | bytes 1572868
  20.0 1.0 %copy-start.1 = (bf16[2,128,1024]{2,1,0:T(8,128)(2,1)S(1)}, bf16[2,128,1024]{2,1,0:T(8,128)(2,1)}, u32[]{:S(2)}) copy-start(bf16[2,128,1024]{2,1,0:T(8,128)(2,1)} %refs_2_.1) | copy-start | bytes 1572868
  21.0 0.9 %copy-start.3 = (bf16[272,128]{1,0:T(8,128)(2,1)S(1)}, bf16[272,128]{1,0:T(8,128)(2,1)}, u32[]{:S(2)}) copy-start(bf16[272,128]{1,0:T(8,128)(2,1)} %pack.1.refs_5_) | copy-start | bytes 208900
  28.6 0.7 %copy-start.2 = (f32[768,128]{1,0:T(8,128)}, f32[768,128]{1,0:T(8,128)S(1)}, u32[]{:S(2)}) copy-start(f32[768,128]{1,0:T(8,128)S(1)} %get-tuple-element.15.part_ref) | copy-start | bytes 1179652
  29.4 0.6 %copy-start.6 = (bf16[256,128]{1,0:T(8,128)(2,1)}, bf16[256,128]{1,0:T(8,128)(2,1)S(1)}, u32[]{:S(2)}) copy-start(bf16[256,128]{1,0:T(8,128)(2,1)S(1)} %get-tuple-element.14.leaf_ref) | copy-start | bytes 196612
  30.0 1.4 %collective-permute-start.7 = (bf16[768,128]{1,0:T(8,128)(2,1)S(1)}, bf16[768,128]{1,0:T(8,128)(2,1)S(1)}, u32[]{:S(2)}, u32[]{:S(2)}) collective-permute-start(bf16[768,128]{1,0:T(8,128)(2,1)S(1)} %get-tuple-element.16), channel_id=1, source_target_pairs={{0,1},{1,0},{2,3},{3,2},{4,5},{5,4},{6,7},{7,6},{8,9},{9,8},{10,11... | collective-permute-start | bytes 589832 | tf_op jit(solution)/shard_map/ppermute | solution.py:306
  31.4 0.7 %copy-start.8 = (bf16[768,128]{1,0:T(8,128)(2,1)}, bf16[768,128]{1,0:T(8,128)(2,1)S(1)}, u32[]{:S(2)}) copy-start(bf16[768,128]{1,0:T(8,128)(2,1)S(1)} %collective-permute-done.7.other_ref) | copy-start | bytes 589828
  33.9 8.0 %collective-permute-start.8 = (bf16[256,128]{1,0:T(8,128)(2,1)}, bf16[256,128]{1,0:T(8,128)(2,1)S(1)}, u32[]{:S(2)}, u32[]{:S(2)}) collective-permute-start(bf16[256,128]{1,0:T(8,128)(2,1)} %get-tuple-element.18), channel_id=1, source_target_pairs={{2,0},{0,2},{6,4},{4,6},{10,8},{8,10},{14,12},{12,14},{18,16},{16,... | collective-permute-start | bytes 196616 | tf_op jit(solution)/shard_map/ppermute | solution.py:309
  37.2 6.4 %collective-permute-start.9 = (bf16[256,128]{1,0:T(8,128)(2,1)}, bf16[256,128]{1,0:T(8,128)(2,1)S(1)}, u32[]{:S(2)}, u32[]{:S(2)}) collective-permute-start(bf16[256,128]{1,0:T(8,128)(2,1)} %get-tuple-element.19), channel_id=1, source_target_pairs={{4,0},{0,4},{12,8},{8,12},{20,16},{16,20},{28,24},{24,28}} | collective-permute-start | bytes 196616 | tf_op jit(solution)/shard_map/ppermute | solution.py:309
  40.6 7.3 %collective-permute-start.10 = (bf16[256,128]{1,0:T(8,128)(2,1)}, bf16[256,128]{1,0:T(8,128)(2,1)S(1)}, u32[]{:S(2)}, u32[]{:S(2)}) collective-permute-start(bf16[256,128]{1,0:T(8,128)(2,1)} %get-tuple-element.20), channel_id=1, source_target_pairs={{6,0},{2,4},{14,8},{10,12},{22,16},{18,20},{30,24},{26,28}} | collective-permute-start | bytes 196616 | tf_op jit(solution)/shard_map/ppermute | solution.py:309
  41.9 6.0 %copy-start.9 = (bf16[256,128]{1,0:T(8,128)(2,1)}, bf16[256,128]{1,0:T(8,128)(2,1)S(1)}, u32[]{:S(2)}) copy-start(bf16[256,128]{1,0:T(8,128)(2,1)S(1)} %collective-permute-done.8.refs_0_) | copy-start | bytes 196612
  43.5 4.3 %copy-start.10 = (bf16[256,128]{1,0:T(8,128)(2,1)}, bf16[256,128]{1,0:T(8,128)(2,1)S(1)}, u32[]{:S(2)}) copy-start(bf16[256,128]{1,0:T(8,128)(2,1)S(1)} %collective-permute-done.9.refs_1_) | copy-start | bytes 196612
  47.9 0.6 %copy-start.11 = (bf16[256,128]{1,0:T(8,128)(2,1)}, bf16[256,128]{1,0:T(8,128)(2,1)S(1)}, u32[]{:S(2)}) copy-start(bf16[256,128]{1,0:T(8,128)(2,1)S(1)} %collective-permute-done.10.refs_2_) | copy-start | bytes 196612

commit v2 on v1

--- a/solution.py
+++ b/solution.py
@@ -34,18 +34,19 @@
     return ((index >> shift) << shift) + (1 << (depth - level))
 
 
-def on_path(reader, owner, depth):
-    return any(owner_of(reader, level, depth) == owner for level in range(depth + 1))
-
-
-def down_pairs(mask, count):
-    depth = depth_of(count)
-    pairs = []
-    for owner in range(0, count, 2):
-        reader = owner ^ (mask << 1)
-        if on_path(reader, owner, depth):
-            pairs.append((owner, reader))
-    return pairs
+def owner_at(index, level, depth):
+    owner = owner_of(index, 0, depth)
+    for place in range(1, depth + 1):
+        owner = jnp.where(level == place, owner_of(index, place, depth), owner)
+    return owner
+
+
+def chip_pairs(mask, count):
+    return [(i, i ^ (mask << 1)) for i in range(0, count, 2)]
+
+
+def limit(mib):
+    return pltpu.CompilerParams(vmem_limit_bytes=mib * 1024 * 1024)
 
 
 def pack_kernel(lengths_ref, key_ref, value_ref, pack_ref):
@@ -65,6 +66,7 @@
         out_shape=jax.ShapeDtypeStruct((2 * rows + TAIL, width), BF16),
         in_specs=[pl.BlockSpec(memory_space=pltpu.SMEM), first, first],
         out_specs=pl.BlockSpec((2 * rows + TAIL, width), lambda step: (0, 0)),
+        compiler_params=limit(1),
         name="pack",
     )(lengths, keys, values)
 
@@ -228,7 +230,7 @@
             pltpu.VMEM((total, width), BF16),
             pltpu.VMEM((total, width), BF16),
         ],
-        compiler_params=pltpu.CompilerParams(vmem_limit_bytes=40 * 1024 * 1024),
+        compiler_params=limit(24),
         name="attend",
     )(lengths, queries, grads, keys, values, own, mate, *near, *far)
 
@@ -261,16 +263,21 @@
         in_specs=[vmem] * 2,
         out_specs=[vmem] * (1 + masks),
         scratch_shapes=[pltpu.VMEM(part.shape, F32)],
+        compiler_params=limit(4),
         name="combine",
     )(part, other)
 
 
-def final_kernel(leaf_ref, own_ref, *refs):
+def final_kernel(depth, leaf_ref, own_ref, *refs):
     arrived, (keys_ref, values_ref) = refs[:-2], refs[-2:]
     rows = keys_ref.shape[1]
+    index = lax.axis_index("leaf")
+    parity = index & 1
+    level = depth - trailing_zeros(index, depth)
     total = own_ref[...]
-    for ref in arrived:
-        total = total + ref[...].astype(F32)
+    for mask, ref in enumerate(arrived, 1):
+        mine = (parity == 0) & (owner_at(index ^ (mask << 1), level, depth) == index)
+        total = total + jnp.where(mine, ref[...].astype(F32), 0.0)
     total = total.astype(BF16)
     keys_ref[0] = total[:rows]
     values_ref[0] = total[rows:]
@@ -278,13 +285,14 @@
     values_ref[1] = leaf_ref[rows:, :]
 
 
-def final_call(leaf, own, arrived, shape):
+def final_call(leaf, own, arrived, shape, depth):
     vmem = pl.BlockSpec(memory_space=pltpu.VMEM)
     return pl.pallas_call(
-        final_kernel,
+        functools.partial(final_kernel, depth),
         out_shape=[jax.ShapeDtypeStruct(shape, BF16)] * 2,
         in_specs=[vmem] * (2 + len(arrived)),
         out_specs=[vmem] * 2,
+        compiler_params=limit(2),
         name="final",
     )(leaf, own, *arrived)
 
@@ -294,22 +302,21 @@
     depth = depth_of(count)
     masks = range(1, count // 2)
     swap_pairs = [(i, i ^ 1) for i in range(count)]
-    forward_pairs = [(i, i + 1) for i in range(0, count, 2)]
 
     pack = make_pack(lengths, key_states, value_states)
-    near = [lax.ppermute(pack, "leaf", down_pairs(m, count)) for m in masks]
+    near = [lax.ppermute(pack, "leaf", chip_pairs(m, count)) for m in masks]
     mate = lax.ppermute(pack, "leaf", swap_pairs)
-    far = [lax.ppermute(block, "leaf", forward_pairs) for block in near]
+    far = [lax.ppermute(block, "leaf", swap_pairs) for block in near]
     grad_queries, leaf, swap, part = main_call(
         lengths, queries, grad_output, key_states, value_states, pack, mate, near, far, depth
     )
     other = lax.ppermute(swap, "leaf", swap_pairs)
     own, *sends = combine_call(part, other, depth)
     arrived = [
-        lax.ppermute(block, "leaf", [(b, a) for a, b in down_pairs(m, count)])
+        lax.ppermute(block, "leaf", chip_pairs(m, count))
         for m, block in zip(masks, sends)
     ]
-    grad_keys, grad_values = final_call(leaf, own, arrived, key_states.shape)
+    grad_keys, grad_values = final_call(leaf, own, arrived, key_states.shape, depth)
     return grad_queries, grad_keys, grad_values
 
 

time: 50.7 us -> 43.7 us (0.86)
  Pallas kernels: 11.6 us -> 8.04 us
  starting transfers between devices: 23.5 us -> 20.1 us
  waiting for transfers between devices: 8.61 us -> 9.88 us
  local copies, waits for them, and re-layouts: 5.64 us -> 4.42 us
    ppermute x9, starting transfers between devices: 23 us -> 19.9 us  [the longest x3 10.2 us: body(): near = [lax.ppermute(pack, 'leaf', chip_pairs(m, count)) for m in masks]]
    pallas_call x1, Pallas kernels: 1.8 us -> 0.07 us  [combine_call(): pl.pallas_call(functools.partial(combine_kernel, depth), out_shape=[jax.S...]
    unnamed x24 -> x14, local copies, waits for them, and re-layouts: 5.64 us -> 4.42 us
    ppermute x9, waiting for transfers between devices: 7.5 us -> 8.57 us  [the longest x3 3.69 us: body(): lax.ppermute(block, 'leaf', chip_pairs(m, count))]
    pallas_call x1, Pallas kernels: 1.67 us -> 0.69 us  [final_call(): pl.pallas_call(functools.partial(final_kernel, depth), out_shape=[jax.Sha...]
    pallas_call x1, Pallas kernels: 1.47 us -> 0.55 us  [make_pack(): pl.pallas_call(pack_kernel, grid=(1,), out_shape=jax.ShapeDtypeStruct((2...]
where the time goes in v2:
time: 43.7 us; the launch traced here: 43.2 us
  starting transfers between devices  20.1 us (46%)
  waiting for transfers between devices  9.88 us (23%)
  Pallas kernels  8.04 us (18%)
  local copies, waits for them, and re-layouts  4.42 us (10%)
  between operations  0.75 us (2%)
    ppermute x3, starting transfers between devices, body(): near = [lax.ppermute(pack, 'leaf', chip_pairs(m, count)) for m in masks]  10.2 us
    ppermute x3, starting transfers between devices, body(): lax.ppermute(block, 'leaf', chip_pairs(m, count))  9.21 us
    pallas_call x1, Pallas kernels, main_call(): pl.pallas_call(functools.partial(main_kernel, depth, heads), out_shape=(j...  6.73 us
    unnamed x14, local copies, waits for them, and re-layouts  4.42 us
    ppermute x3, waiting for transfers between devices, body(): lax.ppermute(block, 'leaf', chip_pairs(m, count))  3.69 us
    ppermute x3, waiting for transfers between devices, body(): near = [lax.ppermute(pack, 'leaf', chip_pairs(m, count)) for m in masks]  3.64 us
    ppermute x1, waiting for transfers between devices, body(): other = lax.ppermute(swap, 'leaf', swap_pairs)  1.3 us
    ppermute x3, waiting for transfers between devices, body(): far = [lax.ppermute(block, 'leaf', swap_pairs) for block in near]  1.24 us
  transfers between devices with their start and end apart: 11, of which 5 were waited for; matrix products, arithmetic and copies ran while one was open for 0% of the time, Pallas kernels for 0%

profile of v2, /device:TPU:0, one launch (start us, length us, event | category | flops | bytes accessed | tf_op | source)
XLA Modules:
  0.0 43.2 jit_solution(11627849190816409718)
XLA Ops:
  0.6 0.8 %copy-done.2 = bf16[2,128,128]{2,1,0:T(8,128)(2,1)S(1)} copy-done((bf16[2,128,128]{2,1,0:T(8,128)(2,1)S(1)}, bf16[2,128,128]{2,1,0:T(8,128)(2,1)}, u32[]{:S(2)}) %copy-start.2) | copy-done | bytes 65560
  1.5 0.8 %copy-done.4 = bf16[2,128,128]{2,1,0:T(8,128)(2,1)S(1)} copy-done((bf16[2,128,128]{2,1,0:T(8,128)(2,1)S(1)}, bf16[2,128,128]{2,1,0:T(8,128)(2,1)}, u32[]{:S(2)}) %copy-start.4) | copy-done | bytes 65560
  2.3 0.7 %copy-done.5 = s32[2]{0:T(128)S(1)} copy-done((s32[2]{0:T(128)S(1)}, s32[2]{0:T(128)}, u32[]{:S(2)}) %copy-start.5) | copy-done | bytes 32
  3.0 0.5 %pack.1.refs_5_ = bf16[272,128]{1,0:T(8,128)(2,1)S(1)} custom-call(s32[2]{0:T(128)S(1)} %copy-done.5, bf16[2,128,128]{2,1,0:T(8,128)(2,1)S(1)} %copy-done.2, bf16[2,128,128]{2,1,0:T(8,128)(2,1)S(1)} %copy-done.4), custom_call_target="tpu_custom_call" | custom-call | tf_op jit(solution)/shard_map/pack/pallas_call | solution.py:63
  3.5 5.8 %collective-permute-start.3 = (bf16[272,128]{1,0:T(8,128)(2,1)S(1)}, bf16[272,128]{1,0:T(8,128)(2,1)S(1)}, u32[]{:S(2)}, u32[]{:S(2)}) collective-permute-start(bf16[272,128]{1,0:T(8,128)(2,1)S(1)} %pack.1.refs_5_), channel_id=1, source_target_pairs={{0,6},{2,4},{4,2},{6,0},{8,14},{10,12},{12,10},{14,8},{16,22},{18,... | collective-permute-start | bytes 208904 | tf_op jit(solution)/shard_map/ppermute | solution.py:307
  9.3 2.4 %collective-permute-start.2 = (bf16[272,128]{1,0:T(8,128)(2,1)S(1)}, bf16[272,128]{1,0:T(8,128)(2,1)S(1)}, u32[]{:S(2)}, u32[]{:S(2)}) collective-permute-start(bf16[272,128]{1,0:T(8,128)(2,1)S(1)} %pack.1.refs_5_), channel_id=1, source_target_pairs={{0,4},{2,6},{4,0},{6,2},{8,12},{10,14},{12,8},{14,10},{16,20},{18,... | collective-permute-start | bytes 208904 | tf_op jit(solution)/shard_map/ppermute | solution.py:307
  11.8 2.0 %collective-permute-start.1 = (bf16[272,128]{1,0:T(8,128)(2,1)S(1)}, bf16[272,128]{1,0:T(8,128)(2,1)S(1)}, u32[]{:S(2)}, u32[]{:S(2)}) collective-permute-start(bf16[272,128]{1,0:T(8,128)(2,1)S(1)} %pack.1.refs_5_), channel_id=1, source_target_pairs={{0,2},{2,0},{4,6},{6,4},{8,10},{10,8},{12,14},{14,12},{16,18},{18,... | collective-permute-start | bytes 208904 | tf_op jit(solution)/shard_map/ppermute | solution.py:307
  13.7 0.1 collective-permute-start
  13.8 0.0 collective-permute-done.3.refs_9_
  13.8 0.5 %collective-permute-start.6 = (bf16[272,128]{1,0:T(8,128)(2,1)S(1)}, bf16[272,128]{1,0:T(8,128)(2,1)S(1)}, u32[]{:S(2)}, u32[]{:S(2)}) collective-permute-start(bf16[272,128]{1,0:T(8,128)(2,1)S(1)} %collective-permute-done.3.refs_9_), channel_id=1, source_target_pairs={{0,1},{1,0},{2,3},{3,2},{4,5},{5,4},{6,7},{7,6},{8,9},{9,8},{10,11... | collective-permute-start | bytes 208904 | tf_op jit(solution)/shard_map/ppermute | solution.py:309
  14.3 1.2 %collective-permute-done.2.refs_8_ = bf16[272,128]{1,0:T(8,128)(2,1)S(1)} collective-permute-done((bf16[272,128]{1,0:T(8,128)(2,1)S(1)}, bf16[272,128]{1,0:T(8,128)(2,1)S(1)}, u32[]{:S(2)}, u32[]{:S(2)}) %collective-permute-start.2) | collective-permute-done | bytes 69664 | tf_op jit(solution)/shard_map/ppermute | solution.py:307
  15.5 0.0 collective-permute-start.5
  15.5 2.4 %collective-permute-done.1.refs_7_ = bf16[272,128]{1,0:T(8,128)(2,1)S(1)} collective-permute-done((bf16[272,128]{1,0:T(8,128)(2,1)S(1)}, bf16[272,128]{1,0:T(8,128)(2,1)S(1)}, u32[]{:S(2)}, u32[]{:S(2)}) %collective-permute-start.1) | collective-permute-done | bytes 69664 | tf_op jit(solution)/shard_map/ppermute | solution.py:307
  18.0 0.0 collective-permute-start.4
  18.0 0.0 collective-permute-done.refs_6_
  18.0 0.0 collective-permute-done.6.refs_12_
  18.0 0.0 collective-permute-done.5.refs_11_
  18.0 1.2 %collective-permute-done.4.refs_10_ = bf16[272,128]{1,0:T(8,128)(2,1)S(1)} collective-permute-done((bf16[272,128]{1,0:T(8,128)(2,1)S(1)}, bf16[272,128]{1,0:T(8,128)(2,1)S(1)}, u32[]{:S(2)}, u32[]{:S(2)}) %collective-permute-start.4) | collective-permute-done | bytes 69664 | tf_op jit(solution)/shard_map/ppermute | solution.py:309
  19.2 0.0 copy-done.3
  19.2 1.0 %copy-done = bf16[2,128,1024]{2,1,0:T(8,128)(2,1)S(1)} copy-done((bf16[2,128,1024]{2,1,0:T(8,128)(2,1)S(1)}, bf16[2,128,1024]{2,1,0:T(8,128)(2,1)}, u32[]{:S(2)}) %copy-start) | copy-done | bytes 524312
  20.3 1.0 %copy-done.1 = bf16[2,128,1024]{2,1,0:T(8,128)(2,1)S(1)} copy-done((bf16[2,128,1024]{2,1,0:T(8,128)(2,1)S(1)}, bf16[2,128,1024]{2,1,0:T(8,128)(2,1)}, u32[]{:S(2)}) %copy-start.1) | copy-done | bytes 524312
  21.3 6.7 %attend.1 = (bf16[2,128,1024]{2,1,0:T(8,128)(2,1)}, bf16[256,128]{1,0:T(8,128)(2,1)S(1)}, bf16[768,128]{1,0:T(8,128)(2,1)S(1)}, f32[768,128]{1,0:T(8,128)S(1)}) custom-call(s32[2]{0:T(128)S(1)} %copy-done.6, bf16[2,128,1024]{2,1,0:T(8,128)(2,1)S(1)} %copy-done, bf16[2,128,1024]{2,1,0:T(8,128)(2,1)S(1)} %copy-done.1, bf16[2,128,128]{2,1,0:T(8,128)(2,1)S(1)} %copy-done.3, ...), custom_call_target="tpu_custom_call" | custom-call | tf_op jit(solution)/shard_map/attend/pallas_call | solution.py:213
  28.0 0.1 collective-permute-start.7
  28.2 1.3 %collective-permute-done.7.other_ref = bf16[768,128]{1,0:T(8,128)(2,1)S(1)} collective-permute-done((bf16[768,128]{1,0:T(8,128)(2,1)S(1)}, bf16[768,128]{1,0:T(8,128)(2,1)S(1)}, u32[]{:S(2)}, u32[]{:S(2)}) %collective-permute-start.7) | collective-permute-done | bytes 196640 | tf_op jit(solution)/shard_map/ppermute | solution.py:313
  29.5 0.1 combine.1
  29.6 2.0 %collective-permute-start.8 = (bf16[256,128]{1,0:T(8,128)(2,1)S(1)}, bf16[256,128]{1,0:T(8,128)(2,1)S(1)}, u32[]{:S(2)}, u32[]{:S(2)}) collective-permute-start(bf16[256,128]{1,0:T(8,128)(2,1)S(1)} %get-tuple-element.18), channel_id=1, source_target_pairs={{0,2},{2,0},{4,6},{6,4},{8,10},{10,8},{12,14},{14,12},{16,18},{18,... | collective-permute-start | bytes 196616 | tf_op jit(solution)/shard_map/ppermute | solution.py:316
  31.5 3.9 %collective-permute-start.9 = (bf16[256,128]{1,0:T(8,128)(2,1)S(1)}, bf16[256,128]{1,0:T(8,128)(2,1)S(1)}, u32[]{:S(2)}, u32[]{:S(2)}) collective-permute-start(bf16[256,128]{1,0:T(8,128)(2,1)S(1)} %get-tuple-element.19), channel_id=1, source_target_pairs={{0,4},{2,6},{4,0},{6,2},{8,12},{10,14},{12,8},{14,10},{16,20},{18,... | collective-permute-start | bytes 196616 | tf_op jit(solution)/shard_map/ppermute | solution.py:316
  35.4 3.3 %collective-permute-start.10 = (bf16[256,128]{1,0:T(8,128)(2,1)S(1)}, bf16[256,128]{1,0:T(8,128)(2,1)S(1)}, u32[]{:S(2)}, u32[]{:S(2)}) collective-permute-start(bf16[256,128]{1,0:T(8,128)(2,1)S(1)} %get-tuple-element.20), channel_id=1, source_target_pairs={{0,6},{2,4},{4,2},{6,0},{8,14},{10,12},{12,10},{14,8},{16,22},{18,... | collective-permute-start | bytes 196616 | tf_op jit(solution)/shard_map/ppermute | solution.py:316
  38.8 0.0 collective-permute-done.8.refs_0_
  38.8 0.0 collective-permute-done.9.refs_1_
  38.8 3.7 %collective-permute-done.10.refs_2_ = bf16[256,128]{1,0:T(8,128)(2,1)S(1)} collective-permute-done((bf16[256,128]{1,0:T(8,128)(2,1)S(1)}, bf16[256,128]{1,0:T(8,128)(2,1)S(1)}, u32[]{:S(2)}, u32[]{:S(2)}) %collective-permute-start.10) | collective-permute-done | bytes 65568 | tf_op jit(solution)/shard_map/ppermute | solution.py:316
  42.5 0.7 %final.1 = (bf16[2,128,128]{2,1,0:T(8,128)(2,1)}, bf16[2,128,128]{2,1,0:T(8,128)(2,1)}) custom-call(bf16[256,128]{1,0:T(8,128)(2,1)S(1)} %get-tuple-element.14.leaf_ref, f32[256,128]{1,0:T(8,128)S(1)} %get-tuple-element.17.own_ref, bf16[256,128]{1,0:T(8,128)(2,1)S(1)} %collective-permute-done.8.refs_0_, bf16[256,128]{1,0:T(8,128)(2,1)S(1)} %collective-permute-done.9.refs_1_, ...), custom_call_target="tpu_custom_call" | custom-call | tf_op jit(solution)/shard_map/final/pallas_call | solution.py:290
  (8 shorter events, 0.0 us)
Async XLA Ops:
  0.6 0.8 %copy-start.2 = (bf16[2,128,128]{2,1,0:T(8,128)(2,1)S(1)}, bf16[2,128,128]{2,1,0:T(8,128)(2,1)}, u32[]{:S(2)}) copy-start(bf16[2,128,128]{2,1,0:T(8,128)(2,1)} %refs_3_.1) | copy-start | bytes 196612
  1.5 0.8 %copy-start.4 = (bf16[2,128,128]{2,1,0:T(8,128)(2,1)S(1)}, bf16[2,128,128]{2,1,0:T(8,128)(2,1)}, u32[]{:S(2)}) copy-start(bf16[2,128,128]{2,1,0:T(8,128)(2,1)} %refs_4_.1) | copy-start | bytes 196612
  2.3 0.7 %copy-start.5 = (s32[2]{0:T(128)S(1)}, s32[2]{0:T(128)}, u32[]{:S(2)}) copy-start(s32[2]{0:T(128)} %refs_0_.1) | copy-start | bytes 28
  3.0 16.3 %copy-start.3 = (bf16[2,128,128]{2,1,0:T(8,128)(2,1)S(1)}, bf16[2,128,128]{2,1,0:T(8,128)(2,1)}, u32[]{:S(2)}) copy-start(bf16[2,128,128]{2,1,0:T(8,128)(2,1)} %refs_3_.1) | copy-start | bytes 196612
  3.0 16.3 %copy-start.6 = (s32[2]{0:T(128)S(1)}, s32[2]{0:T(128)}, u32[]{:S(2)}) copy-start(s32[2]{0:T(128)} %refs_0_.1) | copy-start | bytes 28
  3.5 10.3 %collective-permute-start.3 = (bf16[272,128]{1,0:T(8,128)(2,1)S(1)}, bf16[272,128]{1,0:T(8,128)(2,1)S(1)}, u32[]{:S(2)}, u32[]{:S(2)}) collective-permute-start(bf16[272,128]{1,0:T(8,128)(2,1)S(1)} %pack.1.refs_5_), channel_id=1, source_target_pairs={{0,6},{2,4},{4,2},{6,0},{8,14},{10,12},{12,10},{14,8},{16,22},{18,... | collective-permute-start | bytes 208904 | tf_op jit(solution)/shard_map/ppermute | solution.py:307
  9.3 6.2 %collective-permute-start.2 = (bf16[272,128]{1,0:T(8,128)(2,1)S(1)}, bf16[272,128]{1,0:T(8,128)(2,1)S(1)}, u32[]{:S(2)}, u32[]{:S(2)}) collective-permute-start(bf16[272,128]{1,0:T(8,128)(2,1)S(1)} %pack.1.refs_5_), channel_id=1, source_target_pairs={{0,4},{2,6},{4,0},{6,2},{8,12},{10,14},{12,8},{14,10},{16,20},{18,... | collective-permute-start | bytes 208904 | tf_op jit(solution)/shard_map/ppermute | solution.py:307
  11.8 6.2 %collective-permute-start.1 = (bf16[272,128]{1,0:T(8,128)(2,1)S(1)}, bf16[272,128]{1,0:T(8,128)(2,1)S(1)}, u32[]{:S(2)}, u32[]{:S(2)}) collective-permute-start(bf16[272,128]{1,0:T(8,128)(2,1)S(1)} %pack.1.refs_5_), channel_id=1, source_target_pairs={{0,2},{2,0},{4,6},{6,4},{8,10},{10,8},{12,14},{14,12},{16,18},{18,... | collective-permute-start | bytes 208904 | tf_op jit(solution)/shard_map/ppermute | solution.py:307
  13.7 4.2 %collective-permute-start = (bf16[272,128]{1,0:T(8,128)(2,1)S(1)}, bf16[272,128]{1,0:T(8,128)(2,1)S(1)}, u32[]{:S(2)}, u32[]{:S(2)}) collective-permute-start(bf16[272,128]{1,0:T(8,128)(2,1)S(1)} %pack.1.refs_5_), channel_id=1, source_target_pairs={{0,1},{1,0},{2,3},{3,2},{4,5},{5,4},{6,7},{7,6},{8,9},{9,8},{10,11... | collective-permute-start | bytes 208904 | tf_op jit(solution)/shard_map/ppermute | solution.py:308
  13.8 4.1 %collective-permute-start.6 = (bf16[272,128]{1,0:T(8,128)(2,1)S(1)}, bf16[272,128]{1,0:T(8,128)(2,1)S(1)}, u32[]{:S(2)}, u32[]{:S(2)}) collective-permute-start(bf16[272,128]{1,0:T(8,128)(2,1)S(1)} %collective-permute-done.3.refs_9_), channel_id=1, source_target_pairs={{0,1},{1,0},{2,3},{3,2},{4,5},{5,4},{6,7},{7,6},{8,9},{9,8},{10,11... | collective-permute-start | bytes 208904 | tf_op jit(solution)/shard_map/ppermute | solution.py:309
  15.5 2.4 %collective-permute-start.5 = (bf16[272,128]{1,0:T(8,128)(2,1)S(1)}, bf16[272,128]{1,0:T(8,128)(2,1)S(1)}, u32[]{:S(2)}, u32[]{:S(2)}) collective-permute-start(bf16[272,128]{1,0:T(8,128)(2,1)S(1)} %collective-permute-done.2.refs_8_), channel_id=1, source_target_pairs={{0,1},{1,0},{2,3},{3,2},{4,5},{5,4},{6,7},{7,6},{8,9},{9,8},{10,11... | collective-permute-start | bytes 208904 | tf_op jit(solution)/shard_map/ppermute | solution.py:309
  18.0 1.3 %collective-permute-start.4 = (bf16[272,128]{1,0:T(8,128)(2,1)S(1)}, bf16[272,128]{1,0:T(8,128)(2,1)S(1)}, u32[]{:S(2)}, u32[]{:S(2)}) collective-permute-start(bf16[272,128]{1,0:T(8,128)(2,1)S(1)} %collective-permute-done.1.refs_7_), channel_id=1, source_target_pairs={{0,1},{1,0},{2,3},{3,2},{4,5},{5,4},{6,7},{7,6},{8,9},{9,8},{10,11... | collective-permute-start | bytes 208904 | tf_op jit(solution)/shard_map/ppermute | solution.py:309
  19.2 1.0 %copy-start = (bf16[2,128,1024]{2,1,0:T(8,128)(2,1)S(1)}, bf16[2,128,1024]{2,1,0:T(8,128)(2,1)}, u32[]{:S(2)}) copy-start(bf16[2,128,1024]{2,1,0:T(8,128)(2,1)} %refs_1_.1) | copy-start | bytes 1572868
  20.3 1.0 %copy-start.1 = (bf16[2,128,1024]{2,1,0:T(8,128)(2,1)S(1)}, bf16[2,128,1024]{2,1,0:T(8,128)(2,1)}, u32[]{:S(2)}) copy-start(bf16[2,128,1024]{2,1,0:T(8,128)(2,1)} %refs_2_.1) | copy-start | bytes 1572868
  28.0 1.4 %collective-permute-start.7 = (bf16[768,128]{1,0:T(8,128)(2,1)S(1)}, bf16[768,128]{1,0:T(8,128)(2,1)S(1)}, u32[]{:S(2)}, u32[]{:S(2)}) collective-permute-start(bf16[768,128]{1,0:T(8,128)(2,1)S(1)} %get-tuple-element.16), channel_id=1, source_target_pairs={{0,1},{1,0},{2,3},{3,2},{4,5},{5,4},{6,7},{7,6},{8,9},{9,8},{10,11... | collective-permute-start | bytes 589832 | tf_op jit(solution)/shard_map/ppermute | solution.py:313
  29.6 9.2 %collective-permute-start.8 = (bf16[256,128]{1,0:T(8,128)(2,1)S(1)}, bf16[256,128]{1,0:T(8,128)(2,1)S(1)}, u32[]{:S(2)}, u32[]{:S(2)}) collective-permute-start(bf16[256,128]{1,0:T(8,128)(2,1)S(1)} %get-tuple-element.18), channel_id=1, source_target_pairs={{0,2},{2,0},{4,6},{6,4},{8,10},{10,8},{12,14},{14,12},{16,18},{18,... | collective-permute-start | bytes 196616 | tf_op jit(solution)/shard_map/ppermute | solution.py:316
  31.5 7.3 %collective-permute-start.9 = (bf16[256,128]{1,0:T(8,128)(2,1)S(1)}, bf16[256,128]{1,0:T(8,128)(2,1)S(1)}, u32[]{:S(2)}, u32[]{:S(2)}) collective-permute-start(bf16[256,128]{1,0:T(8,128)(2,1)S(1)} %get-tuple-element.19), channel_id=1, source_target_pairs={{0,4},{2,6},{4,0},{6,2},{8,12},{10,14},{12,8},{14,10},{16,20},{18,... | collective-permute-start | bytes 196616 | tf_op jit(solution)/shard_map/ppermute | solution.py:316
  35.4 7.1 %collective-permute-start.10 = (bf16[256,128]{1,0:T(8,128)(2,1)S(1)}, bf16[256,128]{1,0:T(8,128)(2,1)S(1)}, u32[]{:S(2)}, u32[]{:S(2)}) collective-permute-start(bf16[256,128]{1,0:T(8,128)(2,1)S(1)} %get-tuple-element.20), channel_id=1, source_target_pairs={{0,6},{2,4},{4,2},{6,0},{8,14},{10,12},{12,10},{14,8},{16,22},{18,... | collective-permute-start | bytes 196616 | tf_op jit(solution)/shard_map/ppermute | solution.py:316

commit v3 on v2

--- a/solution.py
+++ b/solution.py
@@ -42,7 +42,7 @@
 
 
 def chip_pairs(mask, count):
-    return [(i, i ^ (mask << 1)) for i in range(0, count, 2)]
+    return [(i, i ^ (mask << 1)) for i in range(count)]
 
 
 def limit(mib):
@@ -66,14 +66,43 @@
         out_shape=jax.ShapeDtypeStruct((2 * rows + TAIL, width), BF16),
         in_specs=[pl.BlockSpec(memory_space=pltpu.SMEM), first, first],
         out_specs=pl.BlockSpec((2 * rows + TAIL, width), lambda step: (0, 0)),
-        compiler_params=limit(1),
         name="pack",
     )(lengths, keys, values)
 
 
+def rows_kernel(heads, lengths_ref, query_ref, grad_ref, query_s, cot_s):
+    rows = query_ref.shape[1]
+    width = query_ref.shape[2] // heads
+    row = lax.broadcasted_iota(jnp.int32, (rows, width), 0)
+    for segment in range(2):
+        live = row < lengths_ref[segment]
+        for head in range(heads):
+            here = pl.ds((segment * heads + head) * rows, rows)
+            columns = slice(head * width, (head + 1) * width)
+            query_s[here, :] = query_ref[segment, :, columns]
+            cot = grad_ref[segment, :, columns]
+            cot_s[here, :] = jnp.where(live, cot, jnp.zeros((), BF16))
+
+
+def rows_call(lengths, queries, grads, width):
+    heads = queries.shape[2] // width
+    rows = queries.shape[1]
+    vmem = pl.BlockSpec(memory_space=pltpu.VMEM)
+    shape = jax.ShapeDtypeStruct((2 * heads * rows, width), BF16)
+    return pl.pallas_call(
+        functools.partial(rows_kernel, heads),
+        out_shape=(shape, shape),
+        in_specs=[pl.BlockSpec(memory_space=pltpu.SMEM), vmem, vmem],
+        out_specs=(vmem, vmem),
+        compiler_params=limit(8),
+        cost_estimate=pl.CostEstimate(flops=0, bytes_accessed=4 << 20, transcendentals=0),
+        name="rows",
+    )(lengths, queries, grads)
+
+
 def main_kernel(depth, heads, *refs):
     masks = (1 << (depth - 1)) - 1
-    lengths_ref, query_ref, grad_ref, key_ref, value_ref, own_ref, mate_ref = refs[:7]
+    lengths_ref, query_s, cot_s, key_ref, value_ref, own_ref, mate_ref = refs[:7]
     near = refs[7 : 7 + masks]
     far = refs[7 + masks : 7 + 2 * masks]
     (
@@ -87,8 +116,6 @@
         keys_t,
         low_s,
         ds_s,
-        query_s,
-        cot_s,
     ) = refs[7 + 2 * masks :]
     rows, width = key_ref.shape[1:]
     index = lax.axis_index("leaf")
@@ -136,18 +163,12 @@
     step_rows = 2 * rows
     for segment in range(2):
         count = (depth + 1 + segment) * rows
-        live = row < lengths_ref[segment]
         keys_wide = jnp.concatenate([keys_s[:count, :], extra_s[segment, :count, :]], 1)
         for pair in range(heads // 2):
             at = (segment * (heads // 2) + pair) * step_rows
             here = slice(at, at + step_rows)
             columns = [slice(h * width, (h + 1) * width) for h in (2 * pair, 2 * pair + 1)]
-            query = jnp.concatenate([query_ref[segment, :, c] for c in columns], 0)
-            cot = jnp.concatenate(
-                [jnp.where(live, grad_ref[segment, :, c], jnp.zeros((), BF16)) for c in columns], 0
-            )
-            query_s[here, :] = query
-            cot_s[here, :] = cot
+            query, cot = query_s[here, :], cot_s[here, :]
             scores = lax.dot_general(
                 keys_wide,
                 jnp.concatenate([query, ruled], 1),
@@ -204,16 +225,16 @@
         put(part_ref, range(depth))
 
 
-def main_call(lengths, queries, grads, keys, values, own, mate, near, far, depth):
+def main_call(lengths, queries, cot, keys, values, own, mate, near, far, depth):
     rows, width = keys.shape[1:]
-    heads = queries.shape[2] // width
+    heads = queries.shape[0] // (2 * rows)
     slots = (depth + 2) * rows
     total = 2 * heads * rows
     vmem = pl.BlockSpec(memory_space=pltpu.VMEM)
     return pl.pallas_call(
         functools.partial(main_kernel, depth, heads),
         out_shape=(
-            jax.ShapeDtypeStruct(queries.shape, BF16),
+            jax.ShapeDtypeStruct((2, rows, heads * width), BF16),
             jax.ShapeDtypeStruct((2 * rows, width), BF16),
             jax.ShapeDtypeStruct((depth * 2 * rows, width), BF16),
             jax.ShapeDtypeStruct((depth * 2 * rows, width), F32),
@@ -227,12 +248,10 @@
             pltpu.VMEM((width, slots), BF16),
             pltpu.VMEM((slots, total), BF16),
             pltpu.VMEM((slots, total), BF16),
-            pltpu.VMEM((total, width), BF16),
-            pltpu.VMEM((total, width), BF16),
         ],
         compiler_params=limit(24),
         name="attend",
-    )(lengths, queries, grads, keys, values, own, mate, *near, *far)
+    )(lengths, queries, cot, keys, values, own, mate, *near, *far)
 
 
 def combine_kernel(depth, part_ref, other_ref, own_ref, *rest):
@@ -306,9 +325,11 @@
     pack = make_pack(lengths, key_states, value_states)
     near = [lax.ppermute(pack, "leaf", chip_pairs(m, count)) for m in masks]
     mate = lax.ppermute(pack, "leaf", swap_pairs)
+    query_rows, cot = rows_call(lengths, queries, grad_output, key_states.shape[2])
+    near, query_rows, cot = lax.optimization_barrier((near, query_rows, cot))
     far = [lax.ppermute(block, "leaf", swap_pairs) for block in near]
     grad_queries, leaf, swap, part = main_call(
-        lengths, queries, grad_output, key_states, value_states, pack, mate, near, far, depth
+        lengths, query_rows, cot, key_states, value_states, pack, mate, near, far, depth
     )
     other = lax.ppermute(swap, "leaf", swap_pairs)
     own, *sends = combine_call(part, other, depth)

time: 43.7 us -> 29.4 us (0.67)
  starting transfers between devices: 20.1 us -> 8.65 us
  local copies, waits for them, and re-layouts: 4.42 us -> 2.1 us
  waiting for transfers between devices: 9.88 us -> 7.96 us
  Pallas kernels: 8.04 us -> 9.71 us
    ppermute x3, starting transfers between devices: 10.2 us -> 4.46 us  [body(): near = [lax.ppermute(pack, 'leaf', chip_pairs(m, count)) for m in masks]]
    ppermute x3, starting transfers between devices: 9.21 us -> 3.55 us  [body(): lax.ppermute(block, 'leaf', chip_pairs(m, count))]
    unnamed x14 -> x12, local copies, waits for them, and re-layouts: 4.42 us -> 2.1 us
    ppermute x3, waiting for transfers between devices: 3.64 us -> 1.57 us  [body(): near = [lax.ppermute(pack, 'leaf', chip_pairs(m, count)) for m in masks]]
    pallas_call x1, Pallas kernels: 0.55 us -> 1.47 us  [make_pack(): pl.pallas_call(pack_kernel, grid=(1,), out_shape=jax.ShapeDtypeStruct((2...]
    pallas_call x0 -> x1, Pallas kernels: none -> 0.78 us  [rows_call(): pl.pallas_call(functools.partial(rows_kernel, heads), out_shape=(shape, s...]
  transfers between devices with their start and end apart: 11 -> 11, of which waited for: 5 -> 9; matrix products, arithmetic and copies ran while one was open for 0% -> 0% of each run, Pallas kernels for 0% -> 3%
where the time goes in v3:
time: 29.4 us; the launch traced here: 29.1 us
  Pallas kernels  9.71 us (33%)
  starting transfers between devices  8.65 us (29%)
  waiting for transfers between devices  7.96 us (27%)
  local copies, waits for them, and re-layouts  2.1 us (7%)
  between operations  0.69 us (2%)
    pallas_call x1, Pallas kernels, main_call(): pl.pallas_call(functools.partial(main_kernel, depth, heads), out_shape=(j...  6.71 us
    ppermute x3, starting transfers between devices, body(): near = [lax.ppermute(pack, 'leaf', chip_pairs(m, count)) for m in masks]  4.46 us
    ppermute x3, waiting for transfers between devices, body(): lax.ppermute(block, 'leaf', chip_pairs(m, count))  3.82 us
    ppermute x3, starting transfers between devices, body(): lax.ppermute(block, 'leaf', chip_pairs(m, count))  3.55 us
    unnamed x12, local copies, waits for them, and re-layouts  2.1 us
    ppermute x3, waiting for transfers between devices, body(): near = [lax.ppermute(pack, 'leaf', chip_pairs(m, count)) for m in masks]  1.57 us
    pallas_call x1, Pallas kernels, make_pack(): pl.pallas_call(pack_kernel, grid=(1,), out_shape=jax.ShapeDtypeStruct((2...  1.47 us
    ppermute x1, waiting for transfers between devices, body(): other = lax.ppermute(swap, 'leaf', swap_pairs)  1.32 us
  transfers between devices with their start and end apart: 11, of which 9 were waited for; matrix products, arithmetic and copies ran while one was open for 0% of the time, Pallas kernels for 3%

profile of v3, /device:TPU:0, one launch (start us, length us, event | category | flops | bytes accessed | tf_op | source)
XLA Modules:
  0.0 29.1 jit_solution(11706184352362487273)
XLA Ops:
  0.6 0.0 copy-start.5
  0.6 0.0 copy-start.3
  0.7 1.5 %pack.1.refs_5_ = bf16[272,128]{1,0:T(8,128)(2,1)} custom-call(s32[2]{0:T(128)} %refs_0_.1, bf16[2,128,128]{2,1,0:T(8,128)(2,1)} %refs_3_.1, bf16[2,128,128]{2,1,0:T(8,128)(2,1)} %refs_4_.1), custom_call_target="tpu_custom_call" | custom-call | tf_op jit(solution)/shard_map/pack/pallas_call | solution.py:63
  2.1 3.9 %collective-permute-start.2 = (bf16[272,128]{1,0:T(8,128)(2,1)}, bf16[272,128]{1,0:T(8,128)(2,1)S(1)}, u32[]{:S(2)}, u32[]{:S(2)}) collective-permute-start(bf16[272,128]{1,0:T(8,128)(2,1)} %pack.1.refs_5_), channel_id=1, source_target_pairs={{0,6},{1,7},{2,4},{3,5},{4,2},{5,3},{6,0},{7,1},{8,14},{9,15},{10,... | collective-permute-start | bytes 208904 | tf_op jit(solution)/shard_map/ppermute | solution.py:326
  6.0 0.5 %collective-permute-start.1 = (bf16[272,128]{1,0:T(8,128)(2,1)}, bf16[272,128]{1,0:T(8,128)(2,1)S(1)}, u32[]{:S(2)}, u32[]{:S(2)}) collective-permute-start(bf16[272,128]{1,0:T(8,128)(2,1)} %pack.1.refs_5_), channel_id=1, source_target_pairs={{0,4},{1,5},{2,6},{3,7},{4,0},{5,1},{6,2},{7,3},{8,12},{9,13},{10,... | collective-permute-start | bytes 208904 | tf_op jit(solution)/shard_map/ppermute | solution.py:326
  6.5 0.1 collective-permute-start
  6.6 0.0 collective-permute-start.3
  6.6 1.0 %copy-done = bf16[2,128,1024]{2,1,0:T(8,128)(2,1)S(1)} copy-done((bf16[2,128,1024]{2,1,0:T(8,128)(2,1)S(1)}, bf16[2,128,1024]{2,1,0:T(8,128)(2,1)}, u32[]{:S(2)}) %copy-start) | copy-done | bytes 524312
  7.6 1.0 %copy-done.1 = bf16[2,128,1024]{2,1,0:T(8,128)(2,1)S(1)} copy-done((bf16[2,128,1024]{2,1,0:T(8,128)(2,1)S(1)}, bf16[2,128,1024]{2,1,0:T(8,128)(2,1)}, u32[]{:S(2)}) %copy-start.1) | copy-done | bytes 524312
  8.7 0.8 %rows.1 = (bf16[2048,128]{1,0:T(8,128)(2,1)S(1)}, bf16[2048,128]{1,0:T(8,128)(2,1)S(1)}) custom-call(s32[2]{0:T(128)S(1)} %copy-done.5, bf16[2,128,1024]{2,1,0:T(8,128)(2,1)S(1)} %copy-done, bf16[2,128,1024]{2,1,0:T(8,128)(2,1)S(1)} %copy-done.1), custom_call_target="tpu_custom_call" | custom-call | bytes 4194304 | tf_op jit(solution)/shard_map/rows/pallas_call | solution.py:92
  9.5 0.0 collective-permute-done.2.refs_9_
  9.5 1.1 %collective-permute-done.1.refs_8_ = bf16[272,128]{1,0:T(8,128)(2,1)S(1)} collective-permute-done((bf16[272,128]{1,0:T(8,128)(2,1)}, bf16[272,128]{1,0:T(8,128)(2,1)S(1)}, u32[]{:S(2)}, u32[]{:S(2)}) %collective-permute-start.1) | collective-permute-done | bytes 69664 | tf_op jit(solution)/shard_map/ppermute | solution.py:326
  10.5 0.5 %collective-permute-done.refs_7_ = bf16[272,128]{1,0:T(8,128)(2,1)S(1)} collective-permute-done((bf16[272,128]{1,0:T(8,128)(2,1)}, bf16[272,128]{1,0:T(8,128)(2,1)S(1)}, u32[]{:S(2)}, u32[]{:S(2)}) %collective-permute-start) | collective-permute-done | bytes 69664 | tf_op jit(solution)/shard_map/ppermute | solution.py:326
  11.1 0.0 collective-permute-start.4
  11.1 0.5 %collective-permute-start.5 = (bf16[272,128]{1,0:T(8,128)(2,1)S(1)}, bf16[272,128]{1,0:T(8,128)(2,1)S(1)}, u32[]{:S(2)}, u32[]{:S(2)}) collective-permute-start(bf16[272,128]{1,0:T(8,128)(2,1)S(1)} %collective-permute-done.1.refs_8_), channel_id=1, source_target_pairs={{0,1},{1,0},{2,3},{3,2},{4,5},{5,4},{6,7},{7,6},{8,9},{9,8},{10,11... | collective-permute-start | bytes 208904 | tf_op jit(solution)/shard_map/ppermute | solution.py:330
  11.6 0.0 collective-permute-start.6
  11.6 0.0 collective-permute-done.3.refs_6_
  11.6 0.7 %collective-permute-done.4.refs_10_ = bf16[272,128]{1,0:T(8,128)(2,1)S(1)} collective-permute-done((bf16[272,128]{1,0:T(8,128)(2,1)S(1)}, bf16[272,128]{1,0:T(8,128)(2,1)S(1)}, u32[]{:S(2)}, u32[]{:S(2)}) %collective-permute-start.4) | collective-permute-done | bytes 69664 | tf_op jit(solution)/shard_map/ppermute | solution.py:330
  12.3 0.2 collective-permute-done.5.refs_11_
  12.5 0.4 %collective-permute-done.6.refs_12_ = bf16[272,128]{1,0:T(8,128)(2,1)S(1)} collective-permute-done((bf16[272,128]{1,0:T(8,128)(2,1)S(1)}, bf16[272,128]{1,0:T(8,128)(2,1)S(1)}, u32[]{:S(2)}, u32[]{:S(2)}) %collective-permute-start.6) | collective-permute-done | bytes 69664 | tf_op jit(solution)/shard_map/ppermute | solution.py:330
  12.8 0.0 copy-done.3
  12.8 6.7 %attend.1 = (bf16[2,128,1024]{2,1,0:T(8,128)(2,1)}, bf16[256,128]{1,0:T(8,128)(2,1)S(1)}, bf16[768,128]{1,0:T(8,128)(2,1)S(1)}, f32[768,128]{1,0:T(8,128)S(1)}) custom-call(s32[2]{0:T(128)S(1)} %copy-done.5, bf16[2048,128]{1,0:T(8,128)(2,1)S(1)} %get-tuple-element.22.refs_1_, bf16[2048,128]{1,0:T(8,128)(2,1)S(1)} %get-tuple-element.23.refs_2_, ...), custom_call_target="tpu_custom_call" | custom-call | tf_op jit(solution)/shard_map/attend/pallas_call | solution.py:234
  19.5 0.1 collective-permute-start.7
  19.7 1.3 %collective-permute-done.7.other_ref = bf16[768,128]{1,0:T(8,128)(2,1)S(1)} collective-permute-done((bf16[768,128]{1,0:T(8,128)(2,1)S(1)}, bf16[768,128]{1,0:T(8,128)(2,1)S(1)}, u32[]{:S(2)}, u32[]{:S(2)}) %collective-permute-start.7) | collective-permute-done | bytes 196640 | tf_op jit(solution)/shard_map/ppermute | solution.py:334
  21.0 0.1 combine.1
  21.1 0.7 %collective-permute-start.8 = (bf16[256,128]{1,0:T(8,128)(2,1)S(1)}, bf16[256,128]{1,0:T(8,128)(2,1)S(1)}, u32[]{:S(2)}, u32[]{:S(2)}) collective-permute-start(bf16[256,128]{1,0:T(8,128)(2,1)S(1)} %get-tuple-element.32), channel_id=1, source_target_pairs={{0,2},{1,3},{2,0},{3,1},{4,6},{5,7},{6,4},{7,5},{8,10},{9,11},{10,... | collective-permute-start | bytes 196616 | tf_op jit(solution)/shard_map/ppermute | solution.py:337
  21.7 1.5 %collective-permute-start.9 = (bf16[256,128]{1,0:T(8,128)(2,1)S(1)}, bf16[256,128]{1,0:T(8,128)(2,1)S(1)}, u32[]{:S(2)}, u32[]{:S(2)}) collective-permute-start(bf16[256,128]{1,0:T(8,128)(2,1)S(1)} %get-tuple-element.33), channel_id=1, source_target_pairs={{0,4},{1,5},{2,6},{3,7},{4,0},{5,1},{6,2},{7,3},{8,12},{9,13},{10,... | collective-permute-start | bytes 196616 | tf_op jit(solution)/shard_map/ppermute | solution.py:337
  23.3 1.3 %collective-permute-start.10 = (bf16[256,128]{1,0:T(8,128)(2,1)S(1)}, bf16[256,128]{1,0:T(8,128)(2,1)S(1)}, u32[]{:S(2)}, u32[]{:S(2)}) collective-permute-start(bf16[256,128]{1,0:T(8,128)(2,1)S(1)} %get-tuple-element.34), channel_id=1, source_target_pairs={{0,6},{1,7},{2,4},{3,5},{4,2},{5,3},{6,0},{7,1},{8,14},{9,15},{10,... | collective-permute-start | bytes 196616 | tf_op jit(solution)/shard_map/ppermute | solution.py:337
  24.6 0.8 %collective-permute-done.8.refs_0_ = bf16[256,128]{1,0:T(8,128)(2,1)S(1)} collective-permute-done((bf16[256,128]{1,0:T(8,128)(2,1)S(1)}, bf16[256,128]{1,0:T(8,128)(2,1)S(1)}, u32[]{:S(2)}, u32[]{:S(2)}) %collective-permute-start.8) | collective-permute-done | bytes 65568 | tf_op jit(solution)/shard_map/ppermute | solution.py:337
  25.4 0.6 %collective-permute-done.9.refs_1_ = bf16[256,128]{1,0:T(8,128)(2,1)S(1)} collective-permute-done((bf16[256,128]{1,0:T(8,128)(2,1)S(1)}, bf16[256,128]{1,0:T(8,128)(2,1)S(1)}, u32[]{:S(2)}, u32[]{:S(2)}) %collective-permute-start.9) | collective-permute-done | bytes 65568 | tf_op jit(solution)/shard_map/ppermute | solution.py:337
  26.0 2.4 %collective-permute-done.10.refs_2_ = bf16[256,128]{1,0:T(8,128)(2,1)S(1)} collective-permute-done((bf16[256,128]{1,0:T(8,128)(2,1)S(1)}, bf16[256,128]{1,0:T(8,128)(2,1)S(1)}, u32[]{:S(2)}, u32[]{:S(2)}) %collective-permute-start.10) | collective-permute-done | bytes 65568 | tf_op jit(solution)/shard_map/ppermute | solution.py:337
  28.4 0.7 %final.1 = (bf16[2,128,128]{2,1,0:T(8,128)(2,1)}, bf16[2,128,128]{2,1,0:T(8,128)(2,1)}) custom-call(bf16[256,128]{1,0:T(8,128)(2,1)S(1)} %get-tuple-element.28.leaf_ref, f32[256,128]{1,0:T(8,128)S(1)} %get-tuple-element.31.own_ref, bf16[256,128]{1,0:T(8,128)(2,1)S(1)} %collective-permute-done.8.refs_0_, bf16[256,128]{1,0:T(8,128)(2,1)S(1)} %collective-permute-done.9.refs_1_, ...), custom_call_target="tpu_custom_call" | custom-call | tf_op jit(solution)/shard_map/final/pallas_call | solution.py:309
  (7 shorter events, 0.0 us)
Async XLA Ops:
  0.6 6.0 %copy-start.5 = (s32[2]{0:T(128)S(1)}, s32[2]{0:T(128)}, u32[]{:S(2)}) copy-start(s32[2]{0:T(128)} %refs_0_.1) | copy-start | bytes 28
  0.6 12.2 %copy-start.3 = (bf16[2,128,128]{2,1,0:T(8,128)(2,1)S(1)}, bf16[2,128,128]{2,1,0:T(8,128)(2,1)}, u32[]{:S(2)}) copy-start(bf16[2,128,128]{2,1,0:T(8,128)(2,1)} %refs_3_.1) | copy-start | bytes 196612
  0.7 12.2 %copy-start.4 = (bf16[2,128,128]{2,1,0:T(8,128)(2,1)S(1)}, bf16[2,128,128]{2,1,0:T(8,128)(2,1)}, u32[]{:S(2)}) copy-start(bf16[2,128,128]{2,1,0:T(8,128)(2,1)} %refs_4_.1) | copy-start | bytes 196612
  2.1 7.3 %collective-permute-start.2 = (bf16[272,128]{1,0:T(8,128)(2,1)}, bf16[272,128]{1,0:T(8,128)(2,1)S(1)}, u32[]{:S(2)}, u32[]{:S(2)}) collective-permute-start(bf16[272,128]{1,0:T(8,128)(2,1)} %pack.1.refs_5_), channel_id=1, source_target_pairs={{0,6},{1,7},{2,4},{3,5},{4,2},{5,3},{6,0},{7,1},{8,14},{9,15},{10,... | collective-permute-start | bytes 208904 | tf_op jit(solution)/shard_map/ppermute | solution.py:326
  6.0 4.5 %collective-permute-start.1 = (bf16[272,128]{1,0:T(8,128)(2,1)}, bf16[272,128]{1,0:T(8,128)(2,1)S(1)}, u32[]{:S(2)}, u32[]{:S(2)}) collective-permute-start(bf16[272,128]{1,0:T(8,128)(2,1)} %pack.1.refs_5_), channel_id=1, source_target_pairs={{0,4},{1,5},{2,6},{3,7},{4,0},{5,1},{6,2},{7,3},{8,12},{9,13},{10,... | collective-permute-start | bytes 208904 | tf_op jit(solution)/shard_map/ppermute | solution.py:326
  6.5 4.5 %collective-permute-start = (bf16[272,128]{1,0:T(8,128)(2,1)}, bf16[272,128]{1,0:T(8,128)(2,1)S(1)}, u32[]{:S(2)}, u32[]{:S(2)}) collective-permute-start(bf16[272,128]{1,0:T(8,128)(2,1)} %pack.1.refs_5_), channel_id=1, source_target_pairs={{0,2},{1,3},{2,0},{3,1},{4,6},{5,7},{6,4},{7,5},{8,10},{9,11},{10,... | collective-permute-start | bytes 208904 | tf_op jit(solution)/shard_map/ppermute | solution.py:326
  6.6 5.0 %collective-permute-start.3 = (bf16[272,128]{1,0:T(8,128)(2,1)}, bf16[272,128]{1,0:T(8,128)(2,1)S(1)}, u32[]{:S(2)}, u32[]{:S(2)}) collective-permute-start(bf16[272,128]{1,0:T(8,128)(2,1)} %pack.1.refs_5_), channel_id=1, source_target_pairs={{0,1},{1,0},{2,3},{3,2},{4,5},{5,4},{6,7},{7,6},{8,9},{9,8},{10,11... | collective-permute-start | bytes 208904 | tf_op jit(solution)/shard_map/ppermute | solution.py:327
  6.6 1.0 %copy-start = (bf16[2,128,1024]{2,1,0:T(8,128)(2,1)S(1)}, bf16[2,128,1024]{2,1,0:T(8,128)(2,1)}, u32[]{:S(2)}) copy-start(bf16[2,128,1024]{2,1,0:T(8,128)(2,1)} %query_ref.1) | copy-start | bytes 1572868
  7.6 1.0 %copy-start.1 = (bf16[2,128,1024]{2,1,0:T(8,128)(2,1)S(1)}, bf16[2,128,1024]{2,1,0:T(8,128)(2,1)}, u32[]{:S(2)}) copy-start(bf16[2,128,1024]{2,1,0:T(8,128)(2,1)} %grad_ref.1) | copy-start | bytes 1572868
  8.7 4.1 %copy-start.2 = (bf16[272,128]{1,0:T(8,128)(2,1)S(1)}, bf16[272,128]{1,0:T(8,128)(2,1)}, u32[]{:S(2)}) copy-start(bf16[272,128]{1,0:T(8,128)(2,1)} %pack.1.refs_5_) | copy-start | bytes 208900
  11.1 1.3 %collective-permute-start.4 = (bf16[272,128]{1,0:T(8,128)(2,1)S(1)}, bf16[272,128]{1,0:T(8,128)(2,1)S(1)}, u32[]{:S(2)}, u32[]{:S(2)}) collective-permute-start(bf16[272,128]{1,0:T(8,128)(2,1)S(1)} %collective-permute-done.refs_7_), channel_id=1, source_target_pairs={{0,1},{1,0},{2,3},{3,2},{4,5},{5,4},{6,7},{7,6},{8,9},{9,8},{10,11... | collective-permute-start | bytes 208904 | tf_op jit(solution)/shard_map/ppermute | solution.py:330
  11.1 1.4 %collective-permute-start.5 = (bf16[272,128]{1,0:T(8,128)(2,1)S(1)}, bf16[272,128]{1,0:T(8,128)(2,1)S(1)}, u32[]{:S(2)}, u32[]{:S(2)}) collective-permute-start(bf16[272,128]{1,0:T(8,128)(2,1)S(1)} %collective-permute-done.1.refs_8_), channel_id=1, source_target_pairs={{0,1},{1,0},{2,3},{3,2},{4,5},{5,4},{6,7},{7,6},{8,9},{9,8},{10,11... | collective-permute-start | bytes 208904 | tf_op jit(solution)/shard_map/ppermute | solution.py:330
  11.6 1.3 %collective-permute-start.6 = (bf16[272,128]{1,0:T(8,128)(2,1)S(1)}, bf16[272,128]{1,0:T(8,128)(2,1)S(1)}, u32[]{:S(2)}, u32[]{:S(2)}) collective-permute-start(bf16[272,128]{1,0:T(8,128)(2,1)S(1)} %collective-permute-done.2.refs_9_), channel_id=1, source_target_pairs={{0,1},{1,0},{2,3},{3,2},{4,5},{5,4},{6,7},{7,6},{8,9},{9,8},{10,11... | collective-permute-start | bytes 208904 | tf_op jit(solution)/shard_map/ppermute | solution.py:330
  19.5 1.4 %collective-permute-start.7 = (bf16[768,128]{1,0:T(8,128)(2,1)S(1)}, bf16[768,128]{1,0:T(8,128)(2,1)S(1)}, u32[]{:S(2)}, u32[]{:S(2)}) collective-permute-start(bf16[768,128]{1,0:T(8,128)(2,1)S(1)} %get-tuple-element.30), channel_id=1, source_target_pairs={{0,1},{1,0},{2,3},{3,2},{4,5},{5,4},{6,7},{7,6},{8,9},{9,8},{10,11... | collective-permute-start | bytes 589832 | tf_op jit(solution)/shard_map/ppermute | solution.py:334
  21.1 4.3 %collective-permute-start.8 = (bf16[256,128]{1,0:T(8,128)(2,1)S(1)}, bf16[256,128]{1,0:T(8,128)(2,1)S(1)}, u32[]{:S(2)}, u32[]{:S(2)}) collective-permute-start(bf16[256,128]{1,0:T(8,128)(2,1)S(1)} %get-tuple-element.32), channel_id=1, source_target_pairs={{0,2},{1,3},{2,0},{3,1},{4,6},{5,7},{6,4},{7,5},{8,10},{9,11},{10,... | collective-permute-start | bytes 196616 | tf_op jit(solution)/shard_map/ppermute | solution.py:337
  21.7 4.3 %collective-permute-start.9 = (bf16[256,128]{1,0:T(8,128)(2,1)S(1)}, bf16[256,128]{1,0:T(8,128)(2,1)S(1)}, u32[]{:S(2)}, u32[]{:S(2)}) collective-permute-start(bf16[256,128]{1,0:T(8,128)(2,1)S(1)} %get-tuple-element.33), channel_id=1, source_target_pairs={{0,4},{1,5},{2,6},{3,7},{4,0},{5,1},{6,2},{7,3},{8,12},{9,13},{10,... | collective-permute-start | bytes 196616 | tf_op jit(solution)/shard_map/ppermute | solution.py:337
  23.3 5.2 %collective-permute-start.10 = (bf16[256,128]{1,0:T(8,128)(2,1)S(1)}, bf16[256,128]{1,0:T(8,128)(2,1)S(1)}, u32[]{:S(2)}, u32[]{:S(2)}) collective-permute-start(bf16[256,128]{1,0:T(8,128)(2,1)S(1)} %get-tuple-element.34), channel_id=1, source_target_pairs={{0,6},{1,7},{2,4},{3,5},{4,2},{5,3},{6,0},{7,1},{8,14},{9,15},{10,... | collective-permute-start | bytes 196616 | tf_op jit(solution)/shard_map/ppermute | solution.py:337

commit v4 on v3

--- a/solution.py
+++ b/solution.py
@@ -42,7 +42,7 @@
 
 
 def chip_pairs(mask, count):
-    return [(i, i ^ (mask << 1)) for i in range(count)]
+    return [(i, i if i & 1 else i ^ (mask << 1)) for i in range(count)]
 
 
 def limit(mib):

time: 29.4 us -> 41 us (1.39)
  starting transfers between devices: 8.65 us -> 20.1 us
    ppermute x3, starting transfers between devices: 4.46 us -> 10.2 us  [body(): near = [lax.ppermute(pack, 'leaf', chip_pairs(m, count)) for m in masks]]
    ppermute x3, starting transfers between devices: 3.55 us -> 9.21 us  [body(): lax.ppermute(block, 'leaf', chip_pairs(m, count))]
  transfers between devices with their start and end apart: 11 -> 11, of which waited for: 9 -> 6; matrix products, arithmetic and copies ran while one was open for 0% -> 0% of each run, Pallas kernels for 3% -> 2%
where the time goes in v4:
time: 41 us; the launch traced here: 40.6 us
  starting transfers between devices  20.1 us (49%)
  Pallas kernels  9.71 us (24%)
  waiting for transfers between devices  7.89 us (19%)
  local copies, waits for them, and re-layouts  2.09 us (5%)
  between operations  0.78 us (2%)
    ppermute x3, starting transfers between devices, body(): near = [lax.ppermute(pack, 'leaf', chip_pairs(m, count)) for m in masks]  10.2 us
    ppermute x3, starting transfers between devices, body(): lax.ppermute(block, 'leaf', chip_pairs(m, count))  9.21 us
    pallas_call x1, Pallas kernels, main_call(): pl.pallas_call(functools.partial(main_kernel, depth, heads), out_shape=(j...  6.71 us
    ppermute x3, waiting for transfers between devices, body(): lax.ppermute(block, 'leaf', chip_pairs(m, count))  3.87 us
    unnamed x12, local copies, waits for them, and re-layouts  2.09 us
    pallas_call x1, Pallas kernels, make_pack(): pl.pallas_call(pack_kernel, grid=(1,), out_shape=jax.ShapeDtypeStruct((2...  1.47 us
    ppermute x3, waiting for transfers between devices, body(): near = [lax.ppermute(pack, 'leaf', chip_pairs(m, count)) for m in masks]  1.45 us
    ppermute x1, waiting for transfers between devices, body(): other = lax.ppermute(swap, 'leaf', swap_pairs)  1.32 us
  transfers between devices with their start and end apart: 11, of which 6 were waited for; matrix products, arithmetic and copies ran while one was open for 0% of the time, Pallas kernels for 2%

profile of v4, /device:TPU:0, one launch (start us, length us, event | category | flops | bytes accessed | tf_op | source)
XLA Modules:
  0.0 40.6 jit_solution(4792429430348281222)
XLA Ops:
  0.6 0.0 copy-start.5
  0.6 0.0 copy-start.3
  0.7 1.5 %pack.1.refs_5_ = bf16[272,128]{1,0:T(8,128)(2,1)} custom-call(s32[2]{0:T(128)} %refs_0_.1, bf16[2,128,128]{2,1,0:T(8,128)(2,1)} %refs_3_.1, bf16[2,128,128]{2,1,0:T(8,128)(2,1)} %refs_4_.1), custom_call_target="tpu_custom_call" | custom-call | tf_op jit(solution)/shard_map/pack/pallas_call | solution.py:63
  2.1 5.8 %collective-permute-start.2 = (bf16[272,128]{1,0:T(8,128)(2,1)}, bf16[272,128]{1,0:T(8,128)(2,1)S(1)}, u32[]{:S(2)}, u32[]{:S(2)}) collective-permute-start(bf16[272,128]{1,0:T(8,128)(2,1)} %pack.1.refs_5_), channel_id=1, source_target_pairs={{0,6},{1,1},{2,4},{3,3},{4,2},{5,5},{6,0},{7,7},{8,14},{9,9},{10,1... | collective-permute-start | bytes 208904 | tf_op jit(solution)/shard_map/ppermute | solution.py:326
  7.9 2.4 %collective-permute-start.1 = (bf16[272,128]{1,0:T(8,128)(2,1)}, bf16[272,128]{1,0:T(8,128)(2,1)S(1)}, u32[]{:S(2)}, u32[]{:S(2)}) collective-permute-start(bf16[272,128]{1,0:T(8,128)(2,1)} %pack.1.refs_5_), channel_id=1, source_target_pairs={{0,4},{1,1},{2,6},{3,3},{4,0},{5,5},{6,2},{7,7},{8,12},{9,9},{10,1... | collective-permute-start | bytes 208904 | tf_op jit(solution)/shard_map/ppermute | solution.py:326
  10.3 2.0 %collective-permute-start = (bf16[272,128]{1,0:T(8,128)(2,1)}, bf16[272,128]{1,0:T(8,128)(2,1)S(1)}, u32[]{:S(2)}, u32[]{:S(2)}) collective-permute-start(bf16[272,128]{1,0:T(8,128)(2,1)} %pack.1.refs_5_), channel_id=1, source_target_pairs={{0,2},{1,1},{2,0},{3,3},{4,6},{5,5},{6,4},{7,7},{8,10},{9,9},{10,8... | collective-permute-start | bytes 208904 | tf_op jit(solution)/shard_map/ppermute | solution.py:326
  12.3 0.1 collective-permute-start.3
  12.4 0.0 copy-start
  12.4 1.0 %copy-done = bf16[2,128,1024]{2,1,0:T(8,128)(2,1)S(1)} copy-done((bf16[2,128,1024]{2,1,0:T(8,128)(2,1)S(1)}, bf16[2,128,1024]{2,1,0:T(8,128)(2,1)}, u32[]{:S(2)}) %copy-start) | copy-done | bytes 524312
  13.5 1.0 %copy-done.1 = bf16[2,128,1024]{2,1,0:T(8,128)(2,1)S(1)} copy-done((bf16[2,128,1024]{2,1,0:T(8,128)(2,1)S(1)}, bf16[2,128,1024]{2,1,0:T(8,128)(2,1)}, u32[]{:S(2)}) %copy-start.1) | copy-done | bytes 524312
  14.5 0.8 %rows.1 = (bf16[2048,128]{1,0:T(8,128)(2,1)S(1)}, bf16[2048,128]{1,0:T(8,128)(2,1)S(1)}) custom-call(s32[2]{0:T(128)S(1)} %copy-done.5, bf16[2,128,1024]{2,1,0:T(8,128)(2,1)S(1)} %copy-done, bf16[2,128,1024]{2,1,0:T(8,128)(2,1)S(1)} %copy-done.1), custom_call_target="tpu_custom_call" | custom-call | bytes 4194304 | tf_op jit(solution)/shard_map/rows/pallas_call | solution.py:92
  15.3 0.0 collective-permute-done.2.refs_9_
  15.3 0.0 collective-permute-done.1.refs_8_
  15.3 1.4 %collective-permute-done.refs_7_ = bf16[272,128]{1,0:T(8,128)(2,1)S(1)} collective-permute-done((bf16[272,128]{1,0:T(8,128)(2,1)}, bf16[272,128]{1,0:T(8,128)(2,1)S(1)}, u32[]{:S(2)}, u32[]{:S(2)}) %collective-permute-start) | collective-permute-done | bytes 69664 | tf_op jit(solution)/shard_map/ppermute | solution.py:326
  16.8 0.0 collective-permute-start.4
  16.8 0.5 %collective-permute-start.5 = (bf16[272,128]{1,0:T(8,128)(2,1)S(1)}, bf16[272,128]{1,0:T(8,128)(2,1)S(1)}, u32[]{:S(2)}, u32[]{:S(2)}) collective-permute-start(bf16[272,128]{1,0:T(8,128)(2,1)S(1)} %collective-permute-done.1.refs_8_), channel_id=1, source_target_pairs={{0,1},{1,0},{2,3},{3,2},{4,5},{5,4},{6,7},{7,6},{8,9},{9,8},{10,11... | collective-permute-start | bytes 208904 | tf_op jit(solution)/shard_map/ppermute | solution.py:330
  17.3 0.0 collective-permute-start.6
  17.3 0.0 collective-permute-done.3.refs_6_
  17.3 0.7 %collective-permute-done.4.refs_10_ = bf16[272,128]{1,0:T(8,128)(2,1)S(1)} collective-permute-done((bf16[272,128]{1,0:T(8,128)(2,1)S(1)}, bf16[272,128]{1,0:T(8,128)(2,1)S(1)}, u32[]{:S(2)}, u32[]{:S(2)}) %collective-permute-start.4) | collective-permute-done | bytes 69664 | tf_op jit(solution)/shard_map/ppermute | solution.py:330
  18.0 0.2 collective-permute-done.5.refs_11_
  18.2 0.4 collective-permute-done.6.refs_12_
  18.5 6.7 %attend.1 = (bf16[2,128,1024]{2,1,0:T(8,128)(2,1)}, bf16[256,128]{1,0:T(8,128)(2,1)S(1)}, bf16[768,128]{1,0:T(8,128)(2,1)S(1)}, f32[768,128]{1,0:T(8,128)S(1)}) custom-call(s32[2]{0:T(128)S(1)} %copy-done.5, bf16[2048,128]{1,0:T(8,128)(2,1)S(1)} %get-tuple-element.22.refs_1_, bf16[2048,128]{1,0:T(8,128)(2,1)S(1)} %get-tuple-element.23.refs_2_, ...), custom_call_target="tpu_custom_call" | custom-call | tf_op jit(solution)/shard_map/attend/pallas_call | solution.py:234
  25.3 0.1 collective-permute-start.7
  25.4 1.3 %collective-permute-done.7.other_ref = bf16[768,128]{1,0:T(8,128)(2,1)S(1)} collective-permute-done((bf16[768,128]{1,0:T(8,128)(2,1)S(1)}, bf16[768,128]{1,0:T(8,128)(2,1)S(1)}, u32[]{:S(2)}, u32[]{:S(2)}) %collective-permute-start.7) | collective-permute-done | bytes 196640 | tf_op jit(solution)/shard_map/ppermute | solution.py:334
  26.7 0.1 combine.1
  26.8 2.6 %collective-permute-start.8 = (bf16[256,128]{1,0:T(8,128)(2,1)S(1)}, bf16[256,128]{1,0:T(8,128)(2,1)S(1)}, u32[]{:S(2)}, u32[]{:S(2)}) collective-permute-start(bf16[256,128]{1,0:T(8,128)(2,1)S(1)} %get-tuple-element.32), channel_id=1, source_target_pairs={{0,2},{1,1},{2,0},{3,3},{4,6},{5,5},{6,4},{7,7},{8,10},{9,9},{10,8... | collective-permute-start | bytes 196616 | tf_op jit(solution)/shard_map/ppermute | solution.py:337
  29.4 3.4 %collective-permute-start.9 = (bf16[256,128]{1,0:T(8,128)(2,1)S(1)}, bf16[256,128]{1,0:T(8,128)(2,1)S(1)}, u32[]{:S(2)}, u32[]{:S(2)}) collective-permute-start(bf16[256,128]{1,0:T(8,128)(2,1)S(1)} %get-tuple-element.33), channel_id=1, source_target_pairs={{0,4},{1,1},{2,6},{3,3},{4,0},{5,5},{6,2},{7,7},{8,12},{9,9},{10,1... | collective-permute-start | bytes 196616 | tf_op jit(solution)/shard_map/ppermute | solution.py:337
  32.8 3.2 %collective-permute-start.10 = (bf16[256,128]{1,0:T(8,128)(2,1)S(1)}, bf16[256,128]{1,0:T(8,128)(2,1)S(1)}, u32[]{:S(2)}, u32[]{:S(2)}) collective-permute-start(bf16[256,128]{1,0:T(8,128)(2,1)S(1)} %get-tuple-element.34), channel_id=1, source_target_pairs={{0,6},{1,1},{2,4},{3,3},{4,2},{5,5},{6,0},{7,7},{8,14},{9,9},{10,1... | collective-permute-start | bytes 196616 | tf_op jit(solution)/shard_map/ppermute | solution.py:337
  36.0 0.0 collective-permute-done.8.refs_0_
  36.0 0.0 collective-permute-done.9.refs_1_
  36.0 3.9 %collective-permute-done.10.refs_2_ = bf16[256,128]{1,0:T(8,128)(2,1)S(1)} collective-permute-done((bf16[256,128]{1,0:T(8,128)(2,1)S(1)}, bf16[256,128]{1,0:T(8,128)(2,1)S(1)}, u32[]{:S(2)}, u32[]{:S(2)}) %collective-permute-start.10) | collective-permute-done | bytes 65568 | tf_op jit(solution)/shard_map/ppermute | solution.py:337
  39.9 0.7 %final.1 = (bf16[2,128,128]{2,1,0:T(8,128)(2,1)}, bf16[2,128,128]{2,1,0:T(8,128)(2,1)}) custom-call(bf16[256,128]{1,0:T(8,128)(2,1)S(1)} %get-tuple-element.28.leaf_ref, f32[256,128]{1,0:T(8,128)S(1)} %get-tuple-element.31.own_ref, bf16[256,128]{1,0:T(8,128)(2,1)S(1)} %collective-permute-done.8.refs_0_, bf16[256,128]{1,0:T(8,128)(2,1)S(1)} %collective-permute-done.9.refs_1_, ...), custom_call_target="tpu_custom_call" | custom-call | tf_op jit(solution)/shard_map/final/pallas_call | solution.py:309
  (7 shorter events, 0.0 us)
Async XLA Ops:
  0.6 11.8 %copy-start.5 = (s32[2]{0:T(128)S(1)}, s32[2]{0:T(128)}, u32[]{:S(2)}) copy-start(s32[2]{0:T(128)} %refs_0_.1) | copy-start | bytes 28
  0.6 17.9 %copy-start.3 = (bf16[2,128,128]{2,1,0:T(8,128)(2,1)S(1)}, bf16[2,128,128]{2,1,0:T(8,128)(2,1)}, u32[]{:S(2)}) copy-start(bf16[2,128,128]{2,1,0:T(8,128)(2,1)} %refs_3_.1) | copy-start | bytes 196612
  0.7 17.9 %copy-start.4 = (bf16[2,128,128]{2,1,0:T(8,128)(2,1)S(1)}, bf16[2,128,128]{2,1,0:T(8,128)(2,1)}, u32[]{:S(2)}) copy-start(bf16[2,128,128]{2,1,0:T(8,128)(2,1)} %refs_4_.1) | copy-start | bytes 196612
  2.1 13.2 %collective-permute-start.2 = (bf16[272,128]{1,0:T(8,128)(2,1)}, bf16[272,128]{1,0:T(8,128)(2,1)S(1)}, u32[]{:S(2)}, u32[]{:S(2)}) collective-permute-start(bf16[272,128]{1,0:T(8,128)(2,1)} %pack.1.refs_5_), channel_id=1, source_target_pairs={{0,6},{1,1},{2,4},{3,3},{4,2},{5,5},{6,0},{7,7},{8,14},{9,9},{10,1... | collective-permute-start | bytes 208904 | tf_op jit(solution)/shard_map/ppermute | solution.py:326
  7.9 7.4 %collective-permute-start.1 = (bf16[272,128]{1,0:T(8,128)(2,1)}, bf16[272,128]{1,0:T(8,128)(2,1)S(1)}, u32[]{:S(2)}, u32[]{:S(2)}) collective-permute-start(bf16[272,128]{1,0:T(8,128)(2,1)} %pack.1.refs_5_), channel_id=1, source_target_pairs={{0,4},{1,1},{2,6},{3,3},{4,0},{5,5},{6,2},{7,7},{8,12},{9,9},{10,1... | collective-permute-start | bytes 208904 | tf_op jit(solution)/shard_map/ppermute | solution.py:326
  10.3 6.4 %collective-permute-start = (bf16[272,128]{1,0:T(8,128)(2,1)}, bf16[272,128]{1,0:T(8,128)(2,1)S(1)}, u32[]{:S(2)}, u32[]{:S(2)}) collective-permute-start(bf16[272,128]{1,0:T(8,128)(2,1)} %pack.1.refs_5_), channel_id=1, source_target_pairs={{0,2},{1,1},{2,0},{3,3},{4,6},{5,5},{6,4},{7,7},{8,10},{9,9},{10,8... | collective-permute-start | bytes 208904 | tf_op jit(solution)/shard_map/ppermute | solution.py:326
  12.3 4.9 %collective-permute-start.3 = (bf16[272,128]{1,0:T(8,128)(2,1)}, bf16[272,128]{1,0:T(8,128)(2,1)S(1)}, u32[]{:S(2)}, u32[]{:S(2)}) collective-permute-start(bf16[272,128]{1,0:T(8,128)(2,1)} %pack.1.refs_5_), channel_id=1, source_target_pairs={{0,1},{1,0},{2,3},{3,2},{4,5},{5,4},{6,7},{7,6},{8,9},{9,8},{10,11... | collective-permute-start | bytes 208904 | tf_op jit(solution)/shard_map/ppermute | solution.py:327
  12.4 1.0 %copy-start = (bf16[2,128,1024]{2,1,0:T(8,128)(2,1)S(1)}, bf16[2,128,1024]{2,1,0:T(8,128)(2,1)}, u32[]{:S(2)}) copy-start(bf16[2,128,1024]{2,1,0:T(8,128)(2,1)} %query_ref.1) | copy-start | bytes 1572868
  13.5 1.0 %copy-start.1 = (bf16[2,128,1024]{2,1,0:T(8,128)(2,1)S(1)}, bf16[2,128,1024]{2,1,0:T(8,128)(2,1)}, u32[]{:S(2)}) copy-start(bf16[2,128,1024]{2,1,0:T(8,128)(2,1)} %grad_ref.1) | copy-start | bytes 1572868
  14.5 4.0 %copy-start.2 = (bf16[272,128]{1,0:T(8,128)(2,1)S(1)}, bf16[272,128]{1,0:T(8,128)(2,1)}, u32[]{:S(2)}) copy-start(bf16[272,128]{1,0:T(8,128)(2,1)} %pack.1.refs_5_) | copy-start | bytes 208900
  16.8 1.3 %collective-permute-start.4 = (bf16[272,128]{1,0:T(8,128)(2,1)S(1)}, bf16[272,128]{1,0:T(8,128)(2,1)S(1)}, u32[]{:S(2)}, u32[]{:S(2)}) collective-permute-start(bf16[272,128]{1,0:T(8,128)(2,1)S(1)} %collective-permute-done.refs_7_), channel_id=1, source_target_pairs={{0,1},{1,0},{2,3},{3,2},{4,5},{5,4},{6,7},{7,6},{8,9},{9,8},{10,11... | collective-permute-start | bytes 208904 | tf_op jit(solution)/shard_map/ppermute | solution.py:330
  16.8 1.4 %collective-permute-start.5 = (bf16[272,128]{1,0:T(8,128)(2,1)S(1)}, bf16[272,128]{1,0:T(8,128)(2,1)S(1)}, u32[]{:S(2)}, u32[]{:S(2)}) collective-permute-start(bf16[272,128]{1,0:T(8,128)(2,1)S(1)} %collective-permute-done.1.refs_8_), channel_id=1, source_target_pairs={{0,1},{1,0},{2,3},{3,2},{4,5},{5,4},{6,7},{7,6},{8,9},{9,8},{10,11... | collective-permute-start | bytes 208904 | tf_op jit(solution)/shard_map/ppermute | solution.py:330
  17.3 1.3 %collective-permute-start.6 = (bf16[272,128]{1,0:T(8,128)(2,1)S(1)}, bf16[272,128]{1,0:T(8,128)(2,1)S(1)}, u32[]{:S(2)}, u32[]{:S(2)}) collective-permute-start(bf16[272,128]{1,0:T(8,128)(2,1)S(1)} %collective-permute-done.2.refs_9_), channel_id=1, source_target_pairs={{0,1},{1,0},{2,3},{3,2},{4,5},{5,4},{6,7},{7,6},{8,9},{9,8},{10,11... | collective-permute-start | bytes 208904 | tf_op jit(solution)/shard_map/ppermute | solution.py:330
  25.3 1.4 %collective-permute-start.7 = (bf16[768,128]{1,0:T(8,128)(2,1)S(1)}, bf16[768,128]{1,0:T(8,128)(2,1)S(1)}, u32[]{:S(2)}, u32[]{:S(2)}) collective-permute-start(bf16[768,128]{1,0:T(8,128)(2,1)S(1)} %get-tuple-element.30), channel_id=1, source_target_pairs={{0,1},{1,0},{2,3},{3,2},{4,5},{5,4},{6,7},{7,6},{8,9},{9,8},{10,11... | collective-permute-start | bytes 589832 | tf_op jit(solution)/shard_map/ppermute | solution.py:334
  26.8 9.2 %collective-permute-start.8 = (bf16[256,128]{1,0:T(8,128)(2,1)S(1)}, bf16[256,128]{1,0:T(8,128)(2,1)S(1)}, u32[]{:S(2)}, u32[]{:S(2)}) collective-permute-start(bf16[256,128]{1,0:T(8,128)(2,1)S(1)} %get-tuple-element.32), channel_id=1, source_target_pairs={{0,2},{1,1},{2,0},{3,3},{4,6},{5,5},{6,4},{7,7},{8,10},{9,9},{10,8... | collective-permute-start | bytes 196616 | tf_op jit(solution)/shard_map/ppermute | solution.py:337
  29.4 6.6 %collective-permute-start.9 = (bf16[256,128]{1,0:T(8,128)(2,1)S(1)}, bf16[256,128]{1,0:T(8,128)(2,1)S(1)}, u32[]{:S(2)}, u32[]{:S(2)}) collective-permute-start(bf16[256,128]{1,0:T(8,128)(2,1)S(1)} %get-tuple-element.33), channel_id=1, source_target_pairs={{0,4},{1,1},{2,6},{3,3},{4,0},{5,5},{6,2},{7,7},{8,12},{9,9},{10,1... | collective-permute-start | bytes 196616 | tf_op jit(solution)/shard_map/ppermute | solution.py:337
  32.8 7.1 %collective-permute-start.10 = (bf16[256,128]{1,0:T(8,128)(2,1)S(1)}, bf16[256,128]{1,0:T(8,128)(2,1)S(1)}, u32[]{:S(2)}, u32[]{:S(2)}) collective-permute-start(bf16[256,128]{1,0:T(8,128)(2,1)S(1)} %get-tuple-element.34), channel_id=1, source_target_pairs={{0,6},{1,1},{2,4},{3,3},{4,2},{5,5},{6,0},{7,7},{8,14},{9,9},{10,1... | collective-permute-start | bytes 196616 | tf_op jit(solution)/shard_map/ppermute | solution.py:337

commit v5 on v4

--- a/solution.py
+++ b/solution.py
@@ -41,33 +41,62 @@
     return owner
 
 
-def chip_pairs(mask, count):
-    return [(i, i if i & 1 else i ^ (mask << 1)) for i in range(count)]
-
-
 def limit(mib):
     return pltpu.CompilerParams(vmem_limit_bytes=mib * 1024 * 1024)
 
 
-def pack_kernel(lengths_ref, key_ref, value_ref, pack_ref):
+def pack_kernel(lengths_ref, key_ref, value_ref, pack_ref, length_s, tail_s, sems):
     rows = key_ref.shape[1]
-    pack_ref[0:rows, :] = key_ref[0]
-    pack_ref[rows : 2 * rows, :] = value_ref[0]
-    length = lengths_ref[0].astype(F32)
-    pack_ref[2 * rows :, :] = jnp.full((TAIL, pack_ref.shape[1]), length, F32).astype(BF16)
+    copies = [
+        pltpu.make_async_copy(lengths_ref, length_s, sems.at[0]),
+        pltpu.make_async_copy(key_ref.at[0], pack_ref.at[pl.ds(0, rows)], sems.at[1]),
+        pltpu.make_async_copy(value_ref.at[0], pack_ref.at[pl.ds(rows, rows)], sems.at[2]),
+    ]
+    for copy in copies:
+        copy.start()
+    copies[0].wait()
+    tail_s[...] = jnp.full(tail_s.shape, length_s[0].astype(F32), F32).astype(BF16)
+    last = pltpu.make_async_copy(tail_s, pack_ref.at[pl.ds(2 * rows, TAIL)], sems.at[3])
+    last.start()
+    for copy in copies[1:] + [last]:
+        copy.wait()
 
 
 def make_pack(lengths, keys, values):
     rows, width = keys.shape[1:]
-    first = pl.BlockSpec((1, rows, width), lambda step: (0, 0, 0))
+    hbm = pl.BlockSpec(memory_space=pltpu.HBM)
     return pl.pallas_call(
         pack_kernel,
-        grid=(1,),
         out_shape=jax.ShapeDtypeStruct((2 * rows + TAIL, width), BF16),
-        in_specs=[pl.BlockSpec(memory_space=pltpu.SMEM), first, first],
-        out_specs=pl.BlockSpec((2 * rows + TAIL, width), lambda step: (0, 0)),
+        in_specs=[hbm, hbm, hbm],
+        out_specs=hbm,
+        scratch_shapes=[
+            pltpu.SMEM((2,), jnp.int32),
+            pltpu.VMEM((TAIL, width), BF16),
+            pltpu.SemaphoreType.DMA((4,)),
+        ],
         name="pack",
     )(lengths, keys, values)
+
+
+def pass_on_kernel(first, *refs):
+    other_ref, arrived_ref, out_ref = refs
+    index = lax.axis_index("leaf")
+    core, x = index & 1, (index >> 1) & 1
+    take = core == 1 if first else (core == 0) | (x == 1)
+    out_ref[...] = jnp.where(take, arrived_ref[...], other_ref[...])
+
+
+def pass_on(first, other, arrived):
+    vmem = pl.BlockSpec(memory_space=pltpu.VMEM)
+    return pl.pallas_call(
+        functools.partial(pass_on_kernel, first),
+        out_shape=jax.ShapeDtypeStruct(other.shape, other.dtype),
+        in_specs=[vmem, vmem],
+        out_specs=vmem,
+        compiler_params=limit(1),
+        name="pass_on",
+    )(other, arrived)
 
 
 def rows_kernel(heads, lengths_ref, query_ref, grad_ref, query_s, cot_s):
@@ -100,11 +129,38 @@
     )(lengths, queries, grads)
 
 
-def main_kernel(depth, heads, *refs):
+def direct_path(depth, index, refs):
     masks = (1 << (depth - 1)) - 1
-    lengths_ref, query_s, cot_s, key_ref, value_ref, own_ref, mate_ref = refs[:7]
-    near = refs[7 : 7 + masks]
-    far = refs[7 + masks : 7 + 2 * masks]
+    own, mate = refs[0][...], refs[1][...]
+    near, far = refs[2 : 2 + masks], refs[2 + masks :]
+    odd = index & 1 == 1
+    even = index - (index & 1)
+    blocks = []
+    for level in range(depth):
+        pick = (even ^ owner_of(even, level, depth)) >> 1
+        block = jnp.where(odd, mate, own)
+        for mask in range(1, masks + 1):
+            other = jnp.where(odd, far[mask - 1][...], near[mask - 1][...])
+            block = jnp.where(pick == mask, other, block)
+        blocks.append(block)
+    return blocks + [jnp.where(odd, own, mate)]
+
+
+def two_step_path(index, refs):
+    own, mate, along_x, sent_on, swapped = [ref[...] for ref in refs]
+    odd, x, y = index & 1 == 1, (index >> 1) & 1 == 1, (index >> 2) & 1 == 1
+    even_own = jnp.where(odd, mate, own)
+    odd_own = jnp.where(odd, own, mate)
+    even_other = jnp.where(odd, swapped, along_x)
+    odd_other = jnp.where(odd, sent_on, swapped)
+    same = jnp.where(x, even_other, even_own)
+    second = jnp.where(x, even_own, even_other)
+    return [jnp.where(y, odd_other, same), jnp.where(y, same, odd_other), second, odd_own]
+
+
+def main_kernel(depth, heads, sources, *refs):
+    lengths_ref, query_s, cot_s, key_ref, value_ref = refs[:5]
+    path_refs = refs[5 : 5 + sources]
     (
         grad_query_ref,
         leaf_ref,
@@ -116,7 +172,7 @@
         keys_t,
         low_s,
         ds_s,
-    ) = refs[7 + 2 * masks :]
+    ) = refs[5 + sources :]
     rows, width = key_ref.shape[1:]
     index = lax.axis_index("leaf")
     parity = index & 1
@@ -125,6 +181,10 @@
     lane = lax.broadcasted_iota(jnp.int32, (rows, width), 1)
     row = lax.broadcasted_iota(jnp.int32, (rows, width), 0)
     row_f = row.astype(F32)
+    if depth == 3:
+        path = two_step_path(index, path_refs)
+    else:
+        path = direct_path(depth, index, path_refs)
 
     levels = depth + 2
     for level in range(levels):
@@ -133,15 +193,7 @@
             key_block, value_block = key_ref[1], value_ref[1]
             length = jnp.full((1, width), lengths_ref[1].astype(F32), F32)
         else:
-            if level == depth:
-                block = jnp.where(parity == 1, own_ref[...], mate_ref[...])
-            else:
-                even = index - parity
-                pick = (even ^ owner_of(even, level, depth)) >> 1
-                block = jnp.where(parity == 1, mate_ref[...], own_ref[...])
-                for mask in range(1, masks + 1):
-                    other = jnp.where(parity == 1, far[mask - 1][...], near[mask - 1][...])
-                    block = jnp.where(pick == mask, other, block)
+            block = path[level]
             key_block, value_block = block[:rows], block[rows : 2 * rows]
             length = block[2 * rows : 2 * rows + 1].astype(F32)
         keys_s[span, :] = key_block
@@ -214,32 +266,45 @@
             ref[at : at + rows, :] = grad_keys[span].astype(ref.dtype)
             ref[at + rows : at + 2 * rows, :] = grad_values[span].astype(ref.dtype)
 
-    @pl.when(parity == 1)
-    def _():
-        put(swap_ref, range(depth))
-        put(part_ref, [depth])
-
-    @pl.when(parity == 0)
-    def _():
-        put(swap_ref, [depth])
-        put(part_ref, range(depth))
-
-
-def main_call(lengths, queries, cot, keys, values, own, mate, near, far, depth):
+    if depth == 3:
+        y = (index >> 2) & 1
+        for odd in range(2):
+            for side in range(2):
+
+                @pl.when((parity == odd) & (y == side))
+                def _():
+                    put(swap_ref, [side ^ odd ^ 1, 3 - odd])
+                    put(part_ref, [side ^ odd, 2 + odd])
+
+    else:
+
+        @pl.when(parity == 1)
+        def _():
+            put(swap_ref, range(depth))
+            put(part_ref, [depth])
+
+        @pl.when(parity == 0)
+        def _():
+            put(swap_ref, [depth])
+            put(part_ref, range(depth))
+
+
+def main_call(lengths, queries, cot, keys, values, path, depth):
     rows, width = keys.shape[1:]
     heads = queries.shape[0] // (2 * rows)
     slots = (depth + 2) * rows
     total = 2 * heads * rows
-    vmem = pl.BlockSpec(memory_space=pltpu.VMEM)
-    return pl.pallas_call(
-        functools.partial(main_kernel, depth, heads),
+    parts = 2 if depth == 3 else depth
+    vmem = pl.BlockSpec(memory_space=pltpu.VMEM)
+    return pl.pallas_call(
+        functools.partial(main_kernel, depth, heads, len(path)),
         out_shape=(
             jax.ShapeDtypeStruct((2, rows, heads * width), BF16),
             jax.ShapeDtypeStruct((2 * rows, width), BF16),
-            jax.ShapeDtypeStruct((depth * 2 * rows, width), BF16),
-            jax.ShapeDtypeStruct((depth * 2 * rows, width), F32),
+            jax.ShapeDtypeStruct((parts * 2 * rows, width), BF16),
+            jax.ShapeDtypeStruct((parts * 2 * rows, width), F32),
         ),
-        in_specs=[pl.BlockSpec(memory_space=pltpu.SMEM)] + [vmem] * (6 + len(near) + len(far)),
+        in_specs=[pl.BlockSpec(memory_space=pltpu.SMEM)] + [vmem] * (4 + len(path)),
         out_specs=(vmem,) * 4,
         scratch_shapes=[
             pltpu.VMEM((slots, width), BF16),
@@ -251,7 +316,7 @@
         ],
         compiler_params=limit(24),
         name="attend",
-    )(lengths, queries, cot, keys, values, own, mate, *near, *far)
+    )(lengths, queries, cot, keys, values, *path)
 
 
 def combine_kernel(depth, part_ref, other_ref, own_ref, *rest):
@@ -287,6 +352,55 @@
     )(part, other)
 
 
+def fold_kernel(part_ref, other_ref, keep_ref, send_ref):
+    half = send_ref.shape[0]
+    x = (lax.axis_index("leaf") >> 1) & 1
+    both = part_ref[...] + other_ref[...].astype(F32)
+    keep_ref[...] = both
+    send_ref[...] = jnp.where(x == 1, both[:half], both[half:]).astype(BF16)
+
+
+def fold_call(part, other):
+    vmem = pl.BlockSpec(memory_space=pltpu.VMEM)
+    return pl.pallas_call(
+        fold_kernel,
+        out_shape=[
+            jax.ShapeDtypeStruct(part.shape, F32),
+            jax.ShapeDtypeStruct((part.shape[0] // 2, part.shape[1]), BF16),
+        ],
+        in_specs=[vmem] * 2,
+        out_specs=[vmem] * 2,
+        compiler_params=limit(4),
+        name="fold",
+    )(part, other)
+
+
+def fold_x_kernel(keep_ref, other_ref, own_ref, send_ref):
+    half = send_ref.shape[0]
+    index = lax.axis_index("leaf")
+    odd, x = index & 1 == 1, (index >> 1) & 1 == 1
+    other = other_ref[...].astype(F32)
+    first = keep_ref[:half, :] + other
+    second = keep_ref[half:, :] + jnp.where(odd, 0.0, other)
+    send_ref[...] = first.astype(BF16)
+    own_ref[...] = jnp.where(odd, keep_ref[half:, :], jnp.where(x, second, first))
+
+
+def fold_x_call(keep, other):
+    vmem = pl.BlockSpec(memory_space=pltpu.VMEM)
+    return pl.pallas_call(
+        fold_x_kernel,
+        out_shape=[
+            jax.ShapeDtypeStruct(other.shape, F32),
+            jax.ShapeDtypeStruct(other.shape, BF16),
+        ],
+        in_specs=[vmem] * 2,
+        out_specs=[vmem] * 2,
+        compiler_params=limit(4),
+        name="fold_x",
+    )(keep, other)
+
+
 def final_kernel(depth, leaf_ref, own_ref, *refs):
     arrived, (keys_ref, values_ref) = refs[:-2], refs[-2:]
     rows = keys_ref.shape[1]
@@ -295,6 +409,10 @@
     level = depth - trailing_zeros(index, depth)
     total = own_ref[...]
     for mask, ref in enumerate(arrived, 1):
+        if depth == 3:
+            mine = index & 3 == 0
+            total = total + jnp.where(mine, ref[...].astype(F32), 0.0)
+            continue
         mine = (parity == 0) & (owner_at(index ^ (mask << 1), level, depth) == index)
         total = total + jnp.where(mine, ref[...].astype(F32), 0.0)
     total = total.astype(BF16)
@@ -320,23 +438,35 @@
     count = lax.axis_size("leaf")
     depth = depth_of(count)
     masks = range(1, count // 2)
-    swap_pairs = [(i, i ^ 1) for i in range(count)]
+
+    def move(block, flip):
+        return lax.ppermute(block, "leaf", [(i, i ^ flip) for i in range(count)])
 
     pack = make_pack(lengths, key_states, value_states)
-    near = [lax.ppermute(pack, "leaf", chip_pairs(m, count)) for m in masks]
-    mate = lax.ppermute(pack, "leaf", swap_pairs)
-    query_rows, cot = rows_call(lengths, queries, grad_output, key_states.shape[2])
-    near, query_rows, cot = lax.optimization_barrier((near, query_rows, cot))
-    far = [lax.ppermute(block, "leaf", swap_pairs) for block in near]
+    if depth == 3:
+        along_y = move(pack, 5)
+        mate = move(pack, 1)
+        query_rows, cot = rows_call(lengths, queries, grad_output, key_states.shape[2])
+        along_x = move(pass_on(True, pack, along_y), 2)
+        sent_on = pass_on(False, along_y, along_x)
+        swapped = move(sent_on, 1)
+        path = [pack, mate, along_x, sent_on, swapped]
+    else:
+        near = [move(pack, m << 1) for m in masks]
+        mate = move(pack, 1)
+        query_rows, cot = rows_call(lengths, queries, grad_output, key_states.shape[2])
+        path = [pack, mate, *near, *[move(block, 1) for block in near]]
     grad_queries, leaf, swap, part = main_call(
-        lengths, query_rows, cot, key_states, value_states, pack, mate, near, far, depth
+        lengths, query_rows, cot, key_states, value_states, path, depth
     )
-    other = lax.ppermute(swap, "leaf", swap_pairs)
-    own, *sends = combine_call(part, other, depth)
-    arrived = [
-        lax.ppermute(block, "leaf", chip_pairs(m, count))
-        for m, block in zip(masks, sends)
-    ]
+    other = move(swap, 1)
+    if depth == 3:
+        keep, send = fold_call(part, other)
+        own, send = fold_x_call(keep, move(send, 2))
+        arrived = [move(send, 5)]
+    else:
+        own, *sends = combine_call(part, other, depth)
+        arrived = [move(block, m << 1) for m, block in zip(masks, sends)]
     grad_keys, grad_values = final_call(leaf, own, arrived, key_states.shape, depth)
     return grad_queries, grad_keys, grad_values
 

time: 41 us -> 35.8 us (0.87)
  starting transfers between devices: 20.1 us -> 8.35 us
  waiting for transfers between devices: 7.89 us -> 12 us
  Pallas kernels: 9.71 us -> 11.4 us
  local copies, waits for them, and re-layouts: 2.09 us -> 3.04 us
    ppermute x11 -> x7, starting transfers between devices: 20.1 us -> 8.35 us  [move(): return lax.ppermute(block, 'leaf', [(i, i ^ flip) for i in range(count)])]
    ppermute x11 -> x7, waiting for transfers between devices: 7.89 us -> 12 us  [move(): return lax.ppermute(block, 'leaf', [(i, i ^ flip) for i in range(count)])]
    pallas_call x3 -> x6, Pallas kernels: 8.24 us -> 9.91 us  [the longest x1 6.67 us: main_call(): pl.pallas_call(functools.partial(main_kernel, depth, heads, len(path)), o...]
    unnamed x12 -> x14, local copies, waits for them, and re-layouts: 2.09 us -> 3.04 us
  transfers between devices with their start and end apart: 11 -> 7, of which waited for: 6 -> 5; matrix products, arithmetic and copies ran while one was open for 0% -> 0% of each run, Pallas kernels for 2% -> 2%
where the time goes in v5:
time: 35.8 us; the launch traced here: 35.5 us
  waiting for transfers between devices  12 us (34%)
  Pallas kernels  11.4 us (32%)
  starting transfers between devices  8.35 us (23%)
  local copies, waits for them, and re-layouts  3.04 us (8%)
  between operations  0.72 us (2%)
    ppermute x7, waiting for transfers between devices, move(): return lax.ppermute(block, 'leaf', [(i, i ^ flip) for i in range(count)])  12 us
    ppermute x7, starting transfers between devices, move(): return lax.ppermute(block, 'leaf', [(i, i ^ flip) for i in range(count)])  8.35 us
    pallas_call x1, Pallas kernels, main_call(): pl.pallas_call(functools.partial(main_kernel, depth, heads, len(path)), o...  6.67 us
    pallas_call x1, Pallas kernels, make_pack(): pl.pallas_call(pack_kernel, out_shape=jax.ShapeDtypeStruct((2 * rows + TA...  3.13 us
    unnamed x14, local copies, waits for them, and re-layouts  3.04 us
    pallas_call x1, Pallas kernels, rows_call(): pl.pallas_call(functools.partial(rows_kernel, heads), out_shape=(shape, s...  0.78 us
  transfers between devices with their start and end apart: 7, of which 5 were waited for; matrix products, arithmetic and copies ran while one was open for 0% of the time, Pallas kernels for 2%

profile of v5, /device:TPU:0, one launch (start us, length us, event | category | flops | bytes accessed | tf_op | source)
XLA Modules:
  0.0 35.5 jit_solution(17794131110871458741)
XLA Ops:
  0.6 3.1 %pack.1.refs_0_.refs_5_ = bf16[272,128]{1,0:T(8,128)(2,1)} custom-call(s32[2]{0:T(128)} %refs_0_.1, bf16[2,128,128]{2,1,0:T(8,128)(2,1)} %refs_3_.1, bf16[2,128,128]{2,1,0:T(8,128)(2,1)} %refs_4_.1), custom_call_target="tpu_custom_call" | custom-call | tf_op jit(solution)/shard_map/pack/pallas_call | solution.py:68
  3.8 2.5 %collective-permute-start.1 = (bf16[272,128]{1,0:T(8,128)(2,1)}, bf16[272,128]{1,0:T(8,128)(2,1)S(1)}, u32[]{:S(2)}, u32[]{:S(2)}) collective-permute-start(bf16[272,128]{1,0:T(8,128)(2,1)} %pack.1.refs_0_.refs_5_), channel_id=1, source_target_pairs={{0,5},{1,4},{2,7},{3,6},{4,1},{5,0},{6,3},{7,2},{8,13},{9,12},{10,... | collective-permute-start | bytes 208904 | tf_op jit(solution)/shard_map/ppermute | solution.py:443
  6.2 2.9 %collective-permute-done.1.refs_1_.refs_0_ = bf16[272,128]{1,0:T(8,128)(2,1)S(1)} collective-permute-done((bf16[272,128]{1,0:T(8,128)(2,1)}, bf16[272,128]{1,0:T(8,128)(2,1)S(1)}, u32[]{:S(2)}, u32[]{:S(2)}) %collective-permute-start.1) | collective-permute-done | bytes 69664 | tf_op jit(solution)/shard_map/ppermute | solution.py:443
  9.1 0.0 copy-start
  9.1 0.9 %copy-done = bf16[272,128]{1,0:T(8,128)(2,1)S(1)} copy-done((bf16[272,128]{1,0:T(8,128)(2,1)S(1)}, bf16[272,128]{1,0:T(8,128)(2,1)}, u32[]{:S(2)}) %copy-start) | copy-done | bytes 69656
  10.0 0.0 copy-start.1
  10.0 0.0 copy-start.6
  10.0 2.3 %collective-permute-start.2 = (bf16[272,128]{1,0:T(8,128)(2,1)S(1)}, bf16[272,128]{1,0:T(8,128)(2,1)S(1)}, u32[]{:S(2)}, u32[]{:S(2)}) collective-permute-start(bf16[272,128]{1,0:T(8,128)(2,1)S(1)} %pass_on.2), channel_id=1, source_target_pairs={{0,2},{1,3},{2,0},{3,1},{4,6},{5,7},{6,4},{7,5},{8,10},{9,11},{10,... | collective-permute-start | bytes 208904 | tf_op jit(solution)/shard_map/ppermute | solution.py:443
  12.4 0.0 copy-done.1
  12.4 0.0 collective-permute-start
  12.4 2.5 %collective-permute-done.2.refs_1_.refs_7_ = bf16[272,128]{1,0:T(8,128)(2,1)S(1)} collective-permute-done((bf16[272,128]{1,0:T(8,128)(2,1)S(1)}, bf16[272,128]{1,0:T(8,128)(2,1)S(1)}, u32[]{:S(2)}, u32[]{:S(2)}) %collective-permute-start.2) | collective-permute-done | bytes 69664 | tf_op jit(solution)/shard_map/ppermute | solution.py:443
  14.9 0.1 collective-permute-start.3
  14.9 0.0 copy-done.6
  14.9 0.0 copy-start.2
  15.0 1.0 %copy-done.2 = bf16[2,128,1024]{2,1,0:T(8,128)(2,1)S(1)} copy-done((bf16[2,128,1024]{2,1,0:T(8,128)(2,1)S(1)}, bf16[2,128,1024]{2,1,0:T(8,128)(2,1)}, u32[]{:S(2)}) %copy-start.2) | copy-done | bytes 524312
  16.0 0.0 copy-start.3
  16.0 1.0 %copy-done.3 = bf16[2,128,1024]{2,1,0:T(8,128)(2,1)S(1)} copy-done((bf16[2,128,1024]{2,1,0:T(8,128)(2,1)S(1)}, bf16[2,128,1024]{2,1,0:T(8,128)(2,1)}, u32[]{:S(2)}) %copy-start.3) | copy-done | bytes 524312
  17.0 0.0 copy-start.4
  17.0 0.0 copy-start.5
  17.0 0.8 %rows.1 = (bf16[2048,128]{1,0:T(8,128)(2,1)S(1)}, bf16[2048,128]{1,0:T(8,128)(2,1)S(1)}) custom-call(s32[2]{0:T(128)S(1)} %copy-done.6, bf16[2,128,1024]{2,1,0:T(8,128)(2,1)S(1)} %copy-done.2, bf16[2,128,1024]{2,1,0:T(8,128)(2,1)S(1)} %copy-done.3), custom_call_target="tpu_custom_call" | custom-call | bytes 4194304 | tf_op jit(solution)/shard_map/rows/pallas_call | solution.py:121
  17.8 0.0 collective-permute-done.refs_6_
  17.8 0.0 collective-permute-done.3.refs_9_
  17.8 0.0 copy-done.4
  17.9 0.0 copy-done.5
  17.9 6.7 %attend.1 = (bf16[2,128,1024]{2,1,0:T(8,128)(2,1)}, bf16[256,128]{1,0:T(8,128)(2,1)S(1)}, bf16[512,128]{1,0:T(8,128)(2,1)S(1)}, f32[512,128]{1,0:T(8,128)S(1)}) custom-call(s32[2]{0:T(128)S(1)} %copy-done.6, bf16[2048,128]{1,0:T(8,128)(2,1)S(1)} %get-tuple-element.15.refs_1_, bf16[2048,128]{1,0:T(8,128)(2,1)S(1)} %get-tuple-element.16.refs_2_, ...), custom_call_target="tpu_custom_call" | custom-call | tf_op jit(solution)/shard_map/attend/pallas_call | solution.py:299
  24.6 0.5 %collective-permute-start.4 = (bf16[512,128]{1,0:T(8,128)(2,1)S(1)}, bf16[512,128]{1,0:T(8,128)(2,1)S(1)}, u32[]{:S(2)}, u32[]{:S(2)}) collective-permute-start(bf16[512,128]{1,0:T(8,128)(2,1)S(1)} %get-tuple-element.20), channel_id=1, source_target_pairs={{0,1},{1,0},{2,3},{3,2},{4,5},{5,4},{6,7},{7,6},{8,9},{9,8},{10,11... | collective-permute-start | bytes 393224 | tf_op jit(solution)/shard_map/ppermute | solution.py:443
  25.1 1.0 %collective-permute-done.4.other_ref = bf16[512,128]{1,0:T(8,128)(2,1)S(1)} collective-permute-done((bf16[512,128]{1,0:T(8,128)(2,1)S(1)}, bf16[512,128]{1,0:T(8,128)(2,1)S(1)}, u32[]{:S(2)}, u32[]{:S(2)}) %collective-permute-start.4) | collective-permute-done | bytes 131104 | tf_op jit(solution)/shard_map/ppermute | solution.py:443
  26.1 1.9 %collective-permute-start.5 = (bf16[256,128]{1,0:T(8,128)(2,1)S(1)}, bf16[256,128]{1,0:T(8,128)(2,1)S(1)}, u32[]{:S(2)}, u32[]{:S(2)}) collective-permute-start(bf16[256,128]{1,0:T(8,128)(2,1)S(1)} %get-tuple-element.22), channel_id=1, source_target_pairs={{0,2},{1,3},{2,0},{3,1},{4,6},{5,7},{6,4},{7,5},{8,10},{9,11},{10,... | collective-permute-start | bytes 196616 | tf_op jit(solution)/shard_map/ppermute | solution.py:443
  28.0 2.6 %collective-permute-done.5.other_ref = bf16[256,128]{1,0:T(8,128)(2,1)S(1)} collective-permute-done((bf16[256,128]{1,0:T(8,128)(2,1)S(1)}, bf16[256,128]{1,0:T(8,128)(2,1)S(1)}, u32[]{:S(2)}, u32[]{:S(2)}) %collective-permute-start.5) | collective-permute-done | bytes 65568 | tf_op jit(solution)/shard_map/ppermute | solution.py:443
  30.7 1.0 %collective-permute-start.6 = (bf16[256,128]{1,0:T(8,128)(2,1)S(1)}, bf16[256,128]{1,0:T(8,128)(2,1)S(1)}, u32[]{:S(2)}, u32[]{:S(2)}) collective-permute-start(bf16[256,128]{1,0:T(8,128)(2,1)S(1)} %get-tuple-element.24), channel_id=1, source_target_pairs={{0,5},{1,4},{2,7},{3,6},{4,1},{5,0},{6,3},{7,2},{8,13},{9,12},{10,... | collective-permute-start | bytes 196616 | tf_op jit(solution)/shard_map/ppermute | solution.py:443
  31.7 3.1 %collective-permute-done.6.refs_0_ = bf16[256,128]{1,0:T(8,128)(2,1)S(1)} collective-permute-done((bf16[256,128]{1,0:T(8,128)(2,1)S(1)}, bf16[256,128]{1,0:T(8,128)(2,1)S(1)}, u32[]{:S(2)}, u32[]{:S(2)}) %collective-permute-start.6) | collective-permute-done | bytes 65568 | tf_op jit(solution)/shard_map/ppermute | solution.py:443
  34.8 0.7 %final.1 = (bf16[2,128,128]{2,1,0:T(8,128)(2,1)}, bf16[2,128,128]{2,1,0:T(8,128)(2,1)}) custom-call(bf16[256,128]{1,0:T(8,128)(2,1)S(1)} %get-tuple-element.18.leaf_ref, f32[256,128]{1,0:T(8,128)S(1)} %get-tuple-element.23.own_ref, bf16[256,128]{1,0:T(8,128)(2,1)S(1)} %collective-permute-done.6.refs_0_), custom_call_target="tpu_custom_call" | custom-call | tf_op jit(solution)/shard_map/final/pallas_call | solution.py:427
  (4 shorter events, 0.1 us)
Async XLA Ops:
  3.8 5.3 %collective-permute-start.1 = (bf16[272,128]{1,0:T(8,128)(2,1)}, bf16[272,128]{1,0:T(8,128)(2,1)S(1)}, u32[]{:S(2)}, u32[]{:S(2)}) collective-permute-start(bf16[272,128]{1,0:T(8,128)(2,1)} %pack.1.refs_0_.refs_5_), channel_id=1, source_target_pairs={{0,5},{1,4},{2,7},{3,6},{4,1},{5,0},{6,3},{7,2},{8,13},{9,12},{10,... | collective-permute-start | bytes 208904 | tf_op jit(solution)/shard_map/ppermute | solution.py:443
  9.1 0.9 %copy-start = (bf16[272,128]{1,0:T(8,128)(2,1)S(1)}, bf16[272,128]{1,0:T(8,128)(2,1)}, u32[]{:S(2)}) copy-start(bf16[272,128]{1,0:T(8,128)(2,1)} %pack.1.refs_0_.refs_5_) | copy-start | bytes 208900
  10.0 2.4 %copy-start.1 = (bf16[272,128]{1,0:T(8,128)(2,1)S(1)}, bf16[272,128]{1,0:T(8,128)(2,1)}, u32[]{:S(2)}) copy-start(bf16[272,128]{1,0:T(8,128)(2,1)} %pack.1.refs_0_.refs_5_) | copy-start | bytes 208900
  10.0 4.9 %copy-start.6 = (s32[2]{0:T(128)S(1)}, s32[2]{0:T(128)}, u32[]{:S(2)}) copy-start(s32[2]{0:T(128)} %refs_0_.1) | copy-start | bytes 28
  10.0 4.8 %collective-permute-start.2 = (bf16[272,128]{1,0:T(8,128)(2,1)S(1)}, bf16[272,128]{1,0:T(8,128)(2,1)S(1)}, u32[]{:S(2)}, u32[]{:S(2)}) collective-permute-start(bf16[272,128]{1,0:T(8,128)(2,1)S(1)} %pass_on.2), channel_id=1, source_target_pairs={{0,2},{1,3},{2,0},{3,1},{4,6},{5,7},{6,4},{7,5},{8,10},{9,11},{10,... | collective-permute-start | bytes 208904 | tf_op jit(solution)/shard_map/ppermute | solution.py:443
  12.4 5.5 %collective-permute-start = (bf16[272,128]{1,0:T(8,128)(2,1)S(1)}, bf16[272,128]{1,0:T(8,128)(2,1)S(1)}, u32[]{:S(2)}, u32[]{:S(2)}) collective-permute-start(bf16[272,128]{1,0:T(8,128)(2,1)S(1)} %copy-done.1), channel_id=1, source_target_pairs={{0,1},{1,0},{2,3},{3,2},{4,5},{5,4},{6,7},{7,6},{8,9},{9,8},{10,11... | collective-permute-start | bytes 208904 | tf_op jit(solution)/shard_map/ppermute | solution.py:443
  14.9 3.0 %collective-permute-start.3 = (bf16[272,128]{1,0:T(8,128)(2,1)S(1)}, bf16[272,128]{1,0:T(8,128)(2,1)S(1)}, u32[]{:S(2)}, u32[]{:S(2)}) collective-permute-start(bf16[272,128]{1,0:T(8,128)(2,1)S(1)} %pass_on.3.refs_8_), channel_id=1, source_target_pairs={{0,1},{1,0},{2,3},{3,2},{4,5},{5,4},{6,7},{7,6},{8,9},{9,8},{10,11... | collective-permute-start | bytes 208904 | tf_op jit(solution)/shard_map/ppermute | solution.py:443
  14.9 1.0 %copy-start.2 = (bf16[2,128,1024]{2,1,0:T(8,128)(2,1)S(1)}, bf16[2,128,1024]{2,1,0:T(8,128)(2,1)}, u32[]{:S(2)}) copy-start(bf16[2,128,1024]{2,1,0:T(8,128)(2,1)} %query_ref.1) | copy-start | bytes 1572868
  16.0 1.0 %copy-start.3 = (bf16[2,128,1024]{2,1,0:T(8,128)(2,1)S(1)}, bf16[2,128,1024]{2,1,0:T(8,128)(2,1)}, u32[]{:S(2)}) copy-start(bf16[2,128,1024]{2,1,0:T(8,128)(2,1)} %grad_ref.1) | copy-start | bytes 1572868
  17.0 0.8 %copy-start.4 = (bf16[2,128,128]{2,1,0:T(8,128)(2,1)S(1)}, bf16[2,128,128]{2,1,0:T(8,128)(2,1)}, u32[]{:S(2)}) copy-start(bf16[2,128,128]{2,1,0:T(8,128)(2,1)} %refs_3_.1) | copy-start | bytes 196612
  17.0 0.9 %copy-start.5 = (bf16[2,128,128]{2,1,0:T(8,128)(2,1)S(1)}, bf16[2,128,128]{2,1,0:T(8,128)(2,1)}, u32[]{:S(2)}) copy-start(bf16[2,128,128]{2,1,0:T(8,128)(2,1)} %refs_4_.1) | copy-start | bytes 196612
  24.6 1.5 %collective-permute-start.4 = (bf16[512,128]{1,0:T(8,128)(2,1)S(1)}, bf16[512,128]{1,0:T(8,128)(2,1)S(1)}, u32[]{:S(2)}, u32[]{:S(2)}) collective-permute-start(bf16[512,128]{1,0:T(8,128)(2,1)S(1)} %get-tuple-element.20), channel_id=1, source_target_pairs={{0,1},{1,0},{2,3},{3,2},{4,5},{5,4},{6,7},{7,6},{8,9},{9,8},{10,11... | collective-permute-start | bytes 393224 | tf_op jit(solution)/shard_map/ppermute | solution.py:443
  26.1 4.5 %collective-permute-start.5 = (bf16[256,128]{1,0:T(8,128)(2,1)S(1)}, bf16[256,128]{1,0:T(8,128)(2,1)S(1)}, u32[]{:S(2)}, u32[]{:S(2)}) collective-permute-start(bf16[256,128]{1,0:T(8,128)(2,1)S(1)} %get-tuple-element.22), channel_id=1, source_target_pairs={{0,2},{1,3},{2,0},{3,1},{4,6},{5,7},{6,4},{7,5},{8,10},{9,11},{10,... | collective-permute-start | bytes 196616 | tf_op jit(solution)/shard_map/ppermute | solution.py:443
  30.7 4.2 %collective-permute-start.6 = (bf16[256,128]{1,0:T(8,128)(2,1)S(1)}, bf16[256,128]{1,0:T(8,128)(2,1)S(1)}, u32[]{:S(2)}, u32[]{:S(2)}) collective-permute-start(bf16[256,128]{1,0:T(8,128)(2,1)S(1)} %get-tuple-element.24), channel_id=1, source_target_pairs={{0,5},{1,4},{2,7},{3,6},{4,1},{5,0},{6,3},{7,2},{8,13},{9,12},{10,... | collective-permute-start | bytes 196616 | tf_op jit(solution)/shard_map/ppermute | solution.py:443

commit v6 on v4

--- a/solution.py
+++ b/solution.py
@@ -41,33 +41,59 @@
     return owner
 
 
-def chip_pairs(mask, count):
-    return [(i, i if i & 1 else i ^ (mask << 1)) for i in range(count)]
+def chip_groups(count):
+    return [list(range(core, count, 2)) for core in range(2)]
 
 
 def limit(mib):
     return pltpu.CompilerParams(vmem_limit_bytes=mib * 1024 * 1024)
 
 
-def pack_kernel(lengths_ref, key_ref, value_ref, pack_ref):
+def pack_kernel(chips, lengths_ref, key_ref, value_ref, pack_ref, packs_ref):
     rows = key_ref.shape[1]
-    pack_ref[0:rows, :] = key_ref[0]
-    pack_ref[rows : 2 * rows, :] = value_ref[0]
-    length = lengths_ref[0].astype(F32)
-    pack_ref[2 * rows :, :] = jnp.full((TAIL, pack_ref.shape[1]), length, F32).astype(BF16)
-
-
-def make_pack(lengths, keys, values):
+    length = jnp.full((TAIL, pack_ref.shape[1]), lengths_ref[0].astype(F32), F32)
+    block = jnp.concatenate([key_ref[0], value_ref[0], length.astype(BF16)], 0)
+    pack_ref[...] = block
+    for chip in range(chips):
+        packs_ref[chip] = block
+
+
+def make_packs(lengths, keys, values, chips):
     rows, width = keys.shape[1:]
     first = pl.BlockSpec((1, rows, width), lambda step: (0, 0, 0))
-    return pl.pallas_call(
-        pack_kernel,
+    height = 2 * rows + TAIL
+    return pl.pallas_call(
+        functools.partial(pack_kernel, chips),
         grid=(1,),
-        out_shape=jax.ShapeDtypeStruct((2 * rows + TAIL, width), BF16),
+        out_shape=(
+            jax.ShapeDtypeStruct((height, width), BF16),
+            jax.ShapeDtypeStruct((chips, height, width), BF16),
+        ),
         in_specs=[pl.BlockSpec(memory_space=pltpu.SMEM), first, first],
-        out_specs=pl.BlockSpec((2 * rows + TAIL, width), lambda step: (0, 0)),
+        out_specs=(
+            pl.BlockSpec((height, width), lambda step: (0, 0)),
+            pl.BlockSpec((chips, height, width), lambda step: (0, 0, 0)),
+        ),
         name="pack",
     )(lengths, keys, values)
+
+
+def levels_kernel(depth, packs_ref, out_ref):
+    index = lax.axis_index("leaf")
+    for level in range(depth):
+        out_ref[level] = packs_ref[owner_of(index, level, depth) >> 1]
+
+
+def levels_call(packs, depth):
+    vmem = pl.BlockSpec(memory_space=pltpu.VMEM)
+    return pl.pallas_call(
+        functools.partial(levels_kernel, depth),
+        out_shape=jax.ShapeDtypeStruct((depth,) + packs.shape[1:], BF16),
+        in_specs=[vmem],
+        out_specs=vmem,
+        compiler_params=limit(1 + depth // 4),
+        name="levels",
+    )(packs)
 
 
 def rows_kernel(heads, lengths_ref, query_ref, grad_ref, query_s, cot_s):
@@ -101,10 +127,7 @@
 
 
 def main_kernel(depth, heads, *refs):
-    masks = (1 << (depth - 1)) - 1
-    lengths_ref, query_s, cot_s, key_ref, value_ref, own_ref, mate_ref = refs[:7]
-    near = refs[7 : 7 + masks]
-    far = refs[7 + masks : 7 + 2 * masks]
+    lengths_ref, query_s, cot_s, key_ref, value_ref, own_ref, mate_ref, near, far = refs[:9]
     (
         grad_query_ref,
         leaf_ref,
@@ -116,7 +139,7 @@
         keys_t,
         low_s,
         ds_s,
-    ) = refs[7 + 2 * masks :]
+    ) = refs[9:]
     rows, width = key_ref.shape[1:]
     index = lax.axis_index("leaf")
     parity = index & 1
@@ -136,12 +159,7 @@
             if level == depth:
                 block = jnp.where(parity == 1, own_ref[...], mate_ref[...])
             else:
-                even = index - parity
-                pick = (even ^ owner_of(even, level, depth)) >> 1
-                block = jnp.where(parity == 1, mate_ref[...], own_ref[...])
-                for mask in range(1, masks + 1):
-                    other = jnp.where(parity == 1, far[mask - 1][...], near[mask - 1][...])
-                    block = jnp.where(pick == mask, other, block)
+                block = jnp.where(parity == 1, far[level], near[level])
             key_block, value_block = block[:rows], block[rows : 2 * rows]
             length = block[2 * rows : 2 * rows + 1].astype(F32)
         keys_s[span, :] = key_block
@@ -239,7 +257,7 @@
             jax.ShapeDtypeStruct((depth * 2 * rows, width), BF16),
             jax.ShapeDtypeStruct((depth * 2 * rows, width), F32),
         ),
-        in_specs=[pl.BlockSpec(memory_space=pltpu.SMEM)] + [vmem] * (6 + len(near) + len(far)),
+        in_specs=[pl.BlockSpec(memory_space=pltpu.SMEM)] + [vmem] * 8,
         out_specs=(vmem,) * 4,
         scratch_shapes=[
             pltpu.VMEM((slots, width), BF16),
@@ -251,11 +269,10 @@
         ],
         compiler_params=limit(24),
         name="attend",
-    )(lengths, queries, cot, keys, values, own, mate, *near, *far)
-
-
-def combine_kernel(depth, part_ref, other_ref, own_ref, *rest):
-    sends, both = rest[:-1], rest[-1]
+    )(lengths, queries, cot, keys, values, own, mate, near, far)
+
+
+def combine_kernel(depth, part_ref, other_ref, own_ref, sends_ref, both):
     block = own_ref.shape[0]
     index = lax.axis_index("leaf")
     both[...] = part_ref[...] + other_ref[...].astype(F32)
@@ -265,38 +282,40 @@
 
     own_level = depth - trailing_zeros(index, depth)
     own_ref[...] = take(jnp.where(index & 1 == 1, 0, own_level))
-    for mask, ref in enumerate(sends, 1):
-        target = (index - (index & 1)) ^ (mask << 1)
-        ref[...] = take(depth - trailing_zeros(target, depth)).astype(BF16)
+    for chip in range(sends_ref.shape[0]):
+        level = 0 if chip == 0 else depth - ((2 * chip) & -(2 * chip)).bit_length() + 1
+        sends_ref[chip] = both[level * block : (level + 1) * block, :].astype(BF16)
 
 
 def combine_call(part, other, depth):
-    masks = (1 << (depth - 1)) - 1
+    chips = 1 << (depth - 1)
     block = part.shape[0] // depth
     width = part.shape[1]
     vmem = pl.BlockSpec(memory_space=pltpu.VMEM)
     return pl.pallas_call(
         functools.partial(combine_kernel, depth),
-        out_shape=[jax.ShapeDtypeStruct((block, width), F32)]
-        + [jax.ShapeDtypeStruct((block, width), BF16)] * masks,
+        out_shape=(
+            jax.ShapeDtypeStruct((block, width), F32),
+            jax.ShapeDtypeStruct((chips, block, width), BF16),
+        ),
         in_specs=[vmem] * 2,
-        out_specs=[vmem] * (1 + masks),
+        out_specs=(vmem,) * 2,
         scratch_shapes=[pltpu.VMEM(part.shape, F32)],
         compiler_params=limit(4),
         name="combine",
     )(part, other)
 
 
-def final_kernel(depth, leaf_ref, own_ref, *refs):
-    arrived, (keys_ref, values_ref) = refs[:-2], refs[-2:]
+def final_kernel(depth, leaf_ref, own_ref, arrived_ref, keys_ref, values_ref):
     rows = keys_ref.shape[1]
     index = lax.axis_index("leaf")
-    parity = index & 1
     level = depth - trailing_zeros(index, depth)
     total = own_ref[...]
-    for mask, ref in enumerate(arrived, 1):
-        mine = (parity == 0) & (owner_at(index ^ (mask << 1), level, depth) == index)
-        total = total + jnp.where(mine, ref[...].astype(F32), 0.0)
+    for chip in range(arrived_ref.shape[0]):
+        sender = jnp.full((), 2 * chip, jnp.int32)
+        mine = (sender != index) & (owner_at(sender, level, depth) == index)
+        mine = mine & (index & 1 == 0)
+        total = total + jnp.where(mine, arrived_ref[chip].astype(F32), 0.0)
     total = total.astype(BF16)
     keys_ref[0] = total[:rows]
     values_ref[0] = total[rows:]
@@ -309,34 +328,34 @@
     return pl.pallas_call(
         functools.partial(final_kernel, depth),
         out_shape=[jax.ShapeDtypeStruct(shape, BF16)] * 2,
-        in_specs=[vmem] * (2 + len(arrived)),
+        in_specs=[vmem] * 3,
         out_specs=[vmem] * 2,
         compiler_params=limit(2),
         name="final",
-    )(leaf, own, *arrived)
+    )(leaf, own, arrived)
 
 
 def body(queries, key_states, value_states, grad_output, lengths):
     count = lax.axis_size("leaf")
     depth = depth_of(count)
-    masks = range(1, count // 2)
     swap_pairs = [(i, i ^ 1) for i in range(count)]
-
-    pack = make_pack(lengths, key_states, value_states)
-    near = [lax.ppermute(pack, "leaf", chip_pairs(m, count)) for m in masks]
+    groups = chip_groups(count)
+
+    def exchange(blocks):
+        return lax.all_to_all(blocks, "leaf", 0, 0, axis_index_groups=groups, tiled=True)
+
+    pack, packs = make_packs(lengths, key_states, value_states, count // 2)
     mate = lax.ppermute(pack, "leaf", swap_pairs)
+    near = exchange(packs)
     query_rows, cot = rows_call(lengths, queries, grad_output, key_states.shape[2])
-    near, query_rows, cot = lax.optimization_barrier((near, query_rows, cot))
-    far = [lax.ppermute(block, "leaf", swap_pairs) for block in near]
+    near = levels_call(near, depth)
+    far = lax.ppermute(near, "leaf", swap_pairs)
     grad_queries, leaf, swap, part = main_call(
         lengths, query_rows, cot, key_states, value_states, pack, mate, near, far, depth
     )
     other = lax.ppermute(swap, "leaf", swap_pairs)
-    own, *sends = combine_call(part, other, depth)
-    arrived = [
-        lax.ppermute(block, "leaf", chip_pairs(m, count))
-        for m, block in zip(masks, sends)
-    ]
+    own, sends = combine_call(part, other, depth)
+    arrived = exchange(sends)
     grad_keys, grad_values = final_call(leaf, own, arrived, key_states.shape, depth)
     return grad_queries, grad_keys, grad_values
 

time: 41 us -> 33.9 us (0.83)
  blocking collectives: 0 us -> 20.2 us
  starting transfers between devices: 20.1 us -> 0.2 us
  waiting for transfers between devices: 7.89 us -> 1.76 us
  local copies, waits for them, and re-layouts: 2.09 us -> 0.79 us
    all_to_all x0 -> x2, blocking collectives: none -> 20.2 us  [exchange(): lax.all_to_all(blocks, 'leaf', 0, 0, axis_index_groups=groups, tiled=True)]
    ppermute x9 -> x1, starting transfers between devices: 19.9 us -> 0.07 us  [body(): far = lax.ppermute(near, 'leaf', swap_pairs)]
    ppermute x9 -> x1, waiting for transfers between devices: 6.57 us -> 0.01 us  [body(): far = lax.ppermute(near, 'leaf', swap_pairs)]
    unnamed x12, local copies, waits for them, and re-layouts: 2.09 us -> 0.79 us
    ppermute x1, waiting for transfers between devices: 0.01 us -> 0.45 us  [body(): mate = lax.ppermute(pack, 'leaf', swap_pairs)]
    pallas_call x2 -> x3, Pallas kernels: 1.54 us -> 1.72 us  [the longest x1 1.62 us: make_packs(): pl.pallas_call(functools.partial(pack_kernel, chips), grid=(1,), out_shap...]
  transfers between devices with their start and end apart: 11 -> 3, of which waited for: 6 -> 2; matrix products, arithmetic and copies ran while one was open for 0% -> 0% of each run, Pallas kernels for 2% -> 2%
where the time goes in v6:
time: 33.9 us; the launch traced here: 33.6 us
  blocking collectives  20.2 us (60%)
  Pallas kernels  9.92 us (29%)
  waiting for transfers between devices  1.76 us (5%)
  local copies, waits for them, and re-layouts  0.79 us (2%)
  between operations  0.7 us (2%)
    all_to_all x2, blocking collectives, exchange(): lax.all_to_all(blocks, 'leaf', 0, 0, axis_index_groups=groups, tiled=True)  20.2 us
    pallas_call x1, Pallas kernels, main_call(): pl.pallas_call(functools.partial(main_kernel, depth, heads), out_shape=(j...  6.72 us
    pallas_call x1, Pallas kernels, make_packs(): pl.pallas_call(functools.partial(pack_kernel, chips), grid=(1,), out_shap...  1.62 us
    ppermute x1, waiting for transfers between devices, body(): other = lax.ppermute(swap, 'leaf', swap_pairs)  1.31 us
    unnamed x12, local copies, waits for them, and re-layouts  0.79 us
    pallas_call x1, Pallas kernels, rows_call(): pl.pallas_call(functools.partial(rows_kernel, heads), out_shape=(shape, s...  0.78 us
    pallas_call x1, Pallas kernels, final_call(): pl.pallas_call(functools.partial(final_kernel, depth), out_shape=[jax.Sha...  0.71 us
  transfers between devices with their start and end apart: 3, of which 2 were waited for; matrix products, arithmetic and copies ran while one was open for 0% of the time, Pallas kernels for 2%

profile of v6, /device:TPU:0, one launch (start us, length us, event | category | flops | bytes accessed | tf_op | source)
XLA Modules:
  0.0 33.6 jit_solution(2607724956683061723)
XLA Ops:
  0.6 0.0 copy-start.1
  0.6 1.6 %pack.1 = (bf16[272,128]{1,0:T(8,128)(2,1)}, bf16[4,272,128]{2,1,0:T(8,128)(2,1)}) custom-call(s32[2]{0:T(128)} %refs_0_.1, bf16[2,128,128]{2,1,0:T(8,128)(2,1)} %refs_3_.1, bf16[2,128,128]{2,1,0:T(8,128)(2,1)} %refs_4_.1), custom_call_target="tpu_custom_call" | custom-call | tf_op jit(solution)/shard_map/pack/pallas_call | solution.py:65
  2.3 0.0 copy-start
  2.3 11.5 %all_to_all.10.packs_ref = bf16[4,272,128]{2,1,0:T(8,128)(2,1)S(1)} all-to-all(bf16[4,272,128]{2,1,0:T(8,128)(2,1)} %get-tuple-element.18), channel_id=1, replica_groups={{0,2,4,6},{1,3,5,7},{8,10,12,14},{9,11,13,15},{16,18,20,22},{17,19,21,2..., dimensions={0} | all-to-all | bytes 557056 | tf_op jit(solution)/shard_map/all_to_all | solution.py:345
  13.7 0.0 copy-start.4
  13.8 0.0 copy-start.5
  13.8 0.1 collective-permute-start.1
  13.9 0.8 %copy-done.4 = bf16[272,128]{1,0:T(8,128)(2,1)S(1)} copy-done((bf16[272,128]{1,0:T(8,128)(2,1)S(1)}, bf16[272,128]{1,0:T(8,128)(2,1)}, u32[]{:S(2)}) %copy-start.4) | copy-done | bytes 69656
  14.6 0.0 copy-start.2
  14.6 0.0 copy-start.3
  14.6 0.0 collective-permute-start
  14.6 0.0 copy-done.1
  14.6 0.0 copy-done
  14.7 0.0 copy-done.5
  14.7 0.8 %rows.1 = (bf16[2048,128]{1,0:T(8,128)(2,1)S(1)}, bf16[2048,128]{1,0:T(8,128)(2,1)S(1)}) custom-call(s32[2]{0:T(128)S(1)} %copy-done.5, bf16[2,128,1024]{2,1,0:T(8,128)(2,1)S(1)} %copy-done, bf16[2,128,1024]{2,1,0:T(8,128)(2,1)S(1)} %copy-done.1), custom_call_target="tpu_custom_call" | custom-call | bytes 4194304 | tf_op jit(solution)/shard_map/rows/pallas_call | solution.py:118
  15.5 0.4 %collective-permute-done.refs_6_ = bf16[272,128]{1,0:T(8,128)(2,1)S(1)} collective-permute-done((bf16[272,128]{1,0:T(8,128)(2,1)S(1)}, bf16[272,128]{1,0:T(8,128)(2,1)S(1)}, u32[]{:S(2)}, u32[]{:S(2)}) %collective-permute-start) | collective-permute-done | bytes 69664 | tf_op jit(solution)/shard_map/ppermute | solution.py:348
  15.9 0.0 collective-permute-done.1.refs_8_
  15.9 0.0 copy-done.2
  15.9 0.0 copy-done.3
  15.9 6.7 %attend.1 = (bf16[2,128,1024]{2,1,0:T(8,128)(2,1)}, bf16[256,128]{1,0:T(8,128)(2,1)S(1)}, bf16[768,128]{1,0:T(8,128)(2,1)S(1)}, f32[768,128]{1,0:T(8,128)S(1)}) custom-call(s32[2]{0:T(128)S(1)} %copy-done.5, bf16[2048,128]{1,0:T(8,128)(2,1)S(1)} %get-tuple-element.15.refs_1_, bf16[2048,128]{1,0:T(8,128)(2,1)S(1)} %get-tuple-element.16.refs_2_, ...), custom_call_target="tpu_custom_call" | custom-call | tf_op jit(solution)/shard_map/attend/pallas_call | solution.py:252
  22.6 0.1 collective-permute-start.2
  22.8 1.3 %collective-permute-done.2.other_ref = bf16[768,128]{1,0:T(8,128)(2,1)S(1)} collective-permute-done((bf16[768,128]{1,0:T(8,128)(2,1)S(1)}, bf16[768,128]{1,0:T(8,128)(2,1)S(1)}, u32[]{:S(2)}, u32[]{:S(2)}) %collective-permute-start.2) | collective-permute-done | bytes 196640 | tf_op jit(solution)/shard_map/ppermute | solution.py:356
  24.1 0.1 combine.1
  24.2 8.7 %all_to_all.11.arrived_ref = bf16[4,256,128]{2,1,0:T(8,128)(2,1)S(1)} all-to-all(bf16[4,256,128]{2,1,0:T(8,128)(2,1)S(1)} %get-tuple-element.24), channel_id=1, replica_groups={{0,2,4,6},{1,3,5,7},{8,10,12,14},{9,11,13,15},{16,18,20,22},{17,19,21,2..., dimensions={0} | all-to-all | bytes 524288 | tf_op jit(solution)/shard_map/all_to_all | solution.py:345
  32.8 0.7 %final.1 = (bf16[2,128,128]{2,1,0:T(8,128)(2,1)}, bf16[2,128,128]{2,1,0:T(8,128)(2,1)}) custom-call(bf16[256,128]{1,0:T(8,128)(2,1)S(1)} %get-tuple-element.20.leaf_ref, f32[256,128]{1,0:T(8,128)S(1)} %get-tuple-element.23.own_ref, bf16[4,256,128]{2,1,0:T(8,128)(2,1)S(1)} %all_to_all.11.arrived_ref), custom_call_target="tpu_custom_call" | custom-call | tf_op jit(solution)/shard_map/final/pallas_call | solution.py:328
  (1 shorter events, 0.0 us)
Async XLA Ops:
  0.6 14.0 %copy-start.1 = (bf16[2,128,1024]{2,1,0:T(8,128)(2,1)S(1)}, bf16[2,128,1024]{2,1,0:T(8,128)(2,1)}, u32[]{:S(2)}) copy-start(bf16[2,128,1024]{2,1,0:T(8,128)(2,1)} %grad_ref.1) | copy-start | bytes 1572868
  2.3 12.4 %copy-start = (bf16[2,128,1024]{2,1,0:T(8,128)(2,1)S(1)}, bf16[2,128,1024]{2,1,0:T(8,128)(2,1)}, u32[]{:S(2)}) copy-start(bf16[2,128,1024]{2,1,0:T(8,128)(2,1)} %query_ref.1) | copy-start | bytes 1572868
  13.7 0.9 %copy-start.4 = (bf16[272,128]{1,0:T(8,128)(2,1)S(1)}, bf16[272,128]{1,0:T(8,128)(2,1)}, u32[]{:S(2)}) copy-start(bf16[272,128]{1,0:T(8,128)(2,1)} %get-tuple-element.17.refs_5_) | copy-start | bytes 208900
  13.8 0.9 %copy-start.5 = (s32[2]{0:T(128)S(1)}, s32[2]{0:T(128)}, u32[]{:S(2)}) copy-start(s32[2]{0:T(128)} %refs_0_.1) | copy-start | bytes 28
  13.8 2.1 %collective-permute-start.1 = (bf16[3,272,128]{2,1,0:T(8,128)(2,1)S(1)}, bf16[3,272,128]{2,1,0:T(8,128)(2,1)S(1)}, u32[]{:S(2)}, u32[]{:S(2)}) collective-permute-start(bf16[3,272,128]{2,1,0:T(8,128)(2,1)S(1)} %levels.1.refs_7_), channel_id=1, source_target_pairs={{0,1},{1,0},{2,3},{3,2},{4,5},{5,4},{6,7},{7,6},{8,9},{9,8},{10,11... | collective-permute-start | bytes 626696 | tf_op jit(solution)/shard_map/ppermute | solution.py:352
  14.6 1.3 %copy-start.2 = (bf16[2,128,128]{2,1,0:T(8,128)(2,1)S(1)}, bf16[2,128,128]{2,1,0:T(8,128)(2,1)}, u32[]{:S(2)}) copy-start(bf16[2,128,128]{2,1,0:T(8,128)(2,1)} %refs_3_.1) | copy-start | bytes 196612
  14.6 1.3 %copy-start.3 = (bf16[2,128,128]{2,1,0:T(8,128)(2,1)S(1)}, bf16[2,128,128]{2,1,0:T(8,128)(2,1)}, u32[]{:S(2)}) copy-start(bf16[2,128,128]{2,1,0:T(8,128)(2,1)} %refs_4_.1) | copy-start | bytes 196612
  14.6 1.3 %collective-permute-start = (bf16[272,128]{1,0:T(8,128)(2,1)S(1)}, bf16[272,128]{1,0:T(8,128)(2,1)S(1)}, u32[]{:S(2)}, u32[]{:S(2)}) collective-permute-start(bf16[272,128]{1,0:T(8,128)(2,1)S(1)} %copy-done.4), channel_id=1, source_target_pairs={{0,1},{1,0},{2,3},{3,2},{4,5},{5,4},{6,7},{7,6},{8,9},{9,8},{10,11... | collective-permute-start | bytes 208904 | tf_op jit(solution)/shard_map/ppermute | solution.py:348
  22.6 1.4 %collective-permute-start.2 = (bf16[768,128]{1,0:T(8,128)(2,1)S(1)}, bf16[768,128]{1,0:T(8,128)(2,1)S(1)}, u32[]{:S(2)}, u32[]{:S(2)}) collective-permute-start(bf16[768,128]{1,0:T(8,128)(2,1)S(1)} %get-tuple-element.22), channel_id=1, source_target_pairs={{0,1},{1,0},{2,3},{3,2},{4,5},{5,4},{6,7},{7,6},{8,9},{9,8},{10,11... | collective-permute-start | bytes 589832 | tf_op jit(solution)/shard_map/ppermute | solution.py:356

commit v7 on v4

v7 whole, which is shorter than its diff:
```python
import functools

import jax
import jax.numpy as jnp
from jax import lax
from jax.experimental import pallas as pl
from jax.experimental.pallas import tpu as pltpu
from jax.sharding import PartitionSpec as P

BF16 = jnp.bfloat16
F32 = jnp.float32
TAIL = 16
BIG = -1e30
LOG2E = 1.4426950408889634
NT = (((1,), (1,)), ((), ()))
NN = (((1,), (0,)), ((), ()))


def depth_of(count):
    return count.bit_length() - 1


def trailing_zeros(index, depth):
    total = jnp.zeros((), jnp.int32)
    for bit in range(depth):
        total = total + jnp.where((index & ((2 << bit) - 1)) == 0, 1, 0)
    return total


def owner_of(index, level, depth):
    if level == 0:
        return index * 0
    shift = depth - level + 1
    return ((index >> shift) << shift) + (1 << (depth - level))


def level_of_even(index, depth):
    return depth - trailing_zeros(index, depth)


def owner_at(index, level, depth):
    owner = owner_of(index, 0, depth)
    for place in range(1, depth + 1):
        owner = jnp.where(level == place, owner_of(index, place, depth), owner)
    return owner


def limit(mib):
    return pltpu.CompilerParams(vmem_limit_bytes=mib * 1024 * 1024)


def make_pack(lengths, other_lengths, keys, values, other_keys, other_values):
    odd = lax.axis_index("leaf") & 1 == 1
    length = jnp.where(odd, other_lengths[0], lengths[0]).astype(BF16)
    return jnp.concatenate(
        [
            jnp.where(odd, other_keys[0], keys[0]),
            jnp.where(odd, other_values[0], values[0]),
            jnp.full((TAIL, keys.shape[2]), length, BF16),
        ],
        0,
    )


def rows_kernel(heads, lengths_ref, query_ref, grad_ref, query_s, cot_s):
    rows = query_ref.shape[1]
    width = query_ref.shape[2] // heads
    row = lax.broadcasted_iota(jnp.int32, (rows, width), 0)
    for segment in range(2):
        live = row < lengths_ref[segment]
        for head in range(heads):
            here = pl.ds((segment * heads + head) * rows, rows)
            columns = slice(head * width, (head + 1) * width)
            query_s[here, :] = query_ref[segment, :, columns]
            cot = grad_ref[segment, :, columns]
            cot_s[here, :] = jnp.where(live, cot, jnp.zeros((), BF16))


def rows_call(lengths, queries, grads, width):
    heads = queries.shape[2] // width
    rows = queries.shape[1]
    vmem = pl.BlockSpec(memory_space=pltpu.VMEM)
    shape = jax.ShapeDtypeStruct((2 * heads * rows, width), BF16)
    return pl.pallas_call(
        functools.partial(rows_kernel, heads),
        out_shape=(shape, shape),
        in_specs=[pl.BlockSpec(memory_space=pltpu.SMEM), vmem, vmem],
        out_specs=(vmem, vmem),
        compiler_params=limit(8),
        cost_estimate=pl.CostEstimate(flops=0, bytes_accessed=4 << 20, transcendentals=0),
        name="rows",
    )(lengths, queries, grads)


def main_kernel(depth, heads, *refs):
    masks = (1 << (depth - 1)) - 1
    lengths_ref, other_lengths_ref, query_s, cot_s = refs[:4]
    key_ref, value_ref, other_key_ref, other_value_ref, pack_ref = refs[4:9]
    near, refs = refs[9 : 9 + masks], refs[9 + masks :]
    grad_query_ref, leaf_ref, part_ref = refs[:3]
    sends, refs = refs[3 : 3 + masks], refs[3 + masks :]
    keys_s, values_s, extra_s, keys_t, low_s, ds_s, terms_s = refs
    rows, width = key_ref.shape[1:]
    index = lax.axis_index("leaf")
    odd = index & 1 == 1
    even = index - (index & 1)
    own_level = depth - trailing_zeros(index, depth)
    scale = width ** (-0.5)
    lane = lax.broadcasted_iota(jnp.int32, (rows, width), 1)
    row = lax.broadcasted_iota(jnp.int32, (rows, width), 0)
    row_f = row.astype(F32)

    levels = depth + 2
    for level in range(levels):
        span = slice(level * rows, (level + 1) * rows)
        if level == depth + 1:
            key_block, value_block, length = key_ref[1], value_ref[1], lengths_ref[1]
        elif level == depth:
            key_block = jnp.where(odd, key_ref[0], other_key_ref[0])
            value_block = jnp.where(odd, value_ref[0], other_value_ref[0])
            length = jnp.where(odd, lengths_ref[0], other_lengths_ref[0])
        else:
            pick = (even ^ owner_of(even, level, depth)) >> 1
            block = pack_ref[...]
            for mask in range(1, masks + 1):
                block = jnp.where(pick == mask, near[mask - 1][...], block)
            key_block, value_block = block[:rows], block[rows : 2 * rows]
            length = block[2 * rows : 2 * rows + 1].astype(F32)
        if level >= depth:
            length = jnp.full((1, width), length.astype(F32), F32)
        keys_s[span, :] = key_block
        values_s[span, :] = value_block
        keys_t[:, span] = key_block.T
        dead = row_f >= length
        for segment in range(2):
            if segment == 0 and level == depth + 1:
                continue
            level_of = own_level if segment == 0 else depth + 1
            diagonal = jnp.where(row > 0, row, -1)
            column = jnp.where(level == level_of, diagonal, -1)
            column = jnp.where(dead | (level > level_of), 0, column)
            extra_s[segment, span, :] = jnp.where(lane == column, 1.0, 0.0).astype(BF16)

    ruled = jnp.where((lane > row) | (lane == 0), BIG, 0.0).astype(BF16)
    ruled = jnp.concatenate([ruled, ruled], 0)

    step_rows = 2 * rows
    for segment in range(2):
        count = (depth + 1 + segment) * rows
        keys_wide = jnp.concatenate([keys_s[:count, :], extra_s[segment, :count, :]], 1)
        for pair in range(heads // 2):
            at = (segment * (heads // 2) + pair) * step_rows
            here = slice(at, at + step_rows)
            columns = [slice(h * width, (h + 1) * width) for h in (2 * pair, 2 * pair + 1)]
            query, cot = query_s[here, :], cot_s[here, :]
            scores = lax.dot_general(
                keys_wide,
                jnp.concatenate([query, ruled], 1),
                NT,
                preferred_element_type=F32,
            )
            top = jnp.max(scores, axis=0, keepdims=True)
            weights = jnp.exp2((scores - top) * (scale * LOG2E))
            total = jnp.sum(weights, axis=0, keepdims=True)
            weights = weights * (1.0 / total)
            low_s[:count, here] = weights.astype(BF16)
            grad_weights = lax.dot_general(
                values_s[:count, :], cot, NT, preferred_element_type=F32
            )
            delta = jnp.sum(weights * grad_weights, axis=0, keepdims=True)
            grad_scores = (weights * (grad_weights - delta)).astype(BF16)
            ds_s[:count, here] = grad_scores
            grad_query = lax.dot_general(
                keys_t[:, :count], grad_scores, NN, preferred_element_type=F32
            )
            grad_query = (grad_query * scale).astype(BF16).T
            for n, c in enumerate(columns):
                grad_query_ref[segment, :, c] = grad_query[n * rows : (n + 1) * rows]

    inner = (depth + 1) * rows
    half = heads * rows
    grad_keys = lax.dot_general(ds_s[:inner, :], query_s[...], NN, preferred_element_type=F32)
    grad_keys = grad_keys * scale
    grad_values = lax.dot_general(low_s[:inner, :], cot_s[...], NN, preferred_element_type=F32)
    leaf_keys = lax.dot_general(
        ds_s[inner:, half:], query_s[half:, :], NN, preferred_element_type=F32
    )
    leaf_values = lax.dot_general(
        low_s[inner:, half:], cot_s[half:, :], NN, preferred_element_type=F32
    )
    leaf_ref[0:rows, :] = (leaf_keys * scale).astype(BF16)
    leaf_ref[rows : 2 * rows, :] = leaf_values.astype(BF16)

    for level in range(depth + 1):
        span = slice(level * rows, (level + 1) * rows)
        terms_s[level, :rows, :] = grad_keys[span]
        terms_s[level, rows:, :] = grad_values[span]
    part_ref[0] = terms_s[level_of_even(even, depth)]
    part_ref[1] = terms_s[depth]
    for mask, ref in enumerate(sends, 1):
        ref[...] = terms_s[level_of_even(even ^ (mask << 1), depth)].astype(BF16)


def main_call(smalls, queries, cot, arrays, near, depth):
    rows, width = arrays[0].shape[1:]
    heads = queries.shape[0] // (2 * rows)
    slots = (depth + 2) * rows
    total = 2 * heads * rows
    smem = pl.BlockSpec(memory_space=pltpu.SMEM)
    vmem = pl.BlockSpec(memory_space=pltpu.VMEM)
    return pl.pallas_call(
        functools.partial(main_kernel, depth, heads),
        out_shape=[
            jax.ShapeDtypeStruct((2, rows, heads * width), BF16),
            jax.ShapeDtypeStruct((2 * rows, width), BF16),
            jax.ShapeDtypeStruct((2, 2 * rows, width), F32),
        ]
        + [jax.ShapeDtypeStruct((2 * rows, width), BF16)] * len(near),
        in_specs=[smem] * 2 + [vmem] * (2 + len(arrays) + len(near)),
        out_specs=[vmem] * (3 + len(near)),
        scratch_shapes=[
            pltpu.VMEM((slots, width), BF16),
            pltpu.VMEM((slots, width), BF16),
            pltpu.VMEM((2, slots, width), BF16),
            pltpu.VMEM((width, slots), BF16),
            pltpu.VMEM((slots, total), BF16),
            pltpu.VMEM((slots, total), BF16),
            pltpu.VMEM((depth + 1, 2 * rows, width), F32),
        ],
        compiler_params=limit(24),
        name="attend",
    )(*smalls, queries, cot, *arrays, *near)


def fold_kernel(depth, part_ref, *refs):
    arrived, (keep_ref, send_ref) = refs[:-2], refs[-2:]
    index = lax.axis_index("leaf")
    odd = index & 1 == 1
    even = index - (index & 1)
    level = level_of_even(even, depth)
    total = part_ref[0]
    for mask, ref in enumerate(arrived, 1):
        mine = owner_at(even ^ (mask << 1), level, depth) == even
        total = total + jnp.where(mine, ref[...].astype(F32), 0.0)
    keep_ref[...] = jnp.where(odd, part_ref[1], total)
    send_ref[...] = jnp.where(odd, total, part_ref[1]).astype(BF16)


def fold_call(part, arrived, depth):
    vmem = pl.BlockSpec(memory_space=pltpu.VMEM)
    return pl.pallas_call(
        functools.partial(fold_kernel, depth),
        out_shape=[
            jax.ShapeDtypeStruct(part.shape[1:], F32),
            jax.ShapeDtypeStruct(part.shape[1:], BF16),
        ],
        in_specs=[vmem] * (1 + len(arrived)),
        out_specs=[vmem] * 2,
        compiler_params=limit(3),
        name="fold",
    )(part, *arrived)


def final_kernel(leaf_ref, keep_ref, other_ref, keys_ref, values_ref):
    rows = keys_ref.shape[1]
    total = (keep_ref[...] + other_ref[...].astype(F32)).astype(BF16)
    keys_ref[0] = total[:rows]
    values_ref[0] = total[rows:]
    keys_ref[1] = leaf_ref[:rows, :]
    values_ref[1] = leaf_ref[rows:, :]


def final_call(leaf, keep, other, shape):
    vmem = pl.BlockSpec(memory_space=pltpu.VMEM)
    return pl.pallas_call(
        final_kernel,
        out_shape=[jax.ShapeDtypeStruct(shape, BF16)] * 2,
        in_specs=[vmem] * 3,
        out_specs=[vmem] * 2,
        compiler_params=limit(2),
        name="final",
    )(leaf, keep, other)


def body(queries, key_states, value_states, grad_output, lengths):
    count = lax.axis_size("leaf")
    depth = depth_of(count)
    masks = range(1, count // 2)

    def move(block, flip):
        return lax.ppermute(block, "leaf", [(i, i ^ flip) for i in range(count)])

    def exchange(blocks):
        moved = {m: move(blocks[m], m << 1) for m in reversed(masks)}
        return [moved[m] for m in masks]

    other_keys, other_values = move(key_states, 1), move(value_states, 1)
    other_lengths = move(lengths, 1)
    pack = make_pack(lengths, other_lengths, key_states, value_states, other_keys, other_values)
    near = exchange({m: pack for m in masks})
    query_rows, cot = rows_call(lengths, queries, grad_output, key_states.shape[2])
    arrays = (key_states, value_states, other_keys, other_values, pack)
    grad_queries, leaf, part, *sends = main_call(
        (lengths, other_lengths), query_rows, cot, arrays, near, depth
    )
    arrived = exchange(dict(zip(masks, sends)))
    keep, send = fold_call(part, arrived, depth)
    grad_keys, grad_values = final_call(leaf, keep, move(send, 1), key_states.shape)
    return grad_queries, grad_keys, grad_values


def solution(mesh):
    segments = P(("dp", "leaf"), None, None)
    return jax.shard_map(
        body,
        mesh=mesh,
        in_specs=(segments, segments, segments, segments, P(("dp", "leaf"))),
        out_specs=(segments, segments, segments),
        check_vma=False,
    )
```

time: 41 us -> 29 us (0.71)
  starting transfers between devices: 20.1 us -> 8.94 us
  Pallas kernels: 9.71 us -> 8.22 us
  other arithmetic: 0 us -> 0.88 us
  waiting for transfers between devices: 7.89 us -> 7.11 us
  between operations: 0.78 us -> 1.43 us
    ppermute x11 -> x10, starting transfers between devices: 20.1 us -> 8.94 us  [move(): return lax.ppermute(block, 'leaf', [(i, i ^ flip) for i in range(count)])]
    pallas_call x4 -> x3, Pallas kernels: 8.94 us -> 7.44 us  [the longest x1 6.71 us: main_call(): pl.pallas_call(functools.partial(main_kernel, depth, heads), out_shape=[j...]
    select_n x0 -> x2, other arithmetic: none -> 0.78 us  [the longest x1 0.77 us: make_pack(): jnp.where(odd, other_keys[0], keys[0])]
    ppermute x11 -> x10, waiting for transfers between devices: 7.89 us -> 7.11 us  [move(): return lax.ppermute(block, 'leaf', [(i, i ^ flip) for i in range(count)])]
    unnamed x12 -> x10, local copies, waits for them, and re-layouts: 2.09 us -> 2.1 us
  transfers between devices with their start and end apart: 11 -> 10, of which waited for: 6 -> 7; matrix products, arithmetic and copies ran while one was open for 0% -> 3% of each run, Pallas kernels for 2% -> 3%
where the time goes in v7:
time: 29 us; the launch traced here: 28.7 us
  starting transfers between devices  8.94 us (31%)
  Pallas kernels  8.22 us (28%)
  waiting for transfers between devices  7.11 us (25%)
  local copies, waits for them, and re-layouts  2.11 us (7%)
  between operations  1.43 us (5%)
  other arithmetic  0.88 us (3%)
    ppermute x10, starting transfers between devices, move(): return lax.ppermute(block, 'leaf', [(i, i ^ flip) for i in range(count)])  8.94 us
    ppermute x10, waiting for transfers between devices, move(): return lax.ppermute(block, 'leaf', [(i, i ^ flip) for i in range(count)])  7.11 us
    pallas_call x1, Pallas kernels, main_call(): pl.pallas_call(functools.partial(main_kernel, depth, heads), out_shape=[j...  6.71 us
    unnamed x10, local copies, waits for them, and re-layouts  2.1 us
    pallas_call x1, Pallas kernels, rows_call(): pl.pallas_call(functools.partial(rows_kernel, heads), out_shape=(shape, s...  0.78 us
    select_n x1, other arithmetic, make_pack(): jnp.where(odd, other_keys[0], keys[0])  0.77 us
    pallas_call x1, Pallas kernels, final_call(): pl.pallas_call(final_kernel, out_shape=[jax.ShapeDtypeStruct(shape, BF16)...  0.67 us
  transfers between devices with their start and end apart: 10, of which 7 were waited for; matrix products, arithmetic and copies ran while one was open for 3% of the time, Pallas kernels for 3%

profile of v7, /device:TPU:0, one launch (start us, length us, event | category | flops | bytes accessed | tf_op | source)
XLA Modules:
  0.0 28.7 jit_solution(14031971435739453694)
XLA Ops:
  0.6 0.0 copy-start.3
  0.6 0.5 %collective-permute-start.1 = (bf16[2,128,128]{2,1,0:T(8,128)(2,1)}, bf16[2,128,128]{2,1,0:T(8,128)(2,1)S(1)}, u32[]{:S(2)}, u32[]{:S(2)}) collective-permute-start(bf16[2,128,128]{2,1,0:T(8,128)(2,1)} %refs_4_.1), channel_id=1, source_target_pairs={{0,1},{1,0},{2,3},{3,2},{4,5},{5,4},{6,7},{7,6},{8,9},{9,8},{10,11... | collective-permute-start | bytes 196616 | tf_op jit(solution)/shard_map/ppermute | solution.py:291
  1.2 0.1 collective-permute-start
  1.2 0.4 %collective-permute-start.2 = (bf16[2,128,128]{2,1,0:T(8,128)(2,1)}, bf16[2,128,128]{2,1,0:T(8,128)(2,1)S(1)}, u32[]{:S(2)}, u32[]{:S(2)}) collective-permute-start(bf16[2,128,128]{2,1,0:T(8,128)(2,1)} %refs_5_.1), channel_id=1, source_target_pairs={{0,1},{1,0},{2,3},{3,2},{4,5},{5,4},{6,7},{7,6},{8,9},{9,8},{10,11... | collective-permute-start | bytes 196616 | tf_op jit(solution)/shard_map/ppermute | solution.py:291
  1.7 0.7 %collective-permute-done.refs_1_ = s32[2]{0:T(128)S(1)} collective-permute-done((s32[2]{0:T(128)}, s32[2]{0:T(128)S(1)}, u32[]{:S(2)}, u32[]{:S(2)}) %collective-permute-start) | collective-permute-done | bytes 40 | tf_op jit(solution)/shard_map/ppermute | solution.py:291
  3.1 0.0 collective-permute-done.1.refs_6_
  3.1 0.8 %fusion.1 = bf16[128,128]{1,0:T(8,128)(2,1)S(1)} fusion(bf16[2,128,128]{2,1,0:T(8,128)(2,1)S(1)} %collective-permute-done.1.refs_6_, bf16[2,128,128]{2,1,0:T(8,128)(2,1)} %refs_4_.1, pred[]{:T(512)S(6)} %eq.3), kind=kLoop, calls=%fused_computation.4 | loop fusion | flops 16384 | bytes 98305 | tf_op jit(solution)/shard_map/jit(_where)/select_n | solution.py:57
  3.9 0.0 collective-permute-done.2.refs_7_
  3.9 0.0 copy-start.4
  3.9 0.0 copy-start.2
  4.0 0.1 maximum_maximum_fusion.refs_8_
  4.1 3.7 %collective-permute-start.5 = (bf16[272,128]{1,0:T(8,128)(2,1)S(1)}, bf16[272,128]{1,0:T(8,128)(2,1)S(1)}, u32[]{:S(2)}, u32[]{:S(2)}) collective-permute-start(bf16[272,128]{1,0:T(8,128)(2,1)S(1)} %maximum_maximum_fusion.refs_8_), channel_id=1, source_target_pairs={{0,6},{1,7},{2,4},{3,5},{4,2},{5,3},{6,0},{7,1},{8,14},{9,15},{10,... | collective-permute-start | bytes 208904 | tf_op jit(solution)/shard_map/ppermute | solution.py:291
  7.8 0.5 %collective-permute-start.4 = (bf16[272,128]{1,0:T(8,128)(2,1)S(1)}, bf16[272,128]{1,0:T(8,128)(2,1)S(1)}, u32[]{:S(2)}, u32[]{:S(2)}) collective-permute-start(bf16[272,128]{1,0:T(8,128)(2,1)S(1)} %maximum_maximum_fusion.refs_8_), channel_id=1, source_target_pairs={{0,4},{1,5},{2,6},{3,7},{4,0},{5,1},{6,2},{7,3},{8,12},{9,13},{10,... | collective-permute-start | bytes 208904 | tf_op jit(solution)/shard_map/ppermute | solution.py:291
  8.3 0.1 collective-permute-start.3
  8.4 1.0 %copy-done = bf16[2,128,1024]{2,1,0:T(8,128)(2,1)S(1)} copy-done((bf16[2,128,1024]{2,1,0:T(8,128)(2,1)S(1)}, bf16[2,128,1024]{2,1,0:T(8,128)(2,1)}, u32[]{:S(2)}) %copy-start) | copy-done | bytes 524312
  9.5 1.0 %copy-done.1 = bf16[2,128,1024]{2,1,0:T(8,128)(2,1)S(1)} copy-done((bf16[2,128,1024]{2,1,0:T(8,128)(2,1)S(1)}, bf16[2,128,1024]{2,1,0:T(8,128)(2,1)}, u32[]{:S(2)}) %copy-start.1) | copy-done | bytes 524312
  10.5 0.8 %rows.1 = (bf16[2048,128]{1,0:T(8,128)(2,1)S(1)}, bf16[2048,128]{1,0:T(8,128)(2,1)S(1)}) custom-call(s32[2]{0:T(128)S(1)} %copy-done.4, bf16[2,128,1024]{2,1,0:T(8,128)(2,1)S(1)} %copy-done, bf16[2,128,1024]{2,1,0:T(8,128)(2,1)S(1)} %copy-done.1), custom_call_target="tpu_custom_call" | custom-call | bytes 4194304 | tf_op jit(solution)/shard_map/rows/pallas_call | solution.py:84
  11.3 0.0 collective-permute-done.5.refs_11_
  11.3 0.8 %collective-permute-done.4.refs_10_ = bf16[272,128]{1,0:T(8,128)(2,1)S(1)} collective-permute-done((bf16[272,128]{1,0:T(8,128)(2,1)S(1)}, bf16[272,128]{1,0:T(8,128)(2,1)S(1)}, u32[]{:S(2)}, u32[]{:S(2)}) %collective-permute-start.4) | collective-permute-done | bytes 69664 | tf_op jit(solution)/shard_map/ppermute | solution.py:291
  12.1 0.5 %collective-permute-done.3.refs_9_ = bf16[272,128]{1,0:T(8,128)(2,1)S(1)} collective-permute-done((bf16[272,128]{1,0:T(8,128)(2,1)S(1)}, bf16[272,128]{1,0:T(8,128)(2,1)S(1)}, u32[]{:S(2)}, u32[]{:S(2)}) %collective-permute-start.3) | collective-permute-done | bytes 69664 | tf_op jit(solution)/shard_map/ppermute | solution.py:291
  12.6 0.0 copy-done.2
  12.6 6.7 %attend.1 = (bf16[2,128,1024]{2,1,0:T(8,128)(2,1)}, bf16[256,128]{1,0:T(8,128)(2,1)S(1)}, f32[2,256,128]{2,1,0:T(8,128)S(1)}, bf16[256,128]{1,0:T(8,128)(2,1)S(1...) custom-call(s32[2]{0:T(128)S(1)} %copy-done.4, s32[2]{0:T(128)S(1)} %collective-permute-done.refs_1_, ...), custom_call_target="tpu_custom_call" | custom-call | tf_op jit(solution)/shard_map/attend/pallas_call | solution.py:211
  19.3 1.1 %collective-permute-start.6 = (bf16[256,128]{1,0:T(8,128)(2,1)S(1)}, bf16[256,128]{1,0:T(8,128)(2,1)S(1)}, u32[]{:S(2)}, u32[]{:S(2)}) collective-permute-start(bf16[256,128]{1,0:T(8,128)(2,1)S(1)} %get-tuple-element.20), channel_id=1, source_target_pairs={{0,2},{1,3},{2,0},{3,1},{4,6},{5,7},{6,4},{7,5},{8,10},{9,11},{10,... | collective-permute-start | bytes 196616 | tf_op jit(solution)/shard_map/ppermute | solution.py:291
  20.4 1.1 %collective-permute-start.7 = (bf16[256,128]{1,0:T(8,128)(2,1)S(1)}, bf16[256,128]{1,0:T(8,128)(2,1)S(1)}, u32[]{:S(2)}, u32[]{:S(2)}) collective-permute-start(bf16[256,128]{1,0:T(8,128)(2,1)S(1)} %get-tuple-element.21), channel_id=1, source_target_pairs={{0,4},{1,5},{2,6},{3,7},{4,0},{5,1},{6,2},{7,3},{8,12},{9,13},{10,... | collective-permute-start | bytes 196616 | tf_op jit(solution)/shard_map/ppermute | solution.py:291
  21.5 1.3 %collective-permute-start.8 = (bf16[256,128]{1,0:T(8,128)(2,1)S(1)}, bf16[256,128]{1,0:T(8,128)(2,1)S(1)}, u32[]{:S(2)}, u32[]{:S(2)}) collective-permute-start(bf16[256,128]{1,0:T(8,128)(2,1)S(1)} %get-tuple-element.22), channel_id=1, source_target_pairs={{0,6},{1,7},{2,4},{3,5},{4,2},{5,3},{6,0},{7,1},{8,14},{9,15},{10,... | collective-permute-start | bytes 196616 | tf_op jit(solution)/shard_map/ppermute | solution.py:291
  22.8 0.8 %collective-permute-done.6.refs_0_ = bf16[256,128]{1,0:T(8,128)(2,1)S(1)} collective-permute-done((bf16[256,128]{1,0:T(8,128)(2,1)S(1)}, bf16[256,128]{1,0:T(8,128)(2,1)S(1)}, u32[]{:S(2)}, u32[]{:S(2)}) %collective-permute-start.6) | collective-permute-done | bytes 65568 | tf_op jit(solution)/shard_map/ppermute | solution.py:291
  23.6 1.7 %collective-permute-done.7.refs_1_ = bf16[256,128]{1,0:T(8,128)(2,1)S(1)} collective-permute-done((bf16[256,128]{1,0:T(8,128)(2,1)S(1)}, bf16[256,128]{1,0:T(8,128)(2,1)S(1)}, u32[]{:S(2)}, u32[]{:S(2)}) %collective-permute-start.7) | collective-permute-done | bytes 65568 | tf_op jit(solution)/shard_map/ppermute | solution.py:291
  25.3 1.4 %collective-permute-done.8.refs_2_ = bf16[256,128]{1,0:T(8,128)(2,1)S(1)} collective-permute-done((bf16[256,128]{1,0:T(8,128)(2,1)S(1)}, bf16[256,128]{1,0:T(8,128)(2,1)S(1)}, u32[]{:S(2)}, u32[]{:S(2)}) %collective-permute-start.8) | collective-permute-done | bytes 65568 | tf_op jit(solution)/shard_map/ppermute | solution.py:291
  26.6 0.1 fold.1
  26.7 0.1 collective-permute-start.9
  26.8 1.2 %collective-permute-done.9.other_ref = bf16[256,128]{1,0:T(8,128)(2,1)S(1)} collective-permute-done((bf16[256,128]{1,0:T(8,128)(2,1)S(1)}, bf16[256,128]{1,0:T(8,128)(2,1)S(1)}, u32[]{:S(2)}, u32[]{:S(2)}) %collective-permute-start.9) | collective-permute-done | bytes 65568 | tf_op jit(solution)/shard_map/ppermute | solution.py:291
  28.0 0.7 %final.1 = (bf16[2,128,128]{2,1,0:T(8,128)(2,1)}, bf16[2,128,128]{2,1,0:T(8,128)(2,1)}) custom-call(bf16[256,128]{1,0:T(8,128)(2,1)S(1)} %get-tuple-element.18.leaf_ref, f32[256,128]{1,0:T(8,128)S(1)} %get-tuple-element.23.keep_ref, bf16[256,128]{1,0:T(8,128)(2,1)S(1)} %collective-permute-done.9.other_ref), custom_call_target="tpu_custom_call" | custom-call | tf_op jit(solution)/shard_map/final/pallas_call | solution.py:275
  (7 shorter events, 0.0 us)
Async XLA Ops:
  0.6 3.3 %copy-start.3 = (bf16[2,128,128]{2,1,0:T(8,128)(2,1)S(1)}, bf16[2,128,128]{2,1,0:T(8,128)(2,1)}, u32[]{:S(2)}) copy-start(bf16[2,128,128]{2,1,0:T(8,128)(2,1)} %refs_5_.1) | copy-start | bytes 196612
  0.6 2.5 %collective-permute-start.1 = (bf16[2,128,128]{2,1,0:T(8,128)(2,1)}, bf16[2,128,128]{2,1,0:T(8,128)(2,1)S(1)}, u32[]{:S(2)}, u32[]{:S(2)}) collective-permute-start(bf16[2,128,128]{2,1,0:T(8,128)(2,1)} %refs_4_.1), channel_id=1, source_target_pairs={{0,1},{1,0},{2,3},{3,2},{4,5},{5,4},{6,7},{7,6},{8,9},{9,8},{10,11... | collective-permute-start | bytes 196616 | tf_op jit(solution)/shard_map/ppermute | solution.py:291
  1.2 1.3 %collective-permute-start = (s32[2]{0:T(128)}, s32[2]{0:T(128)S(1)}, u32[]{:S(2)}, u32[]{:S(2)}) collective-permute-start(s32[2]{0:T(128)} %refs_0_.1), channel_id=1, source_target_pairs={{0,1},{1,0},{2,3},{3,2},{4,5},{5,4},{6,7},{7,6},{8,9},{9,8},{10,11... | collective-permute-start | bytes 32 | tf_op jit(solution)/shard_map/ppermute | solution.py:291
  1.2 2.7 %collective-permute-start.2 = (bf16[2,128,128]{2,1,0:T(8,128)(2,1)}, bf16[2,128,128]{2,1,0:T(8,128)(2,1)S(1)}, u32[]{:S(2)}, u32[]{:S(2)}) collective-permute-start(bf16[2,128,128]{2,1,0:T(8,128)(2,1)} %refs_5_.1), channel_id=1, source_target_pairs={{0,1},{1,0},{2,3},{3,2},{4,5},{5,4},{6,7},{7,6},{8,9},{9,8},{10,11... | collective-permute-start | bytes 196616 | tf_op jit(solution)/shard_map/ppermute | solution.py:291
  3.9 4.5 %copy-start.4 = (s32[2]{0:T(128)S(1)}, s32[2]{0:T(128)}, u32[]{:S(2)}) copy-start(s32[2]{0:T(128)} %refs_0_.1) | copy-start | bytes 28
  3.9 8.7 %copy-start.2 = (bf16[2,128,128]{2,1,0:T(8,128)(2,1)S(1)}, bf16[2,128,128]{2,1,0:T(8,128)(2,1)}, u32[]{:S(2)}) copy-start(bf16[2,128,128]{2,1,0:T(8,128)(2,1)} %refs_4_.1) | copy-start | bytes 196612
  4.1 7.2 %collective-permute-start.5 = (bf16[272,128]{1,0:T(8,128)(2,1)S(1)}, bf16[272,128]{1,0:T(8,128)(2,1)S(1)}, u32[]{:S(2)}, u32[]{:S(2)}) collective-permute-start(bf16[272,128]{1,0:T(8,128)(2,1)S(1)} %maximum_maximum_fusion.refs_8_), channel_id=1, source_target_pairs={{0,6},{1,7},{2,4},{3,5},{4,2},{5,3},{6,0},{7,1},{8,14},{9,15},{10,... | collective-permute-start | bytes 208904 | tf_op jit(solution)/shard_map/ppermute | solution.py:291
  7.8 4.3 %collective-permute-start.4 = (bf16[272,128]{1,0:T(8,128)(2,1)S(1)}, bf16[272,128]{1,0:T(8,128)(2,1)S(1)}, u32[]{:S(2)}, u32[]{:S(2)}) collective-permute-start(bf16[272,128]{1,0:T(8,128)(2,1)S(1)} %maximum_maximum_fusion.refs_8_), channel_id=1, source_target_pairs={{0,4},{1,5},{2,6},{3,7},{4,0},{5,1},{6,2},{7,3},{8,12},{9,13},{10,... | collective-permute-start | bytes 208904 | tf_op jit(solution)/shard_map/ppermute | solution.py:291
  8.3 4.3 %collective-permute-start.3 = (bf16[272,128]{1,0:T(8,128)(2,1)S(1)}, bf16[272,128]{1,0:T(8,128)(2,1)S(1)}, u32[]{:S(2)}, u32[]{:S(2)}) collective-permute-start(bf16[272,128]{1,0:T(8,128)(2,1)S(1)} %maximum_maximum_fusion.refs_8_), channel_id=1, source_target_pairs={{0,2},{1,3},{2,0},{3,1},{4,6},{5,7},{6,4},{7,5},{8,10},{9,11},{10,... | collective-permute-start | bytes 208904 | tf_op jit(solution)/shard_map/ppermute | solution.py:291
  8.4 1.0 %copy-start = (bf16[2,128,1024]{2,1,0:T(8,128)(2,1)S(1)}, bf16[2,128,1024]{2,1,0:T(8,128)(2,1)}, u32[]{:S(2)}) copy-start(bf16[2,128,1024]{2,1,0:T(8,128)(2,1)} %query_ref.1) | copy-start | bytes 1572868
  9.5 1.0 %copy-start.1 = (bf16[2,128,1024]{2,1,0:T(8,128)(2,1)S(1)}, bf16[2,128,1024]{2,1,0:T(8,128)(2,1)}, u32[]{:S(2)}) copy-start(bf16[2,128,1024]{2,1,0:T(8,128)(2,1)} %grad_ref.1) | copy-start | bytes 1572868
  19.3 4.3 %collective-permute-start.6 = (bf16[256,128]{1,0:T(8,128)(2,1)S(1)}, bf16[256,128]{1,0:T(8,128)(2,1)S(1)}, u32[]{:S(2)}, u32[]{:S(2)}) collective-permute-start(bf16[256,128]{1,0:T(8,128)(2,1)S(1)} %get-tuple-element.20), channel_id=1, source_target_pairs={{0,2},{1,3},{2,0},{3,1},{4,6},{5,7},{6,4},{7,5},{8,10},{9,11},{10,... | collective-permute-start | bytes 196616 | tf_op jit(solution)/shard_map/ppermute | solution.py:291
  20.4 4.9 %collective-permute-start.7 = (bf16[256,128]{1,0:T(8,128)(2,1)S(1)}, bf16[256,128]{1,0:T(8,128)(2,1)S(1)}, u32[]{:S(2)}, u32[]{:S(2)}) collective-permute-start(bf16[256,128]{1,0:T(8,128)(2,1)S(1)} %get-tuple-element.21), channel_id=1, source_target_pairs={{0,4},{1,5},{2,6},{3,7},{4,0},{5,1},{6,2},{7,3},{8,12},{9,13},{10,... | collective-permute-start | bytes 196616 | tf_op jit(solution)/shard_map/ppermute | solution.py:291
  21.5 5.2 %collective-permute-start.8 = (bf16[256,128]{1,0:T(8,128)(2,1)S(1)}, bf16[256,128]{1,0:T(8,128)(2,1)S(1)}, u32[]{:S(2)}, u32[]{:S(2)}) collective-permute-start(bf16[256,128]{1,0:T(8,128)(2,1)S(1)} %get-tuple-element.22), channel_id=1, source_target_pairs={{0,6},{1,7},{2,4},{3,5},{4,2},{5,3},{6,0},{7,1},{8,14},{9,15},{10,... | collective-permute-start | bytes 196616 | tf_op jit(solution)/shard_map/ppermute | solution.py:291
  26.7 1.3 %collective-permute-start.9 = (bf16[256,128]{1,0:T(8,128)(2,1)S(1)}, bf16[256,128]{1,0:T(8,128)(2,1)S(1)}, u32[]{:S(2)}, u32[]{:S(2)}) collective-permute-start(bf16[256,128]{1,0:T(8,128)(2,1)S(1)} %get-tuple-element.24), channel_id=1, source_target_pairs={{0,1},{1,0},{2,3},{3,2},{4,5},{5,4},{6,7},{7,6},{8,9},{9,8},{10,11... | collective-permute-start | bytes 196616 | tf_op jit(solution)/shard_map/ppermute | solution.py:291

commit v8 on v0

v8 whole, which is shorter than its diff:
```python
import functools

import jax
import jax.numpy as jnp
from jax import lax
from jax.experimental import pallas as pl
from jax.experimental.pallas import tpu as pltpu
from jax.sharding import PartitionSpec as P

BF16 = jnp.bfloat16
F32 = jnp.float32
TAIL = 16
BIG = -1e30
LOG2E = 1.4426950408889634
NT = (((1,), (1,)), ((), ()))
NN = (((1,), (0,)), ((), ()))


def depth_of(count):
    return count.bit_length() - 1


def trailing_zeros(index, depth):
    total = jnp.zeros((), jnp.int32)
    for bit in range(depth):
        total = total + jnp.where((index & ((2 << bit) - 1)) == 0, 1, 0)
    return total


def owner_of(index, level, depth):
    if level == 0:
        return index * 0
    shift = depth - level + 1
    return ((index >> shift) << shift) + (1 << (depth - level))


def level_of_even(index, depth):
    return depth - trailing_zeros(index, depth)


def owner_at(index, level, depth):
    owner = owner_of(index, 0, depth)
    for place in range(1, depth + 1):
        owner = jnp.where(level == place, owner_of(index, place, depth), owner)
    return owner


def call(kernel, name, mib, scalars, arrays, outs, scratch=(), flops=0):
    smem = pl.BlockSpec(memory_space=pltpu.SMEM)
    vmem = pl.BlockSpec(memory_space=pltpu.VMEM)
    return pl.pallas_call(
        kernel,
        out_shape=[jax.ShapeDtypeStruct(shape, kind) for shape, kind in outs],
        in_specs=[smem] * len(scalars) + [vmem] * len(arrays),
        out_specs=[vmem] * len(outs),
        scratch_shapes=[pltpu.VMEM(shape, kind) for shape, kind in scratch],
        compiler_params=pltpu.CompilerParams(vmem_limit_bytes=mib * 1024 * 1024),
        cost_estimate=pl.CostEstimate(flops=flops, bytes_accessed=1 << 20, transcendentals=0),
        name=name,
    )(*scalars, *arrays)


def ruled_columns(rows, width):
    lane = lax.broadcasted_iota(jnp.int32, (rows, width), 1)
    row = lax.broadcasted_iota(jnp.int32, (rows, width), 0)
    ruled = jnp.where((lane > row) | (lane == 0), BIG, 0.0).astype(BF16)
    return jnp.concatenate([ruled, ruled], 0)


def mask_columns(length, before, same, rows, width):
    lane = lax.broadcasted_iota(jnp.int32, (rows, width), 1)
    row = lax.broadcasted_iota(jnp.int32, (rows, width), 0)
    column = jnp.where(same & (row > 0), row, -1)
    live = (row.astype(F32) < length) & (before | same)
    column = jnp.where(live, column, 0)
    return jnp.where(lane == column, 1.0, 0.0).astype(BF16)


def block_scores(keys_wide, values, query_wide, cot, factor):
    scores = lax.dot_general(keys_wide, query_wide, NT, preferred_element_type=F32)
    top = jnp.max(scores, axis=0, keepdims=True)
    raised = jnp.exp2((scores - top) * factor)
    total = jnp.sum(raised, axis=0, keepdims=True)
    grad_weights = lax.dot_general(values, cot, NT, preferred_element_type=F32)
    partial = jnp.sum(raised * grad_weights, axis=0, keepdims=True)
    return raised, grad_weights, top, total, partial


def early_kernel(depth, heads, lengths_ref, query_ref, grad_ref, key_ref, value_ref, *refs):
    own_ref, mate_ref, query_s, cot_s, raised_s, weights_s, stats_s, keys_s = refs
    rows, width = key_ref.shape[1:]
    index = lax.axis_index("leaf")
    odd = index & 1 == 1
    factor = width ** (-0.5) * LOG2E
    step = 2 * rows
    row = lax.broadcasted_iota(jnp.int32, (rows, width), 0)
    block = jnp.where(odd, own_ref[...], mate_ref[...])
    length = block[2 * rows : 2 * rows + 1].astype(F32)
    keys = [block[:rows], key_ref[1]]
    values = [block[rows : 2 * rows], value_ref[1]]
    keys_s[:rows, :] = keys[0]
    keys_s[rows:, :] = keys[1]
    yes, no = jnp.full((), True), jnp.full((), False)
    ruled = ruled_columns(rows, width)
    leaf_length = jnp.full((1, width), lengths_ref[1].astype(F32), F32)
    wide = [
        [
            jnp.concatenate([keys[0], mask_columns(length, no, odd, rows, width)], 1),
        ],
        [
            jnp.concatenate([keys[0], mask_columns(length, yes, no, rows, width)], 1),
            jnp.concatenate([keys[1], mask_columns(leaf_length, no, yes, rows, width)], 1),
        ],
    ]
    for segment in range(2):
        live = row < lengths_ref[segment]
        for pair in range(heads // 2):
            at = (segment * (heads // 2) + pair) * step
            here = slice(at, at + step)
            columns = [slice(h * width, (h + 1) * width) for h in (2 * pair, 2 * pair + 1)]
            query = jnp.concatenate([query_ref[segment, :, c] for c in columns], 0)
            cot = jnp.concatenate(
                [jnp.where(live, grad_ref[segment, :, c], jnp.zeros((), BF16)) for c in columns], 0
            )
            query_s[here, :] = query
            cot_s[here, :] = cot
            query_wide = jnp.concatenate([query, ruled], 1)
            for place in range(1 + segment):
                span = slice(place * rows, (place + 1) * rows)
                raised, grad_weights, top, total, partial = block_scores(
                    wide[segment][place], values[place], query_wide, cot, factor
                )
                raised_s[span, here] = raised
                weights_s[span, here] = grad_weights
                for n, line in enumerate((top, total, partial)):
                    stats_s[3 * place + n : 3 * place + n + 1, here] = line


def middle_kernel(depth, heads, query_s, cot_s, stats_ref, pack_ref, *refs):
    masks = (1 << (depth - 1)) - 1
    near, refs = refs[:masks], refs[masks:]
    ds_s, joined_s, keys_t, part_ref = refs[:4]
    sends, refs = refs[4 : 4 + masks], refs[4 + masks :]
    raised_s, weights_s, low_s, terms_s = refs
    width = pack_ref.shape[1]
    rows = (pack_ref.shape[0] - TAIL) // 2
    index = lax.axis_index("leaf")
    even = index - (index & 1)
    own_level = depth - trailing_zeros(index, depth)
    scale = width ** (-0.5)
    factor = scale * LOG2E
    step = 2 * rows
    yes, no = jnp.full((), True), jnp.full((), False)
    ruled = ruled_columns(rows, width)
    values = []
    wide = [[], []]
    for level in range(depth):
        pick = (even ^ owner_of(even, level, depth)) >> 1
        block = pack_ref[...]
        for mask in range(1, masks + 1):
            block = jnp.where(pick == mask, near[mask - 1][...], block)
        keys = block[:rows]
        values.append(block[rows : 2 * rows])
        length = block[2 * rows : 2 * rows + 1].astype(F32)
        keys_t[:, level * rows : (level + 1) * rows] = keys.T
        inner = mask_columns(length, level < own_level, level == own_level, rows, width)
        outer = mask_columns(length, yes, no, rows, width)
        wide[0].append(jnp.concatenate([keys, inner], 1))
        wide[1].append(jnp.concatenate([keys, outer], 1))

    grad_keys = grad_values = None
    half = heads * rows
    for segment in range(2):
        for pair in range(heads // 2):
            at = (segment * (heads // 2) + pair) * step
            here = slice(at, at + step)
            query, cot = query_s[here, :], cot_s[here, :]
            query_wide = jnp.concatenate([query, ruled], 1)
            tops, totals, partials = [], [], []
            for place in range(1 + segment):
                tops.append(stats_ref[3 * place : 3 * place + 1, here])
                totals.append(stats_ref[3 * place + 1 : 3 * place + 2, here])
                partials.append(stats_ref[3 * place + 2 : 3 * place + 3, here])
            for level in range(depth):
                span = slice(level * rows, (level + 1) * rows)
                raised, grad_weights, top, total, partial = block_scores(
                    wide[segment][level], values[level], query_wide, cot, factor
                )
                raised_s[span, here] = raised
                weights_s[span, here] = grad_weights
                tops.append(top)
                totals.append(total)
                partials.append(partial)
            highest = functools.reduce(jnp.maximum, tops)
            shares = [jnp.exp2((top - highest) * factor) for top in tops]
            total = sum(share * part for share, part in zip(shares, totals))
            inverse = 1.0 / total
            shares = [share * inverse for share in shares]
            delta = sum(share * part for share, part in zip(shares, partials))
            joined_s[0:1, here] = delta
            for place in range(1 + segment):
                joined_s[1 + place : 2 + place, here] = shares[place]
            for level in range(depth):
                span = slice(level * rows, (level + 1) * rows)
                weights = raised_s[span, here] * shares[1 + segment + level]
                low_s[span, here] = weights.astype(BF16)
                ds_s[span, here] = (weights * (weights_s[span, here] - delta)).astype(BF16)
        now = slice(segment * half, (segment + 1) * half)
        more_keys = lax.dot_general(
            ds_s[:, now], query_s[now, :], NN, preferred_element_type=F32
        )
        more_values = lax.dot_general(
            low_s[:, now], cot_s[now, :], NN, preferred_element_type=F32
        )
        grad_keys = more_keys if segment == 0 else grad_keys + more_keys
        grad_values = more_values if segment == 0 else grad_values + more_values
    for level in range(depth):
        span = slice(level * rows, (level + 1) * rows)
        terms_s[level, :rows, :] = grad_keys[span] * scale
        terms_s[level, rows:, :] = grad_values[span]
    part_ref[...] = terms_s[level_of_even(even, depth)]
    for mask, ref in enumerate(sends, 1):
        ref[...] = terms_s[level_of_even(even ^ (mask << 1), depth)].astype(BF16)


def late_kernel(heads, query_s, cot_s, raised_ref, weights_ref, joined_ref, ds_ref, *refs):
    keys_t, keys_s, grad_query_ref, leaf_ref, part_ref, low_s, ds_s = refs
    width = keys_s.shape[1]
    rows = keys_s.shape[0] // 2
    scale = width ** (-0.5)
    step = 2 * rows
    half = heads * rows
    near_t = keys_s[...].T
    for segment in range(2):
        count = (1 + segment) * rows
        for pair in range(heads // 2):
            at = (segment * (heads // 2) + pair) * step
            here = slice(at, at + step)
            delta = joined_ref[0:1, here]
            for place in range(1 + segment):
                span = slice(place * rows, (place + 1) * rows)
                weights = raised_ref[span, here] * joined_ref[1 + place : 2 + place, here]
                low_s[span, here] = weights.astype(BF16)
                ds_s[span, here] = (weights * (weights_ref[span, here] - delta)).astype(BF16)
            grad_query = lax.dot_general(
                keys_t[...], ds_ref[:, here], NN, preferred_element_type=F32
            ) + lax.dot_general(
                near_t[:, :count], ds_s[:count, here], NN, preferred_element_type=F32
            )
            grad_query = (grad_query * scale).astype(BF16).T
            for n in range(2):
                c = slice((2 * pair + n) * width, (2 * pair + n + 1) * width)
                grad_query_ref[segment, :, c] = grad_query[n * rows : (n + 1) * rows]
    part_ref[:rows, :] = scale * lax.dot_general(
        ds_s[:rows, :], query_s[...], NN, preferred_element_type=F32
    )
    part_ref[rows:, :] = lax.dot_general(
        low_s[:rows, :], cot_s[...], NN, preferred_element_type=F32
    )
    leaf_keys = scale * lax.dot_general(
        ds_s[rows:, half:], query_s[half:, :], NN, preferred_element_type=F32
    )
    leaf_values = lax.dot_general(
        low_s[rows:, half:], cot_s[half:, :], NN, preferred_element_type=F32
    )
    leaf_ref[:rows, :] = leaf_keys.astype(BF16)
    leaf_ref[rows:, :] = leaf_values.astype(BF16)


def fold_kernel(depth, even_ref, last_ref, *refs):
    arrived, (keep_ref, send_ref) = refs[:-2], refs[-2:]
    index = lax.axis_index("leaf")
    odd = index & 1 == 1
    even = index - (index & 1)
    level = level_of_even(even, depth)
    total = even_ref[...]
    for mask, ref in enumerate(arrived, 1):
        mine = owner_at(even ^ (mask << 1), level, depth) == even
        total = total + jnp.where(mine, ref[...].astype(F32), 0.0)
    keep_ref[...] = jnp.where(odd, last_ref[...], total)
    send_ref[...] = jnp.where(odd, total, last_ref[...]).astype(BF16)


def final_kernel(leaf_ref, keep_ref, other_ref, keys_ref, values_ref):
    rows = keys_ref.shape[1]
    total = (keep_ref[...] + other_ref[...].astype(F32)).astype(BF16)
    keys_ref[0] = total[:rows]
    values_ref[0] = total[rows:]
    keys_ref[1] = leaf_ref[:rows, :]
    values_ref[1] = leaf_ref[rows:, :]


def body(queries, key_states, value_states, grad_output, lengths):
    count = lax.axis_size("leaf")
    depth = depth_of(count)
    masks = range(1, count // 2)
    rows, width = key_states.shape[1:]
    heads = queries.shape[2] // width
    total = 2 * heads * rows
    inner = depth * rows
    terms = (2 * rows, width)

    def move(block, flip):
        return lax.ppermute(block, "leaf", [(i, i ^ flip) for i in range(count)])

    def exchange(blocks):
        moved = {m: move(blocks[m], m << 1) for m in reversed(masks)}
        return [moved[m] for m in masks]

    length = jnp.full((TAIL, width), lengths[0].astype(BF16), BF16)
    own = jnp.concatenate([key_states[0], value_states[0], length], 0)
    mate = move(own, 1)
    pack = jnp.where(lax.axis_index("leaf") & 1 == 1, mate, own)
    near = exchange({m: pack for m in masks})
    query_rows, cot, raised, weights, stats, last_keys = call(
        functools.partial(early_kernel, depth, heads),
        "early",
        8,
        (lengths,),
        (queries, grad_output, key_states, value_states, own, mate),
        [
            ((total, width), BF16),
            ((total, width), BF16),
            ((2 * rows, total), F32),
            ((2 * rows, total), F32),
            ((8, total), F32),
            ((2 * rows, width), BF16),
        ],
        flops=4 * 2 * rows * total * width,
    )
    ds, joined, keys_t, even_part, *sends = call(
        functools.partial(middle_kernel, depth, heads),
        "middle",
        24,
        (),
        (query_rows, cot, stats, pack, *near),
        [
            ((inner, total), BF16),
            ((8, total), F32),
            ((width, inner), BF16),
            (terms, F32),
        ]
        + [(terms, BF16)] * len(near),
        scratch=[
            ((inner, total), F32),
            ((inner, total), F32),
            ((inner, total), BF16),
            ((depth,) + terms, F32),
        ],
        flops=8 * inner * total * width,
    )
    arrived = exchange(dict(zip(masks, sends)))
    grad_queries, leaf, last_part = call(
        functools.partial(late_kernel, heads),
        "late",
        8,
        (),
        (query_rows, cot, raised, weights, joined, ds, keys_t, last_keys),
        [((2, rows, heads * width), BF16), (terms, BF16), (terms, F32)],
        scratch=[((2 * rows, total), BF16), ((2 * rows, total), BF16)],
        flops=8 * 2 * rows * total * width,
    )
    keep, send = call(
        functools.partial(fold_kernel, depth),
        "fold",
        3,
        (),
        (even_part, last_part, *arrived),
        [(terms, F32), (terms, BF16)],
    )
    grad_keys, grad_values = call(
        final_kernel,
        "final",
        2,
        (),
        (leaf, keep, move(send, 1)),
        [(key_states.shape, BF16)] * 2,
    )
    return grad_queries, grad_keys, grad_values


def solution(mesh):
    segments = P(("dp", "leaf"), None, None)
    return jax.shard_map(
        body,
        mesh=mesh,
        in_specs=(segments, segments, segments, segments, P(("dp", "leaf"))),
        out_specs=(segments, segments, segments),
        check_vma=False,
    )
```

time: 84.2 us -> 28 us (0.33)
  blocking collectives: 27.1 us -> 0 us
  local copies, waits for them, and re-layouts: 18.6 us -> 5.25 us
  matrix products: 11.6 us -> 0 us
  other arithmetic: 10.1 us -> 0.86 us
  Pallas kernels: 0 us -> 6.7 us
  waiting for transfers between devices: 10.7 us -> 5.47 us
  starting transfers between devices: 4.53 us -> 8.64 us
    all_gather x2 -> x0, blocking collectives: 17.6 us -> none  [the longest x1 8.95 us: body(): lax.all_gather(key_states[0:1], 'leaf', axis=0, tiled=True)]
    dot_general x12 -> x0, matrix products: 11.6 us -> none  [the longest x2 3.61 us: attend_grad(): jnp.einsum('hqk,kd->qhd', weights_low, value_flat, preferred_element_type...]
    slice x16 -> x0, local copies, waits for them, and re-layouts: 10.5 us -> none  [the longest x2 3.58 us: body(): grad_output[segment]]
    unnamed x1 -> x0, blocking collectives: 9.46 us -> none
    pallas_call x0 -> x5, Pallas kernels: none -> 6.7 us  [call(): pl.pallas_call(kernel, out_shape=[jax.ShapeDtypeStruct(shape, kind) for s...]
    ppermute x6 -> x8, waiting for transfers between devices: 10.7 us -> 5.47 us  [move(): return lax.ppermute(block, 'leaf', [(i, i ^ flip) for i in range(count)])]
    ppermute x6 -> x8, starting transfers between devices: 4.53 us -> 8.64 us  [move(): return lax.ppermute(block, 'leaf', [(i, i ^ flip) for i in range(count)])]
    add x8 -> x0, other arithmetic: 2.05 us -> none  [the longest x3 1.02 us: body(): inner_key_terms[:shared_count] + other_keys]
  transfers between devices with their start and end apart: 6 -> 8, of which waited for: 4 -> 4; matrix products, arithmetic and copies ran while one was open for 10% -> 0% of each run, Pallas kernels for 0% -> 12%
where the time goes in v8:
time: 28 us; the launch traced here: 27.6 us
  starting transfers between devices  8.64 us (31%)
  Pallas kernels  6.7 us (24%)
  waiting for transfers between devices  5.47 us (20%)
  local copies, waits for them, and re-layouts  5.25 us (19%)
  other arithmetic  0.86 us (3%)
  between operations  0.72 us (3%)
    ppermute x8, starting transfers between devices, move(): return lax.ppermute(block, 'leaf', [(i, i ^ flip) for i in range(count)])  8.64 us
    pallas_call x5, Pallas kernels, call(): pl.pallas_call(kernel, out_shape=[jax.ShapeDtypeStruct(shape, kind) for s...  6.7 us
    ppermute x8, waiting for transfers between devices, move(): return lax.ppermute(block, 'leaf', [(i, i ^ flip) for i in range(count)])  5.47 us
    unnamed x10, local copies, waits for them, and re-layouts  4.41 us
    squeeze x1, local copies, waits for them, and re-layouts, body(): own = jnp.concatenate([key_states[0], value_states[0], length], 0)  0.78 us
    another operation x1, other arithmetic  0.66 us
  transfers between devices with their start and end apart: 8, of which 4 were waited for; matrix products, arithmetic and copies ran while one was open for 0% of the time, Pallas kernels for 12%

profile of v8, /device:TPU:0, one launch (start us, length us, event | category | flops | bytes accessed | tf_op | source)
XLA Modules:
  0.0 27.6 jit_solution(10600696655565162693)
XLA Ops:
  0.6 0.7 %convert.3 = bf16[2]{0:T(256)(128)(2,1)S(1)} convert(s32[2]{0:T(128)} %lengths_ref.1) | non-fusion elementwise | flops 2 | bytes 12 | tf_op jit(solution)/shard_map/convert
  1.4 0.8 %slice_bitcast_fusion = (bf16[128,128]{1,0:T(8,128)(2,1)S(1)}, bf16[128,128]{1,0:T(8,128)(2,1)S(1)}) fusion(bf16[2,128,128]{2,1,0:T(8,128)(2,1)} %value_ref.1, bf16[2,128,128]{2,1,0:T(8,128)(2,1)} %key_ref.1), kind=kLoop, calls=%fused_computation.2 | loop fusion | bytes 131072 | tf_op jit(solution)/shard_map/squeeze | solution.py:311
  2.1 0.1 maximum_maximum_fusion.refs_0_
  2.2 0.5 %collective-permute-start = (bf16[272,128]{1,0:T(8,128)(2,1)S(1)}, bf16[272,128]{1,0:T(8,128)(2,1)S(1)}, u32[]{:S(2)}, u32[]{:S(2)}) collective-permute-start(bf16[272,128]{1,0:T(8,128)(2,1)S(1)} %maximum_maximum_fusion.refs_0_), channel_id=1, source_target_pairs={{0,1},{1,0},{2,3},{3,2},{4,5},{5,4},{6,7},{7,6},{8,9},{9,8},{10,11... | collective-permute-start | bytes 208904 | tf_op jit(solution)/shard_map/ppermute | solution.py:304
  2.8 0.9 %collective-permute-done.refs_1_ = bf16[272,128]{1,0:T(8,128)(2,1)S(1)} collective-permute-done((bf16[272,128]{1,0:T(8,128)(2,1)S(1)}, bf16[272,128]{1,0:T(8,128)(2,1)S(1)}, u32[]{:S(2)}, u32[]{:S(2)}) %collective-permute-start) | collective-permute-done | bytes 69664 | tf_op jit(solution)/shard_map/ppermute | solution.py:304
  3.7 0.1 broadcast_select_fusion.pack_ref
  3.8 3.9 %collective-permute-start.3 = (bf16[272,128]{1,0:T(8,128)(2,1)S(1)}, bf16[272,128]{1,0:T(8,128)(2,1)S(1)}, u32[]{:S(2)}, u32[]{:S(2)}) collective-permute-start(bf16[272,128]{1,0:T(8,128)(2,1)S(1)} %broadcast_select_fusion.pack_ref), channel_id=1, source_target_pairs={{0,6},{1,7},{2,4},{3,5},{4,2},{5,3},{6,0},{7,1},{8,14},{9,15},{10,... | collective-permute-start | bytes 208904 | tf_op jit(solution)/shard_map/ppermute | solution.py:304
  7.6 0.5 %collective-permute-start.2 = (bf16[272,128]{1,0:T(8,128)(2,1)S(1)}, bf16[272,128]{1,0:T(8,128)(2,1)S(1)}, u32[]{:S(2)}, u32[]{:S(2)}) collective-permute-start(bf16[272,128]{1,0:T(8,128)(2,1)S(1)} %broadcast_select_fusion.pack_ref), channel_id=1, source_target_pairs={{0,4},{1,5},{2,6},{3,7},{4,0},{5,1},{6,2},{7,3},{8,12},{9,13},{10,... | collective-permute-start | bytes 208904 | tf_op jit(solution)/shard_map/ppermute | solution.py:304
  8.1 0.1 collective-permute-start.1
  8.3 0.0 copy-start
  8.3 1.0 %copy-done = bf16[2,128,1024]{2,1,0:T(8,128)(2,1)S(1)} copy-done((bf16[2,128,1024]{2,1,0:T(8,128)(2,1)S(1)}, bf16[2,128,1024]{2,1,0:T(8,128)(2,1)}, u32[]{:S(2)}) %copy-start) | copy-done | bytes 524312
  9.3 0.0 copy-start.1
  9.3 1.0 %copy-done.1 = bf16[2,128,1024]{2,1,0:T(8,128)(2,1)S(1)} copy-done((bf16[2,128,1024]{2,1,0:T(8,128)(2,1)S(1)}, bf16[2,128,1024]{2,1,0:T(8,128)(2,1)}, u32[]{:S(2)}) %copy-start.1) | copy-done | bytes 524312
  10.4 0.8 %copy-done.2 = bf16[2,128,128]{2,1,0:T(8,128)(2,1)S(1)} copy-done((bf16[2,128,128]{2,1,0:T(8,128)(2,1)S(1)}, bf16[2,128,128]{2,1,0:T(8,128)(2,1)}, u32[]{:S(2)}) %copy-start.2) | copy-done | bytes 65560
  11.2 0.8 %copy-done.3 = bf16[2,128,128]{2,1,0:T(8,128)(2,1)S(1)} copy-done((bf16[2,128,128]{2,1,0:T(8,128)(2,1)S(1)}, bf16[2,128,128]{2,1,0:T(8,128)(2,1)}, u32[]{:S(2)}) %copy-start.3) | copy-done | bytes 65560
  12.0 0.7 %copy-done.4 = s32[2]{0:T(128)S(1)} copy-done((s32[2]{0:T(128)S(1)}, s32[2]{0:T(128)}, u32[]{:S(2)}) %copy-start.4) | copy-done | bytes 32
  12.7 1.6 %early.1 = (bf16[2048,128]{1,0:T(8,128)(2,1)S(1)}, bf16[2048,128]{1,0:T(8,128)(2,1)S(1)}, f32[256,2048]{1,0:T(8,128)S(1)}, f32[256,2048]{1,0:T(8,128)S(1)}, f32[...) custom-call(s32[2]{0:T(128)S(1)} %copy-done.4, bf16[2,128,1024]{2,1,0:T(8,128)(2,1)S(1)} %copy-done, ...), custom_call_target="tpu_custom_call" | custom-call | flops 268435456 | bytes 1048576 | tf_op jit(solution)/shard_map/early/pallas_call | solution.py:51
  14.3 0.0 collective-permute-done.3.refs_2_
  14.3 0.0 collective-permute-done.2.refs_1_
  14.3 0.0 collective-permute-done.1.refs_0_
  14.3 2.6 %middle.1 = (bf16[384,2048]{1,0:T(8,128)(2,1)S(1)}, f32[8,2048]{1,0:T(8,128)S(1)}, bf16[128,384]{1,0:T(8,128)(2,1)S(1)}, f32[256,128]{1,0:T(8,128)S(1)}, bf16[25...) custom-call(bf16[2048,128]{1,0:T(8,128)(2,1)S(1)} %get-tuple-element.23.query_s, ...), custom_call_target="tpu_custom_call" | custom-call | flops 805306368 | bytes 1048576 | tf_op jit(solution)/shard_map/middle/pallas_call | solution.py:51
  16.9 2.0 %collective-permute-start.4 = (bf16[256,128]{1,0:T(8,128)(2,1)S(1)}, bf16[256,128]{1,0:T(8,128)(2,1)S(1)}, u32[]{:S(2)}, u32[]{:S(2)}) collective-permute-start(bf16[256,128]{1,0:T(8,128)(2,1)S(1)} %get-tuple-element.36), channel_id=1, source_target_pairs={{0,2},{1,3},{2,0},{3,1},{4,6},{5,7},{6,4},{7,5},{8,10},{9,11},{10,... | collective-permute-start | bytes 196616 | tf_op jit(solution)/shard_map/ppermute | solution.py:304
  18.9 1.5 %collective-permute-start.5 = (bf16[256,128]{1,0:T(8,128)(2,1)S(1)}, bf16[256,128]{1,0:T(8,128)(2,1)S(1)}, u32[]{:S(2)}, u32[]{:S(2)}) collective-permute-start(bf16[256,128]{1,0:T(8,128)(2,1)S(1)} %get-tuple-element.37), channel_id=1, source_target_pairs={{0,4},{1,5},{2,6},{3,7},{4,0},{5,1},{6,2},{7,3},{8,12},{9,13},{10,... | collective-permute-start | bytes 196616 | tf_op jit(solution)/shard_map/ppermute | solution.py:304
  20.4 0.1 collective-permute-start.6
  20.5 1.8 %late.1 = (bf16[2,128,1024]{2,1,0:T(8,128)(2,1)}, bf16[256,128]{1,0:T(8,128)(2,1)S(1)}, f32[256,128]{1,0:T(8,128)S(1)}) custom-call(bf16[2048,128]{1,0:T(8,128)(2,1)S(1)} %get-tuple-element.23.query_s, bf16[2048,128]{1,0:T(8,128)(2,1)S(1)} %get-tuple-element.24.cot_s, f32[256,2048]{1,0:T(8,128)S(1)} %get-tuple-element.25.raised_ref, ...), custom_call_target="tpu_custom_call" | custom-call | flops 536870912 | bytes 1048576 | tf_op jit(solution)/shard_map/late/pallas_call | solution.py:51
  22.3 0.0 collective-permute-done.4.refs_0_
  22.3 1.6 %collective-permute-done.5.refs_1_ = bf16[256,128]{1,0:T(8,128)(2,1)S(1)} collective-permute-done((bf16[256,128]{1,0:T(8,128)(2,1)S(1)}, bf16[256,128]{1,0:T(8,128)(2,1)S(1)}, u32[]{:S(2)}, u32[]{:S(2)}) %collective-permute-start.5) | collective-permute-done | bytes 65568 | tf_op jit(solution)/shard_map/ppermute | solution.py:304
  23.9 1.7 %collective-permute-done.6.refs_2_ = bf16[256,128]{1,0:T(8,128)(2,1)S(1)} collective-permute-done((bf16[256,128]{1,0:T(8,128)(2,1)S(1)}, bf16[256,128]{1,0:T(8,128)(2,1)S(1)}, u32[]{:S(2)}, u32[]{:S(2)}) %collective-permute-start.6) | collective-permute-done | bytes 65568 | tf_op jit(solution)/shard_map/ppermute | solution.py:304
  25.6 0.1 fold.1
  25.7 0.1 collective-permute-start.7
  25.7 1.2 %collective-permute-done.7.other_ref = bf16[256,128]{1,0:T(8,128)(2,1)S(1)} collective-permute-done((bf16[256,128]{1,0:T(8,128)(2,1)S(1)}, bf16[256,128]{1,0:T(8,128)(2,1)S(1)}, u32[]{:S(2)}, u32[]{:S(2)}) %collective-permute-start.7) | collective-permute-done | bytes 65568 | tf_op jit(solution)/shard_map/ppermute | solution.py:304
  27.0 0.7 %final.1 = (bf16[2,128,128]{2,1,0:T(8,128)(2,1)}, bf16[2,128,128]{2,1,0:T(8,128)(2,1)}) custom-call(bf16[256,128]{1,0:T(8,128)(2,1)S(1)} %get-tuple-element.33.leaf_ref, f32[256,128]{1,0:T(8,128)S(1)} %get-tuple-element.39.keep_ref, bf16[256,128]{1,0:T(8,128)(2,1)S(1)} %collective-permute-done.7.other_ref), custom_call_target="tpu_custom_call" | custom-call | bytes 1048576 | tf_op jit(solution)/shard_map/final/pallas_call | solution.py:51
  (5 shorter events, 0.1 us)
Async XLA Ops:
  2.2 1.4 %collective-permute-start = (bf16[272,128]{1,0:T(8,128)(2,1)S(1)}, bf16[272,128]{1,0:T(8,128)(2,1)S(1)}, u32[]{:S(2)}, u32[]{:S(2)}) collective-permute-start(bf16[272,128]{1,0:T(8,128)(2,1)S(1)} %maximum_maximum_fusion.refs_0_), channel_id=1, source_target_pairs={{0,1},{1,0},{2,3},{3,2},{4,5},{5,4},{6,7},{7,6},{8,9},{9,8},{10,11... | collective-permute-start | bytes 208904 | tf_op jit(solution)/shard_map/ppermute | solution.py:304
  3.8 10.5 %collective-permute-start.3 = (bf16[272,128]{1,0:T(8,128)(2,1)S(1)}, bf16[272,128]{1,0:T(8,128)(2,1)S(1)}, u32[]{:S(2)}, u32[]{:S(2)}) collective-permute-start(bf16[272,128]{1,0:T(8,128)(2,1)S(1)} %broadcast_select_fusion.pack_ref), channel_id=1, source_target_pairs={{0,6},{1,7},{2,4},{3,5},{4,2},{5,3},{6,0},{7,1},{8,14},{9,15},{10,... | collective-permute-start | bytes 208904 | tf_op jit(solution)/shard_map/ppermute | solution.py:304
  7.6 6.6 %collective-permute-start.2 = (bf16[272,128]{1,0:T(8,128)(2,1)S(1)}, bf16[272,128]{1,0:T(8,128)(2,1)S(1)}, u32[]{:S(2)}, u32[]{:S(2)}) collective-permute-start(bf16[272,128]{1,0:T(8,128)(2,1)S(1)} %broadcast_select_fusion.pack_ref), channel_id=1, source_target_pairs={{0,4},{1,5},{2,6},{3,7},{4,0},{5,1},{6,2},{7,3},{8,12},{9,13},{10,... | collective-permute-start | bytes 208904 | tf_op jit(solution)/shard_map/ppermute | solution.py:304
  8.1 6.1 %collective-permute-start.1 = (bf16[272,128]{1,0:T(8,128)(2,1)S(1)}, bf16[272,128]{1,0:T(8,128)(2,1)S(1)}, u32[]{:S(2)}, u32[]{:S(2)}) collective-permute-start(bf16[272,128]{1,0:T(8,128)(2,1)S(1)} %broadcast_select_fusion.pack_ref), channel_id=1, source_target_pairs={{0,2},{1,3},{2,0},{3,1},{4,6},{5,7},{6,4},{7,5},{8,10},{9,11},{10,... | collective-permute-start | bytes 208904 | tf_op jit(solution)/shard_map/ppermute | solution.py:304
  8.3 1.0 %copy-start = (bf16[2,128,1024]{2,1,0:T(8,128)(2,1)S(1)}, bf16[2,128,1024]{2,1,0:T(8,128)(2,1)}, u32[]{:S(2)}) copy-start(bf16[2,128,1024]{2,1,0:T(8,128)(2,1)} %query_ref.1) | copy-start | bytes 1572868
  9.3 1.0 %copy-start.1 = (bf16[2,128,1024]{2,1,0:T(8,128)(2,1)S(1)}, bf16[2,128,1024]{2,1,0:T(8,128)(2,1)}, u32[]{:S(2)}) copy-start(bf16[2,128,1024]{2,1,0:T(8,128)(2,1)} %grad_ref.1) | copy-start | bytes 1572868
  10.4 0.8 %copy-start.2 = (bf16[2,128,128]{2,1,0:T(8,128)(2,1)S(1)}, bf16[2,128,128]{2,1,0:T(8,128)(2,1)}, u32[]{:S(2)}) copy-start(bf16[2,128,128]{2,1,0:T(8,128)(2,1)} %key_ref.1) | copy-start | bytes 196612
  11.2 0.8 %copy-start.3 = (bf16[2,128,128]{2,1,0:T(8,128)(2,1)S(1)}, bf16[2,128,128]{2,1,0:T(8,128)(2,1)}, u32[]{:S(2)}) copy-start(bf16[2,128,128]{2,1,0:T(8,128)(2,1)} %value_ref.1) | copy-start | bytes 196612
  12.0 0.7 %copy-start.4 = (s32[2]{0:T(128)S(1)}, s32[2]{0:T(128)}, u32[]{:S(2)}) copy-start(s32[2]{0:T(128)} %lengths_ref.1) | copy-start | bytes 28
  16.9 5.3 %collective-permute-start.4 = (bf16[256,128]{1,0:T(8,128)(2,1)S(1)}, bf16[256,128]{1,0:T(8,128)(2,1)S(1)}, u32[]{:S(2)}, u32[]{:S(2)}) collective-permute-start(bf16[256,128]{1,0:T(8,128)(2,1)S(1)} %get-tuple-element.36), channel_id=1, source_target_pairs={{0,2},{1,3},{2,0},{3,1},{4,6},{5,7},{6,4},{7,5},{8,10},{9,11},{10,... | collective-permute-start | bytes 196616 | tf_op jit(solution)/shard_map/ppermute | solution.py:304
  18.9 5.0 %collective-permute-start.5 = (bf16[256,128]{1,0:T(8,128)(2,1)S(1)}, bf16[256,128]{1,0:T(8,128)(2,1)S(1)}, u32[]{:S(2)}, u32[]{:S(2)}) collective-permute-start(bf16[256,128]{1,0:T(8,128)(2,1)S(1)} %get-tuple-element.37), channel_id=1, source_target_pairs={{0,4},{1,5},{2,6},{3,7},{4,0},{5,1},{6,2},{7,3},{8,12},{9,13},{10,... | collective-permute-start | bytes 196616 | tf_op jit(solution)/shard_map/ppermute | solution.py:304
  20.4 5.2 %collective-permute-start.6 = (bf16[256,128]{1,0:T(8,128)(2,1)S(1)}, bf16[256,128]{1,0:T(8,128)(2,1)S(1)}, u32[]{:S(2)}, u32[]{:S(2)}) collective-permute-start(bf16[256,128]{1,0:T(8,128)(2,1)S(1)} %get-tuple-element.38), channel_id=1, source_target_pairs={{0,6},{1,7},{2,4},{3,5},{4,2},{5,3},{6,0},{7,1},{8,14},{9,15},{10,... | collective-permute-start | bytes 196616 | tf_op jit(solution)/shard_map/ppermute | solution.py:304
  25.7 1.3 %collective-permute-start.7 = (bf16[256,128]{1,0:T(8,128)(2,1)S(1)}, bf16[256,128]{1,0:T(8,128)(2,1)S(1)}, u32[]{:S(2)}, u32[]{:S(2)}) collective-permute-start(bf16[256,128]{1,0:T(8,128)(2,1)S(1)} %get-tuple-element.40), channel_id=1, source_target_pairs={{0,1},{1,0},{2,3},{3,2},{4,5},{5,4},{6,7},{7,6},{8,9},{9,8},{10,11... | collective-permute-start | bytes 196616 | tf_op jit(solution)/shard_map/ppermute | solution.py:304

commit v9 on v8

--- a/solution.py
+++ b/solution.py
@@ -45,19 +45,18 @@
     return owner
 
 
-def call(kernel, name, mib, scalars, arrays, outs, scratch=(), flops=0):
-    smem = pl.BlockSpec(memory_space=pltpu.SMEM)
+def call(kernel, name, mib, arrays, outs, scratch=(), flops=0):
     vmem = pl.BlockSpec(memory_space=pltpu.VMEM)
     return pl.pallas_call(
         kernel,
         out_shape=[jax.ShapeDtypeStruct(shape, kind) for shape, kind in outs],
-        in_specs=[smem] * len(scalars) + [vmem] * len(arrays),
+        in_specs=[vmem] * len(arrays),
         out_specs=[vmem] * len(outs),
         scratch_shapes=[pltpu.VMEM(shape, kind) for shape, kind in scratch],
         compiler_params=pltpu.CompilerParams(vmem_limit_bytes=mib * 1024 * 1024),
         cost_estimate=pl.CostEstimate(flops=flops, bytes_accessed=1 << 20, transcendentals=0),
         name=name,
-    )(*scalars, *arrays)
+    )(*arrays)
 
 
 def ruled_columns(rows, width):
@@ -86,34 +85,34 @@
     return raised, grad_weights, top, total, partial
 
 
-def early_kernel(depth, heads, lengths_ref, query_ref, grad_ref, key_ref, value_ref, *refs):
-    own_ref, mate_ref, query_s, cot_s, raised_s, weights_s, stats_s, keys_s = refs
-    rows, width = key_ref.shape[1:]
+def early_kernel(depth, heads, query_ref, grad_ref, held_ref, tails_ref, *refs):
+    other_key_ref, other_value_ref, other_tails_ref = refs[:3]
+    query_s, cot_s, raised_s, weights_s, stats_s, keys_s = refs[3:]
+    rows, width = held_ref.shape[1:]
     index = lax.axis_index("leaf")
     odd = index & 1 == 1
     factor = width ** (-0.5) * LOG2E
     step = 2 * rows
     row = lax.broadcasted_iota(jnp.int32, (rows, width), 0)
-    block = jnp.where(odd, own_ref[...], mate_ref[...])
-    length = block[2 * rows : 2 * rows + 1].astype(F32)
-    keys = [block[:rows], key_ref[1]]
-    values = [block[rows : 2 * rows], value_ref[1]]
+    lengths = [tails_ref[segment, 0:1, :].astype(F32) for segment in range(2)]
+    length = jnp.where(odd, lengths[0], other_tails_ref[0, 0:1, :].astype(F32))
+    keys = [jnp.where(odd, held_ref[0], other_key_ref[0]), held_ref[1]]
+    values = [jnp.where(odd, held_ref[2], other_value_ref[0]), held_ref[3]]
     keys_s[:rows, :] = keys[0]
     keys_s[rows:, :] = keys[1]
     yes, no = jnp.full((), True), jnp.full((), False)
     ruled = ruled_columns(rows, width)
-    leaf_length = jnp.full((1, width), lengths_ref[1].astype(F32), F32)
     wide = [
         [
             jnp.concatenate([keys[0], mask_columns(length, no, odd, rows, width)], 1),
         ],
         [
             jnp.concatenate([keys[0], mask_columns(length, yes, no, rows, width)], 1),
-            jnp.concatenate([keys[1], mask_columns(leaf_length, no, yes, rows, width)], 1),
+            jnp.concatenate([keys[1], mask_columns(lengths[1], no, yes, rows, width)], 1),
         ],
     ]
     for segment in range(2):
-        live = row < lengths_ref[segment]
+        live = row.astype(F32) < lengths[segment]
         for pair in range(heads // 2):
             at = (segment * (heads // 2) + pair) * step
             here = slice(at, at + step)
@@ -307,17 +306,28 @@
         moved = {m: move(blocks[m], m << 1) for m in reversed(masks)}
         return [moved[m] for m in masks]
 
-    length = jnp.full((TAIL, width), lengths[0].astype(BF16), BF16)
-    own = jnp.concatenate([key_states[0], value_states[0], length], 0)
-    mate = move(own, 1)
-    pack = jnp.where(lax.axis_index("leaf") & 1 == 1, mate, own)
+    other_keys, other_values = move(key_states, 1), move(value_states, 1)
+    tails = jnp.broadcast_to(lengths.astype(BF16)[:, None, None], (2, TAIL, width))
+    other_tails = move(tails, 1)
+    held = jnp.concatenate([key_states, value_states], 0)
+    held, other_keys, other_values, other_tails = lax.optimization_barrier(
+        (held, other_keys, other_values, other_tails)
+    )
+    odd = lax.axis_index("leaf") & 1 == 1
+    pack = jnp.concatenate(
+        [
+            jnp.where(odd, other_keys[0], held[0]),
+            jnp.where(odd, other_values[0], held[2]),
+            jnp.where(odd, other_tails[0], tails[0]),
+        ],
+        0,
+    )
     near = exchange({m: pack for m in masks})
     query_rows, cot, raised, weights, stats, last_keys = call(
         functools.partial(early_kernel, depth, heads),
         "early",
         8,
-        (lengths,),
-        (queries, grad_output, key_states, value_states, own, mate),
+        (queries, grad_output, held, tails, other_keys, other_values, other_tails),
         [
             ((total, width), BF16),
             ((total, width), BF16),
@@ -332,7 +342,6 @@
         functools.partial(middle_kernel, depth, heads),
         "middle",
         24,
-        (),
         (query_rows, cot, stats, pack, *near),
         [
             ((inner, total), BF16),
@@ -354,7 +363,6 @@
         functools.partial(late_kernel, heads),
         "late",
         8,
-        (),
         (query_rows, cot, raised, weights, joined, ds, keys_t, last_keys),
         [((2, rows, heads * width), BF16), (terms, BF16), (terms, F32)],
         scratch=[((2 * rows, total), BF16), ((2 * rows, total), BF16)],
@@ -364,7 +372,6 @@
         functools.partial(fold_kernel, depth),
         "fold",
         3,
-        (),
         (even_part, last_part, *arrived),
         [(terms, F32), (terms, BF16)],
     )
@@ -372,7 +379,6 @@
         final_kernel,
         "final",
         2,
-        (),
         (leaf, keep, move(send, 1)),
         [(key_states.shape, BF16)] * 2,
     )

time: 28 us -> 24.7 us (0.88)
  local copies, waits for them, and re-layouts: 5.25 us -> 2.16 us
  other arithmetic: 0.86 us -> 1.61 us
  waiting for transfers between devices: 5.47 us -> 4.78 us
  Pallas kernels: 6.7 us -> 6.13 us
  starting transfers between devices: 8.64 us -> 9.09 us
    unnamed x10 -> x4, local copies, waits for them, and re-layouts: 4.41 us -> 2.08 us
    concatenate x1 -> x2, other arithmetic: 0.1 us -> 0.89 us  [the longest x1 0.88 us: body(): held = jnp.concatenate([key_states, value_states], 0)]
    squeeze x1 -> x0, local copies, waits for them, and re-layouts: 0.78 us -> none  [body(): own = jnp.concatenate([key_states[0], value_states[0], length], 0)]
    ppermute x8 -> x10, waiting for transfers between devices: 5.47 us -> 4.78 us  [move(): return lax.ppermute(block, 'leaf', [(i, i ^ flip) for i in range(count)])]
    another operation x1 -> x0, other arithmetic: 0.66 us -> none
    convert_element_type x0 -> x1, other arithmetic: none -> 0.66 us  [body(): lengths.astype(BF16)[:, None, None]]
    pallas_call x5, Pallas kernels: 6.7 us -> 6.13 us  [call(): pl.pallas_call(kernel, out_shape=[jax.ShapeDtypeStruct(shape, kind) for s...]
    ppermute x8 -> x10, starting transfers between devices: 8.64 us -> 9.09 us  [move(): return lax.ppermute(block, 'leaf', [(i, i ^ flip) for i in range(count)])]
  transfers between devices with their start and end apart: 8 -> 10, of which waited for: 4 -> 7; matrix products, arithmetic and copies ran while one was open for 0% -> 4% of each run, Pallas kernels for 12% -> 11%
where the time goes in v9:
time: 24.7 us; the launch traced here: 24.5 us
  starting transfers between devices  9.09 us (37%)
  Pallas kernels  6.13 us (25%)
  waiting for transfers between devices  4.78 us (19%)
  local copies, waits for them, and re-layouts  2.16 us (9%)
  other arithmetic  1.61 us (7%)
  between operations  0.71 us (3%)
    ppermute x10, starting transfers between devices, move(): return lax.ppermute(block, 'leaf', [(i, i ^ flip) for i in range(count)])  9.09 us
    pallas_call x5, Pallas kernels, call(): pl.pallas_call(kernel, out_shape=[jax.ShapeDtypeStruct(shape, kind) for s...  6.13 us
    ppermute x10, waiting for transfers between devices, move(): return lax.ppermute(block, 'leaf', [(i, i ^ flip) for i in range(count)])  4.78 us
    unnamed x4, local copies, waits for them, and re-layouts  2.08 us
    concatenate x1, other arithmetic, body(): held = jnp.concatenate([key_states, value_states], 0)  0.88 us
    convert_element_type x1, other arithmetic, body(): lengths.astype(BF16)[:, None, None]  0.66 us
  transfers between devices with their start and end apart: 10, of which 7 were waited for; matrix products, arithmetic and copies ran while one was open for 4% of the time, Pallas kernels for 11%

profile of v9, /device:TPU:0, one launch (start us, length us, event | category | flops | bytes accessed | tf_op | source)
XLA Modules:
  0.0 24.5 jit_solution(4358948457321716841)
XLA Ops:
  0.6 0.7 %convert_element_type.3 = bf16[2]{0:T(256)(128)(2,1)S(1)} convert(s32[2]{0:T(128)} %param.9) | non-fusion elementwise | flops 2 | bytes 12 | tf_op jit(solution)/shard_map/convert_element_type | solution.py:310
  1.3 0.1 broadcast_in_dim.10.tails_ref
  1.4 0.5 %collective-permute-start.2 = (bf16[2,16,128]{2,1,0:T(8,128)(2,1)S(1)}, bf16[2,16,128]{2,1,0:T(8,128)(2,1)S(1)}, u32[]{:S(2)}, u32[]{:S(2)}) collective-permute-start(bf16[2,16,128]{2,1,0:T(8,128)(2,1)S(1)} %broadcast_in_dim.10.tails_ref), channel_id=1, source_target_pairs={{0,1},{1,0},{2,3},{3,2},{4,5},{5,4},{6,7},{7,6},{8,9},{9,8},{10,11... | collective-permute-start | bytes 24584 | tf_op jit(solution)/shard_map/ppermute | solution.py:303
  1.8 0.1 collective-permute-start
  1.9 0.4 %collective-permute-start.1 = (bf16[2,128,128]{2,1,0:T(8,128)(2,1)}, bf16[2,128,128]{2,1,0:T(8,128)(2,1)S(1)}, u32[]{:S(2)}, u32[]{:S(2)}) collective-permute-start(bf16[2,128,128]{2,1,0:T(8,128)(2,1)} %param.7), channel_id=1, source_target_pairs={{0,1},{1,0},{2,3},{3,2},{4,5},{5,4},{6,7},{7,6},{8,9},{9,8},{10,11... | collective-permute-start | bytes 196616 | tf_op jit(solution)/shard_map/ppermute | solution.py:303
  2.3 0.9 %pad_maximum_fusion.held_ref = bf16[4,128,128]{2,1,0:T(8,128)(2,1)S(1)} fusion(bf16[2,128,128]{2,1,0:T(8,128)(2,1)} %param.7, bf16[2,128,128]{2,1,0:T(8,128)(2,1)} %param.6), kind=kLoop, calls=%fused_computation | loop fusion | flops 65536 | bytes 262144 | tf_op jit(solution)/shard_map/concatenate | solution.py:312
  3.2 0.0 collective-permute-done.2.refs_2_
  3.2 0.1 collective-permute-done.refs_0_
  3.3 0.2 collective-permute-done.1.refs_1_
  3.5 3.9 %collective-permute-start.5 = (bf16[272,128]{1,0:T(8,128)(2,1)S(1)}, bf16[272,128]{1,0:T(8,128)(2,1)S(1)}, u32[]{:S(2)}, u32[]{:S(2)}) collective-permute-start(bf16[272,128]{1,0:T(8,128)(2,1)S(1)} %pad_maximum_fusion.1.pack_ref), channel_id=1, source_target_pairs={{0,6},{1,7},{2,4},{3,5},{4,2},{5,3},{6,0},{7,1},{8,14},{9,15},{10,... | collective-permute-start | bytes 208904 | tf_op jit(solution)/shard_map/ppermute | solution.py:303
  7.4 0.5 %collective-permute-start.4 = (bf16[272,128]{1,0:T(8,128)(2,1)S(1)}, bf16[272,128]{1,0:T(8,128)(2,1)S(1)}, u32[]{:S(2)}, u32[]{:S(2)}) collective-permute-start(bf16[272,128]{1,0:T(8,128)(2,1)S(1)} %pad_maximum_fusion.1.pack_ref), channel_id=1, source_target_pairs={{0,4},{1,5},{2,6},{3,7},{4,0},{5,1},{6,2},{7,3},{8,12},{9,13},{10,... | collective-permute-start | bytes 208904 | tf_op jit(solution)/shard_map/ppermute | solution.py:303
  7.9 0.1 collective-permute-start.3
  8.0 0.0 copy-start
  8.0 1.0 %copy-done = bf16[2,128,1024]{2,1,0:T(8,128)(2,1)S(1)} copy-done((bf16[2,128,1024]{2,1,0:T(8,128)(2,1)S(1)}, bf16[2,128,1024]{2,1,0:T(8,128)(2,1)}, u32[]{:S(2)}) %copy-start) | copy-done | bytes 524312
  9.1 0.0 copy-start.1
  9.1 1.0 %copy-done.1 = bf16[2,128,1024]{2,1,0:T(8,128)(2,1)S(1)} copy-done((bf16[2,128,1024]{2,1,0:T(8,128)(2,1)S(1)}, bf16[2,128,1024]{2,1,0:T(8,128)(2,1)}, u32[]{:S(2)}) %copy-start.1) | copy-done | bytes 524312
  10.1 1.0 %early.1 = (bf16[2048,128]{1,0:T(8,128)(2,1)S(1)}, bf16[2048,128]{1,0:T(8,128)(2,1)S(1)}, f32[256,2048]{1,0:T(8,128)S(1)}, f32[256,2048]{1,0:T(8,128)S(1)}, f32[...) custom-call(bf16[2,128,1024]{2,1,0:T(8,128)(2,1)S(1)} %copy-done, bf16[2,128,1024]{2,1,0:T(8,128)(2,1)S(1)} %copy-done.1, ...), custom_call_target="tpu_custom_call" | custom-call | flops 268435456 | bytes 1048576 | tf_op jit(solution)/shard_map/early/pallas_call | solution.py:50
  11.1 0.0 collective-permute-done.5.refs_2_
  11.1 0.6 %collective-permute-done.4.refs_1_ = bf16[272,128]{1,0:T(8,128)(2,1)S(1)} collective-permute-done((bf16[272,128]{1,0:T(8,128)(2,1)S(1)}, bf16[272,128]{1,0:T(8,128)(2,1)S(1)}, u32[]{:S(2)}, u32[]{:S(2)}) %collective-permute-start.4) | collective-permute-done | bytes 69664 | tf_op jit(solution)/shard_map/ppermute | solution.py:303
  11.7 0.5 %collective-permute-done.3.refs_0_ = bf16[272,128]{1,0:T(8,128)(2,1)S(1)} collective-permute-done((bf16[272,128]{1,0:T(8,128)(2,1)S(1)}, bf16[272,128]{1,0:T(8,128)(2,1)S(1)}, u32[]{:S(2)}, u32[]{:S(2)}) %collective-permute-start.3) | collective-permute-done | bytes 69664 | tf_op jit(solution)/shard_map/ppermute | solution.py:303
  12.2 2.6 %middle.1 = (bf16[384,2048]{1,0:T(8,128)(2,1)S(1)}, f32[8,2048]{1,0:T(8,128)S(1)}, bf16[128,384]{1,0:T(8,128)(2,1)S(1)}, f32[256,128]{1,0:T(8,128)S(1)}, bf16[25...) custom-call(bf16[2048,128]{1,0:T(8,128)(2,1)S(1)} %get-tuple-element.31.query_s, ...), custom_call_target="tpu_custom_call" | custom-call | flops 805306368 | bytes 1048576 | tf_op jit(solution)/shard_map/middle/pallas_call | solution.py:50
  14.8 1.0 %collective-permute-start.6 = (bf16[256,128]{1,0:T(8,128)(2,1)S(1)}, bf16[256,128]{1,0:T(8,128)(2,1)S(1)}, u32[]{:S(2)}, u32[]{:S(2)}) collective-permute-start(bf16[256,128]{1,0:T(8,128)(2,1)S(1)} %get-tuple-element.44), channel_id=1, source_target_pairs={{0,2},{1,3},{2,0},{3,1},{4,6},{5,7},{6,4},{7,5},{8,10},{9,11},{10,... | collective-permute-start | bytes 196616 | tf_op jit(solution)/shard_map/ppermute | solution.py:303
  15.8 1.4 %collective-permute-start.7 = (bf16[256,128]{1,0:T(8,128)(2,1)S(1)}, bf16[256,128]{1,0:T(8,128)(2,1)S(1)}, u32[]{:S(2)}, u32[]{:S(2)}) collective-permute-start(bf16[256,128]{1,0:T(8,128)(2,1)S(1)} %get-tuple-element.45), channel_id=1, source_target_pairs={{0,4},{1,5},{2,6},{3,7},{4,0},{5,1},{6,2},{7,3},{8,12},{9,13},{10,... | collective-permute-start | bytes 196616 | tf_op jit(solution)/shard_map/ppermute | solution.py:303
  17.2 1.1 %collective-permute-start.8 = (bf16[256,128]{1,0:T(8,128)(2,1)S(1)}, bf16[256,128]{1,0:T(8,128)(2,1)S(1)}, u32[]{:S(2)}, u32[]{:S(2)}) collective-permute-start(bf16[256,128]{1,0:T(8,128)(2,1)S(1)} %get-tuple-element.46), channel_id=1, source_target_pairs={{0,6},{1,7},{2,4},{3,5},{4,2},{5,3},{6,0},{7,1},{8,14},{9,15},{10,... | collective-permute-start | bytes 196616 | tf_op jit(solution)/shard_map/ppermute | solution.py:303
  18.4 1.8 %late.1 = (bf16[2,128,1024]{2,1,0:T(8,128)(2,1)}, bf16[256,128]{1,0:T(8,128)(2,1)S(1)}, f32[256,128]{1,0:T(8,128)S(1)}) custom-call(bf16[2048,128]{1,0:T(8,128)(2,1)S(1)} %get-tuple-element.31.query_s, bf16[2048,128]{1,0:T(8,128)(2,1)S(1)} %get-tuple-element.32.cot_s, f32[256,2048]{1,0:T(8,128)S(1)} %get-tuple-element.33.raised_ref, ...), custom_call_target="tpu_custom_call" | custom-call | flops 536870912 | bytes 1048576 | tf_op jit(solution)/shard_map/late/pallas_call | solution.py:50
  20.2 0.0 collective-permute-done.6.refs_0_
  20.2 0.5 %collective-permute-done.7.refs_1_ = bf16[256,128]{1,0:T(8,128)(2,1)S(1)} collective-permute-done((bf16[256,128]{1,0:T(8,128)(2,1)S(1)}, bf16[256,128]{1,0:T(8,128)(2,1)S(1)}, u32[]{:S(2)}, u32[]{:S(2)}) %collective-permute-start.7) | collective-permute-done | bytes 65568 | tf_op jit(solution)/shard_map/ppermute | solution.py:303
  20.7 1.7 %collective-permute-done.8.refs_2_ = bf16[256,128]{1,0:T(8,128)(2,1)S(1)} collective-permute-done((bf16[256,128]{1,0:T(8,128)(2,1)S(1)}, bf16[256,128]{1,0:T(8,128)(2,1)S(1)}, u32[]{:S(2)}, u32[]{:S(2)}) %collective-permute-start.8) | collective-permute-done | bytes 65568 | tf_op jit(solution)/shard_map/ppermute | solution.py:303
  22.4 0.1 fold.1
  22.5 0.1 collective-permute-start.9
  22.6 1.2 %collective-permute-done.9.other_ref = bf16[256,128]{1,0:T(8,128)(2,1)S(1)} collective-permute-done((bf16[256,128]{1,0:T(8,128)(2,1)S(1)}, bf16[256,128]{1,0:T(8,128)(2,1)S(1)}, u32[]{:S(2)}, u32[]{:S(2)}) %collective-permute-start.9) | collective-permute-done | bytes 65568 | tf_op jit(solution)/shard_map/ppermute | solution.py:303
  23.8 0.7 %final.1 = (bf16[2,128,128]{2,1,0:T(8,128)(2,1)}, bf16[2,128,128]{2,1,0:T(8,128)(2,1)}) custom-call(bf16[256,128]{1,0:T(8,128)(2,1)S(1)} %get-tuple-element.41.leaf_ref, f32[256,128]{1,0:T(8,128)S(1)} %get-tuple-element.47.keep_ref, bf16[256,128]{1,0:T(8,128)(2,1)S(1)} %collective-permute-done.9.other_ref), custom_call_target="tpu_custom_call" | custom-call | bytes 1048576 | tf_op jit(solution)/shard_map/final/pallas_call | solution.py:50
  (3 shorter events, 0.1 us)
Async XLA Ops:
  1.4 1.9 %collective-permute-start.2 = (bf16[2,16,128]{2,1,0:T(8,128)(2,1)S(1)}, bf16[2,16,128]{2,1,0:T(8,128)(2,1)S(1)}, u32[]{:S(2)}, u32[]{:S(2)}) collective-permute-start(bf16[2,16,128]{2,1,0:T(8,128)(2,1)S(1)} %broadcast_in_dim.10.tails_ref), channel_id=1, source_target_pairs={{0,1},{1,0},{2,3},{3,2},{4,5},{5,4},{6,7},{7,6},{8,9},{9,8},{10,11... | collective-permute-start | bytes 24584 | tf_op jit(solution)/shard_map/ppermute | solution.py:303
  1.8 1.5 %collective-permute-start = (bf16[2,128,128]{2,1,0:T(8,128)(2,1)}, bf16[2,128,128]{2,1,0:T(8,128)(2,1)S(1)}, u32[]{:S(2)}, u32[]{:S(2)}) collective-permute-start(bf16[2,128,128]{2,1,0:T(8,128)(2,1)} %param.6), channel_id=1, source_target_pairs={{0,1},{1,0},{2,3},{3,2},{4,5},{5,4},{6,7},{7,6},{8,9},{9,8},{10,11... | collective-permute-start | bytes 196616 | tf_op jit(solution)/shard_map/ppermute | solution.py:303
  1.9 1.5 %collective-permute-start.1 = (bf16[2,128,128]{2,1,0:T(8,128)(2,1)}, bf16[2,128,128]{2,1,0:T(8,128)(2,1)S(1)}, u32[]{:S(2)}, u32[]{:S(2)}) collective-permute-start(bf16[2,128,128]{2,1,0:T(8,128)(2,1)} %param.7), channel_id=1, source_target_pairs={{0,1},{1,0},{2,3},{3,2},{4,5},{5,4},{6,7},{7,6},{8,9},{9,8},{10,11... | collective-permute-start | bytes 196616 | tf_op jit(solution)/shard_map/ppermute | solution.py:303
  3.5 7.6 %collective-permute-start.5 = (bf16[272,128]{1,0:T(8,128)(2,1)S(1)}, bf16[272,128]{1,0:T(8,128)(2,1)S(1)}, u32[]{:S(2)}, u32[]{:S(2)}) collective-permute-start(bf16[272,128]{1,0:T(8,128)(2,1)S(1)} %pad_maximum_fusion.1.pack_ref), channel_id=1, source_target_pairs={{0,6},{1,7},{2,4},{3,5},{4,2},{5,3},{6,0},{7,1},{8,14},{9,15},{10,... | collective-permute-start | bytes 208904 | tf_op jit(solution)/shard_map/ppermute | solution.py:303
  7.4 4.3 %collective-permute-start.4 = (bf16[272,128]{1,0:T(8,128)(2,1)S(1)}, bf16[272,128]{1,0:T(8,128)(2,1)S(1)}, u32[]{:S(2)}, u32[]{:S(2)}) collective-permute-start(bf16[272,128]{1,0:T(8,128)(2,1)S(1)} %pad_maximum_fusion.1.pack_ref), channel_id=1, source_target_pairs={{0,4},{1,5},{2,6},{3,7},{4,0},{5,1},{6,2},{7,3},{8,12},{9,13},{10,... | collective-permute-start | bytes 208904 | tf_op jit(solution)/shard_map/ppermute | solution.py:303
  7.9 4.3 %collective-permute-start.3 = (bf16[272,128]{1,0:T(8,128)(2,1)S(1)}, bf16[272,128]{1,0:T(8,128)(2,1)S(1)}, u32[]{:S(2)}, u32[]{:S(2)}) collective-permute-start(bf16[272,128]{1,0:T(8,128)(2,1)S(1)} %pad_maximum_fusion.1.pack_ref), channel_id=1, source_target_pairs={{0,2},{1,3},{2,0},{3,1},{4,6},{5,7},{6,4},{7,5},{8,10},{9,11},{10,... | collective-permute-start | bytes 208904 | tf_op jit(solution)/shard_map/ppermute | solution.py:303
  8.0 1.0 %copy-start = (bf16[2,128,1024]{2,1,0:T(8,128)(2,1)S(1)}, bf16[2,128,1024]{2,1,0:T(8,128)(2,1)}, u32[]{:S(2)}) copy-start(bf16[2,128,1024]{2,1,0:T(8,128)(2,1)} %query_ref.1) | copy-start | bytes 1572868
  9.1 1.0 %copy-start.1 = (bf16[2,128,1024]{2,1,0:T(8,128)(2,1)S(1)}, bf16[2,128,1024]{2,1,0:T(8,128)(2,1)}, u32[]{:S(2)}) copy-start(bf16[2,128,1024]{2,1,0:T(8,128)(2,1)} %grad_ref.1) | copy-start | bytes 1572868
  14.8 5.3 %collective-permute-start.6 = (bf16[256,128]{1,0:T(8,128)(2,1)S(1)}, bf16[256,128]{1,0:T(8,128)(2,1)S(1)}, u32[]{:S(2)}, u32[]{:S(2)}) collective-permute-start(bf16[256,128]{1,0:T(8,128)(2,1)S(1)} %get-tuple-element.44), channel_id=1, source_target_pairs={{0,2},{1,3},{2,0},{3,1},{4,6},{5,7},{6,4},{7,5},{8,10},{9,11},{10,... | collective-permute-start | bytes 196616 | tf_op jit(solution)/shard_map/ppermute | solution.py:303
  15.8 4.9 %collective-permute-start.7 = (bf16[256,128]{1,0:T(8,128)(2,1)S(1)}, bf16[256,128]{1,0:T(8,128)(2,1)S(1)}, u32[]{:S(2)}, u32[]{:S(2)}) collective-permute-start(bf16[256,128]{1,0:T(8,128)(2,1)S(1)} %get-tuple-element.45), channel_id=1, source_target_pairs={{0,4},{1,5},{2,6},{3,7},{4,0},{5,1},{6,2},{7,3},{8,12},{9,13},{10,... | collective-permute-start | bytes 196616 | tf_op jit(solution)/shard_map/ppermute | solution.py:303
  17.2 5.2 %collective-permute-start.8 = (bf16[256,128]{1,0:T(8,128)(2,1)S(1)}, bf16[256,128]{1,0:T(8,128)(2,1)S(1)}, u32[]{:S(2)}, u32[]{:S(2)}) collective-permute-start(bf16[256,128]{1,0:T(8,128)(2,1)S(1)} %get-tuple-element.46), channel_id=1, source_target_pairs={{0,6},{1,7},{2,4},{3,5},{4,2},{5,3},{6,0},{7,1},{8,14},{9,15},{10,... | collective-permute-start | bytes 196616 | tf_op jit(solution)/shard_map/ppermute | solution.py:303
  22.5 1.3 %collective-permute-start.9 = (bf16[256,128]{1,0:T(8,128)(2,1)S(1)}, bf16[256,128]{1,0:T(8,128)(2,1)S(1)}, u32[]{:S(2)}, u32[]{:S(2)}) collective-permute-start(bf16[256,128]{1,0:T(8,128)(2,1)S(1)} %get-tuple-element.48), channel_id=1, source_target_pairs={{0,1},{1,0},{2,3},{3,2},{4,5},{5,4},{6,7},{7,6},{8,9},{9,8},{10,11... | collective-permute-start | bytes 196616 | tf_op jit(solution)/shard_map/ppermute | solution.py:303

commit v10 on v9

--- a/solution.py
+++ b/solution.py
@@ -139,7 +139,7 @@
     masks = (1 << (depth - 1)) - 1
     near, refs = refs[:masks], refs[masks:]
     ds_s, joined_s, keys_t, part_ref = refs[:4]
-    sends, refs = refs[4 : 4 + masks], refs[4 + masks :]
+    sends, refs = refs[4:-4], refs[-4:]
     raised_s, weights_s, low_s, terms_s = refs
     width = pack_ref.shape[1]
     rows = (pack_ref.shape[0] - TAIL) // 2
@@ -218,6 +218,17 @@
         terms_s[level, :rows, :] = grad_keys[span] * scale
         terms_s[level, rows:, :] = grad_values[span]
     part_ref[...] = terms_s[level_of_even(even, depth)]
+    if depth == 3:
+        odd, straight, across = leaving_levels(index)
+        swap_ref, hold_ref = sends
+        mine, theirs = jnp.where(odd, across, straight), jnp.where(odd, straight, across)
+        diagonal = terms_s[straight]
+        first, second = diagonal[:rows], diagonal[rows:]
+        hold_ref[: 2 * rows, :] = terms_s[mine]
+        hold_ref[2 * rows :, :] = jnp.where(odd, second, first)
+        swap_ref[: 2 * rows, :] = terms_s[theirs].astype(BF16)
+        swap_ref[2 * rows :, :] = jnp.where(odd, first, second).astype(BF16)
+        return
     for mask, ref in enumerate(sends, 1):
         ref[...] = terms_s[level_of_even(even ^ (mask << 1), depth)].astype(BF16)
 
@@ -266,6 +277,31 @@
     leaf_ref[rows:, :] = leaf_values.astype(BF16)
 
 
+def leaving_levels(index):
+    x, y = (index >> 1) & 1, (index >> 2) & 1
+    return index & 1 == 1, 1 - y, jnp.where(x == 1, y, 2)
+
+
+def pair_kernel(hold_ref, other_ref, send_ref, diagonal_ref):
+    cut = send_ref.shape[0]
+    both = (hold_ref[...] + other_ref[...].astype(F32)).astype(BF16)
+    send_ref[...] = both[:cut]
+    diagonal_ref[...] = both[cut:]
+
+
+def gather_kernel(even_ref, last_ref, arrived_ref, diagonal_ref, keep_ref, send_ref):
+    rows = diagonal_ref.shape[0]
+    index = lax.axis_index("leaf")
+    odd, near = index & 1 == 1, (index >> 1) & 1 == 0
+    total = even_ref[...] + jnp.where(odd | near, arrived_ref[...].astype(F32), 0.0)
+    half = jnp.where(near, diagonal_ref[...].astype(F32), 0.0)
+    first = total[:rows] + jnp.where(odd, 0.0, half)
+    second = total[rows:] + jnp.where(odd, half, 0.0)
+    total = jnp.concatenate([first, second], 0)
+    keep_ref[...] = jnp.where(odd, last_ref[...], total)
+    send_ref[...] = jnp.where(odd, total, last_ref[...]).astype(BF16)
+
+
 def fold_kernel(depth, even_ref, last_ref, *refs):
     arrived, (keep_ref, send_ref) = refs[:-2], refs[-2:]
     index = lax.axis_index("leaf")
@@ -299,8 +335,9 @@
     inner = depth * rows
     terms = (2 * rows, width)
 
-    def move(block, flip):
-        return lax.ppermute(block, "leaf", [(i, i ^ flip) for i in range(count)])
+    def move(block, flip, odd_flip=None):
+        flips = (flip, flip if odd_flip is None else odd_flip)
+        return lax.ppermute(block, "leaf", [(i, i ^ flips[i & 1]) for i in range(count)])
 
     def exchange(blocks):
         moved = {m: move(blocks[m], m << 1) for m in reversed(masks)}
@@ -338,6 +375,10 @@
         ],
         flops=4 * 2 * rows * total * width,
     )
+    if depth == 3:
+        leaving = [((3 * rows, width), BF16), ((3 * rows, width), F32)]
+    else:
+        leaving = [(terms, BF16)] * len(near)
     ds, joined, keys_t, even_part, *sends = call(
         functools.partial(middle_kernel, depth, heads),
         "middle",
@@ -349,7 +390,7 @@
             ((width, inner), BF16),
             (terms, F32),
         ]
-        + [(terms, BF16)] * len(near),
+        + leaving,
         scratch=[
             ((inner, total), F32),
             ((inner, total), F32),
@@ -358,7 +399,17 @@
         ],
         flops=8 * inner * total * width,
     )
-    arrived = exchange(dict(zip(masks, sends)))
+    if depth == 3:
+        swap, hold = sends
+        send, diagonal = call(
+            pair_kernel, "pair", 2, (hold, move(swap, 1)), [(terms, BF16), ((rows, width), BF16)]
+        )
+        diagonal = move(diagonal, 6)
+        arrived = [move(send, 4, 2), diagonal]
+        fold = gather_kernel
+    else:
+        arrived = exchange(dict(zip(masks, sends)))
+        fold = functools.partial(fold_kernel, depth)
     grad_queries, leaf, last_part = call(
         functools.partial(late_kernel, heads),
         "late",
@@ -369,7 +420,7 @@
         flops=8 * 2 * rows * total * width,
     )
     keep, send = call(
-        functools.partial(fold_kernel, depth),
+        fold,
         "fold",
         3,
         (even_part, last_part, *arrived),

time: 24.7 us -> 25 us (1.012)
  waiting for transfers between devices: 4.78 us -> 6.44 us
  starting transfers between devices: 9.09 us -> 7.62 us
    ppermute x10, waiting for transfers between devices: 4.78 us -> 6.44 us  [move(): lax.ppermute(block, 'leaf', [(i, i ^ flips[i & 1]) for i in range(count)])]
    ppermute x10, starting transfers between devices: 9.09 us -> 7.62 us  [move(): lax.ppermute(block, 'leaf', [(i, i ^ flips[i & 1]) for i in range(count)])]
    pallas_call x5 -> x6, Pallas kernels: 6.13 us -> 6.15 us  [call(): pl.pallas_call(kernel, out_shape=[jax.ShapeDtypeStruct(shape, kind) for s...]
  transfers between devices with their start and end apart: 10 -> 10, of which waited for: 7 -> 6; matrix products, arithmetic and copies ran while one was open for 4% -> 4% of each run, Pallas kernels for 11% -> 11%
where the time goes in v10:
time: 25 us; the launch traced here: 24.7 us
  starting transfers between devices  7.62 us (30%)
  waiting for transfers between devices  6.44 us (26%)
  Pallas kernels  6.15 us (25%)
  local copies, waits for them, and re-layouts  2.16 us (9%)
  other arithmetic  1.61 us (6%)
  between operations  0.73 us (3%)
    ppermute x10, starting transfers between devices, move(): lax.ppermute(block, 'leaf', [(i, i ^ flips[i & 1]) for i in range(count)])  7.62 us
    ppermute x10, waiting for transfers between devices, move(): lax.ppermute(block, 'leaf', [(i, i ^ flips[i & 1]) for i in range(count)])  6.44 us
    pallas_call x6, Pallas kernels, call(): pl.pallas_call(kernel, out_shape=[jax.ShapeDtypeStruct(shape, kind) for s...  6.15 us
    unnamed x4, local copies, waits for them, and re-layouts  2.08 us
    concatenate x1, other arithmetic, body(): held = jnp.concatenate([key_states, value_states], 0)  0.88 us
    convert_element_type x1, other arithmetic, body(): lengths.astype(BF16)[:, None, None]  0.66 us
  transfers between devices with their start and end apart: 10, of which 6 were waited for; matrix products, arithmetic and copies ran while one was open for 4% of the time, Pallas kernels for 11%

profile of v10, /device:TPU:0, one launch (start us, length us, event | category | flops | bytes accessed | tf_op | source)
XLA Modules:
  0.0 24.7 jit_solution(9631286098699046675)
XLA Ops:
  0.6 0.7 %convert_element_type.3 = bf16[2]{0:T(256)(128)(2,1)S(1)} convert(s32[2]{0:T(128)} %param.9) | non-fusion elementwise | flops 2 | bytes 12 | tf_op jit(solution)/shard_map/convert_element_type | solution.py:347
  1.3 0.1 broadcast_in_dim.10.tails_ref
  1.4 0.5 %collective-permute-start.2 = (bf16[2,16,128]{2,1,0:T(8,128)(2,1)S(1)}, bf16[2,16,128]{2,1,0:T(8,128)(2,1)S(1)}, u32[]{:S(2)}, u32[]{:S(2)}) collective-permute-start(bf16[2,16,128]{2,1,0:T(8,128)(2,1)S(1)} %broadcast_in_dim.10.tails_ref), channel_id=1, source_target_pairs={{0,1},{1,0},{2,3},{3,2},{4,5},{5,4},{6,7},{7,6},{8,9},{9,8},{10,11... | collective-permute-start | bytes 24584 | tf_op jit(solution)/shard_map/ppermute | solution.py:340
  1.8 0.1 collective-permute-start
  1.9 0.4 %collective-permute-start.1 = (bf16[2,128,128]{2,1,0:T(8,128)(2,1)}, bf16[2,128,128]{2,1,0:T(8,128)(2,1)S(1)}, u32[]{:S(2)}, u32[]{:S(2)}) collective-permute-start(bf16[2,128,128]{2,1,0:T(8,128)(2,1)} %param.7), channel_id=1, source_target_pairs={{0,1},{1,0},{2,3},{3,2},{4,5},{5,4},{6,7},{7,6},{8,9},{9,8},{10,11... | collective-permute-start | bytes 196616 | tf_op jit(solution)/shard_map/ppermute | solution.py:340
  2.3 0.9 %pad_maximum_fusion.held_ref = bf16[4,128,128]{2,1,0:T(8,128)(2,1)S(1)} fusion(bf16[2,128,128]{2,1,0:T(8,128)(2,1)} %param.7, bf16[2,128,128]{2,1,0:T(8,128)(2,1)} %param.6), kind=kLoop, calls=%fused_computation | loop fusion | flops 65536 | bytes 262144 | tf_op jit(solution)/shard_map/concatenate | solution.py:349
  3.2 0.0 collective-permute-done.2.refs_2_
  3.2 0.1 collective-permute-done.refs_0_
  3.3 0.2 collective-permute-done.1.refs_1_
  3.5 2.9 %collective-permute-start.3 = (bf16[272,128]{1,0:T(8,128)(2,1)S(1)}, bf16[272,128]{1,0:T(8,128)(2,1)S(1)}, u32[]{:S(2)}, u32[]{:S(2)}) collective-permute-start(bf16[272,128]{1,0:T(8,128)(2,1)S(1)} %pad_maximum_fusion.1.pack_ref), channel_id=1, source_target_pairs={{0,2},{1,3},{2,0},{3,1},{4,6},{5,7},{6,4},{7,5},{8,10},{9,11},{10,... | collective-permute-start | bytes 208904 | tf_op jit(solution)/shard_map/ppermute | solution.py:340
  6.4 1.5 %collective-permute-start.4 = (bf16[272,128]{1,0:T(8,128)(2,1)S(1)}, bf16[272,128]{1,0:T(8,128)(2,1)S(1)}, u32[]{:S(2)}, u32[]{:S(2)}) collective-permute-start(bf16[272,128]{1,0:T(8,128)(2,1)S(1)} %pad_maximum_fusion.1.pack_ref), channel_id=1, source_target_pairs={{0,4},{1,5},{2,6},{3,7},{4,0},{5,1},{6,2},{7,3},{8,12},{9,13},{10,... | collective-permute-start | bytes 208904 | tf_op jit(solution)/shard_map/ppermute | solution.py:340
  8.0 0.0 collective-permute-start.5
  8.0 0.0 copy-start
  8.0 1.0 %copy-done = bf16[2,128,1024]{2,1,0:T(8,128)(2,1)S(1)} copy-done((bf16[2,128,1024]{2,1,0:T(8,128)(2,1)S(1)}, bf16[2,128,1024]{2,1,0:T(8,128)(2,1)}, u32[]{:S(2)}) %copy-start) | copy-done | bytes 524312
  9.0 0.0 copy-start.1
  9.0 1.0 %copy-done.1 = bf16[2,128,1024]{2,1,0:T(8,128)(2,1)S(1)} copy-done((bf16[2,128,1024]{2,1,0:T(8,128)(2,1)S(1)}, bf16[2,128,1024]{2,1,0:T(8,128)(2,1)}, u32[]{:S(2)}) %copy-start.1) | copy-done | bytes 524312
  10.1 1.0 %early.1 = (bf16[2048,128]{1,0:T(8,128)(2,1)S(1)}, bf16[2048,128]{1,0:T(8,128)(2,1)S(1)}, f32[256,2048]{1,0:T(8,128)S(1)}, f32[256,2048]{1,0:T(8,128)S(1)}, f32[...) custom-call(bf16[2,128,1024]{2,1,0:T(8,128)(2,1)S(1)} %copy-done, bf16[2,128,1024]{2,1,0:T(8,128)(2,1)S(1)} %copy-done.1, ...), custom_call_target="tpu_custom_call" | custom-call | flops 268435456 | bytes 1048576 | tf_op jit(solution)/shard_map/early/pallas_call | solution.py:50
  11.0 0.0 collective-permute-done.3.refs_0_
  11.1 0.0 collective-permute-done.4.refs_1_
  11.1 2.1 %collective-permute-done.5.refs_2_ = bf16[272,128]{1,0:T(8,128)(2,1)S(1)} collective-permute-done((bf16[272,128]{1,0:T(8,128)(2,1)S(1)}, bf16[272,128]{1,0:T(8,128)(2,1)S(1)}, u32[]{:S(2)}, u32[]{:S(2)}) %collective-permute-start.5) | collective-permute-done | bytes 69664 | tf_op jit(solution)/shard_map/ppermute | solution.py:340
  13.2 2.6 %middle.1 = (bf16[384,2048]{1,0:T(8,128)(2,1)S(1)}, f32[8,2048]{1,0:T(8,128)S(1)}, bf16[128,384]{1,0:T(8,128)(2,1)S(1)}, f32[256,128]{1,0:T(8,128)S(1)}, bf16[38...) custom-call(bf16[2048,128]{1,0:T(8,128)(2,1)S(1)} %get-tuple-element.32.query_s, ...), custom_call_target="tpu_custom_call" | custom-call | flops 805306368 | bytes 1048576 | tf_op jit(solution)/shard_map/middle/pallas_call | solution.py:50
  15.8 0.1 collective-permute-start.6
  15.9 1.3 %collective-permute-done.6.other_ref = bf16[384,128]{1,0:T(8,128)(2,1)S(1)} collective-permute-done((bf16[384,128]{1,0:T(8,128)(2,1)S(1)}, bf16[384,128]{1,0:T(8,128)(2,1)S(1)}, u32[]{:S(2)}, u32[]{:S(2)}) %collective-permute-start.6) | collective-permute-done | bytes 98336 | tf_op jit(solution)/shard_map/ppermute | solution.py:340
  17.2 0.7 %collective-permute-start.7 = (bf16[256,128]{1,0:T(8,128)(2,1)S(1)}, bf16[256,128]{1,0:T(8,128)(2,1)S(1)}, u32[]{:S(2)}, u32[]{:S(2)}) collective-permute-start(bf16[256,128]{1,0:T(8,128)(2,1)S(1)} %get-tuple-element.47), channel_id=1, source_target_pairs={{0,4},{1,3},{2,6},{3,1},{4,0},{5,7},{6,2},{7,5},{8,12},{9,11},{10,... | collective-permute-start | bytes 196616 | tf_op jit(solution)/shard_map/ppermute | solution.py:340
  17.8 1.4 %collective-permute-start.8 = (bf16[128,128]{1,0:T(8,128)(2,1)S(1)}, bf16[128,128]{1,0:T(8,128)(2,1)S(1)}, u32[]{:S(2)}, u32[]{:S(2)}) collective-permute-start(bf16[128,128]{1,0:T(8,128)(2,1)S(1)} %get-tuple-element.48), channel_id=1, source_target_pairs={{0,6},{1,7},{2,4},{3,5},{4,2},{5,3},{6,0},{7,1},{8,14},{9,15},{10,... | collective-permute-start | bytes 98312 | tf_op jit(solution)/shard_map/ppermute | solution.py:340
  19.2 1.8 %late.1 = (bf16[2,128,1024]{2,1,0:T(8,128)(2,1)}, bf16[256,128]{1,0:T(8,128)(2,1)S(1)}, f32[256,128]{1,0:T(8,128)S(1)}) custom-call(bf16[2048,128]{1,0:T(8,128)(2,1)S(1)} %get-tuple-element.32.query_s, bf16[2048,128]{1,0:T(8,128)(2,1)S(1)} %get-tuple-element.33.cot_s, f32[256,2048]{1,0:T(8,128)S(1)} %get-tuple-element.34.raised_ref, ...), custom_call_target="tpu_custom_call" | custom-call | flops 536870912 | bytes 1048576 | tf_op jit(solution)/shard_map/late/pallas_call | solution.py:50
  21.1 1.6 %collective-permute-done.8.diagonal_ref = bf16[128,128]{1,0:T(8,128)(2,1)S(1)} collective-permute-done((bf16[128,128]{1,0:T(8,128)(2,1)S(1)}, bf16[128,128]{1,0:T(8,128)(2,1)S(1)}, u32[]{:S(2)}, u32[]{:S(2)}) %collective-permute-start.8) | collective-permute-done | bytes 32800 | tf_op jit(solution)/shard_map/ppermute | solution.py:340
  22.6 0.0 collective-permute-done.7.arrived_ref
  22.7 0.1 collective-permute-start.9
  22.8 1.2 %collective-permute-done.9.other_ref = bf16[256,128]{1,0:T(8,128)(2,1)S(1)} collective-permute-done((bf16[256,128]{1,0:T(8,128)(2,1)S(1)}, bf16[256,128]{1,0:T(8,128)(2,1)S(1)}, u32[]{:S(2)}, u32[]{:S(2)}) %collective-permute-start.9) | collective-permute-done | bytes 65568 | tf_op jit(solution)/shard_map/ppermute | solution.py:340
  24.0 0.7 %final.1 = (bf16[2,128,128]{2,1,0:T(8,128)(2,1)}, bf16[2,128,128]{2,1,0:T(8,128)(2,1)}) custom-call(bf16[256,128]{1,0:T(8,128)(2,1)S(1)} %get-tuple-element.42.leaf_ref, f32[256,128]{1,0:T(8,128)S(1)} %get-tuple-element.49.keep_ref, bf16[256,128]{1,0:T(8,128)(2,1)S(1)} %collective-permute-done.9.other_ref), custom_call_target="tpu_custom_call" | custom-call | bytes 1048576 | tf_op jit(solution)/shard_map/final/pallas_call | solution.py:50
  (5 shorter events, 0.1 us)
Async XLA Ops:
  1.4 1.9 %collective-permute-start.2 = (bf16[2,16,128]{2,1,0:T(8,128)(2,1)S(1)}, bf16[2,16,128]{2,1,0:T(8,128)(2,1)S(1)}, u32[]{:S(2)}, u32[]{:S(2)}) collective-permute-start(bf16[2,16,128]{2,1,0:T(8,128)(2,1)S(1)} %broadcast_in_dim.10.tails_ref), channel_id=1, source_target_pairs={{0,1},{1,0},{2,3},{3,2},{4,5},{5,4},{6,7},{7,6},{8,9},{9,8},{10,11... | collective-permute-start | bytes 24584 | tf_op jit(solution)/shard_map/ppermute | solution.py:340
  1.8 1.5 %collective-permute-start = (bf16[2,128,128]{2,1,0:T(8,128)(2,1)}, bf16[2,128,128]{2,1,0:T(8,128)(2,1)S(1)}, u32[]{:S(2)}, u32[]{:S(2)}) collective-permute-start(bf16[2,128,128]{2,1,0:T(8,128)(2,1)} %param.6), channel_id=1, source_target_pairs={{0,1},{1,0},{2,3},{3,2},{4,5},{5,4},{6,7},{7,6},{8,9},{9,8},{10,11... | collective-permute-start | bytes 196616 | tf_op jit(solution)/shard_map/ppermute | solution.py:340
  1.9 1.5 %collective-permute-start.1 = (bf16[2,128,128]{2,1,0:T(8,128)(2,1)}, bf16[2,128,128]{2,1,0:T(8,128)(2,1)S(1)}, u32[]{:S(2)}, u32[]{:S(2)}) collective-permute-start(bf16[2,128,128]{2,1,0:T(8,128)(2,1)} %param.7), channel_id=1, source_target_pairs={{0,1},{1,0},{2,3},{3,2},{4,5},{5,4},{6,7},{7,6},{8,9},{9,8},{10,11... | collective-permute-start | bytes 196616 | tf_op jit(solution)/shard_map/ppermute | solution.py:340
  3.5 7.5 %collective-permute-start.3 = (bf16[272,128]{1,0:T(8,128)(2,1)S(1)}, bf16[272,128]{1,0:T(8,128)(2,1)S(1)}, u32[]{:S(2)}, u32[]{:S(2)}) collective-permute-start(bf16[272,128]{1,0:T(8,128)(2,1)S(1)} %pad_maximum_fusion.1.pack_ref), channel_id=1, source_target_pairs={{0,2},{1,3},{2,0},{3,1},{4,6},{5,7},{6,4},{7,5},{8,10},{9,11},{10,... | collective-permute-start | bytes 208904 | tf_op jit(solution)/shard_map/ppermute | solution.py:340
  6.4 4.6 %collective-permute-start.4 = (bf16[272,128]{1,0:T(8,128)(2,1)S(1)}, bf16[272,128]{1,0:T(8,128)(2,1)S(1)}, u32[]{:S(2)}, u32[]{:S(2)}) collective-permute-start(bf16[272,128]{1,0:T(8,128)(2,1)S(1)} %pad_maximum_fusion.1.pack_ref), channel_id=1, source_target_pairs={{0,4},{1,5},{2,6},{3,7},{4,0},{5,1},{6,2},{7,3},{8,12},{9,13},{10,... | collective-permute-start | bytes 208904 | tf_op jit(solution)/shard_map/ppermute | solution.py:340
  8.0 5.2 %collective-permute-start.5 = (bf16[272,128]{1,0:T(8,128)(2,1)S(1)}, bf16[272,128]{1,0:T(8,128)(2,1)S(1)}, u32[]{:S(2)}, u32[]{:S(2)}) collective-permute-start(bf16[272,128]{1,0:T(8,128)(2,1)S(1)} %pad_maximum_fusion.1.pack_ref), channel_id=1, source_target_pairs={{0,6},{1,7},{2,4},{3,5},{4,2},{5,3},{6,0},{7,1},{8,14},{9,15},{10,... | collective-permute-start | bytes 208904 | tf_op jit(solution)/shard_map/ppermute | solution.py:340
  8.0 1.0 %copy-start = (bf16[2,128,1024]{2,1,0:T(8,128)(2,1)S(1)}, bf16[2,128,1024]{2,1,0:T(8,128)(2,1)}, u32[]{:S(2)}) copy-start(bf16[2,128,1024]{2,1,0:T(8,128)(2,1)} %query_ref.1) | copy-start | bytes 1572868
  9.0 1.0 %copy-start.1 = (bf16[2,128,1024]{2,1,0:T(8,128)(2,1)S(1)}, bf16[2,128,1024]{2,1,0:T(8,128)(2,1)}, u32[]{:S(2)}) copy-start(bf16[2,128,1024]{2,1,0:T(8,128)(2,1)} %grad_ref.1) | copy-start | bytes 1572868
  15.8 1.4 %collective-permute-start.6 = (bf16[384,128]{1,0:T(8,128)(2,1)S(1)}, bf16[384,128]{1,0:T(8,128)(2,1)S(1)}, u32[]{:S(2)}, u32[]{:S(2)}) collective-permute-start(bf16[384,128]{1,0:T(8,128)(2,1)S(1)} %get-tuple-element.46), channel_id=1, source_target_pairs={{0,1},{1,0},{2,3},{3,2},{4,5},{5,4},{6,7},{7,6},{8,9},{9,8},{10,11... | collective-permute-start | bytes 294920 | tf_op jit(solution)/shard_map/ppermute | solution.py:340
  17.2 5.5 %collective-permute-start.7 = (bf16[256,128]{1,0:T(8,128)(2,1)S(1)}, bf16[256,128]{1,0:T(8,128)(2,1)S(1)}, u32[]{:S(2)}, u32[]{:S(2)}) collective-permute-start(bf16[256,128]{1,0:T(8,128)(2,1)S(1)} %get-tuple-element.47), channel_id=1, source_target_pairs={{0,4},{1,3},{2,6},{3,1},{4,0},{5,7},{6,2},{7,5},{8,12},{9,11},{10,... | collective-permute-start | bytes 196616 | tf_op jit(solution)/shard_map/ppermute | solution.py:340
  17.8 4.8 %collective-permute-start.8 = (bf16[128,128]{1,0:T(8,128)(2,1)S(1)}, bf16[128,128]{1,0:T(8,128)(2,1)S(1)}, u32[]{:S(2)}, u32[]{:S(2)}) collective-permute-start(bf16[128,128]{1,0:T(8,128)(2,1)S(1)} %get-tuple-element.48), channel_id=1, source_target_pairs={{0,6},{1,7},{2,4},{3,5},{4,2},{5,3},{6,0},{7,1},{8,14},{9,15},{10,... | collective-permute-start | bytes 98312 | tf_op jit(solution)/shard_map/ppermute | solution.py:340
  22.7 1.3 %collective-permute-start.9 = (bf16[256,128]{1,0:T(8,128)(2,1)S(1)}, bf16[256,128]{1,0:T(8,128)(2,1)S(1)}, u32[]{:S(2)}, u32[]{:S(2)}) collective-permute-start(bf16[256,128]{1,0:T(8,128)(2,1)S(1)} %get-tuple-element.50), channel_id=1, source_target_pairs={{0,1},{1,0},{2,3},{3,2},{4,5},{5,4},{6,7},{7,6},{8,9},{9,8},{10,11... | collective-permute-start | bytes 196616 | tf_op jit(solution)/shard_map/ppermute | solution.py:340

commit v11 on v10

--- a/solution.py
+++ b/solution.py
@@ -9,6 +9,7 @@
 
 BF16 = jnp.bfloat16
 F32 = jnp.float32
+LOCAL = 3
 TAIL = 16
 BIG = -1e30
 LOG2E = 1.4426950408889634
@@ -86,8 +87,8 @@
 
 
 def early_kernel(depth, heads, query_ref, grad_ref, held_ref, tails_ref, *refs):
-    other_key_ref, other_value_ref, other_tails_ref = refs[:3]
-    query_s, cot_s, raised_s, weights_s, stats_s, keys_s = refs[3:]
+    other_key_ref, other_value_ref, other_tails_ref, pack_ref = refs[:4]
+    query_s, cot_s, raised_s, weights_s, stats_s, keys_s = refs[4:]
     rows, width = held_ref.shape[1:]
     index = lax.axis_index("leaf")
     odd = index & 1 == 1
@@ -96,21 +97,26 @@
     row = lax.broadcasted_iota(jnp.int32, (rows, width), 0)
     lengths = [tails_ref[segment, 0:1, :].astype(F32) for segment in range(2)]
     length = jnp.where(odd, lengths[0], other_tails_ref[0, 0:1, :].astype(F32))
-    keys = [jnp.where(odd, held_ref[0], other_key_ref[0]), held_ref[1]]
-    values = [jnp.where(odd, held_ref[2], other_value_ref[0]), held_ref[3]]
-    keys_s[:rows, :] = keys[0]
-    keys_s[rows:, :] = keys[1]
+    even_length = pack_ref[2 * rows : 2 * rows + 1, :].astype(F32)
+    last_keys = jnp.where(odd, held_ref[0], other_key_ref[0])
+    last_values = jnp.where(odd, held_ref[2], other_value_ref[0])
+    keys = [last_keys, pack_ref[:rows, :], held_ref[1]]
+    values = [last_values, pack_ref[rows : 2 * rows, :], held_ref[3]]
     yes, no = jnp.full((), True), jnp.full((), False)
-    ruled = ruled_columns(rows, width)
+    masks = [
+        [(length, no, odd), (even_length, odd, ~odd)],
+        [(length, yes, no), (even_length, yes, no), (lengths[1], no, yes)],
+    ]
     wide = [
         [
-            jnp.concatenate([keys[0], mask_columns(length, no, odd, rows, width)], 1),
-        ],
-        [
-            jnp.concatenate([keys[0], mask_columns(length, yes, no, rows, width)], 1),
-            jnp.concatenate([keys[1], mask_columns(lengths[1], no, yes, rows, width)], 1),
-        ],
+            jnp.concatenate([block, mask_columns(*mask, rows, width)], 1)
+            for block, mask in zip(keys, masks[segment])
+        ]
+        for segment in range(2)
     ]
+    for place in range(LOCAL):
+        keys_s[place * rows : (place + 1) * rows, :] = keys[place]
+    ruled = ruled_columns(rows, width)
     for segment in range(2):
         live = row.astype(F32) < lengths[segment]
         for pair in range(heads // 2):
@@ -124,7 +130,7 @@
             query_s[here, :] = query
             cot_s[here, :] = cot
             query_wide = jnp.concatenate([query, ruled], 1)
-            for place in range(1 + segment):
+            for place in range(LOCAL - 1 + segment):
                 span = slice(place * rows, (place + 1) * rows)
                 raised, grad_weights, top, total, partial = block_scores(
                     wide[segment][place], values[place], query_wide, cot, factor
@@ -138,8 +144,8 @@
 def middle_kernel(depth, heads, query_s, cot_s, stats_ref, pack_ref, *refs):
     masks = (1 << (depth - 1)) - 1
     near, refs = refs[:masks], refs[masks:]
-    ds_s, joined_s, keys_t, part_ref = refs[:4]
-    sends, refs = refs[4:-4], refs[-4:]
+    ds_s, joined_s, keys_t = refs[:3]
+    sends, refs = refs[3:-4], refs[-4:]
     raised_s, weights_s, low_s, terms_s = refs
     width = pack_ref.shape[1]
     rows = (pack_ref.shape[0] - TAIL) // 2
@@ -153,15 +159,27 @@
     ruled = ruled_columns(rows, width)
     values = []
     wide = [[], []]
-    for level in range(depth):
-        pick = (even ^ owner_of(even, level, depth)) >> 1
-        block = pack_ref[...]
-        for mask in range(1, masks + 1):
-            block = jnp.where(pick == mask, near[mask - 1][...], block)
+    if depth == 3:
+        far = (index >> 1) & 1 == 1
+        _, straight, across = leaving_levels(index)
+        remote = [
+            (straight, jnp.where(far, near[0][...], near[1][...])),
+            (across, near[2][...]),
+        ]
+    else:
+        remote = []
+        for place in range(depth - 1):
+            level = place + jnp.where(place < level_of_even(even, depth), 0, 1)
+            pick = (even ^ owner_at(even, level, depth)) >> 1
+            block = pack_ref[...]
+            for mask in range(1, masks + 1):
+                block = jnp.where(pick == mask, near[mask - 1][...], block)
+            remote.append((level, block))
+    for place, (level, block) in enumerate(remote):
         keys = block[:rows]
         values.append(block[rows : 2 * rows])
         length = block[2 * rows : 2 * rows + 1].astype(F32)
-        keys_t[:, level * rows : (level + 1) * rows] = keys.T
+        keys_t[:, place * rows : (place + 1) * rows] = keys.T
         inner = mask_columns(length, level < own_level, level == own_level, rows, width)
         outer = mask_columns(length, yes, no, rows, width)
         wide[0].append(jnp.concatenate([keys, inner], 1))
@@ -176,14 +194,15 @@
             query, cot = query_s[here, :], cot_s[here, :]
             query_wide = jnp.concatenate([query, ruled], 1)
             tops, totals, partials = [], [], []
-            for place in range(1 + segment):
+            local = LOCAL - 1 + segment
+            for place in range(local):
                 tops.append(stats_ref[3 * place : 3 * place + 1, here])
                 totals.append(stats_ref[3 * place + 1 : 3 * place + 2, here])
                 partials.append(stats_ref[3 * place + 2 : 3 * place + 3, here])
-            for level in range(depth):
-                span = slice(level * rows, (level + 1) * rows)
+            for place in range(len(remote)):
+                span = slice(place * rows, (place + 1) * rows)
                 raised, grad_weights, top, total, partial = block_scores(
-                    wide[segment][level], values[level], query_wide, cot, factor
+                    wide[segment][place], values[place], query_wide, cot, factor
                 )
                 raised_s[span, here] = raised
                 weights_s[span, here] = grad_weights
@@ -197,11 +216,11 @@
             shares = [share * inverse for share in shares]
             delta = sum(share * part for share, part in zip(shares, partials))
             joined_s[0:1, here] = delta
-            for place in range(1 + segment):
+            for place in range(local):
                 joined_s[1 + place : 2 + place, here] = shares[place]
-            for level in range(depth):
-                span = slice(level * rows, (level + 1) * rows)
-                weights = raised_s[span, here] * shares[1 + segment + level]
+            for place in range(len(remote)):
+                span = slice(place * rows, (place + 1) * rows)
+                weights = raised_s[span, here] * shares[local + place]
                 low_s[span, here] = weights.astype(BF16)
                 ds_s[span, here] = (weights * (weights_s[span, here] - delta)).astype(BF16)
         now = slice(segment * half, (segment + 1) * half)
@@ -213,41 +232,41 @@
         )
         grad_keys = more_keys if segment == 0 else grad_keys + more_keys
         grad_values = more_values if segment == 0 else grad_values + more_values
-    for level in range(depth):
-        span = slice(level * rows, (level + 1) * rows)
-        terms_s[level, :rows, :] = grad_keys[span] * scale
-        terms_s[level, rows:, :] = grad_values[span]
-    part_ref[...] = terms_s[level_of_even(even, depth)]
+    for place in range(len(remote)):
+        span = slice(place * rows, (place + 1) * rows)
+        terms_s[place, :rows, :] = grad_keys[span] * scale
+        terms_s[place, rows:, :] = grad_values[span]
     if depth == 3:
-        odd, straight, across = leaving_levels(index)
+        odd = index & 1 == 1
         swap_ref, hold_ref = sends
-        mine, theirs = jnp.where(odd, across, straight), jnp.where(odd, straight, across)
-        diagonal = terms_s[straight]
-        first, second = diagonal[:rows], diagonal[rows:]
+        mine, theirs = jnp.where(odd, 1, 0), jnp.where(odd, 0, 1)
+        first, second = terms_s[0, :rows, :], terms_s[0, rows:, :]
         hold_ref[: 2 * rows, :] = terms_s[mine]
         hold_ref[2 * rows :, :] = jnp.where(odd, second, first)
         swap_ref[: 2 * rows, :] = terms_s[theirs].astype(BF16)
         swap_ref[2 * rows :, :] = jnp.where(odd, first, second).astype(BF16)
         return
     for mask, ref in enumerate(sends, 1):
-        ref[...] = terms_s[level_of_even(even ^ (mask << 1), depth)].astype(BF16)
+        level = level_of_even(even ^ (mask << 1), depth)
+        place = level - jnp.where(level < level_of_even(even, depth), 0, 1)
+        ref[...] = terms_s[jnp.clip(place, 0, depth - 2)].astype(BF16)
 
 
 def late_kernel(heads, query_s, cot_s, raised_ref, weights_ref, joined_ref, ds_ref, *refs):
-    keys_t, keys_s, grad_query_ref, leaf_ref, part_ref, low_s, ds_s = refs
+    keys_t, keys_s, grad_query_ref, leaf_ref, last_ref, even_ref, low_s, ds_s = refs
     width = keys_s.shape[1]
-    rows = keys_s.shape[0] // 2
+    rows = keys_s.shape[0] // LOCAL
     scale = width ** (-0.5)
     step = 2 * rows
     half = heads * rows
     near_t = keys_s[...].T
     for segment in range(2):
-        count = (1 + segment) * rows
+        count = (LOCAL - 1 + segment) * rows
         for pair in range(heads // 2):
             at = (segment * (heads // 2) + pair) * step
             here = slice(at, at + step)
             delta = joined_ref[0:1, here]
-            for place in range(1 + segment):
+            for place in range(LOCAL - 1 + segment):
                 span = slice(place * rows, (place + 1) * rows)
                 weights = raised_ref[span, here] * joined_ref[1 + place : 2 + place, here]
                 low_s[span, here] = weights.astype(BF16)
@@ -261,17 +280,22 @@
             for n in range(2):
                 c = slice((2 * pair + n) * width, (2 * pair + n + 1) * width)
                 grad_query_ref[segment, :, c] = grad_query[n * rows : (n + 1) * rows]
-    part_ref[:rows, :] = scale * lax.dot_general(
-        ds_s[:rows, :], query_s[...], NN, preferred_element_type=F32
-    )
-    part_ref[rows:, :] = lax.dot_general(
-        low_s[:rows, :], cot_s[...], NN, preferred_element_type=F32
-    )
+    inner = (LOCAL - 1) * rows
+    grad_keys = scale * lax.dot_general(
+        ds_s[:inner, :], query_s[...], NN, preferred_element_type=F32
+    )
+    grad_values = lax.dot_general(
+        low_s[:inner, :], cot_s[...], NN, preferred_element_type=F32
+    )
+    for place, ref in enumerate((last_ref, even_ref)):
+        span = slice(place * rows, (place + 1) * rows)
+        ref[:rows, :] = grad_keys[span]
+        ref[rows:, :] = grad_values[span]
     leaf_keys = scale * lax.dot_general(
-        ds_s[rows:, half:], query_s[half:, :], NN, preferred_element_type=F32
+        ds_s[inner:, half:], query_s[half:, :], NN, preferred_element_type=F32
     )
     leaf_values = lax.dot_general(
-        low_s[rows:, half:], cot_s[half:, :], NN, preferred_element_type=F32
+        low_s[inner:, half:], cot_s[half:, :], NN, preferred_element_type=F32
     )
     leaf_ref[:rows, :] = leaf_keys.astype(BF16)
     leaf_ref[rows:, :] = leaf_values.astype(BF16)
@@ -282,11 +306,9 @@
     return index & 1 == 1, 1 - y, jnp.where(x == 1, y, 2)
 
 
-def pair_kernel(hold_ref, other_ref, send_ref, diagonal_ref):
-    cut = send_ref.shape[0]
-    both = (hold_ref[...] + other_ref[...].astype(F32)).astype(BF16)
-    send_ref[...] = both[:cut]
-    diagonal_ref[...] = both[cut:]
+def pair_kernel(first, hold_ref, other_ref, after_ref, out_ref):
+    span = slice(first, first + out_ref.shape[0])
+    out_ref[...] = (hold_ref[span, :] + other_ref[span, :].astype(F32)).astype(BF16)
 
 
 def gather_kernel(even_ref, last_ref, arrived_ref, diagonal_ref, keep_ref, send_ref):
@@ -332,7 +354,8 @@
     rows, width = key_states.shape[1:]
     heads = queries.shape[2] // width
     total = 2 * heads * rows
-    inner = depth * rows
+    local = LOCAL * rows
+    inner = (depth - 1) * rows
     terms = (2 * rows, width)
 
     def move(block, flip, odd_flip=None):
@@ -359,27 +382,30 @@
         ],
         0,
     )
-    near = exchange({m: pack for m in masks})
+    if depth == 3:
+        near = [move(pack, flip) for flip in (6, 4, 2)]
+    else:
+        near = exchange({m: pack for m in masks})
     query_rows, cot, raised, weights, stats, last_keys = call(
         functools.partial(early_kernel, depth, heads),
         "early",
-        8,
-        (queries, grad_output, held, tails, other_keys, other_values, other_tails),
+        12,
+        (queries, grad_output, held, tails, other_keys, other_values, other_tails, pack),
         [
             ((total, width), BF16),
             ((total, width), BF16),
-            ((2 * rows, total), F32),
-            ((2 * rows, total), F32),
-            ((8, total), F32),
-            ((2 * rows, width), BF16),
+            ((local, total), F32),
+            ((local, total), F32),
+            ((16, total), F32),
+            ((local, width), BF16),
         ],
-        flops=4 * 2 * rows * total * width,
+        flops=4 * local * total * width,
     )
     if depth == 3:
         leaving = [((3 * rows, width), BF16), ((3 * rows, width), F32)]
     else:
         leaving = [(terms, BF16)] * len(near)
-    ds, joined, keys_t, even_part, *sends = call(
+    ds, joined, keys_t, *sends = call(
         functools.partial(middle_kernel, depth, heads),
         "middle",
         24,
@@ -388,36 +414,40 @@
             ((inner, total), BF16),
             ((8, total), F32),
             ((width, inner), BF16),
-            (terms, F32),
         ]
         + leaving,
         scratch=[
             ((inner, total), F32),
             ((inner, total), F32),
             ((inner, total), BF16),
-            ((depth,) + terms, F32),
+            ((depth - 1,) + terms, F32),
         ],
         flops=8 * inner * total * width,
     )
     if depth == 3:
         swap, hold = sends
-        send, diagonal = call(
-            pair_kernel, "pair", 2, (hold, move(swap, 1)), [(terms, BF16), ((rows, width), BF16)]
-        )
-        diagonal = move(diagonal, 6)
-        arrived = [move(send, 4, 2), diagonal]
+        other = move(swap, 1)
+        send = call(
+            functools.partial(pair_kernel, 0), "pair", 2, (hold, other, other), [(terms, BF16)]
+        )[0]
+        straight = move(send, 4, 2)
+        half = call(
+            functools.partial(pair_kernel, 2 * rows), "pair", 2, (hold, other, send),
+            [((rows, width), BF16)],
+        )[0]
+        arrived = [straight, move(half, 6)]
         fold = gather_kernel
     else:
         arrived = exchange(dict(zip(masks, sends)))
         fold = functools.partial(fold_kernel, depth)
-    grad_queries, leaf, last_part = call(
+    grad_queries, leaf, last_part, even_part = call(
         functools.partial(late_kernel, heads),
         "late",
-        8,
+        12,
         (query_rows, cot, raised, weights, joined, ds, keys_t, last_keys),
-        [((2, rows, heads * width), BF16), (terms, BF16), (terms, F32)],
-        scratch=[((2 * rows, total), BF16), ((2 * rows, total), BF16)],
-        flops=8 * 2 * rows * total * width,
+        [((2, rows, heads * width), BF16), (terms, BF16), (terms, F32), (terms, F32)],
+        scratch=[((local, total), BF16), ((local, total), BF16)],
+        flops=8 * local * total * width,
     )
     keep, send = call(
         fold,

time: 25 us -> 24.5 us (0.980)
  waiting for transfers between devices: 6.44 us -> 4.73 us
  starting transfers between devices: 7.62 us -> 8.53 us
  Pallas kernels: 6.15 us -> 6.45 us
    ppermute x10, waiting for transfers between devices: 6.44 us -> 4.73 us  [move(): lax.ppermute(block, 'leaf', [(i, i ^ flips[i & 1]) for i in range(count)])]
    ppermute x10, starting transfers between devices: 7.62 us -> 8.53 us  [move(): lax.ppermute(block, 'leaf', [(i, i ^ flips[i & 1]) for i in range(count)])]
    pallas_call x6 -> x7, Pallas kernels: 6.15 us -> 6.45 us  [call(): pl.pallas_call(kernel, out_shape=[jax.ShapeDtypeStruct(shape, kind) for s...]
  transfers between devices with their start and end apart: 10 -> 10, of which waited for: 6 -> 7; matrix products, arithmetic and copies ran while one was open for 4% -> 4% of each run, Pallas kernels for 11% -> 15%
where the time goes in v11:
time: 24.5 us; the launch traced here: 24.2 us
  starting transfers between devices  8.53 us (35%)
  Pallas kernels  6.45 us (26%)
  waiting for transfers between devices  4.73 us (19%)
  local copies, waits for them, and re-layouts  2.16 us (9%)
  other arithmetic  1.61 us (7%)
  between operations  0.72 us (3%)
    ppermute x10, starting transfers between devices, move(): lax.ppermute(block, 'leaf', [(i, i ^ flips[i & 1]) for i in range(count)])  8.53 us
    pallas_call x7, Pallas kernels, call(): pl.pallas_call(kernel, out_shape=[jax.ShapeDtypeStruct(shape, kind) for s...  6.45 us
    ppermute x10, waiting for transfers between devices, move(): lax.ppermute(block, 'leaf', [(i, i ^ flips[i & 1]) for i in range(count)])  4.73 us
    unnamed x4, local copies, waits for them, and re-layouts  2.08 us
    concatenate x1, other arithmetic, body(): held = jnp.concatenate([key_states, value_states], 0)  0.88 us
    convert_element_type x1, other arithmetic, body(): lengths.astype(BF16)[:, None, None]  0.66 us
  transfers between devices with their start and end apart: 10, of which 7 were waited for; matrix products, arithmetic and copies ran while one was open for 4% of the time, Pallas kernels for 15%

profile of v11, /device:TPU:0, one launch (start us, length us, event | category | flops | bytes accessed | tf_op | source)
XLA Modules:
  0.0 24.2 jit_solution(2864722788530168816)
XLA Ops:
  0.6 0.7 %convert_element_type.3 = bf16[2]{0:T(256)(128)(2,1)S(1)} convert(s32[2]{0:T(128)} %param.9) | non-fusion elementwise | flops 2 | bytes 12 | tf_op jit(solution)/shard_map/convert_element_type | solution.py:370
  1.3 0.1 broadcast_in_dim.10.tails_ref
  1.4 0.5 %collective-permute-start.2 = (bf16[2,16,128]{2,1,0:T(8,128)(2,1)S(1)}, bf16[2,16,128]{2,1,0:T(8,128)(2,1)S(1)}, u32[]{:S(2)}, u32[]{:S(2)}) collective-permute-start(bf16[2,16,128]{2,1,0:T(8,128)(2,1)S(1)} %broadcast_in_dim.10.tails_ref), channel_id=1, source_target_pairs={{0,1},{1,0},{2,3},{3,2},{4,5},{5,4},{6,7},{7,6},{8,9},{9,8},{10,11... | collective-permute-start | bytes 24584 | tf_op jit(solution)/shard_map/ppermute | solution.py:363
  1.8 0.1 collective-permute-start
  1.9 0.4 %collective-permute-start.1 = (bf16[2,128,128]{2,1,0:T(8,128)(2,1)}, bf16[2,128,128]{2,1,0:T(8,128)(2,1)S(1)}, u32[]{:S(2)}, u32[]{:S(2)}) collective-permute-start(bf16[2,128,128]{2,1,0:T(8,128)(2,1)} %param.7), channel_id=1, source_target_pairs={{0,1},{1,0},{2,3},{3,2},{4,5},{5,4},{6,7},{7,6},{8,9},{9,8},{10,11... | collective-permute-start | bytes 196616 | tf_op jit(solution)/shard_map/ppermute | solution.py:363
  2.3 0.9 %pad_maximum_fusion.held_ref = bf16[4,128,128]{2,1,0:T(8,128)(2,1)S(1)} fusion(bf16[2,128,128]{2,1,0:T(8,128)(2,1)} %param.7, bf16[2,128,128]{2,1,0:T(8,128)(2,1)} %param.6), kind=kLoop, calls=%fused_computation | loop fusion | flops 65536 | bytes 262144 | tf_op jit(solution)/shard_map/concatenate | solution.py:372
  3.2 0.0 collective-permute-done.2.refs_2_
  3.2 0.1 collective-permute-done.refs_0_
  3.3 0.2 collective-permute-done.1.refs_1_
  3.5 3.9 %collective-permute-start.3 = (bf16[272,128]{1,0:T(8,128)(2,1)S(1)}, bf16[272,128]{1,0:T(8,128)(2,1)S(1)}, u32[]{:S(2)}, u32[]{:S(2)}) collective-permute-start(bf16[272,128]{1,0:T(8,128)(2,1)S(1)} %pad_maximum_fusion.1.refs_3_.pack_ref), channel_id=1, source_target_pairs={{0,6},{1,7},{2,4},{3,5},{4,2},{5,3},{6,0},{7,1},{8,14},{9,15},{10,... | collective-permute-start | bytes 208904 | tf_op jit(solution)/shard_map/ppermute | solution.py:363
  7.4 0.5 %collective-permute-start.4 = (bf16[272,128]{1,0:T(8,128)(2,1)S(1)}, bf16[272,128]{1,0:T(8,128)(2,1)S(1)}, u32[]{:S(2)}, u32[]{:S(2)}) collective-permute-start(bf16[272,128]{1,0:T(8,128)(2,1)S(1)} %pad_maximum_fusion.1.refs_3_.pack_ref), channel_id=1, source_target_pairs={{0,4},{1,5},{2,6},{3,7},{4,0},{5,1},{6,2},{7,3},{8,12},{9,13},{10,... | collective-permute-start | bytes 208904 | tf_op jit(solution)/shard_map/ppermute | solution.py:363
  7.9 0.1 collective-permute-start.5
  8.0 0.0 copy-start
  8.0 1.0 %copy-done = bf16[2,128,1024]{2,1,0:T(8,128)(2,1)S(1)} copy-done((bf16[2,128,1024]{2,1,0:T(8,128)(2,1)S(1)}, bf16[2,128,1024]{2,1,0:T(8,128)(2,1)}, u32[]{:S(2)}) %copy-start) | copy-done | bytes 524312
  9.1 0.0 copy-start.1
  9.1 1.0 %copy-done.1 = bf16[2,128,1024]{2,1,0:T(8,128)(2,1)S(1)} copy-done((bf16[2,128,1024]{2,1,0:T(8,128)(2,1)S(1)}, bf16[2,128,1024]{2,1,0:T(8,128)(2,1)}, u32[]{:S(2)}) %copy-start.1) | copy-done | bytes 524312
  10.1 1.5 %early.1 = (bf16[2048,128]{1,0:T(8,128)(2,1)S(1)}, bf16[2048,128]{1,0:T(8,128)(2,1)S(1)}, f32[384,2048]{1,0:T(8,128)S(1)}, f32[384,2048]{1,0:T(8,128)S(1)}, f32[...) custom-call(bf16[2,128,1024]{2,1,0:T(8,128)(2,1)S(1)} %copy-done, bf16[2,128,1024]{2,1,0:T(8,128)(2,1)S(1)} %copy-done.1, ...), custom_call_target="tpu_custom_call" | custom-call | flops 402653184 | bytes 1048576 | tf_op jit(solution)/shard_map/early/pallas_call | solution.py:51
  11.6 0.0 collective-permute-done.3.refs_0_
  11.6 0.1 collective-permute-done.4.refs_1_
  11.7 0.5 %collective-permute-done.5.refs_2_ = bf16[272,128]{1,0:T(8,128)(2,1)S(1)} collective-permute-done((bf16[272,128]{1,0:T(8,128)(2,1)S(1)}, bf16[272,128]{1,0:T(8,128)(2,1)S(1)}, u32[]{:S(2)}, u32[]{:S(2)}) %collective-permute-start.5) | collective-permute-done | bytes 69664 | tf_op jit(solution)/shard_map/ppermute | solution.py:363
  12.2 2.1 %middle.1 = (bf16[256,2048]{1,0:T(8,128)(2,1)S(1)}, f32[8,2048]{1,0:T(8,128)S(1)}, bf16[128,256]{1,0:T(8,128)(2,1)S(1)}, bf16[384,128]{1,0:T(8,128)(2,1)S(1)}, f32[384,128]{1,0:T(8,128)S(1)}) custom-call(bf16[2048,128]{1,0:T(8,128)(2,1)S(1)} %get-tuple-element.30.query_s, bf16[2048,128]{1,0:T(8,128)(2,1)S(1)} %get-tuple-element.31.cot_s, ...), custom_call_target="tpu_custom_call" | custom-call | flops 536870912 | bytes 1048576 | tf_op jit(solution)/shard_map/middle/pallas_call | solution.py:51
  14.3 0.1 collective-permute-start.6
  14.4 1.3 %collective-permute-done.6.other_ref.after_ref = bf16[384,128]{1,0:T(8,128)(2,1)S(1)} collective-permute-done((bf16[384,128]{1,0:T(8,128)(2,1)S(1)}, bf16[384,128]{1,0:T(8,128)(2,1)S(1)}, u32[]{:S(2)}, u32[]{:S(2)}) %collective-permute-start.6) | collective-permute-done | bytes 98336 | tf_op jit(solution)/shard_map/ppermute | solution.py:363
  15.7 1.6 %collective-permute-start.7 = (bf16[256,128]{1,0:T(8,128)(2,1)S(1)}, bf16[256,128]{1,0:T(8,128)(2,1)S(1)}, u32[]{:S(2)}, u32[]{:S(2)}) collective-permute-start(bf16[256,128]{1,0:T(8,128)(2,1)S(1)} %pair.2.after_ref), channel_id=1, source_target_pairs={{0,4},{1,3},{2,6},{3,1},{4,0},{5,7},{6,2},{7,5},{8,12},{9,11},{10,... | collective-permute-start | bytes 196616 | tf_op jit(solution)/shard_map/ppermute | solution.py:363
  17.3 1.3 %collective-permute-start.8 = (bf16[128,128]{1,0:T(8,128)(2,1)S(1)}, bf16[128,128]{1,0:T(8,128)(2,1)S(1)}, u32[]{:S(2)}, u32[]{:S(2)}) collective-permute-start(bf16[128,128]{1,0:T(8,128)(2,1)S(1)} %pair.3), channel_id=1, source_target_pairs={{0,6},{1,7},{2,4},{3,5},{4,2},{5,3},{6,0},{7,1},{8,14},{9,15},{10,... | collective-permute-start | bytes 98312 | tf_op jit(solution)/shard_map/ppermute | solution.py:363
  18.6 2.2 %late.1 = (bf16[2,128,1024]{2,1,0:T(8,128)(2,1)}, bf16[256,128]{1,0:T(8,128)(2,1)S(1)}, f32[256,128]{1,0:T(8,128)S(1)}, f32[256,128]{1,0:T(8,128)S(1)}) custom-call(bf16[2048,128]{1,0:T(8,128)(2,1)S(1)} %get-tuple-element.30.query_s, bf16[2048,128]{1,0:T(8,128)(2,1)S(1)} %get-tuple-element.31.cot_s, f32[384,2048]{1,0:T(8,128)S(1)} %get-tuple-element.32.raised_ref, ...), custom_call_target="tpu_custom_call" | custom-call | flops 805306368 | bytes 1048576 | tf_op jit(solution)/shard_map/late/pallas_call | solution.py:51
  20.8 1.4 %collective-permute-done.8.diagonal_ref = bf16[128,128]{1,0:T(8,128)(2,1)S(1)} collective-permute-done((bf16[128,128]{1,0:T(8,128)(2,1)S(1)}, bf16[128,128]{1,0:T(8,128)(2,1)S(1)}, u32[]{:S(2)}, u32[]{:S(2)}) %collective-permute-start.8) | collective-permute-done | bytes 32800 | tf_op jit(solution)/shard_map/ppermute | solution.py:363
  22.1 0.0 collective-permute-done.7.arrived_ref
  22.2 0.1 collective-permute-start.9
  22.3 1.2 %collective-permute-done.9.other_ref = bf16[256,128]{1,0:T(8,128)(2,1)S(1)} collective-permute-done((bf16[256,128]{1,0:T(8,128)(2,1)S(1)}, bf16[256,128]{1,0:T(8,128)(2,1)S(1)}, u32[]{:S(2)}, u32[]{:S(2)}) %collective-permute-start.9) | collective-permute-done | bytes 65568 | tf_op jit(solution)/shard_map/ppermute | solution.py:363
  23.5 0.7 %final.1 = (bf16[2,128,128]{2,1,0:T(8,128)(2,1)}, bf16[2,128,128]{2,1,0:T(8,128)(2,1)}) custom-call(bf16[256,128]{1,0:T(8,128)(2,1)S(1)} %get-tuple-element.40.leaf_ref, f32[256,128]{1,0:T(8,128)S(1)} %get-tuple-element.45.keep_ref, bf16[256,128]{1,0:T(8,128)(2,1)S(1)} %collective-permute-done.9.other_ref), custom_call_target="tpu_custom_call" | custom-call | bytes 1048576 | tf_op jit(solution)/shard_map/final/pallas_call | solution.py:51
  (6 shorter events, 0.1 us)
Async XLA Ops:
  1.4 1.9 %collective-permute-start.2 = (bf16[2,16,128]{2,1,0:T(8,128)(2,1)S(1)}, bf16[2,16,128]{2,1,0:T(8,128)(2,1)S(1)}, u32[]{:S(2)}, u32[]{:S(2)}) collective-permute-start(bf16[2,16,128]{2,1,0:T(8,128)(2,1)S(1)} %broadcast_in_dim.10.tails_ref), channel_id=1, source_target_pairs={{0,1},{1,0},{2,3},{3,2},{4,5},{5,4},{6,7},{7,6},{8,9},{9,8},{10,11... | collective-permute-start | bytes 24584 | tf_op jit(solution)/shard_map/ppermute | solution.py:363
  1.8 1.5 %collective-permute-start = (bf16[2,128,128]{2,1,0:T(8,128)(2,1)}, bf16[2,128,128]{2,1,0:T(8,128)(2,1)S(1)}, u32[]{:S(2)}, u32[]{:S(2)}) collective-permute-start(bf16[2,128,128]{2,1,0:T(8,128)(2,1)} %param.6), channel_id=1, source_target_pairs={{0,1},{1,0},{2,3},{3,2},{4,5},{5,4},{6,7},{7,6},{8,9},{9,8},{10,11... | collective-permute-start | bytes 196616 | tf_op jit(solution)/shard_map/ppermute | solution.py:363
  1.9 1.5 %collective-permute-start.1 = (bf16[2,128,128]{2,1,0:T(8,128)(2,1)}, bf16[2,128,128]{2,1,0:T(8,128)(2,1)S(1)}, u32[]{:S(2)}, u32[]{:S(2)}) collective-permute-start(bf16[2,128,128]{2,1,0:T(8,128)(2,1)} %param.7), channel_id=1, source_target_pairs={{0,1},{1,0},{2,3},{3,2},{4,5},{5,4},{6,7},{7,6},{8,9},{9,8},{10,11... | collective-permute-start | bytes 196616 | tf_op jit(solution)/shard_map/ppermute | solution.py:363
  3.5 8.1 %collective-permute-start.3 = (bf16[272,128]{1,0:T(8,128)(2,1)S(1)}, bf16[272,128]{1,0:T(8,128)(2,1)S(1)}, u32[]{:S(2)}, u32[]{:S(2)}) collective-permute-start(bf16[272,128]{1,0:T(8,128)(2,1)S(1)} %pad_maximum_fusion.1.refs_3_.pack_ref), channel_id=1, source_target_pairs={{0,6},{1,7},{2,4},{3,5},{4,2},{5,3},{6,0},{7,1},{8,14},{9,15},{10,... | collective-permute-start | bytes 208904 | tf_op jit(solution)/shard_map/ppermute | solution.py:363
  7.4 4.3 %collective-permute-start.4 = (bf16[272,128]{1,0:T(8,128)(2,1)S(1)}, bf16[272,128]{1,0:T(8,128)(2,1)S(1)}, u32[]{:S(2)}, u32[]{:S(2)}) collective-permute-start(bf16[272,128]{1,0:T(8,128)(2,1)S(1)} %pad_maximum_fusion.1.refs_3_.pack_ref), channel_id=1, source_target_pairs={{0,4},{1,5},{2,6},{3,7},{4,0},{5,1},{6,2},{7,3},{8,12},{9,13},{10,... | collective-permute-start | bytes 208904 | tf_op jit(solution)/shard_map/ppermute | solution.py:363
  7.9 4.3 %collective-permute-start.5 = (bf16[272,128]{1,0:T(8,128)(2,1)S(1)}, bf16[272,128]{1,0:T(8,128)(2,1)S(1)}, u32[]{:S(2)}, u32[]{:S(2)}) collective-permute-start(bf16[272,128]{1,0:T(8,128)(2,1)S(1)} %pad_maximum_fusion.1.refs_3_.pack_ref), channel_id=1, source_target_pairs={{0,2},{1,3},{2,0},{3,1},{4,6},{5,7},{6,4},{7,5},{8,10},{9,11},{10,... | collective-permute-start | bytes 208904 | tf_op jit(solution)/shard_map/ppermute | solution.py:363
  8.0 1.0 %copy-start = (bf16[2,128,1024]{2,1,0:T(8,128)(2,1)S(1)}, bf16[2,128,1024]{2,1,0:T(8,128)(2,1)}, u32[]{:S(2)}) copy-start(bf16[2,128,1024]{2,1,0:T(8,128)(2,1)} %query_ref.1) | copy-start | bytes 1572868
  9.1 1.0 %copy-start.1 = (bf16[2,128,1024]{2,1,0:T(8,128)(2,1)S(1)}, bf16[2,128,1024]{2,1,0:T(8,128)(2,1)}, u32[]{:S(2)}) copy-start(bf16[2,128,1024]{2,1,0:T(8,128)(2,1)} %grad_ref.1) | copy-start | bytes 1572868
  14.3 1.4 %collective-permute-start.6 = (bf16[384,128]{1,0:T(8,128)(2,1)S(1)}, bf16[384,128]{1,0:T(8,128)(2,1)S(1)}, u32[]{:S(2)}, u32[]{:S(2)}) collective-permute-start(bf16[384,128]{1,0:T(8,128)(2,1)S(1)} %get-tuple-element.44), channel_id=1, source_target_pairs={{0,1},{1,0},{2,3},{3,2},{4,5},{5,4},{6,7},{7,6},{8,9},{9,8},{10,11... | collective-permute-start | bytes 294920 | tf_op jit(solution)/shard_map/ppermute | solution.py:363
  15.7 6.5 %collective-permute-start.7 = (bf16[256,128]{1,0:T(8,128)(2,1)S(1)}, bf16[256,128]{1,0:T(8,128)(2,1)S(1)}, u32[]{:S(2)}, u32[]{:S(2)}) collective-permute-start(bf16[256,128]{1,0:T(8,128)(2,1)S(1)} %pair.2.after_ref), channel_id=1, source_target_pairs={{0,4},{1,3},{2,6},{3,1},{4,0},{5,7},{6,2},{7,5},{8,12},{9,11},{10,... | collective-permute-start | bytes 196616 | tf_op jit(solution)/shard_map/ppermute | solution.py:363
  17.3 4.9 %collective-permute-start.8 = (bf16[128,128]{1,0:T(8,128)(2,1)S(1)}, bf16[128,128]{1,0:T(8,128)(2,1)S(1)}, u32[]{:S(2)}, u32[]{:S(2)}) collective-permute-start(bf16[128,128]{1,0:T(8,128)(2,1)S(1)} %pair.3), channel_id=1, source_target_pairs={{0,6},{1,7},{2,4},{3,5},{4,2},{5,3},{6,0},{7,1},{8,14},{9,15},{10,... | collective-permute-start | bytes 98312 | tf_op jit(solution)/shard_map/ppermute | solution.py:363
  22.2 1.3 %collective-permute-start.9 = (bf16[256,128]{1,0:T(8,128)(2,1)S(1)}, bf16[256,128]{1,0:T(8,128)(2,1)S(1)}, u32[]{:S(2)}, u32[]{:S(2)}) collective-permute-start(bf16[256,128]{1,0:T(8,128)(2,1)S(1)} %get-tuple-element.46), channel_id=1, source_target_pairs={{0,1},{1,0},{2,3},{3,2},{4,5},{5,4},{6,7},{7,6},{8,9},{9,8},{10,11... | collective-permute-start | bytes 196616 | tf_op jit(solution)/shard_map/ppermute | solution.py:363

commit v12 on v11

--- a/solution.py
+++ b/solution.py
@@ -239,11 +239,10 @@
     if depth == 3:
         odd = index & 1 == 1
         swap_ref, hold_ref = sends
-        mine, theirs = jnp.where(odd, 1, 0), jnp.where(odd, 0, 1)
-        first, second = terms_s[0, :rows, :], terms_s[0, rows:, :]
-        hold_ref[: 2 * rows, :] = terms_s[mine]
+        first, second = terms_s[1, :rows, :], terms_s[1, rows:, :]
+        hold_ref[: 2 * rows, :] = terms_s[0]
         hold_ref[2 * rows :, :] = jnp.where(odd, second, first)
-        swap_ref[: 2 * rows, :] = terms_s[theirs].astype(BF16)
+        swap_ref[: 2 * rows, :] = terms_s[0].astype(BF16)
         swap_ref[2 * rows :, :] = jnp.where(odd, first, second).astype(BF16)
         return
     for mask, ref in enumerate(sends, 1):
@@ -311,12 +310,12 @@
     out_ref[...] = (hold_ref[span, :] + other_ref[span, :].astype(F32)).astype(BF16)
 
 
-def gather_kernel(even_ref, last_ref, arrived_ref, diagonal_ref, keep_ref, send_ref):
-    rows = diagonal_ref.shape[0]
+def gather_kernel(even_ref, last_ref, arrived_ref, half_ref, keep_ref, send_ref):
+    rows = half_ref.shape[0]
     index = lax.axis_index("leaf")
     odd, near = index & 1 == 1, (index >> 1) & 1 == 0
-    total = even_ref[...] + jnp.where(odd | near, arrived_ref[...].astype(F32), 0.0)
-    half = jnp.where(near, diagonal_ref[...].astype(F32), 0.0)
+    total = even_ref[...] + jnp.where(near, arrived_ref[...].astype(F32), 0.0)
+    half = half_ref[...].astype(F32)
     first = total[:rows] + jnp.where(odd, 0.0, half)
     second = total[rows:] + jnp.where(odd, half, 0.0)
     total = jnp.concatenate([first, second], 0)
@@ -358,9 +357,8 @@
     inner = (depth - 1) * rows
     terms = (2 * rows, width)
 
-    def move(block, flip, odd_flip=None):
-        flips = (flip, flip if odd_flip is None else odd_flip)
-        return lax.ppermute(block, "leaf", [(i, i ^ flips[i & 1]) for i in range(count)])
+    def move(block, flip):
+        return lax.ppermute(block, "leaf", [(i, i ^ flip) for i in range(count)])
 
     def exchange(blocks):
         moved = {m: move(blocks[m], m << 1) for m in reversed(masks)}
@@ -430,12 +428,13 @@
         send = call(
             functools.partial(pair_kernel, 0), "pair", 2, (hold, other, other), [(terms, BF16)]
         )[0]
-        straight = move(send, 4, 2)
+        far_pairs = [(0, 4), (4, 0), (2, 6), (6, 2), (3, 5), (5, 7), (7, 1), (1, 3)]
+        straight = lax.ppermute(send, "leaf", far_pairs)
         half = call(
             functools.partial(pair_kernel, 2 * rows), "pair", 2, (hold, other, send),
             [((rows, width), BF16)],
         )[0]
-        arrived = [straight, move(half, 6)]
+        arrived = [straight, move(half, 2)]
         fold = gather_kernel
     else:
         arrived = exchange(dict(zip(masks, sends)))

time: 24.5 us -> 23.5 us (0.959)
  waiting for transfers between devices: 4.73 us -> 3.77 us
    ppermute x10, waiting for transfers between devices: 4.73 us -> 3.77 us  [the longest x9 3.76 us: move(): return lax.ppermute(block, 'leaf', [(i, i ^ flip) for i in range(count)])]
  transfers between devices with their start and end apart: 10 -> 10, of which waited for: 7 -> 7; matrix products, arithmetic and copies ran while one was open for 4% -> 4% of each run, Pallas kernels for 15% -> 16%
where the time goes in v12:
time: 23.5 us; the launch traced here: 23.2 us
  starting transfers between devices  8.57 us (36%)
  Pallas kernels  6.41 us (27%)
  waiting for transfers between devices  3.77 us (16%)
  local copies, waits for them, and re-layouts  2.16 us (9%)
  other arithmetic  1.61 us (7%)
  between operations  0.72 us (3%)
    ppermute x9, starting transfers between devices, move(): return lax.ppermute(block, 'leaf', [(i, i ^ flip) for i in range(count)])  7 us
    pallas_call x7, Pallas kernels, call(): pl.pallas_call(kernel, out_shape=[jax.ShapeDtypeStruct(shape, kind) for s...  6.41 us
    ppermute x9, waiting for transfers between devices, move(): return lax.ppermute(block, 'leaf', [(i, i ^ flip) for i in range(count)])  3.76 us
    unnamed x4, local copies, waits for them, and re-layouts  2.08 us
    ppermute x1, starting transfers between devices, body(): straight = lax.ppermute(send, 'leaf', far_pairs)  1.57 us
    concatenate x1, other arithmetic, body(): held = jnp.concatenate([key_states, value_states], 0)  0.88 us
    convert_element_type x1, other arithmetic, body(): lengths.astype(BF16)[:, None, None]  0.66 us
  transfers between devices with their start and end apart: 10, of which 7 were waited for; matrix products, arithmetic and copies ran while one was open for 4% of the time, Pallas kernels for 16%

profile of v12, /device:TPU:0, one launch (start us, length us, event | category | flops | bytes accessed | tf_op | source)
XLA Modules:
  0.0 23.2 jit_solution(2221838279538780714)
XLA Ops:
  0.6 0.7 %convert_element_type.3 = bf16[2]{0:T(256)(128)(2,1)S(1)} convert(s32[2]{0:T(128)} %param.9) | non-fusion elementwise | flops 2 | bytes 12 | tf_op jit(solution)/shard_map/convert_element_type | solution.py:368
  1.3 0.1 broadcast_in_dim.10.tails_ref
  1.4 0.5 %collective-permute-start.2 = (bf16[2,16,128]{2,1,0:T(8,128)(2,1)S(1)}, bf16[2,16,128]{2,1,0:T(8,128)(2,1)S(1)}, u32[]{:S(2)}, u32[]{:S(2)}) collective-permute-start(bf16[2,16,128]{2,1,0:T(8,128)(2,1)S(1)} %broadcast_in_dim.10.tails_ref), channel_id=1, source_target_pairs={{0,1},{1,0},{2,3},{3,2},{4,5},{5,4},{6,7},{7,6},{8,9},{9,8},{10,11... | collective-permute-start | bytes 24584 | tf_op jit(solution)/shard_map/ppermute | solution.py:361
  1.8 0.1 collective-permute-start
  1.9 0.4 %collective-permute-start.1 = (bf16[2,128,128]{2,1,0:T(8,128)(2,1)}, bf16[2,128,128]{2,1,0:T(8,128)(2,1)S(1)}, u32[]{:S(2)}, u32[]{:S(2)}) collective-permute-start(bf16[2,128,128]{2,1,0:T(8,128)(2,1)} %param.7), channel_id=1, source_target_pairs={{0,1},{1,0},{2,3},{3,2},{4,5},{5,4},{6,7},{7,6},{8,9},{9,8},{10,11... | collective-permute-start | bytes 196616 | tf_op jit(solution)/shard_map/ppermute | solution.py:361
  2.3 0.9 %pad_maximum_fusion.held_ref = bf16[4,128,128]{2,1,0:T(8,128)(2,1)S(1)} fusion(bf16[2,128,128]{2,1,0:T(8,128)(2,1)} %param.7, bf16[2,128,128]{2,1,0:T(8,128)(2,1)} %param.6), kind=kLoop, calls=%fused_computation | loop fusion | flops 65536 | bytes 262144 | tf_op jit(solution)/shard_map/concatenate | solution.py:370
  3.2 0.0 collective-permute-done.2.refs_2_
  3.2 0.1 collective-permute-done.refs_0_
  3.3 0.2 collective-permute-done.1.refs_1_
  3.5 3.9 %collective-permute-start.3 = (bf16[272,128]{1,0:T(8,128)(2,1)S(1)}, bf16[272,128]{1,0:T(8,128)(2,1)S(1)}, u32[]{:S(2)}, u32[]{:S(2)}) collective-permute-start(bf16[272,128]{1,0:T(8,128)(2,1)S(1)} %pad_maximum_fusion.1.refs_3_.pack_ref), channel_id=1, source_target_pairs={{0,6},{1,7},{2,4},{3,5},{4,2},{5,3},{6,0},{7,1},{8,14},{9,15},{10,... | collective-permute-start | bytes 208904 | tf_op jit(solution)/shard_map/ppermute | solution.py:361
  7.4 0.5 %collective-permute-start.4 = (bf16[272,128]{1,0:T(8,128)(2,1)S(1)}, bf16[272,128]{1,0:T(8,128)(2,1)S(1)}, u32[]{:S(2)}, u32[]{:S(2)}) collective-permute-start(bf16[272,128]{1,0:T(8,128)(2,1)S(1)} %pad_maximum_fusion.1.refs_3_.pack_ref), channel_id=1, source_target_pairs={{0,4},{1,5},{2,6},{3,7},{4,0},{5,1},{6,2},{7,3},{8,12},{9,13},{10,... | collective-permute-start | bytes 208904 | tf_op jit(solution)/shard_map/ppermute | solution.py:361
  7.9 0.1 collective-permute-start.5
  8.0 0.0 copy-start
  8.0 1.0 %copy-done = bf16[2,128,1024]{2,1,0:T(8,128)(2,1)S(1)} copy-done((bf16[2,128,1024]{2,1,0:T(8,128)(2,1)S(1)}, bf16[2,128,1024]{2,1,0:T(8,128)(2,1)}, u32[]{:S(2)}) %copy-start) | copy-done | bytes 524312
  9.1 0.0 copy-start.1
  9.1 1.0 %copy-done.1 = bf16[2,128,1024]{2,1,0:T(8,128)(2,1)S(1)} copy-done((bf16[2,128,1024]{2,1,0:T(8,128)(2,1)S(1)}, bf16[2,128,1024]{2,1,0:T(8,128)(2,1)}, u32[]{:S(2)}) %copy-start.1) | copy-done | bytes 524312
  10.1 1.5 %early.1 = (bf16[2048,128]{1,0:T(8,128)(2,1)S(1)}, bf16[2048,128]{1,0:T(8,128)(2,1)S(1)}, f32[384,2048]{1,0:T(8,128)S(1)}, f32[384,2048]{1,0:T(8,128)S(1)}, f32[...) custom-call(bf16[2,128,1024]{2,1,0:T(8,128)(2,1)S(1)} %copy-done, bf16[2,128,1024]{2,1,0:T(8,128)(2,1)S(1)} %copy-done.1, ...), custom_call_target="tpu_custom_call" | custom-call | flops 402653184 | bytes 1048576 | tf_op jit(solution)/shard_map/early/pallas_call | solution.py:51
  11.6 0.0 collective-permute-done.3.refs_0_
  11.6 0.1 collective-permute-done.4.refs_1_
  11.7 0.5 %collective-permute-done.5.refs_2_ = bf16[272,128]{1,0:T(8,128)(2,1)S(1)} collective-permute-done((bf16[272,128]{1,0:T(8,128)(2,1)S(1)}, bf16[272,128]{1,0:T(8,128)(2,1)S(1)}, u32[]{:S(2)}, u32[]{:S(2)}) %collective-permute-start.5) | collective-permute-done | bytes 69664 | tf_op jit(solution)/shard_map/ppermute | solution.py:361
  12.2 2.0 %middle.1 = (bf16[256,2048]{1,0:T(8,128)(2,1)S(1)}, f32[8,2048]{1,0:T(8,128)S(1)}, bf16[128,256]{1,0:T(8,128)(2,1)S(1)}, bf16[384,128]{1,0:T(8,128)(2,1)S(1)}, f32[384,128]{1,0:T(8,128)S(1)}) custom-call(bf16[2048,128]{1,0:T(8,128)(2,1)S(1)} %get-tuple-element.30.query_s, bf16[2048,128]{1,0:T(8,128)(2,1)S(1)} %get-tuple-element.31.cot_s, ...), custom_call_target="tpu_custom_call" | custom-call | flops 536870912 | bytes 1048576 | tf_op jit(solution)/shard_map/middle/pallas_call | solution.py:51
  14.2 0.1 collective-permute-start.6
  14.3 1.3 %collective-permute-done.6.other_ref.after_ref = bf16[384,128]{1,0:T(8,128)(2,1)S(1)} collective-permute-done((bf16[384,128]{1,0:T(8,128)(2,1)S(1)}, bf16[384,128]{1,0:T(8,128)(2,1)S(1)}, u32[]{:S(2)}, u32[]{:S(2)}) %collective-permute-start.6) | collective-permute-done | bytes 98336 | tf_op jit(solution)/shard_map/ppermute | solution.py:361
  15.6 1.6 %collective-permute-start.7 = (bf16[256,128]{1,0:T(8,128)(2,1)S(1)}, bf16[256,128]{1,0:T(8,128)(2,1)S(1)}, u32[]{:S(2)}, u32[]{:S(2)}) collective-permute-start(bf16[256,128]{1,0:T(8,128)(2,1)S(1)} %pair.2.after_ref), channel_id=1, source_target_pairs={{0,4},{4,0},{2,6},{6,2},{3,5},{5,7},{7,1},{1,3},{8,12},{12,8},{10,... | collective-permute-start | bytes 196616 | tf_op jit(solution)/shard_map/ppermute | solution.py:432
  17.2 1.4 %collective-permute-start.8 = (bf16[128,128]{1,0:T(8,128)(2,1)S(1)}, bf16[128,128]{1,0:T(8,128)(2,1)S(1)}, u32[]{:S(2)}, u32[]{:S(2)}) collective-permute-start(bf16[128,128]{1,0:T(8,128)(2,1)S(1)} %pair.3), channel_id=1, source_target_pairs={{0,2},{1,3},{2,0},{3,1},{4,6},{5,7},{6,4},{7,5},{8,10},{9,11},{10,... | collective-permute-start | bytes 98312 | tf_op jit(solution)/shard_map/ppermute | solution.py:361
  18.6 2.2 %late.1 = (bf16[2,128,1024]{2,1,0:T(8,128)(2,1)}, bf16[256,128]{1,0:T(8,128)(2,1)S(1)}, f32[256,128]{1,0:T(8,128)S(1)}, f32[256,128]{1,0:T(8,128)S(1)}) custom-call(bf16[2048,128]{1,0:T(8,128)(2,1)S(1)} %get-tuple-element.30.query_s, bf16[2048,128]{1,0:T(8,128)(2,1)S(1)} %get-tuple-element.31.cot_s, f32[384,2048]{1,0:T(8,128)S(1)} %get-tuple-element.32.raised_ref, ...), custom_call_target="tpu_custom_call" | custom-call | flops 805306368 | bytes 1048576 | tf_op jit(solution)/shard_map/late/pallas_call | solution.py:51
  20.8 0.4 %collective-permute-done.8.half_ref = bf16[128,128]{1,0:T(8,128)(2,1)S(1)} collective-permute-done((bf16[128,128]{1,0:T(8,128)(2,1)S(1)}, bf16[128,128]{1,0:T(8,128)(2,1)S(1)}, u32[]{:S(2)}, u32[]{:S(2)}) %collective-permute-start.8) | collective-permute-done | bytes 32800 | tf_op jit(solution)/shard_map/ppermute | solution.py:361
  21.2 0.0 collective-permute-done.7.arrived_ref
  21.3 0.1 collective-permute-start.9
  21.3 1.2 %collective-permute-done.9.other_ref = bf16[256,128]{1,0:T(8,128)(2,1)S(1)} collective-permute-done((bf16[256,128]{1,0:T(8,128)(2,1)S(1)}, bf16[256,128]{1,0:T(8,128)(2,1)S(1)}, u32[]{:S(2)}, u32[]{:S(2)}) %collective-permute-start.9) | collective-permute-done | bytes 65568 | tf_op jit(solution)/shard_map/ppermute | solution.py:361
  22.6 0.7 %final.1 = (bf16[2,128,128]{2,1,0:T(8,128)(2,1)}, bf16[2,128,128]{2,1,0:T(8,128)(2,1)}) custom-call(bf16[256,128]{1,0:T(8,128)(2,1)S(1)} %get-tuple-element.40.leaf_ref, f32[256,128]{1,0:T(8,128)S(1)} %get-tuple-element.45.keep_ref, bf16[256,128]{1,0:T(8,128)(2,1)S(1)} %collective-permute-done.9.other_ref), custom_call_target="tpu_custom_call" | custom-call | bytes 1048576 | tf_op jit(solution)/shard_map/final/pallas_call | solution.py:51
  (6 shorter events, 0.1 us)
Async XLA Ops:
  1.4 1.9 %collective-permute-start.2 = (bf16[2,16,128]{2,1,0:T(8,128)(2,1)S(1)}, bf16[2,16,128]{2,1,0:T(8,128)(2,1)S(1)}, u32[]{:S(2)}, u32[]{:S(2)}) collective-permute-start(bf16[2,16,128]{2,1,0:T(8,128)(2,1)S(1)} %broadcast_in_dim.10.tails_ref), channel_id=1, source_target_pairs={{0,1},{1,0},{2,3},{3,2},{4,5},{5,4},{6,7},{7,6},{8,9},{9,8},{10,11... | collective-permute-start | bytes 24584 | tf_op jit(solution)/shard_map/ppermute | solution.py:361
  1.8 1.5 %collective-permute-start = (bf16[2,128,128]{2,1,0:T(8,128)(2,1)}, bf16[2,128,128]{2,1,0:T(8,128)(2,1)S(1)}, u32[]{:S(2)}, u32[]{:S(2)}) collective-permute-start(bf16[2,128,128]{2,1,0:T(8,128)(2,1)} %param.6), channel_id=1, source_target_pairs={{0,1},{1,0},{2,3},{3,2},{4,5},{5,4},{6,7},{7,6},{8,9},{9,8},{10,11... | collective-permute-start | bytes 196616 | tf_op jit(solution)/shard_map/ppermute | solution.py:361
  1.9 1.5 %collective-permute-start.1 = (bf16[2,128,128]{2,1,0:T(8,128)(2,1)}, bf16[2,128,128]{2,1,0:T(8,128)(2,1)S(1)}, u32[]{:S(2)}, u32[]{:S(2)}) collective-permute-start(bf16[2,128,128]{2,1,0:T(8,128)(2,1)} %param.7), channel_id=1, source_target_pairs={{0,1},{1,0},{2,3},{3,2},{4,5},{5,4},{6,7},{7,6},{8,9},{9,8},{10,11... | collective-permute-start | bytes 196616 | tf_op jit(solution)/shard_map/ppermute | solution.py:361
  3.5 8.1 %collective-permute-start.3 = (bf16[272,128]{1,0:T(8,128)(2,1)S(1)}, bf16[272,128]{1,0:T(8,128)(2,1)S(1)}, u32[]{:S(2)}, u32[]{:S(2)}) collective-permute-start(bf16[272,128]{1,0:T(8,128)(2,1)S(1)} %pad_maximum_fusion.1.refs_3_.pack_ref), channel_id=1, source_target_pairs={{0,6},{1,7},{2,4},{3,5},{4,2},{5,3},{6,0},{7,1},{8,14},{9,15},{10,... | collective-permute-start | bytes 208904 | tf_op jit(solution)/shard_map/ppermute | solution.py:361
  7.4 4.3 %collective-permute-start.4 = (bf16[272,128]{1,0:T(8,128)(2,1)S(1)}, bf16[272,128]{1,0:T(8,128)(2,1)S(1)}, u32[]{:S(2)}, u32[]{:S(2)}) collective-permute-start(bf16[272,128]{1,0:T(8,128)(2,1)S(1)} %pad_maximum_fusion.1.refs_3_.pack_ref), channel_id=1, source_target_pairs={{0,4},{1,5},{2,6},{3,7},{4,0},{5,1},{6,2},{7,3},{8,12},{9,13},{10,... | collective-permute-start | bytes 208904 | tf_op jit(solution)/shard_map/ppermute | solution.py:361
  7.9 4.3 %collective-permute-start.5 = (bf16[272,128]{1,0:T(8,128)(2,1)S(1)}, bf16[272,128]{1,0:T(8,128)(2,1)S(1)}, u32[]{:S(2)}, u32[]{:S(2)}) collective-permute-start(bf16[272,128]{1,0:T(8,128)(2,1)S(1)} %pad_maximum_fusion.1.refs_3_.pack_ref), channel_id=1, source_target_pairs={{0,2},{1,3},{2,0},{3,1},{4,6},{5,7},{6,4},{7,5},{8,10},{9,11},{10,... | collective-permute-start | bytes 208904 | tf_op jit(solution)/shard_map/ppermute | solution.py:361
  8.0 1.0 %copy-start = (bf16[2,128,1024]{2,1,0:T(8,128)(2,1)S(1)}, bf16[2,128,1024]{2,1,0:T(8,128)(2,1)}, u32[]{:S(2)}) copy-start(bf16[2,128,1024]{2,1,0:T(8,128)(2,1)} %query_ref.1) | copy-start | bytes 1572868
  9.1 1.0 %copy-start.1 = (bf16[2,128,1024]{2,1,0:T(8,128)(2,1)S(1)}, bf16[2,128,1024]{2,1,0:T(8,128)(2,1)}, u32[]{:S(2)}) copy-start(bf16[2,128,1024]{2,1,0:T(8,128)(2,1)} %grad_ref.1) | copy-start | bytes 1572868
  14.2 1.4 %collective-permute-start.6 = (bf16[384,128]{1,0:T(8,128)(2,1)S(1)}, bf16[384,128]{1,0:T(8,128)(2,1)S(1)}, u32[]{:S(2)}, u32[]{:S(2)}) collective-permute-start(bf16[384,128]{1,0:T(8,128)(2,1)S(1)} %get-tuple-element.44), channel_id=1, source_target_pairs={{0,1},{1,0},{2,3},{3,2},{4,5},{5,4},{6,7},{7,6},{8,9},{9,8},{10,11... | collective-permute-start | bytes 294920 | tf_op jit(solution)/shard_map/ppermute | solution.py:361
  15.6 5.6 %collective-permute-start.7 = (bf16[256,128]{1,0:T(8,128)(2,1)S(1)}, bf16[256,128]{1,0:T(8,128)(2,1)S(1)}, u32[]{:S(2)}, u32[]{:S(2)}) collective-permute-start(bf16[256,128]{1,0:T(8,128)(2,1)S(1)} %pair.2.after_ref), channel_id=1, source_target_pairs={{0,4},{4,0},{2,6},{6,2},{3,5},{5,7},{7,1},{1,3},{8,12},{12,8},{10,... | collective-permute-start | bytes 196616 | tf_op jit(solution)/shard_map/ppermute | solution.py:432
  17.2 4.0 %collective-permute-start.8 = (bf16[128,128]{1,0:T(8,128)(2,1)S(1)}, bf16[128,128]{1,0:T(8,128)(2,1)S(1)}, u32[]{:S(2)}, u32[]{:S(2)}) collective-permute-start(bf16[128,128]{1,0:T(8,128)(2,1)S(1)} %pair.3), channel_id=1, source_target_pairs={{0,2},{1,3},{2,0},{3,1},{4,6},{5,7},{6,4},{7,5},{8,10},{9,11},{10,... | collective-permute-start | bytes 98312 | tf_op jit(solution)/shard_map/ppermute | solution.py:361
  21.3 1.3 %collective-permute-start.9 = (bf16[256,128]{1,0:T(8,128)(2,1)S(1)}, bf16[256,128]{1,0:T(8,128)(2,1)S(1)}, u32[]{:S(2)}, u32[]{:S(2)}) collective-permute-start(bf16[256,128]{1,0:T(8,128)(2,1)S(1)} %get-tuple-element.46), channel_id=1, source_target_pairs={{0,1},{1,0},{2,3},{3,2},{4,5},{5,4},{6,7},{7,6},{8,9},{9,8},{10,11... | collective-permute-start | bytes 196616 | tf_op jit(solution)/shard_map/ppermute | solution.py:361

commit v13 on v12

--- a/solution.py
+++ b/solution.py
@@ -12,6 +12,7 @@
 LOCAL = 3
 TAIL = 16
 BIG = -1e30
+FAR_PAIRS = [(0, 4), (4, 0), (2, 6), (6, 2), (3, 5), (5, 7), (7, 1), (1, 3)]
 LOG2E = 1.4426950408889634
 NT = (((1,), (1,)), ((), ()))
 NN = (((1,), (0,)), ((), ()))
@@ -86,9 +87,10 @@
     return raised, grad_weights, top, total, partial
 
 
-def early_kernel(depth, heads, query_ref, grad_ref, held_ref, tails_ref, *refs):
+def early_kernel(segment, heads, query_ref, grad_ref, held_ref, tails_ref, *refs):
     other_key_ref, other_value_ref, other_tails_ref, pack_ref = refs[:4]
     query_s, cot_s, raised_s, weights_s, stats_s, keys_s = refs[4:]
+    count = LOCAL - 1 + segment
     rows, width = held_ref.shape[1:]
     index = lax.axis_index("leaf")
     odd = index & 1 == 1
@@ -106,42 +108,38 @@
     masks = [
         [(length, no, odd), (even_length, odd, ~odd)],
         [(length, yes, no), (even_length, yes, no), (lengths[1], no, yes)],
+    ][segment]
+    wide = [
+        jnp.concatenate([block, mask_columns(*mask, rows, width)], 1)
+        for block, mask in zip(keys, masks)
     ]
-    wide = [
-        [
-            jnp.concatenate([block, mask_columns(*mask, rows, width)], 1)
-            for block, mask in zip(keys, masks[segment])
-        ]
-        for segment in range(2)
-    ]
-    for place in range(LOCAL):
+    for place in range(count):
         keys_s[place * rows : (place + 1) * rows, :] = keys[place]
     ruled = ruled_columns(rows, width)
-    for segment in range(2):
-        live = row.astype(F32) < lengths[segment]
-        for pair in range(heads // 2):
-            at = (segment * (heads // 2) + pair) * step
-            here = slice(at, at + step)
-            columns = [slice(h * width, (h + 1) * width) for h in (2 * pair, 2 * pair + 1)]
-            query = jnp.concatenate([query_ref[segment, :, c] for c in columns], 0)
-            cot = jnp.concatenate(
-                [jnp.where(live, grad_ref[segment, :, c], jnp.zeros((), BF16)) for c in columns], 0
+    live = row.astype(F32) < lengths[segment]
+    for pair in range(heads // 2):
+        here = slice(pair * step, (pair + 1) * step)
+        columns = [slice(h * width, (h + 1) * width) for h in (2 * pair, 2 * pair + 1)]
+        query = jnp.concatenate([query_ref[segment, :, c] for c in columns], 0)
+        cot = jnp.concatenate(
+            [jnp.where(live, grad_ref[segment, :, c], jnp.zeros((), BF16)) for c in columns], 0
+        )
+        query_s[here, :] = query
+        cot_s[here, :] = cot
+        query_wide = jnp.concatenate([query, ruled], 1)
+        for place in range(count):
+            span = slice(place * rows, (place + 1) * rows)
+            raised, grad_weights, top, total, partial = block_scores(
+                wide[place], values[place], query_wide, cot, factor
             )
-            query_s[here, :] = query
-            cot_s[here, :] = cot
-            query_wide = jnp.concatenate([query, ruled], 1)
-            for place in range(LOCAL - 1 + segment):
-                span = slice(place * rows, (place + 1) * rows)
-                raised, grad_weights, top, total, partial = block_scores(
-                    wide[segment][place], values[place], query_wide, cot, factor
-                )
-                raised_s[span, here] = raised
-                weights_s[span, here] = grad_weights
-                for n, line in enumerate((top, total, partial)):
-                    stats_s[3 * place + n : 3 * place + n + 1, here] = line
-
-
-def middle_kernel(depth, heads, query_s, cot_s, stats_ref, pack_ref, *refs):
+            raised_s[span, here] = raised
+            weights_s[span, here] = grad_weights
+            for n, line in enumerate((top, total, partial)):
+                stats_s[3 * place + n : 3 * place + n + 1, here] = line
+
+
+def middle_kernel(depth, heads, *refs):
+    queries, cots, stats, pack_ref, refs = refs[:2], refs[2:4], refs[4:6], refs[6], refs[7:]
     masks = (1 << (depth - 1)) - 1
     near, refs = refs[:masks], refs[masks:]
     ds_s, joined_s, keys_t = refs[:3]
@@ -160,11 +158,11 @@
     values = []
     wide = [[], []]
     if depth == 3:
-        far = (index >> 1) & 1 == 1
+        here = index & 1 == (index >> 1) & 1
         _, straight, across = leaving_levels(index)
         remote = [
-            (straight, jnp.where(far, near[0][...], near[1][...])),
-            (across, near[2][...]),
+            (straight, jnp.where(here, near[0][...], near[2][...])),
+            (across, near[1][...]),
         ]
     else:
         remote = []
@@ -191,14 +189,16 @@
         for pair in range(heads // 2):
             at = (segment * (heads // 2) + pair) * step
             here = slice(at, at + step)
-            query, cot = query_s[here, :], cot_s[here, :]
+            part = slice(pair * step, (pair + 1) * step)
+            query, cot = queries[segment][part, :], cots[segment][part, :]
+            stats_ref = stats[segment]
             query_wide = jnp.concatenate([query, ruled], 1)
             tops, totals, partials = [], [], []
             local = LOCAL - 1 + segment
             for place in range(local):
-                tops.append(stats_ref[3 * place : 3 * place + 1, here])
-                totals.append(stats_ref[3 * place + 1 : 3 * place + 2, here])
-                partials.append(stats_ref[3 * place + 2 : 3 * place + 3, here])
+                tops.append(stats_ref[3 * place : 3 * place + 1, part])
+                totals.append(stats_ref[3 * place + 1 : 3 * place + 2, part])
+                partials.append(stats_ref[3 * place + 2 : 3 * place + 3, part])
             for place in range(len(remote)):
                 span = slice(place * rows, (place + 1) * rows)
                 raised, grad_weights, top, total, partial = block_scores(
@@ -225,10 +225,10 @@
                 ds_s[span, here] = (weights * (weights_s[span, here] - delta)).astype(BF16)
         now = slice(segment * half, (segment + 1) * half)
         more_keys = lax.dot_general(
-            ds_s[:, now], query_s[now, :], NN, preferred_element_type=F32
+            ds_s[:, now], queries[segment][...], NN, preferred_element_type=F32
         )
         more_values = lax.dot_general(
-            low_s[:, now], cot_s[now, :], NN, preferred_element_type=F32
+            low_s[:, now], cots[segment][...], NN, preferred_element_type=F32
         )
         grad_keys = more_keys if segment == 0 else grad_keys + more_keys
         grad_values = more_values if segment == 0 else grad_values + more_values
@@ -251,7 +251,9 @@
         ref[...] = terms_s[jnp.clip(place, 0, depth - 2)].astype(BF16)
 
 
-def late_kernel(heads, query_s, cot_s, raised_ref, weights_ref, joined_ref, ds_ref, *refs):
+def late_kernel(heads, *refs):
+    queries, cots, raised, given, refs = refs[:2], refs[2:4], refs[4:6], refs[6:8], refs[8:]
+    joined_ref, ds_ref, refs = refs[0], refs[1], refs[2:]
     keys_t, keys_s, grad_query_ref, leaf_ref, last_ref, even_ref, low_s, ds_s = refs
     width = keys_s.shape[1]
     rows = keys_s.shape[0] // LOCAL
@@ -264,12 +266,13 @@
         for pair in range(heads // 2):
             at = (segment * (heads // 2) + pair) * step
             here = slice(at, at + step)
+            part = slice(pair * step, (pair + 1) * step)
             delta = joined_ref[0:1, here]
             for place in range(LOCAL - 1 + segment):
                 span = slice(place * rows, (place + 1) * rows)
-                weights = raised_ref[span, here] * joined_ref[1 + place : 2 + place, here]
+                weights = raised[segment][span, part] * joined_ref[1 + place : 2 + place, here]
                 low_s[span, here] = weights.astype(BF16)
-                ds_s[span, here] = (weights * (weights_ref[span, here] - delta)).astype(BF16)
+                ds_s[span, here] = (weights * (given[segment][span, part] - delta)).astype(BF16)
             grad_query = lax.dot_general(
                 keys_t[...], ds_ref[:, here], NN, preferred_element_type=F32
             ) + lax.dot_general(
@@ -280,21 +283,26 @@
                 c = slice((2 * pair + n) * width, (2 * pair + n + 1) * width)
                 grad_query_ref[segment, :, c] = grad_query[n * rows : (n + 1) * rows]
     inner = (LOCAL - 1) * rows
-    grad_keys = scale * lax.dot_general(
-        ds_s[:inner, :], query_s[...], NN, preferred_element_type=F32
-    )
-    grad_values = lax.dot_general(
-        low_s[:inner, :], cot_s[...], NN, preferred_element_type=F32
-    )
+
+    def terms(block, sides):
+        return sum(
+            lax.dot_general(
+                block[:inner, n * half : (n + 1) * half], side[...], NN, preferred_element_type=F32
+            )
+            for n, side in enumerate(sides)
+        )
+
+    grad_keys = scale * terms(ds_s, queries)
+    grad_values = terms(low_s, cots)
     for place, ref in enumerate((last_ref, even_ref)):
         span = slice(place * rows, (place + 1) * rows)
         ref[:rows, :] = grad_keys[span]
         ref[rows:, :] = grad_values[span]
     leaf_keys = scale * lax.dot_general(
-        ds_s[inner:, half:], query_s[half:, :], NN, preferred_element_type=F32
+        ds_s[inner:, half:], queries[1][...], NN, preferred_element_type=F32
     )
     leaf_values = lax.dot_general(
-        low_s[inner:, half:], cot_s[half:, :], NN, preferred_element_type=F32
+        low_s[inner:, half:], cots[1][...], NN, preferred_element_type=F32
     )
     leaf_ref[:rows, :] = leaf_keys.astype(BF16)
     leaf_ref[rows:, :] = leaf_values.astype(BF16)
@@ -380,25 +388,36 @@
         ],
         0,
     )
+    def early(segment, even_pack):
+        held_rows = (LOCAL - 1 + segment) * rows
+        arrays = (queries, grad_output, held, tails, other_keys, other_values, other_tails)
+        return call(
+            functools.partial(early_kernel, segment, heads),
+            "early",
+            12,
+            arrays + (even_pack,),
+            [
+                ((total // 2, width), BF16),
+                ((total // 2, width), BF16),
+                ((held_rows, total // 2), F32),
+                ((held_rows, total // 2), F32),
+                ((16, total // 2), F32),
+                ((held_rows, width), BF16),
+            ],
+            flops=2 * held_rows * total * width,
+        )
+
     if depth == 3:
-        near = [move(pack, flip) for flip in (6, 4, 2)]
+        far = lax.ppermute(pack, "leaf", [(b, a) for a, b in FAR_PAIRS])
+        along_x = move(pack, 2)
+        first = early(0, pack)
+        pack, far, first = lax.optimization_barrier((pack, far, first))
+        near = [far, along_x, move(far, 1)]
     else:
         near = exchange({m: pack for m in masks})
-    query_rows, cot, raised, weights, stats, last_keys = call(
-        functools.partial(early_kernel, depth, heads),
-        "early",
-        12,
-        (queries, grad_output, held, tails, other_keys, other_values, other_tails, pack),
-        [
-            ((total, width), BF16),
-            ((total, width), BF16),
-            ((local, total), F32),
-            ((local, total), F32),
-            ((16, total), F32),
-            ((local, width), BF16),
-        ],
-        flops=4 * local * total * width,
-    )
+        first = early(0, pack)
+    sides = [first, early(1, pack)]
+    query_rows, cots, raised, weights, stats, held_keys = zip(*sides)
     if depth == 3:
         leaving = [((3 * rows, width), BF16), ((3 * rows, width), F32)]
     else:
@@ -407,7 +426,7 @@
         functools.partial(middle_kernel, depth, heads),
         "middle",
         24,
-        (query_rows, cot, stats, pack, *near),
+        (*query_rows, *cots, *stats, pack, *near),
         [
             ((inner, total), BF16),
             ((8, total), F32),
@@ -428,8 +447,7 @@
         send = call(
             functools.partial(pair_kernel, 0), "pair", 2, (hold, other, other), [(terms, BF16)]
         )[0]
-        far_pairs = [(0, 4), (4, 0), (2, 6), (6, 2), (3, 5), (5, 7), (7, 1), (1, 3)]
-        straight = lax.ppermute(send, "leaf", far_pairs)
+        straight = lax.ppermute(send, "leaf", FAR_PAIRS)
         half = call(
             functools.partial(pair_kernel, 2 * rows), "pair", 2, (hold, other, send),
             [((rows, width), BF16)],
@@ -443,7 +461,7 @@
         functools.partial(late_kernel, heads),
         "late",
         12,
-        (query_rows, cot, raised, weights, joined, ds, keys_t, last_keys),
+        (*query_rows, *cots, *raised, *weights, joined, ds, keys_t, held_keys[1]),
         [((2, rows, heads * width), BF16), (terms, BF16), (terms, F32), (terms, F32)],
         scratch=[((local, total), BF16), ((local, total), BF16)],
         flops=8 * local * total * width,

time: 23.5 us -> 23 us (0.979)
  starting transfers between devices: 8.57 us -> 7.79 us
  Pallas kernels: 6.41 us -> 6.85 us
    ppermute x9 -> x8, starting transfers between devices: 7 us -> 4.31 us  [move(): return lax.ppermute(block, 'leaf', [(i, i ^ flip) for i in range(count)])]
    ppermute x1 -> x2, starting transfers between devices: 1.57 us -> 3.47 us  [the longest x1 2.92 us: body(): far = lax.ppermute(pack, 'leaf', [(b, a) for a, b in FAR_PAIRS])]
    ppermute x9 -> x8, waiting for transfers between devices: 3.76 us -> 3.17 us  [move(): return lax.ppermute(block, 'leaf', [(i, i ^ flip) for i in range(count)])]
    ppermute x1 -> x2, waiting for transfers between devices: 0.01 us -> 0.47 us  [the longest x1 0.47 us: body(): straight = lax.ppermute(send, 'leaf', FAR_PAIRS)]
    pallas_call x7 -> x8, Pallas kernels: 6.41 us -> 6.85 us  [call(): pl.pallas_call(kernel, out_shape=[jax.ShapeDtypeStruct(shape, kind) for s...]
  transfers between devices with their start and end apart: 10 -> 10, of which waited for: 7 -> 7; matrix products, arithmetic and copies ran while one was open for 4% -> 4% of each run, Pallas kernels for 16% -> 18%
where the time goes in v13:
time: 23 us; the launch traced here: 22.8 us
  starting transfers between devices  7.79 us (34%)
  Pallas kernels  6.85 us (30%)
  waiting for transfers between devices  3.64 us (16%)
  local copies, waits for them, and re-layouts  2.16 us (9%)
  other arithmetic  1.61 us (7%)
  between operations  0.72 us (3%)
    pallas_call x8, Pallas kernels, call(): pl.pallas_call(kernel, out_shape=[jax.ShapeDtypeStruct(shape, kind) for s...  6.85 us
    ppermute x8, starting transfers between devices, move(): return lax.ppermute(block, 'leaf', [(i, i ^ flip) for i in range(count)])  4.31 us
    ppermute x8, waiting for transfers between devices, move(): return lax.ppermute(block, 'leaf', [(i, i ^ flip) for i in range(count)])  3.17 us
    ppermute x1, starting transfers between devices, body(): far = lax.ppermute(pack, 'leaf', [(b, a) for a, b in FAR_PAIRS])  2.92 us
    unnamed x4, local copies, waits for them, and re-layouts  2.08 us
    concatenate x1, other arithmetic, body(): held = jnp.concatenate([key_states, value_states], 0)  0.88 us
    convert_element_type x1, other arithmetic, body(): lengths.astype(BF16)[:, None, None]  0.66 us
    ppermute x1, starting transfers between devices, body(): straight = lax.ppermute(send, 'leaf', FAR_PAIRS)  0.56 us
  transfers between devices with their start and end apart: 10, of which 7 were waited for; matrix products, arithmetic and copies ran while one was open for 4% of the time, Pallas kernels for 18%

profile of v13, /device:TPU:0, one launch (start us, length us, event | category | flops | bytes accessed | tf_op | source)
XLA Modules:
  0.0 22.8 jit_solution(1219812603312839066)
XLA Ops:
  0.6 0.7 %convert_element_type.3 = bf16[2]{0:T(256)(128)(2,1)S(1)} convert(s32[2]{0:T(128)} %param.9) | non-fusion elementwise | flops 2 | bytes 12 | tf_op jit(solution)/shard_map/convert_element_type | solution.py:376
  1.3 0.1 broadcast_in_dim.10.tails_ref
  1.4 0.5 %collective-permute-start.2 = (bf16[2,16,128]{2,1,0:T(8,128)(2,1)S(1)}, bf16[2,16,128]{2,1,0:T(8,128)(2,1)S(1)}, u32[]{:S(2)}, u32[]{:S(2)}) collective-permute-start(bf16[2,16,128]{2,1,0:T(8,128)(2,1)S(1)} %broadcast_in_dim.10.tails_ref), channel_id=1, source_target_pairs={{0,1},{1,0},{2,3},{3,2},{4,5},{5,4},{6,7},{7,6},{8,9},{9,8},{10,11... | collective-permute-start | bytes 24584 | tf_op jit(solution)/shard_map/ppermute | solution.py:369
  1.8 0.1 collective-permute-start
  1.9 0.4 %collective-permute-start.1 = (bf16[2,128,128]{2,1,0:T(8,128)(2,1)}, bf16[2,128,128]{2,1,0:T(8,128)(2,1)S(1)}, u32[]{:S(2)}, u32[]{:S(2)}) collective-permute-start(bf16[2,128,128]{2,1,0:T(8,128)(2,1)} %param.7), channel_id=1, source_target_pairs={{0,1},{1,0},{2,3},{3,2},{4,5},{5,4},{6,7},{7,6},{8,9},{9,8},{10,11... | collective-permute-start | bytes 196616 | tf_op jit(solution)/shard_map/ppermute | solution.py:369
  2.3 0.9 %pad_maximum_fusion.held_ref = bf16[4,128,128]{2,1,0:T(8,128)(2,1)S(1)} fusion(bf16[2,128,128]{2,1,0:T(8,128)(2,1)} %param.7, bf16[2,128,128]{2,1,0:T(8,128)(2,1)} %param.6), kind=kLoop, calls=%fused_computation | loop fusion | flops 65536 | bytes 262144 | tf_op jit(solution)/shard_map/concatenate | solution.py:378
  3.2 0.0 collective-permute-done.2.refs_2_
  3.2 0.1 collective-permute-done.refs_0_
  3.3 0.2 collective-permute-done.1.refs_1_
  3.5 2.9 %collective-permute-start.3 = (bf16[272,128]{1,0:T(8,128)(2,1)S(1)}, bf16[272,128]{1,0:T(8,128)(2,1)S(1)}, u32[]{:S(2)}, u32[]{:S(2)}) collective-permute-start(bf16[272,128]{1,0:T(8,128)(2,1)S(1)} %pad_maximum_fusion.1.refs_3_.refs_6_), channel_id=1, source_target_pairs={{4,0},{0,4},{6,2},{2,6},{5,3},{7,5},{1,7},{3,1},{12,8},{8,12},{14,... | collective-permute-start | bytes 208904 | tf_op jit(solution)/shard_map/ppermute | solution.py:411
  6.4 1.5 %collective-permute-start.4 = (bf16[272,128]{1,0:T(8,128)(2,1)S(1)}, bf16[272,128]{1,0:T(8,128)(2,1)S(1)}, u32[]{:S(2)}, u32[]{:S(2)}) collective-permute-start(bf16[272,128]{1,0:T(8,128)(2,1)S(1)} %pad_maximum_fusion.1.refs_3_.refs_6_), channel_id=1, source_target_pairs={{0,2},{1,3},{2,0},{3,1},{4,6},{5,7},{6,4},{7,5},{8,10},{9,11},{10,... | collective-permute-start | bytes 208904 | tf_op jit(solution)/shard_map/ppermute | solution.py:369
  7.9 0.0 copy-start
  7.9 1.0 %copy-done = bf16[2,128,1024]{2,1,0:T(8,128)(2,1)S(1)} copy-done((bf16[2,128,1024]{2,1,0:T(8,128)(2,1)S(1)}, bf16[2,128,1024]{2,1,0:T(8,128)(2,1)}, u32[]{:S(2)}) %copy-start) | copy-done | bytes 524312
  9.0 0.0 copy-start.1
  9.0 1.0 %copy-done.1 = bf16[2,128,1024]{2,1,0:T(8,128)(2,1)S(1)} copy-done((bf16[2,128,1024]{2,1,0:T(8,128)(2,1)S(1)}, bf16[2,128,1024]{2,1,0:T(8,128)(2,1)}, u32[]{:S(2)}) %copy-start.1) | copy-done | bytes 524312
  10.0 1.0 %early.2 = (bf16[1024,128]{1,0:T(8,128)(2,1)S(1)}, bf16[1024,128]{1,0:T(8,128)(2,1)S(1)}, f32[256,1024]{1,0:T(8,128)S(1)}, f32[256,1024]{1,0:T(8,128)S(1)}, f32[...) custom-call(bf16[2,128,1024]{2,1,0:T(8,128)(2,1)S(1)} %copy-done, bf16[2,128,1024]{2,1,0:T(8,128)(2,1)S(1)} %copy-done.1, ...), custom_call_target="tpu_custom_call" | custom-call | flops 134217728 | bytes 1048576 | tf_op jit(solution)/shard_map/early/pallas_call | solution.py:52
  11.0 0.0 collective-permute-done.3.refs_7_
  11.0 0.0 collective-permute-start.5
  11.0 0.9 %early.3 = (bf16[1024,128]{1,0:T(8,128)(2,1)S(1)}, bf16[1024,128]{1,0:T(8,128)(2,1)S(1)}, f32[384,1024]{1,0:T(8,128)S(1)}, f32[384,1024]{1,0:T(8,128)S(1)}, f32[...) custom-call(bf16[2,128,1024]{2,1,0:T(8,128)(2,1)S(1)} %copy-done, bf16[2,128,1024]{2,1,0:T(8,128)(2,1)S(1)} %copy-done.1, ...), custom_call_target="tpu_custom_call" | custom-call | flops 201326592 | bytes 1048576 | tf_op jit(solution)/shard_map/early/pallas_call | solution.py:52
  12.0 0.0 collective-permute-done.4.refs_8_
  12.0 0.3 %collective-permute-done.5.refs_9_ = bf16[272,128]{1,0:T(8,128)(2,1)S(1)} collective-permute-done((bf16[272,128]{1,0:T(8,128)(2,1)S(1)}, bf16[272,128]{1,0:T(8,128)(2,1)S(1)}, u32[]{:S(2)}, u32[]{:S(2)}) %collective-permute-start.5) | collective-permute-done | bytes 69664 | tf_op jit(solution)/shard_map/ppermute | solution.py:369
  12.3 2.0 %middle.1 = (bf16[256,2048]{1,0:T(8,128)(2,1)S(1)}, f32[8,2048]{1,0:T(8,128)S(1)}, bf16[128,256]{1,0:T(8,128)(2,1)S(1)}, bf16[384,128]{1,0:T(8,128)(2,1)S(1)}, f32[384,128]{1,0:T(8,128)S(1)}) custom-call(bf16[1024,128]{1,0:T(8,128)(2,1)S(1)} %get-tuple-element.47.refs_0_, bf16[1024,128]{1,0:T(8,128)(2,1)S(1)} %get-tuple-element.49.refs_1_, ...), custom_call_target="tpu_custom_call" | custom-call | flops 536870912 | bytes 1048576 | tf_op jit(solution)/shard_map/middle/pallas_call | solution.py:52
  14.3 0.3 %collective-permute-start.6 = (bf16[384,128]{1,0:T(8,128)(2,1)S(1)}, bf16[384,128]{1,0:T(8,128)(2,1)S(1)}, u32[]{:S(2)}, u32[]{:S(2)}) collective-permute-start(bf16[384,128]{1,0:T(8,128)(2,1)S(1)} %get-tuple-element.68), channel_id=1, source_target_pairs={{0,1},{1,0},{2,3},{3,2},{4,5},{5,4},{6,7},{7,6},{8,9},{9,8},{10,11... | collective-permute-start | bytes 294920 | tf_op jit(solution)/shard_map/ppermute | solution.py:369
  14.6 1.1 %collective-permute-done.6.other_ref.after_ref = bf16[384,128]{1,0:T(8,128)(2,1)S(1)} collective-permute-done((bf16[384,128]{1,0:T(8,128)(2,1)S(1)}, bf16[384,128]{1,0:T(8,128)(2,1)S(1)}, u32[]{:S(2)}, u32[]{:S(2)}) %collective-permute-start.6) | collective-permute-done | bytes 98336 | tf_op jit(solution)/shard_map/ppermute | solution.py:369
  15.7 0.6 %collective-permute-start.7 = (bf16[256,128]{1,0:T(8,128)(2,1)S(1)}, bf16[256,128]{1,0:T(8,128)(2,1)S(1)}, u32[]{:S(2)}, u32[]{:S(2)}) collective-permute-start(bf16[256,128]{1,0:T(8,128)(2,1)S(1)} %pair.2.after_ref), channel_id=1, source_target_pairs={{0,4},{4,0},{2,6},{6,2},{3,5},{5,7},{7,1},{1,3},{8,12},{12,8},{10,... | collective-permute-start | bytes 196616 | tf_op jit(solution)/shard_map/ppermute | solution.py:450
  16.3 1.5 %collective-permute-start.8 = (bf16[128,128]{1,0:T(8,128)(2,1)S(1)}, bf16[128,128]{1,0:T(8,128)(2,1)S(1)}, u32[]{:S(2)}, u32[]{:S(2)}) collective-permute-start(bf16[128,128]{1,0:T(8,128)(2,1)S(1)} %pair.3), channel_id=1, source_target_pairs={{0,2},{1,3},{2,0},{3,1},{4,6},{5,7},{6,4},{7,5},{8,10},{9,11},{10,... | collective-permute-start | bytes 98312 | tf_op jit(solution)/shard_map/ppermute | solution.py:369
  17.8 2.2 %late.1 = (bf16[2,128,1024]{2,1,0:T(8,128)(2,1)}, bf16[256,128]{1,0:T(8,128)(2,1)S(1)}, f32[256,128]{1,0:T(8,128)S(1)}, f32[256,128]{1,0:T(8,128)S(1)}) custom-call(bf16[1024,128]{1,0:T(8,128)(2,1)S(1)} %get-tuple-element.47.refs_0_, bf16[1024,128]{1,0:T(8,128)(2,1)S(1)} %get-tuple-element.49.refs_1_, bf16[1024,128]{1,0:T(8,128)(2,1)S(1)} %get-tuple-element.50.refs_2_, ...), custom_call_target="tpu_custom_call" | custom-call | flops 805306368 | bytes 1048576 | tf_op jit(solution)/shard_map/late/pallas_call | solution.py:52
  19.9 0.3 %collective-permute-done.8.half_ref = bf16[128,128]{1,0:T(8,128)(2,1)S(1)} collective-permute-done((bf16[128,128]{1,0:T(8,128)(2,1)S(1)}, bf16[128,128]{1,0:T(8,128)(2,1)S(1)}, u32[]{:S(2)}, u32[]{:S(2)}) %collective-permute-start.8) | collective-permute-done | bytes 32800 | tf_op jit(solution)/shard_map/ppermute | solution.py:369
  20.3 0.5 %collective-permute-done.7.arrived_ref = bf16[256,128]{1,0:T(8,128)(2,1)S(1)} collective-permute-done((bf16[256,128]{1,0:T(8,128)(2,1)S(1)}, bf16[256,128]{1,0:T(8,128)(2,1)S(1)}, u32[]{:S(2)}, u32[]{:S(2)}) %collective-permute-start.7) | collective-permute-done | bytes 65568 | tf_op jit(solution)/shard_map/ppermute | solution.py:450
  20.8 0.1 collective-permute-start.9
  20.8 1.2 %collective-permute-done.9.other_ref = bf16[256,128]{1,0:T(8,128)(2,1)S(1)} collective-permute-done((bf16[256,128]{1,0:T(8,128)(2,1)S(1)}, bf16[256,128]{1,0:T(8,128)(2,1)S(1)}, u32[]{:S(2)}, u32[]{:S(2)}) %collective-permute-start.9) | collective-permute-done | bytes 65568 | tf_op jit(solution)/shard_map/ppermute | solution.py:369
  22.1 0.7 %final.1 = (bf16[2,128,128]{2,1,0:T(8,128)(2,1)}, bf16[2,128,128]{2,1,0:T(8,128)(2,1)}) custom-call(bf16[256,128]{1,0:T(8,128)(2,1)S(1)} %get-tuple-element.64.leaf_ref, f32[256,128]{1,0:T(8,128)S(1)} %get-tuple-element.69.keep_ref, bf16[256,128]{1,0:T(8,128)(2,1)S(1)} %collective-permute-done.9.other_ref), custom_call_target="tpu_custom_call" | custom-call | bytes 1048576 | tf_op jit(solution)/shard_map/final/pallas_call | solution.py:52
  (6 shorter events, 0.1 us)
Async XLA Ops:
  1.4 1.9 %collective-permute-start.2 = (bf16[2,16,128]{2,1,0:T(8,128)(2,1)S(1)}, bf16[2,16,128]{2,1,0:T(8,128)(2,1)S(1)}, u32[]{:S(2)}, u32[]{:S(2)}) collective-permute-start(bf16[2,16,128]{2,1,0:T(8,128)(2,1)S(1)} %broadcast_in_dim.10.tails_ref), channel_id=1, source_target_pairs={{0,1},{1,0},{2,3},{3,2},{4,5},{5,4},{6,7},{7,6},{8,9},{9,8},{10,11... | collective-permute-start | bytes 24584 | tf_op jit(solution)/shard_map/ppermute | solution.py:369
  1.8 1.5 %collective-permute-start = (bf16[2,128,128]{2,1,0:T(8,128)(2,1)}, bf16[2,128,128]{2,1,0:T(8,128)(2,1)S(1)}, u32[]{:S(2)}, u32[]{:S(2)}) collective-permute-start(bf16[2,128,128]{2,1,0:T(8,128)(2,1)} %param.6), channel_id=1, source_target_pairs={{0,1},{1,0},{2,3},{3,2},{4,5},{5,4},{6,7},{7,6},{8,9},{9,8},{10,11... | collective-permute-start | bytes 196616 | tf_op jit(solution)/shard_map/ppermute | solution.py:369
  1.9 1.5 %collective-permute-start.1 = (bf16[2,128,128]{2,1,0:T(8,128)(2,1)}, bf16[2,128,128]{2,1,0:T(8,128)(2,1)S(1)}, u32[]{:S(2)}, u32[]{:S(2)}) collective-permute-start(bf16[2,128,128]{2,1,0:T(8,128)(2,1)} %param.7), channel_id=1, source_target_pairs={{0,1},{1,0},{2,3},{3,2},{4,5},{5,4},{6,7},{7,6},{8,9},{9,8},{10,11... | collective-permute-start | bytes 196616 | tf_op jit(solution)/shard_map/ppermute | solution.py:369
  3.5 7.5 %collective-permute-start.3 = (bf16[272,128]{1,0:T(8,128)(2,1)S(1)}, bf16[272,128]{1,0:T(8,128)(2,1)S(1)}, u32[]{:S(2)}, u32[]{:S(2)}) collective-permute-start(bf16[272,128]{1,0:T(8,128)(2,1)S(1)} %pad_maximum_fusion.1.refs_3_.refs_6_), channel_id=1, source_target_pairs={{4,0},{0,4},{6,2},{2,6},{5,3},{7,5},{1,7},{3,1},{12,8},{8,12},{14,... | collective-permute-start | bytes 208904 | tf_op jit(solution)/shard_map/ppermute | solution.py:411
  6.4 5.5 %collective-permute-start.4 = (bf16[272,128]{1,0:T(8,128)(2,1)S(1)}, bf16[272,128]{1,0:T(8,128)(2,1)S(1)}, u32[]{:S(2)}, u32[]{:S(2)}) collective-permute-start(bf16[272,128]{1,0:T(8,128)(2,1)S(1)} %pad_maximum_fusion.1.refs_3_.refs_6_), channel_id=1, source_target_pairs={{0,2},{1,3},{2,0},{3,1},{4,6},{5,7},{6,4},{7,5},{8,10},{9,11},{10,... | collective-permute-start | bytes 208904 | tf_op jit(solution)/shard_map/ppermute | solution.py:369
  7.9 1.0 %copy-start = (bf16[2,128,1024]{2,1,0:T(8,128)(2,1)S(1)}, bf16[2,128,1024]{2,1,0:T(8,128)(2,1)}, u32[]{:S(2)}) copy-start(bf16[2,128,1024]{2,1,0:T(8,128)(2,1)} %query_ref.3) | copy-start | bytes 1572868
  9.0 1.0 %copy-start.1 = (bf16[2,128,1024]{2,1,0:T(8,128)(2,1)S(1)}, bf16[2,128,1024]{2,1,0:T(8,128)(2,1)}, u32[]{:S(2)}) copy-start(bf16[2,128,1024]{2,1,0:T(8,128)(2,1)} %grad_ref.3) | copy-start | bytes 1572868
  11.0 1.3 %collective-permute-start.5 = (bf16[272,128]{1,0:T(8,128)(2,1)S(1)}, bf16[272,128]{1,0:T(8,128)(2,1)S(1)}, u32[]{:S(2)}, u32[]{:S(2)}) collective-permute-start(bf16[272,128]{1,0:T(8,128)(2,1)S(1)} %collective-permute-done.3.refs_7_), channel_id=1, source_target_pairs={{0,1},{1,0},{2,3},{3,2},{4,5},{5,4},{6,7},{7,6},{8,9},{9,8},{10,11... | collective-permute-start | bytes 208904 | tf_op jit(solution)/shard_map/ppermute | solution.py:369
  14.3 1.4 %collective-permute-start.6 = (bf16[384,128]{1,0:T(8,128)(2,1)S(1)}, bf16[384,128]{1,0:T(8,128)(2,1)S(1)}, u32[]{:S(2)}, u32[]{:S(2)}) collective-permute-start(bf16[384,128]{1,0:T(8,128)(2,1)S(1)} %get-tuple-element.68), channel_id=1, source_target_pairs={{0,1},{1,0},{2,3},{3,2},{4,5},{5,4},{6,7},{7,6},{8,9},{9,8},{10,11... | collective-permute-start | bytes 294920 | tf_op jit(solution)/shard_map/ppermute | solution.py:369
  15.7 5.0 %collective-permute-start.7 = (bf16[256,128]{1,0:T(8,128)(2,1)S(1)}, bf16[256,128]{1,0:T(8,128)(2,1)S(1)}, u32[]{:S(2)}, u32[]{:S(2)}) collective-permute-start(bf16[256,128]{1,0:T(8,128)(2,1)S(1)} %pair.2.after_ref), channel_id=1, source_target_pairs={{0,4},{4,0},{2,6},{6,2},{3,5},{5,7},{7,1},{1,3},{8,12},{12,8},{10,... | collective-permute-start | bytes 196616 | tf_op jit(solution)/shard_map/ppermute | solution.py:450
  16.3 4.0 %collective-permute-start.8 = (bf16[128,128]{1,0:T(8,128)(2,1)S(1)}, bf16[128,128]{1,0:T(8,128)(2,1)S(1)}, u32[]{:S(2)}, u32[]{:S(2)}) collective-permute-start(bf16[128,128]{1,0:T(8,128)(2,1)S(1)} %pair.3), channel_id=1, source_target_pairs={{0,2},{1,3},{2,0},{3,1},{4,6},{5,7},{6,4},{7,5},{8,10},{9,11},{10,... | collective-permute-start | bytes 98312 | tf_op jit(solution)/shard_map/ppermute | solution.py:369
  20.8 1.3 %collective-permute-start.9 = (bf16[256,128]{1,0:T(8,128)(2,1)S(1)}, bf16[256,128]{1,0:T(8,128)(2,1)S(1)}, u32[]{:S(2)}, u32[]{:S(2)}) collective-permute-start(bf16[256,128]{1,0:T(8,128)(2,1)S(1)} %get-tuple-element.70), channel_id=1, source_target_pairs={{0,1},{1,0},{2,3},{3,2},{4,5},{5,4},{6,7},{7,6},{8,9},{9,8},{10,11... | collective-permute-start | bytes 196616 | tf_op jit(solution)/shard_map/ppermute | solution.py:369

commit v14 on v13

--- a/solution.py
+++ b/solution.py
@@ -87,9 +87,17 @@
     return raised, grad_weights, top, total, partial
 
 
+def pack_kernel(held_ref, tails_ref, key_ref, value_ref, other_tails_ref, pack_ref):
+    rows = key_ref.shape[1]
+    odd = lax.axis_index("leaf") & 1 == 1
+    pack_ref[:rows, :] = jnp.where(odd, key_ref[0], held_ref[0])
+    pack_ref[rows : 2 * rows, :] = jnp.where(odd, value_ref[0], held_ref[2])
+    pack_ref[2 * rows :, :] = jnp.where(odd, other_tails_ref[0], tails_ref[0])
+
+
 def early_kernel(segment, heads, query_ref, grad_ref, held_ref, tails_ref, *refs):
     other_key_ref, other_value_ref, other_tails_ref, pack_ref = refs[:4]
-    query_s, cot_s, raised_s, weights_s, stats_s, keys_s = refs[4:]
+    query_s, cot_s, raised_s, weights_s, stats_s = refs[4:9]
     count = LOCAL - 1 + segment
     rows, width = held_ref.shape[1:]
     index = lax.axis_index("leaf")
@@ -113,8 +121,9 @@
         jnp.concatenate([block, mask_columns(*mask, rows, width)], 1)
         for block, mask in zip(keys, masks)
     ]
-    for place in range(count):
-        keys_s[place * rows : (place + 1) * rows, :] = keys[place]
+    for keys_s in refs[9:]:
+        for place in range(count):
+            keys_s[place * rows : (place + 1) * rows, :] = keys[place]
     ruled = ruled_columns(rows, width)
     live = row.astype(F32) < lengths[segment]
     for pair in range(heads // 2):
@@ -251,18 +260,15 @@
         ref[...] = terms_s[jnp.clip(place, 0, depth - 2)].astype(BF16)
 
 
-def late_kernel(heads, *refs):
+def local_kernel(heads, *refs):
     queries, cots, raised, given, refs = refs[:2], refs[2:4], refs[4:6], refs[6:8], refs[8:]
-    joined_ref, ds_ref, refs = refs[0], refs[1], refs[2:]
-    keys_t, keys_s, grad_query_ref, leaf_ref, last_ref, even_ref, low_s, ds_s = refs
-    width = keys_s.shape[1]
-    rows = keys_s.shape[0] // LOCAL
+    joined_ref, ds_s, leaf_ref, last_ref, even_ref, low_s = refs
+    width = leaf_ref.shape[1]
+    rows = leaf_ref.shape[0] // 2
     scale = width ** (-0.5)
     step = 2 * rows
     half = heads * rows
-    near_t = keys_s[...].T
     for segment in range(2):
-        count = (LOCAL - 1 + segment) * rows
         for pair in range(heads // 2):
             at = (segment * (heads // 2) + pair) * step
             here = slice(at, at + step)
@@ -273,15 +279,6 @@
                 weights = raised[segment][span, part] * joined_ref[1 + place : 2 + place, here]
                 low_s[span, here] = weights.astype(BF16)
                 ds_s[span, here] = (weights * (given[segment][span, part] - delta)).astype(BF16)
-            grad_query = lax.dot_general(
-                keys_t[...], ds_ref[:, here], NN, preferred_element_type=F32
-            ) + lax.dot_general(
-                near_t[:, :count], ds_s[:count, here], NN, preferred_element_type=F32
-            )
-            grad_query = (grad_query * scale).astype(BF16).T
-            for n in range(2):
-                c = slice((2 * pair + n) * width, (2 * pair + n + 1) * width)
-                grad_query_ref[segment, :, c] = grad_query[n * rows : (n + 1) * rows]
     inner = (LOCAL - 1) * rows
 
     def terms(block, sides):
@@ -306,6 +303,28 @@
     )
     leaf_ref[:rows, :] = leaf_keys.astype(BF16)
     leaf_ref[rows:, :] = leaf_values.astype(BF16)
+
+
+def late_kernel(heads, ds_ref, local_ref, keys_t, keys_s, grad_query_ref):
+    width = keys_s.shape[1]
+    rows = keys_s.shape[0] // LOCAL
+    scale = width ** (-0.5)
+    step = 2 * rows
+    near_t = keys_s[...].T
+    for segment in range(2):
+        count = (LOCAL - 1 + segment) * rows
+        for pair in range(heads // 2):
+            at = (segment * (heads // 2) + pair) * step
+            here = slice(at, at + step)
+            grad_query = lax.dot_general(
+                keys_t[...], ds_ref[:, here], NN, preferred_element_type=F32
+            ) + lax.dot_general(
+                near_t[:, :count], local_ref[:count, here], NN, preferred_element_type=F32
+            )
+            grad_query = (grad_query * scale).astype(BF16).T
+            for n in range(2):
+                c = slice((2 * pair + n) * width, (2 * pair + n + 1) * width)
+                grad_query_ref[segment, :, c] = grad_query[n * rows : (n + 1) * rows]
 
 
 def leaving_levels(index):
@@ -379,15 +398,15 @@
     held, other_keys, other_values, other_tails = lax.optimization_barrier(
         (held, other_keys, other_values, other_tails)
     )
-    odd = lax.axis_index("leaf") & 1 == 1
-    pack = jnp.concatenate(
-        [
-            jnp.where(odd, other_keys[0], held[0]),
-            jnp.where(odd, other_values[0], held[2]),
-            jnp.where(odd, other_tails[0], tails[0]),
-        ],
-        0,
-    )
+    pack = call(
+        pack_kernel,
+        "pack",
+        1,
+        (held, tails, other_keys, other_values, other_tails),
+        [((2 * rows + TAIL, width), BF16)],
+        flops=1 << 32,
+    )[0]
+
     def early(segment, even_pack):
         held_rows = (LOCAL - 1 + segment) * rows
         arrays = (queries, grad_output, held, tails, other_keys, other_values, other_tails)
@@ -402,8 +421,8 @@
                 ((held_rows, total // 2), F32),
                 ((held_rows, total // 2), F32),
                 ((16, total // 2), F32),
-                ((held_rows, width), BF16),
-            ],
+            ]
+            + [((held_rows, width), BF16)] * segment,
             flops=2 * held_rows * total * width,
         )
 
@@ -416,8 +435,8 @@
     else:
         near = exchange({m: pack for m in masks})
         first = early(0, pack)
-    sides = [first, early(1, pack)]
-    query_rows, cots, raised, weights, stats, held_keys = zip(*sides)
+    *second, held_keys = early(1, pack)
+    query_rows, cots, raised, weights, stats = zip(first, second)
     if depth == 3:
         leaving = [((3 * rows, width), BF16), ((3 * rows, width), F32)]
     else:
@@ -441,9 +460,20 @@
         ],
         flops=8 * inner * total * width,
     )
+    local_ds, leaf, last_part, even_part = call(
+        functools.partial(local_kernel, heads),
+        "local",
+        12,
+        (*query_rows, *cots, *raised, *weights, joined),
+        [((local, total), BF16), (terms, BF16), (terms, F32), (terms, F32)],
+        scratch=[((local, total), BF16)],
+        flops=4 * local * total * width,
+    )
     if depth == 3:
         swap, hold = sends
-        other = move(swap, 1)
+        other, leaf, last_part, even_part, local_ds = lax.optimization_barrier(
+            (move(swap, 1), leaf, last_part, even_part, local_ds)
+        )
         send = call(
             functools.partial(pair_kernel, 0), "pair", 2, (hold, other, other), [(terms, BF16)]
         )[0]
@@ -457,14 +487,13 @@
     else:
         arrived = exchange(dict(zip(masks, sends)))
         fold = functools.partial(fold_kernel, depth)
-    grad_queries, leaf, last_part, even_part = call(
+    (grad_queries,) = call(
         functools.partial(late_kernel, heads),
         "late",
-        12,
-        (*query_rows, *cots, *raised, *weights, joined, ds, keys_t, held_keys[1]),
-        [((2, rows, heads * width), BF16), (terms, BF16), (terms, F32), (terms, F32)],
-        scratch=[((local, total), BF16), ((local, total), BF16)],
-        flops=8 * local * total * width,
+        8,
+        (ds, local_ds, keys_t, held_keys),
+        [((2, rows, heads * width), BF16)],
+        flops=2 * (local + inner) * total * width,
     )
     keep, send = call(
         fold,

time: 23 us -> 22.1 us (0.961)
  local copies, waits for them, and re-layouts: 2.16 us -> 0.09 us
  starting transfers between devices: 7.79 us -> 8.56 us
  waiting for transfers between devices: 3.64 us -> 4.12 us
    unnamed x4, local copies, waits for them, and re-layouts: 2.08 us -> 0.01 us
    ppermute x8, waiting for transfers between devices: 3.17 us -> 3.99 us  [move(): return lax.ppermute(block, 'leaf', [(i, i ^ flip) for i in range(count)])]
    ppermute x8, starting transfers between devices: 4.31 us -> 4.92 us  [move(): return lax.ppermute(block, 'leaf', [(i, i ^ flip) for i in range(count)])]
    ppermute x1, waiting for transfers between devices: 0.47 us -> 0.08 us  [body(): straight = lax.ppermute(send, 'leaf', FAR_PAIRS)]
    pallas_call x8 -> x10, Pallas kernels: 6.85 us -> 6.88 us  [call(): pl.pallas_call(kernel, out_shape=[jax.ShapeDtypeStruct(shape, kind) for s...]
  transfers between devices with their start and end apart: 10 -> 10, of which waited for: 7 -> 6; matrix products, arithmetic and copies ran while one was open for 4% -> 4% of each run, Pallas kernels for 18% -> 19%
where the time goes in v14:
time: 22.1 us; the launch traced here: 21.9 us
  starting transfers between devices  8.56 us (39%)
  Pallas kernels  6.88 us (31%)
  waiting for transfers between devices  4.12 us (19%)
  other arithmetic  1.54 us (7%)
  between operations  0.72 us (3%)
    pallas_call x10, Pallas kernels, call(): pl.pallas_call(kernel, out_shape=[jax.ShapeDtypeStruct(shape, kind) for s...  6.88 us
    ppermute x8, starting transfers between devices, move(): return lax.ppermute(block, 'leaf', [(i, i ^ flip) for i in range(count)])  4.92 us
    ppermute x8, waiting for transfers between devices, move(): return lax.ppermute(block, 'leaf', [(i, i ^ flip) for i in range(count)])  3.99 us
    ppermute x1, starting transfers between devices, body(): far = lax.ppermute(pack, 'leaf', [(b, a) for a, b in FAR_PAIRS])  2.92 us
    concatenate x1, other arithmetic, body(): held = jnp.concatenate([key_states, value_states], 0)  0.88 us
    ppermute x1, starting transfers between devices, body(): straight = lax.ppermute(send, 'leaf', FAR_PAIRS)  0.73 us
    convert_element_type x1, other arithmetic, body(): lengths.astype(BF16)[:, None, None]  0.66 us
  transfers between devices with their start and end apart: 10, of which 6 were waited for; matrix products, arithmetic and copies ran while one was open for 4% of the time, Pallas kernels for 19%

profile of v14, /device:TPU:0, one launch (start us, length us, event | category | flops | bytes accessed | tf_op | source)
XLA Modules:
  0.0 21.9 jit_solution(10102248700878712400)
XLA Ops:
  0.6 0.7 %convert_element_type.3 = bf16[2]{0:T(256)(128)(2,1)S(1)} convert(s32[2]{0:T(128)} %param.9) | non-fusion elementwise | flops 2 | bytes 12 | tf_op jit(solution)/shard_map/convert_element_type | solution.py:395
  1.3 0.1 broadcast_in_dim.2.tails_ref
  1.4 0.5 %collective-permute-start.2 = (bf16[2,16,128]{2,1,0:T(8,128)(2,1)S(1)}, bf16[2,16,128]{2,1,0:T(8,128)(2,1)S(1)}, u32[]{:S(2)}, u32[]{:S(2)}) collective-permute-start(bf16[2,16,128]{2,1,0:T(8,128)(2,1)S(1)} %broadcast_in_dim.2.tails_ref), channel_id=1, source_target_pairs={{0,1},{1,0},{2,3},{3,2},{4,5},{5,4},{6,7},{7,6},{8,9},{9,8},{10,11... | collective-permute-start | bytes 24584 | tf_op jit(solution)/shard_map/ppermute | solution.py:388
  1.8 0.1 collective-permute-start
  1.9 0.4 %collective-permute-start.1 = (bf16[2,128,128]{2,1,0:T(8,128)(2,1)}, bf16[2,128,128]{2,1,0:T(8,128)(2,1)S(1)}, u32[]{:S(2)}, u32[]{:S(2)}) collective-permute-start(bf16[2,128,128]{2,1,0:T(8,128)(2,1)} %param.7), channel_id=1, source_target_pairs={{0,1},{1,0},{2,3},{3,2},{4,5},{5,4},{6,7},{7,6},{8,9},{9,8},{10,11... | collective-permute-start | bytes 196616 | tf_op jit(solution)/shard_map/ppermute | solution.py:388
  2.3 0.9 %pad_maximum_fusion.held_ref = bf16[4,128,128]{2,1,0:T(8,128)(2,1)S(1)} fusion(bf16[2,128,128]{2,1,0:T(8,128)(2,1)} %param.7, bf16[2,128,128]{2,1,0:T(8,128)(2,1)} %param.6), kind=kLoop, calls=%fused_computation | loop fusion | flops 65536 | bytes 262144 | tf_op jit(solution)/shard_map/concatenate | solution.py:397
  3.2 0.0 copy-start
  3.2 0.0 copy-start.1
  3.2 0.0 collective-permute-done.2.other_tails_ref.refs_2_
  3.3 0.0 collective-permute-done.key_ref.refs_0_
  3.3 0.2 collective-permute-done.1.value_ref.refs_1_
  3.5 2.9 %collective-permute-start.3 = (bf16[272,128]{1,0:T(8,128)(2,1)S(1)}, bf16[272,128]{1,0:T(8,128)(2,1)S(1)}, u32[]{:S(2)}, u32[]{:S(2)}) collective-permute-start(bf16[272,128]{1,0:T(8,128)(2,1)S(1)} %pack.1.refs_3_.refs_6_), channel_id=1, source_target_pairs={{4,0},{0,4},{6,2},{2,6},{5,3},{7,5},{1,7},{3,1},{12,8},{8,12},{14,... | collective-permute-start | bytes 208904 | tf_op jit(solution)/shard_map/ppermute | solution.py:430
  6.4 1.5 %collective-permute-start.4 = (bf16[272,128]{1,0:T(8,128)(2,1)S(1)}, bf16[272,128]{1,0:T(8,128)(2,1)S(1)}, u32[]{:S(2)}, u32[]{:S(2)}) collective-permute-start(bf16[272,128]{1,0:T(8,128)(2,1)S(1)} %pack.1.refs_3_.refs_6_), channel_id=1, source_target_pairs={{0,2},{1,3},{2,0},{3,1},{4,6},{5,7},{6,4},{7,5},{8,10},{9,11},{10,... | collective-permute-start | bytes 208904 | tf_op jit(solution)/shard_map/ppermute | solution.py:388
  7.9 0.0 copy-done
  7.9 0.7 %early.2 = (bf16[1024,128]{1,0:T(8,128)(2,1)S(1)}, bf16[1024,128]{1,0:T(8,128)(2,1)S(1)}, f32[256,1024]{1,0:T(8,128)S(1)}, f32[256,1024]{1,0:T(8,128)S(1)}, f32[16,1024]{1,0:T(8,128)S(1)}) custom-call(bf16[2,128,1024]{2,1,0:T(8,128)(2,1)S(1)} %copy-done, bf16[2,128,1024]{2,1,0:T(8,128)(2,1)S(1)} %copy-done.1, ...), custom_call_target="tpu_custom_call" | custom-call | flops 134217728 | bytes 1048576 | tf_op jit(solution)/shard_map/early/pallas_call | solution.py:52
  8.6 0.1 collective-permute-done.3.refs_7_
  8.7 0.0 collective-permute-start.5
  8.7 0.9 %early.3 = (bf16[1024,128]{1,0:T(8,128)(2,1)S(1)}, bf16[1024,128]{1,0:T(8,128)(2,1)S(1)}, f32[384,1024]{1,0:T(8,128)S(1)}, f32[384,1024]{1,0:T(8,128)S(1)}, f32[...) custom-call(bf16[2,128,1024]{2,1,0:T(8,128)(2,1)S(1)} %copy-done, bf16[2,128,1024]{2,1,0:T(8,128)(2,1)S(1)} %copy-done.1, ...), custom_call_target="tpu_custom_call" | custom-call | flops 201326592 | bytes 1048576 | tf_op jit(solution)/shard_map/early/pallas_call | solution.py:52
  9.7 1.6 %collective-permute-done.4.refs_8_ = bf16[272,128]{1,0:T(8,128)(2,1)S(1)} collective-permute-done((bf16[272,128]{1,0:T(8,128)(2,1)S(1)}, bf16[272,128]{1,0:T(8,128)(2,1)S(1)}, u32[]{:S(2)}, u32[]{:S(2)}) %collective-permute-start.4) | collective-permute-done | bytes 69664 | tf_op jit(solution)/shard_map/ppermute | solution.py:388
  11.3 0.0 collective-permute-done.5.refs_9_
  11.3 2.0 %middle.1 = (bf16[256,2048]{1,0:T(8,128)(2,1)S(1)}, f32[8,2048]{1,0:T(8,128)S(1)}, bf16[128,256]{1,0:T(8,128)(2,1)S(1)}, bf16[384,128]{1,0:T(8,128)(2,1)S(1)}, f32[384,128]{1,0:T(8,128)S(1)}) custom-call(bf16[1024,128]{1,0:T(8,128)(2,1)S(1)} %get-tuple-element.52.refs_0_, bf16[1024,128]{1,0:T(8,128)(2,1)S(1)} %get-tuple-element.54.refs_1_, ...), custom_call_target="tpu_custom_call" | custom-call | flops 536870912 | bytes 1048576 | tf_op jit(solution)/shard_map/middle/pallas_call | solution.py:52
  13.3 0.1 collective-permute-start.6
  13.4 1.0 %local.1 = (bf16[384,2048]{1,0:T(8,128)(2,1)S(1)}, bf16[256,128]{1,0:T(8,128)(2,1)S(1)}, f32[256,128]{1,0:T(8,128)S(1)}, f32[256,128]{1,0:T(8,128)S(1)}) custom-call(bf16[1024,128]{1,0:T(8,128)(2,1)S(1)} %get-tuple-element.52.refs_0_, bf16[1024,128]{1,0:T(8,128)(2,1)S(1)} %get-tuple-element.54.refs_1_, bf16[1024,128]{1,0:T(8,128)(2,1)S(1)} %get-tuple-element.55.refs_2_, ...), custom_call_target="tpu_custom_call" | custom-call | flops 402653184 | bytes 1048576 | tf_op jit(solution)/shard_map/local/pallas_call | solution.py:52
  14.4 0.3 %collective-permute-done.6.other_ref.after_ref = bf16[384,128]{1,0:T(8,128)(2,1)S(1)} collective-permute-done((bf16[384,128]{1,0:T(8,128)(2,1)S(1)}, bf16[384,128]{1,0:T(8,128)(2,1)S(1)}, u32[]{:S(2)}, u32[]{:S(2)}) %collective-permute-start.6) | collective-permute-done | bytes 98336 | tf_op jit(solution)/shard_map/ppermute | solution.py:388
  14.7 0.7 %collective-permute-start.7 = (bf16[256,128]{1,0:T(8,128)(2,1)S(1)}, bf16[256,128]{1,0:T(8,128)(2,1)S(1)}, u32[]{:S(2)}, u32[]{:S(2)}) collective-permute-start(bf16[256,128]{1,0:T(8,128)(2,1)S(1)} %pair.2.after_ref), channel_id=1, source_target_pairs={{0,4},{4,0},{2,6},{6,2},{3,5},{5,7},{7,1},{1,3},{8,12},{12,8},{10,... | collective-permute-start | bytes 196616 | tf_op jit(solution)/shard_map/ppermute | solution.py:480
  15.4 2.3 %collective-permute-start.8 = (bf16[128,128]{1,0:T(8,128)(2,1)S(1)}, bf16[128,128]{1,0:T(8,128)(2,1)S(1)}, u32[]{:S(2)}, u32[]{:S(2)}) collective-permute-start(bf16[128,128]{1,0:T(8,128)(2,1)S(1)} %pair.3), channel_id=1, source_target_pairs={{0,2},{1,3},{2,0},{3,1},{4,6},{5,7},{6,4},{7,5},{8,10},{9,11},{10,... | collective-permute-start | bytes 98312 | tf_op jit(solution)/shard_map/ppermute | solution.py:388
  17.7 1.9 %collective-permute-done.8.half_ref = bf16[128,128]{1,0:T(8,128)(2,1)S(1)} collective-permute-done((bf16[128,128]{1,0:T(8,128)(2,1)S(1)}, bf16[128,128]{1,0:T(8,128)(2,1)S(1)}, u32[]{:S(2)}, u32[]{:S(2)}) %collective-permute-start.8) | collective-permute-done | bytes 32800 | tf_op jit(solution)/shard_map/ppermute | solution.py:388
  19.6 0.1 collective-permute-done.7.arrived_ref
  19.8 0.1 collective-permute-start.9
  19.8 1.4 %late.1 = bf16[2,128,1024]{2,1,0:T(8,128)(2,1)} custom-call(bf16[256,2048]{1,0:T(8,128)(2,1)S(1)} %get-tuple-element.60.ds_ref, bf16[384,2048]{1,0:T(8,128)(2,1)S(1)} %get-tuple-element.71.local_ref, bf16[128,256]{1,0:T(8,128)(2,1)S(1)} %get-tuple-element.72.keys_t, bf16[384,128]{1,0:T(8,128)(2,1)S(1)} %get-tuple-element.73.keys_s), custom_call_target="tpu_custom_call" | custom-call | flops 335544320 | bytes 1048576 | tf_op jit(solution)/shard_map/late/pallas_call | solution.py:52
  21.2 0.0 collective-permute-done.9.other_ref
  21.3 0.7 %final.1 = (bf16[2,128,128]{2,1,0:T(8,128)(2,1)}, bf16[2,128,128]{2,1,0:T(8,128)(2,1)}) custom-call(bf16[256,128]{1,0:T(8,128)(2,1)S(1)} %get-tuple-element.74.leaf_ref, f32[256,128]{1,0:T(8,128)S(1)} %get-tuple-element.79.keep_ref, bf16[256,128]{1,0:T(8,128)(2,1)S(1)} %collective-permute-done.9.other_ref), custom_call_target="tpu_custom_call" | custom-call | bytes 1048576 | tf_op jit(solution)/shard_map/final/pallas_call | solution.py:52
  (5 shorter events, 0.1 us)
Async XLA Ops:
  1.4 1.9 %collective-permute-start.2 = (bf16[2,16,128]{2,1,0:T(8,128)(2,1)S(1)}, bf16[2,16,128]{2,1,0:T(8,128)(2,1)S(1)}, u32[]{:S(2)}, u32[]{:S(2)}) collective-permute-start(bf16[2,16,128]{2,1,0:T(8,128)(2,1)S(1)} %broadcast_in_dim.2.tails_ref), channel_id=1, source_target_pairs={{0,1},{1,0},{2,3},{3,2},{4,5},{5,4},{6,7},{7,6},{8,9},{9,8},{10,11... | collective-permute-start | bytes 24584 | tf_op jit(solution)/shard_map/ppermute | solution.py:388
  1.8 1.5 %collective-permute-start = (bf16[2,128,128]{2,1,0:T(8,128)(2,1)}, bf16[2,128,128]{2,1,0:T(8,128)(2,1)S(1)}, u32[]{:S(2)}, u32[]{:S(2)}) collective-permute-start(bf16[2,128,128]{2,1,0:T(8,128)(2,1)} %param.6), channel_id=1, source_target_pairs={{0,1},{1,0},{2,3},{3,2},{4,5},{5,4},{6,7},{7,6},{8,9},{9,8},{10,11... | collective-permute-start | bytes 196616 | tf_op jit(solution)/shard_map/ppermute | solution.py:388
  1.9 1.5 %collective-permute-start.1 = (bf16[2,128,128]{2,1,0:T(8,128)(2,1)}, bf16[2,128,128]{2,1,0:T(8,128)(2,1)S(1)}, u32[]{:S(2)}, u32[]{:S(2)}) collective-permute-start(bf16[2,128,128]{2,1,0:T(8,128)(2,1)} %param.7), channel_id=1, source_target_pairs={{0,1},{1,0},{2,3},{3,2},{4,5},{5,4},{6,7},{7,6},{8,9},{9,8},{10,11... | collective-permute-start | bytes 196616 | tf_op jit(solution)/shard_map/ppermute | solution.py:388
  3.2 4.7 %copy-start = (bf16[2,128,1024]{2,1,0:T(8,128)(2,1)S(1)}, bf16[2,128,1024]{2,1,0:T(8,128)(2,1)}, u32[]{:S(2)}) copy-start(bf16[2,128,1024]{2,1,0:T(8,128)(2,1)} %query_ref.3) | copy-start | bytes 1572868
  3.2 4.7 %copy-start.1 = (bf16[2,128,1024]{2,1,0:T(8,128)(2,1)S(1)}, bf16[2,128,1024]{2,1,0:T(8,128)(2,1)}, u32[]{:S(2)}) copy-start(bf16[2,128,1024]{2,1,0:T(8,128)(2,1)} %grad_ref.3) | copy-start | bytes 1572868
  3.5 5.2 %collective-permute-start.3 = (bf16[272,128]{1,0:T(8,128)(2,1)S(1)}, bf16[272,128]{1,0:T(8,128)(2,1)S(1)}, u32[]{:S(2)}, u32[]{:S(2)}) collective-permute-start(bf16[272,128]{1,0:T(8,128)(2,1)S(1)} %pack.1.refs_3_.refs_6_), channel_id=1, source_target_pairs={{4,0},{0,4},{6,2},{2,6},{5,3},{7,5},{1,7},{3,1},{12,8},{8,12},{14,... | collective-permute-start | bytes 208904 | tf_op jit(solution)/shard_map/ppermute | solution.py:430
  6.4 4.9 %collective-permute-start.4 = (bf16[272,128]{1,0:T(8,128)(2,1)S(1)}, bf16[272,128]{1,0:T(8,128)(2,1)S(1)}, u32[]{:S(2)}, u32[]{:S(2)}) collective-permute-start(bf16[272,128]{1,0:T(8,128)(2,1)S(1)} %pack.1.refs_3_.refs_6_), channel_id=1, source_target_pairs={{0,2},{1,3},{2,0},{3,1},{4,6},{5,7},{6,4},{7,5},{8,10},{9,11},{10,... | collective-permute-start | bytes 208904 | tf_op jit(solution)/shard_map/ppermute | solution.py:388
  8.7 2.6 %collective-permute-start.5 = (bf16[272,128]{1,0:T(8,128)(2,1)S(1)}, bf16[272,128]{1,0:T(8,128)(2,1)S(1)}, u32[]{:S(2)}, u32[]{:S(2)}) collective-permute-start(bf16[272,128]{1,0:T(8,128)(2,1)S(1)} %collective-permute-done.3.refs_7_), channel_id=1, source_target_pairs={{0,1},{1,0},{2,3},{3,2},{4,5},{5,4},{6,7},{7,6},{8,9},{9,8},{10,11... | collective-permute-start | bytes 208904 | tf_op jit(solution)/shard_map/ppermute | solution.py:388
  13.3 1.4 %collective-permute-start.6 = (bf16[384,128]{1,0:T(8,128)(2,1)S(1)}, bf16[384,128]{1,0:T(8,128)(2,1)S(1)}, u32[]{:S(2)}, u32[]{:S(2)}) collective-permute-start(bf16[384,128]{1,0:T(8,128)(2,1)S(1)} %get-tuple-element.61), channel_id=1, source_target_pairs={{0,1},{1,0},{2,3},{3,2},{4,5},{5,4},{6,7},{7,6},{8,9},{9,8},{10,11... | collective-permute-start | bytes 294920 | tf_op jit(solution)/shard_map/ppermute | solution.py:388
  14.7 5.0 %collective-permute-start.7 = (bf16[256,128]{1,0:T(8,128)(2,1)S(1)}, bf16[256,128]{1,0:T(8,128)(2,1)S(1)}, u32[]{:S(2)}, u32[]{:S(2)}) collective-permute-start(bf16[256,128]{1,0:T(8,128)(2,1)S(1)} %pair.2.after_ref), channel_id=1, source_target_pairs={{0,4},{4,0},{2,6},{6,2},{3,5},{5,7},{7,1},{1,3},{8,12},{12,8},{10,... | collective-permute-start | bytes 196616 | tf_op jit(solution)/shard_map/ppermute | solution.py:480
  15.4 4.2 %collective-permute-start.8 = (bf16[128,128]{1,0:T(8,128)(2,1)S(1)}, bf16[128,128]{1,0:T(8,128)(2,1)S(1)}, u32[]{:S(2)}, u32[]{:S(2)}) collective-permute-start(bf16[128,128]{1,0:T(8,128)(2,1)S(1)} %pair.3), channel_id=1, source_target_pairs={{0,2},{1,3},{2,0},{3,1},{4,6},{5,7},{6,4},{7,5},{8,10},{9,11},{10,... | collective-permute-start | bytes 98312 | tf_op jit(solution)/shard_map/ppermute | solution.py:388
  19.8 1.5 %collective-permute-start.9 = (bf16[256,128]{1,0:T(8,128)(2,1)S(1)}, bf16[256,128]{1,0:T(8,128)(2,1)S(1)}, u32[]{:S(2)}, u32[]{:S(2)}) collective-permute-start(bf16[256,128]{1,0:T(8,128)(2,1)S(1)} %get-tuple-element.80), channel_id=1, source_target_pairs={{0,1},{1,0},{2,3},{3,2},{4,5},{5,4},{6,7},{7,6},{8,9},{9,8},{10,11... | collective-permute-start | bytes 196616 | tf_op jit(solution)/shard_map/ppermute | solution.py:388

commit v15 on v14

--- a/solution.py
+++ b/solution.py
@@ -337,7 +337,7 @@
     out_ref[...] = (hold_ref[span, :] + other_ref[span, :].astype(F32)).astype(BF16)
 
 
-def gather_kernel(even_ref, last_ref, arrived_ref, half_ref, keep_ref, send_ref):
+def gather_kernel(even_ref, last_ref, half_ref, arrived_ref, keep_ref, send_ref):
     rows = half_ref.shape[0]
     index = lax.axis_index("leaf")
     odd, near = index & 1 == 1, (index >> 1) & 1 == 0
@@ -474,15 +474,15 @@
         other, leaf, last_part, even_part, local_ds = lax.optimization_barrier(
             (move(swap, 1), leaf, last_part, even_part, local_ds)
         )
-        send = call(
-            functools.partial(pair_kernel, 0), "pair", 2, (hold, other, other), [(terms, BF16)]
-        )[0]
-        straight = lax.ppermute(send, "leaf", FAR_PAIRS)
         half = call(
-            functools.partial(pair_kernel, 2 * rows), "pair", 2, (hold, other, send),
+            functools.partial(pair_kernel, 2 * rows), "pair", 2, (hold, other, other),
             [((rows, width), BF16)],
         )[0]
-        arrived = [straight, move(half, 2)]
+        half_arrived = move(half, 2)
+        send = call(
+            functools.partial(pair_kernel, 0), "pair", 2, (hold, other, half), [(terms, BF16)]
+        )[0]
+        arrived = [half_arrived, lax.ppermute(send, "leaf", FAR_PAIRS)]
         fold = gather_kernel
     else:
         arrived = exchange(dict(zip(masks, sends)))
@@ -495,6 +495,7 @@
         [((2, rows, heads * width), BF16)],
         flops=2 * (local + inner) * total * width,
     )
+    grad_queries, arrived[1] = lax.optimization_barrier((grad_queries, arrived[1]))
     keep, send = call(
         fold,
         "fold",

time: 22.1 us -> 21.9 us (level)
    ppermute x8, waiting for transfers between devices: 3.99 us -> 3.35 us  [move(): return lax.ppermute(block, 'leaf', [(i, i ^ flip) for i in range(count)])]
    ppermute x1, waiting for transfers between devices: 0.08 us -> 0.63 us  [body(): arrived = [half_arrived, lax.ppermute(send, 'leaf', FAR_PAIRS)]]
where the time goes in v15:
time: 21.9 us; the launch traced here: 21.8 us
  starting transfers between devices  8.5 us (39%)
  Pallas kernels  6.86 us (31%)
  waiting for transfers between devices  4.04 us (18%)
  other arithmetic  1.54 us (7%)
  between operations  0.73 us (3%)
    pallas_call x10, Pallas kernels, call(): pl.pallas_call(kernel, out_shape=[jax.ShapeDtypeStruct(shape, kind) for s...  6.86 us
    ppermute x8, starting transfers between devices, move(): return lax.ppermute(block, 'leaf', [(i, i ^ flip) for i in range(count)])  4.86 us
    ppermute x8, waiting for transfers between devices, move(): return lax.ppermute(block, 'leaf', [(i, i ^ flip) for i in range(count)])  3.35 us
    ppermute x1, starting transfers between devices, body(): far = lax.ppermute(pack, 'leaf', [(b, a) for a, b in FAR_PAIRS])  2.92 us
    concatenate x1, other arithmetic, body(): held = jnp.concatenate([key_states, value_states], 0)  0.88 us
    ppermute x1, starting transfers between devices, body(): arrived = [half_arrived, lax.ppermute(send, 'leaf', FAR_PAIRS)]  0.73 us
    convert_element_type x1, other arithmetic, body(): lengths.astype(BF16)[:, None, None]  0.66 us
    ppermute x1, waiting for transfers between devices, body(): arrived = [half_arrived, lax.ppermute(send, 'leaf', FAR_PAIRS)]  0.63 us
  transfers between devices with their start and end apart: 10, of which 6 were waited for; matrix products, arithmetic and copies ran while one was open for 4% of the time, Pallas kernels for 19%

profile of v15, /device:TPU:0, one launch (start us, length us, event | category | flops | bytes accessed | tf_op | source)
XLA Modules:
  0.0 21.8 jit_solution(3963718195027119980)
XLA Ops:
  0.6 0.7 %convert_element_type.3 = bf16[2]{0:T(256)(128)(2,1)S(1)} convert(s32[2]{0:T(128)} %param.9) | non-fusion elementwise | flops 2 | bytes 12 | tf_op jit(solution)/shard_map/convert_element_type | solution.py:395
  1.3 0.1 broadcast_in_dim.2.tails_ref
  1.4 0.5 %collective-permute-start.2 = (bf16[2,16,128]{2,1,0:T(8,128)(2,1)S(1)}, bf16[2,16,128]{2,1,0:T(8,128)(2,1)S(1)}, u32[]{:S(2)}, u32[]{:S(2)}) collective-permute-start(bf16[2,16,128]{2,1,0:T(8,128)(2,1)S(1)} %broadcast_in_dim.2.tails_ref), channel_id=1, source_target_pairs={{0,1},{1,0},{2,3},{3,2},{4,5},{5,4},{6,7},{7,6},{8,9},{9,8},{10,11... | collective-permute-start | bytes 24584 | tf_op jit(solution)/shard_map/ppermute | solution.py:388
  1.8 0.1 collective-permute-start
  1.9 0.4 %collective-permute-start.1 = (bf16[2,128,128]{2,1,0:T(8,128)(2,1)}, bf16[2,128,128]{2,1,0:T(8,128)(2,1)S(1)}, u32[]{:S(2)}, u32[]{:S(2)}) collective-permute-start(bf16[2,128,128]{2,1,0:T(8,128)(2,1)} %param.7), channel_id=1, source_target_pairs={{0,1},{1,0},{2,3},{3,2},{4,5},{5,4},{6,7},{7,6},{8,9},{9,8},{10,11... | collective-permute-start | bytes 196616 | tf_op jit(solution)/shard_map/ppermute | solution.py:388
  2.3 0.9 %pad_maximum_fusion.held_ref = bf16[4,128,128]{2,1,0:T(8,128)(2,1)S(1)} fusion(bf16[2,128,128]{2,1,0:T(8,128)(2,1)} %param.7, bf16[2,128,128]{2,1,0:T(8,128)(2,1)} %param.6), kind=kLoop, calls=%fused_computation | loop fusion | flops 65536 | bytes 262144 | tf_op jit(solution)/shard_map/concatenate | solution.py:397
  3.2 0.0 copy-start
  3.2 0.0 copy-start.1
  3.2 0.0 collective-permute-done.2.other_tails_ref.refs_2_
  3.3 0.0 collective-permute-done.key_ref.refs_0_
  3.3 0.2 collective-permute-done.1.value_ref.refs_1_
  3.5 2.9 %collective-permute-start.3 = (bf16[272,128]{1,0:T(8,128)(2,1)S(1)}, bf16[272,128]{1,0:T(8,128)(2,1)S(1)}, u32[]{:S(2)}, u32[]{:S(2)}) collective-permute-start(bf16[272,128]{1,0:T(8,128)(2,1)S(1)} %pack.1.refs_3_.refs_6_), channel_id=1, source_target_pairs={{4,0},{0,4},{6,2},{2,6},{5,3},{7,5},{1,7},{3,1},{12,8},{8,12},{14,... | collective-permute-start | bytes 208904 | tf_op jit(solution)/shard_map/ppermute | solution.py:430
  6.4 1.5 %collective-permute-start.4 = (bf16[272,128]{1,0:T(8,128)(2,1)S(1)}, bf16[272,128]{1,0:T(8,128)(2,1)S(1)}, u32[]{:S(2)}, u32[]{:S(2)}) collective-permute-start(bf16[272,128]{1,0:T(8,128)(2,1)S(1)} %pack.1.refs_3_.refs_6_), channel_id=1, source_target_pairs={{0,2},{1,3},{2,0},{3,1},{4,6},{5,7},{6,4},{7,5},{8,10},{9,11},{10,... | collective-permute-start | bytes 208904 | tf_op jit(solution)/shard_map/ppermute | solution.py:388
  7.9 0.0 copy-done.1
  7.9 0.7 %early.2 = (bf16[1024,128]{1,0:T(8,128)(2,1)S(1)}, bf16[1024,128]{1,0:T(8,128)(2,1)S(1)}, f32[256,1024]{1,0:T(8,128)S(1)}, f32[256,1024]{1,0:T(8,128)S(1)}, f32[16,1024]{1,0:T(8,128)S(1)}) custom-call(bf16[2,128,1024]{2,1,0:T(8,128)(2,1)S(1)} %copy-done, bf16[2,128,1024]{2,1,0:T(8,128)(2,1)S(1)} %copy-done.1, ...), custom_call_target="tpu_custom_call" | custom-call | flops 134217728 | bytes 1048576 | tf_op jit(solution)/shard_map/early/pallas_call | solution.py:52
  8.6 0.1 collective-permute-done.3.refs_7_
  8.7 0.0 collective-permute-start.5
  8.7 0.9 %early.3 = (bf16[1024,128]{1,0:T(8,128)(2,1)S(1)}, bf16[1024,128]{1,0:T(8,128)(2,1)S(1)}, f32[384,1024]{1,0:T(8,128)S(1)}, f32[384,1024]{1,0:T(8,128)S(1)}, f32[...) custom-call(bf16[2,128,1024]{2,1,0:T(8,128)(2,1)S(1)} %copy-done, bf16[2,128,1024]{2,1,0:T(8,128)(2,1)S(1)} %copy-done.1, ...), custom_call_target="tpu_custom_call" | custom-call | flops 201326592 | bytes 1048576 | tf_op jit(solution)/shard_map/early/pallas_call | solution.py:52
  9.7 1.6 %collective-permute-done.4.refs_8_ = bf16[272,128]{1,0:T(8,128)(2,1)S(1)} collective-permute-done((bf16[272,128]{1,0:T(8,128)(2,1)S(1)}, bf16[272,128]{1,0:T(8,128)(2,1)S(1)}, u32[]{:S(2)}, u32[]{:S(2)}) %collective-permute-start.4) | collective-permute-done | bytes 69664 | tf_op jit(solution)/shard_map/ppermute | solution.py:388
  11.3 0.0 collective-permute-done.5.refs_9_
  11.3 2.0 %middle.1 = (bf16[256,2048]{1,0:T(8,128)(2,1)S(1)}, f32[8,2048]{1,0:T(8,128)S(1)}, bf16[128,256]{1,0:T(8,128)(2,1)S(1)}, bf16[384,128]{1,0:T(8,128)(2,1)S(1)}, f32[384,128]{1,0:T(8,128)S(1)}) custom-call(bf16[1024,128]{1,0:T(8,128)(2,1)S(1)} %get-tuple-element.54.refs_0_, bf16[1024,128]{1,0:T(8,128)(2,1)S(1)} %get-tuple-element.56.refs_1_, ...), custom_call_target="tpu_custom_call" | custom-call | flops 536870912 | bytes 1048576 | tf_op jit(solution)/shard_map/middle/pallas_call | solution.py:52
  13.3 0.1 collective-permute-start.6
  13.4 1.0 %local.1 = (bf16[384,2048]{1,0:T(8,128)(2,1)S(1)}, bf16[256,128]{1,0:T(8,128)(2,1)S(1)}, f32[256,128]{1,0:T(8,128)S(1)}, f32[256,128]{1,0:T(8,128)S(1)}) custom-call(bf16[1024,128]{1,0:T(8,128)(2,1)S(1)} %get-tuple-element.54.refs_0_, bf16[1024,128]{1,0:T(8,128)(2,1)S(1)} %get-tuple-element.56.refs_1_, bf16[1024,128]{1,0:T(8,128)(2,1)S(1)} %get-tuple-element.57.refs_2_, ...), custom_call_target="tpu_custom_call" | custom-call | flops 402653184 | bytes 1048576 | tf_op jit(solution)/shard_map/local/pallas_call | solution.py:52
  14.4 0.3 %collective-permute-done.6.other_ref.after_ref = bf16[384,128]{1,0:T(8,128)(2,1)S(1)} collective-permute-done((bf16[384,128]{1,0:T(8,128)(2,1)S(1)}, bf16[384,128]{1,0:T(8,128)(2,1)S(1)}, u32[]{:S(2)}, u32[]{:S(2)}) %collective-permute-start.6) | collective-permute-done | bytes 98336 | tf_op jit(solution)/shard_map/ppermute | solution.py:388
  14.7 0.7 %collective-permute-start.7 = (bf16[256,128]{1,0:T(8,128)(2,1)S(1)}, bf16[256,128]{1,0:T(8,128)(2,1)S(1)}, u32[]{:S(2)}, u32[]{:S(2)}) collective-permute-start(bf16[256,128]{1,0:T(8,128)(2,1)S(1)} %pair.3), channel_id=1, source_target_pairs={{0,4},{4,0},{2,6},{6,2},{3,5},{5,7},{7,1},{1,3},{8,12},{12,8},{10,... | collective-permute-start | bytes 196616 | tf_op jit(solution)/shard_map/ppermute | solution.py:485
  15.4 2.2 %collective-permute-start.8 = (bf16[128,128]{1,0:T(8,128)(2,1)S(1)}, bf16[128,128]{1,0:T(8,128)(2,1)S(1)}, u32[]{:S(2)}, u32[]{:S(2)}) collective-permute-start(bf16[128,128]{1,0:T(8,128)(2,1)S(1)} %pair.2.after_ref), channel_id=1, source_target_pairs={{0,2},{1,3},{2,0},{3,1},{4,6},{5,7},{6,4},{7,5},{8,10},{9,11},{10,... | collective-permute-start | bytes 98312 | tf_op jit(solution)/shard_map/ppermute | solution.py:388
  17.7 1.4 %late.1 = bf16[2,128,1024]{2,1,0:T(8,128)(2,1)} custom-call(bf16[256,2048]{1,0:T(8,128)(2,1)S(1)} %get-tuple-element.62.ds_ref, bf16[384,2048]{1,0:T(8,128)(2,1)S(1)} %get-tuple-element.73.local_ref, bf16[128,256]{1,0:T(8,128)(2,1)S(1)} %get-tuple-element.74.keys_t, bf16[384,128]{1,0:T(8,128)(2,1)S(1)} %get-tuple-element.75.keys_s), custom_call_target="tpu_custom_call" | custom-call | flops 335544320 | bytes 1048576 | tf_op jit(solution)/shard_map/late/pallas_call | solution.py:52
  19.1 0.6 %collective-permute-done.7.arrived_ref = bf16[256,128]{1,0:T(8,128)(2,1)S(1)} collective-permute-done((bf16[256,128]{1,0:T(8,128)(2,1)S(1)}, bf16[256,128]{1,0:T(8,128)(2,1)S(1)}, u32[]{:S(2)}, u32[]{:S(2)}) %collective-permute-start.7) | collective-permute-done | bytes 65568 | tf_op jit(solution)/shard_map/ppermute | solution.py:485
  19.7 0.0 collective-permute-done.8.half_ref
  19.8 0.1 collective-permute-start.9
  19.8 1.2 %collective-permute-done.9.other_ref = bf16[256,128]{1,0:T(8,128)(2,1)S(1)} collective-permute-done((bf16[256,128]{1,0:T(8,128)(2,1)S(1)}, bf16[256,128]{1,0:T(8,128)(2,1)S(1)}, u32[]{:S(2)}, u32[]{:S(2)}) %collective-permute-start.9) | collective-permute-done | bytes 65568 | tf_op jit(solution)/shard_map/ppermute | solution.py:388
  21.1 0.7 %final.1 = (bf16[2,128,128]{2,1,0:T(8,128)(2,1)}, bf16[2,128,128]{2,1,0:T(8,128)(2,1)}) custom-call(bf16[256,128]{1,0:T(8,128)(2,1)S(1)} %get-tuple-element.79.leaf_ref, f32[256,128]{1,0:T(8,128)S(1)} %get-tuple-element.83.keep_ref, bf16[256,128]{1,0:T(8,128)(2,1)S(1)} %collective-permute-done.9.other_ref), custom_call_target="tpu_custom_call" | custom-call | bytes 1048576 | tf_op jit(solution)/shard_map/final/pallas_call | solution.py:52
  (5 shorter events, 0.1 us)
Async XLA Ops:
  1.4 1.9 %collective-permute-start.2 = (bf16[2,16,128]{2,1,0:T(8,128)(2,1)S(1)}, bf16[2,16,128]{2,1,0:T(8,128)(2,1)S(1)}, u32[]{:S(2)}, u32[]{:S(2)}) collective-permute-start(bf16[2,16,128]{2,1,0:T(8,128)(2,1)S(1)} %broadcast_in_dim.2.tails_ref), channel_id=1, source_target_pairs={{0,1},{1,0},{2,3},{3,2},{4,5},{5,4},{6,7},{7,6},{8,9},{9,8},{10,11... | collective-permute-start | bytes 24584 | tf_op jit(solution)/shard_map/ppermute | solution.py:388
  1.8 1.5 %collective-permute-start = (bf16[2,128,128]{2,1,0:T(8,128)(2,1)}, bf16[2,128,128]{2,1,0:T(8,128)(2,1)S(1)}, u32[]{:S(2)}, u32[]{:S(2)}) collective-permute-start(bf16[2,128,128]{2,1,0:T(8,128)(2,1)} %param.6), channel_id=1, source_target_pairs={{0,1},{1,0},{2,3},{3,2},{4,5},{5,4},{6,7},{7,6},{8,9},{9,8},{10,11... | collective-permute-start | bytes 196616 | tf_op jit(solution)/shard_map/ppermute | solution.py:388
  1.9 1.5 %collective-permute-start.1 = (bf16[2,128,128]{2,1,0:T(8,128)(2,1)}, bf16[2,128,128]{2,1,0:T(8,128)(2,1)S(1)}, u32[]{:S(2)}, u32[]{:S(2)}) collective-permute-start(bf16[2,128,128]{2,1,0:T(8,128)(2,1)} %param.7), channel_id=1, source_target_pairs={{0,1},{1,0},{2,3},{3,2},{4,5},{5,4},{6,7},{7,6},{8,9},{9,8},{10,11... | collective-permute-start | bytes 196616 | tf_op jit(solution)/shard_map/ppermute | solution.py:388
  3.2 4.7 %copy-start = (bf16[2,128,1024]{2,1,0:T(8,128)(2,1)S(1)}, bf16[2,128,1024]{2,1,0:T(8,128)(2,1)}, u32[]{:S(2)}) copy-start(bf16[2,128,1024]{2,1,0:T(8,128)(2,1)} %query_ref.3) | copy-start | bytes 1572868
  3.2 4.7 %copy-start.1 = (bf16[2,128,1024]{2,1,0:T(8,128)(2,1)S(1)}, bf16[2,128,1024]{2,1,0:T(8,128)(2,1)}, u32[]{:S(2)}) copy-start(bf16[2,128,1024]{2,1,0:T(8,128)(2,1)} %grad_ref.3) | copy-start | bytes 1572868
  3.5 5.2 %collective-permute-start.3 = (bf16[272,128]{1,0:T(8,128)(2,1)S(1)}, bf16[272,128]{1,0:T(8,128)(2,1)S(1)}, u32[]{:S(2)}, u32[]{:S(2)}) collective-permute-start(bf16[272,128]{1,0:T(8,128)(2,1)S(1)} %pack.1.refs_3_.refs_6_), channel_id=1, source_target_pairs={{4,0},{0,4},{6,2},{2,6},{5,3},{7,5},{1,7},{3,1},{12,8},{8,12},{14,... | collective-permute-start | bytes 208904 | tf_op jit(solution)/shard_map/ppermute | solution.py:430
  6.4 4.9 %collective-permute-start.4 = (bf16[272,128]{1,0:T(8,128)(2,1)S(1)}, bf16[272,128]{1,0:T(8,128)(2,1)S(1)}, u32[]{:S(2)}, u32[]{:S(2)}) collective-permute-start(bf16[272,128]{1,0:T(8,128)(2,1)S(1)} %pack.1.refs_3_.refs_6_), channel_id=1, source_target_pairs={{0,2},{1,3},{2,0},{3,1},{4,6},{5,7},{6,4},{7,5},{8,10},{9,11},{10,... | collective-permute-start | bytes 208904 | tf_op jit(solution)/shard_map/ppermute | solution.py:388
  8.7 2.6 %collective-permute-start.5 = (bf16[272,128]{1,0:T(8,128)(2,1)S(1)}, bf16[272,128]{1,0:T(8,128)(2,1)S(1)}, u32[]{:S(2)}, u32[]{:S(2)}) collective-permute-start(bf16[272,128]{1,0:T(8,128)(2,1)S(1)} %collective-permute-done.3.refs_7_), channel_id=1, source_target_pairs={{0,1},{1,0},{2,3},{3,2},{4,5},{5,4},{6,7},{7,6},{8,9},{9,8},{10,11... | collective-permute-start | bytes 208904 | tf_op jit(solution)/shard_map/ppermute | solution.py:388
  13.3 1.4 %collective-permute-start.6 = (bf16[384,128]{1,0:T(8,128)(2,1)S(1)}, bf16[384,128]{1,0:T(8,128)(2,1)S(1)}, u32[]{:S(2)}, u32[]{:S(2)}) collective-permute-start(bf16[384,128]{1,0:T(8,128)(2,1)S(1)} %get-tuple-element.63), channel_id=1, source_target_pairs={{0,1},{1,0},{2,3},{3,2},{4,5},{5,4},{6,7},{7,6},{8,9},{9,8},{10,11... | collective-permute-start | bytes 294920 | tf_op jit(solution)/shard_map/ppermute | solution.py:388
  14.7 5.0 %collective-permute-start.7 = (bf16[256,128]{1,0:T(8,128)(2,1)S(1)}, bf16[256,128]{1,0:T(8,128)(2,1)S(1)}, u32[]{:S(2)}, u32[]{:S(2)}) collective-permute-start(bf16[256,128]{1,0:T(8,128)(2,1)S(1)} %pair.3), channel_id=1, source_target_pairs={{0,4},{4,0},{2,6},{6,2},{3,5},{5,7},{7,1},{1,3},{8,12},{12,8},{10,... | collective-permute-start | bytes 196616 | tf_op jit(solution)/shard_map/ppermute | solution.py:485
  15.4 4.3 %collective-permute-start.8 = (bf16[128,128]{1,0:T(8,128)(2,1)S(1)}, bf16[128,128]{1,0:T(8,128)(2,1)S(1)}, u32[]{:S(2)}, u32[]{:S(2)}) collective-permute-start(bf16[128,128]{1,0:T(8,128)(2,1)S(1)} %pair.2.after_ref), channel_id=1, source_target_pairs={{0,2},{1,3},{2,0},{3,1},{4,6},{5,7},{6,4},{7,5},{8,10},{9,11},{10,... | collective-permute-start | bytes 98312 | tf_op jit(solution)/shard_map/ppermute | solution.py:388
  19.8 1.3 %collective-permute-start.9 = (bf16[256,128]{1,0:T(8,128)(2,1)S(1)}, bf16[256,128]{1,0:T(8,128)(2,1)S(1)}, u32[]{:S(2)}, u32[]{:S(2)}) collective-permute-start(bf16[256,128]{1,0:T(8,128)(2,1)S(1)} %get-tuple-element.84), channel_id=1, source_target_pairs={{0,1},{1,0},{2,3},{3,2},{4,5},{5,4},{6,7},{7,6},{8,9},{9,8},{10,11... | collective-permute-start | bytes 196616 | tf_op jit(solution)/shard_map/ppermute | solution.py:388
